TPU v7x, 32 devices: a whole 2x2x4 slice. The times are simulated.
32 devices in a mesh: table: 8 (over z, y), ctx: 4 (over x, core).
Axes of the slice: x: 2, y: 2, z: 4, core: 2. Of those that a mesh axis runs over, the one named last changes fastest.
Arguments:
- table: bfloat16 [16384, 512], P(('table', 'ctx')), may hold values from -6 to 6
- item_owner: int32 [8192, 2], P(('table', 'ctx')), may hold values from 0 to 31, as said below
- item_row: int32 [8192, 2], P(('table', 'ctx')), may hold values from 0 to 511
- segment_ids: int32 [8, 1024], P('table', 'ctx'), may hold values from 0 to 1, never falling along the last dimension, each value on 1 to 896 neighbouring positions
- w_in: bfloat16 [512, 2048], replicated, may hold values from -0.5 to 0.5
- w_out: bfloat16 [512, 512], replicated, may hold values from -0.25 to 0.25
- cotangent: bfloat16 [8192, 512], P(('table', 'ctx')), may hold values from -6 to 6
Outputs:
- layer_out: bfloat16 [8192, 512], P(('table', 'ctx'))
- row_grad: float32 [16384, 512], P(('table', 'ctx'))
Inputs may be any that keep to these rules, and one draw needn't show every extreme that they name: `item_owner`: among the 512 ids of one device's events no owner is named more than 32 times; one owner, the same for every device, is named exactly 32 times by every device.
All inputs are finite; a program needn't handle non-finite values.
Results may differ from a plain program's by a relative error of at most 0.0095.
Values may be sent and summed in bfloat16 or wider, within the bound.
No kernel may reach another device: no remote copies, remote signals or barrier semaphores. Data moves between devices by JAX's collectives and lax.ppermute only.
A program may use at most 64 MiB of HBM per device.

v0:
```python
import jax
import jax.numpy as jnp
from jax import lax
from jax.sharding import PartitionSpec as P

HEADS = 4
HEAD_DIM = 128
NIDS = 2


EPS = 1e-06


def silu_grad(values):
    sigma = jax.nn.sigmoid(values)
    return sigma * (1.0 + values * (1.0 - sigma))


def normalize(values):
    centred = values - jnp.mean(values, -1, keepdims=True)
    inverse = lax.rsqrt(jnp.mean(centred * centred, -1, keepdims=True) + EPS)
    return (centred * inverse, inverse)


def norm_back(grad_norm, normed, inverse):
    mean_grad = jnp.mean(grad_norm, -1, keepdims=True)
    mean_cross = jnp.mean(grad_norm * normed, -1, keepdims=True)
    return (grad_norm - mean_grad - normed * mean_cross) * inverse


def split_heads(values):
    return values.reshape(values.shape[0], HEADS, HEAD_DIM)


def visible(query_pos, query_seg, key_pos, key_seg):
    return (query_seg[:, None] == key_seg[None, :]) & (key_pos[None, :] <= query_pos[:, None])


def local(table, item_owner, item_row, segment_ids, w_in, w_out, cotangent):
    table_count = lax.axis_size("table")
    ctx_count = lax.axis_size("ctx")
    owners = table_count * ctx_count
    events = cotangent.shape[0]
    width = table.shape[1]
    id_count = events * NIDS
    capacity = 2 * ((id_count + owners - 1) // owners)
    scale = HEAD_DIM ** (-0.5)
    owner_flat = item_owner.reshape(-1)
    row_flat = item_row.reshape(-1)
    onehot = (owner_flat[:, None] == jnp.arange(owners, dtype=jnp.int32)[None, :]).astype(jnp.int32)
    earlier = jnp.cumsum(onehot, 0) - onehot
    ranks = jnp.sum(earlier * onehot, 1)
    slots = owner_flat * capacity + ranks
    wanted = jnp.zeros((owners * capacity,), jnp.int32).at[slots].set(row_flat)
    asked = lax.all_to_all(
        wanted.reshape(owners, capacity), ("table", "ctx"), split_axis=0, concat_axis=0, tiled=True
    )
    fetched = lax.all_to_all(
        table[asked], ("table", "ctx"), split_axis=0, concat_axis=0, tiled=True
    )
    picked = (
        fetched.reshape(owners * capacity, width)[slots]
        .astype(jnp.float32)
        .reshape(events, NIDS, width)
    )
    embedded = jnp.sum(picked, 1).astype(jnp.bfloat16)
    normed, inverse = normalize(embedded.astype(jnp.float32))
    before = jnp.dot(normed.astype(jnp.bfloat16), w_in, preferred_element_type=jnp.float32)
    proj = jax.nn.silu(before).astype(jnp.bfloat16)
    gate = proj[:, :width]
    values = proj[:, width : 2 * width]
    queries = proj[:, 2 * width : 3 * width]
    keys_in = proj[:, 3 * width :]
    own_pos = lax.axis_index("ctx") * events + jnp.arange(events, dtype=jnp.int32)
    own_seg = segment_ids.reshape(-1)
    key_piece = lax.all_gather(keys_in, "ctx", axis=0, tiled=True)
    value_piece = lax.all_gather(values, "ctx", axis=0, tiled=True)
    seg_piece = lax.all_gather(own_seg, "ctx", axis=0, tiled=True)
    count = key_piece.shape[0]
    key_pos = jnp.arange(count, dtype=jnp.int32)
    raw = (
        jnp.einsum(
            "qhd,khd->hqk",
            split_heads(queries),
            split_heads(key_piece),
            preferred_element_type=jnp.float32,
        )
        * scale
    )
    mask = visible(own_pos, own_seg, key_pos, seg_piece)[None]
    weights = jnp.where(mask, jax.nn.silu(raw), 0.0).astype(jnp.bfloat16)
    added = jnp.einsum(
        "hqk,khd->qhd", weights, split_heads(value_piece), preferred_element_type=jnp.float32
    )
    attended = added.reshape(events, width)
    att_norm, att_inverse = normalize(attended)
    mixed = (att_norm * gate.astype(jnp.float32)).astype(jnp.bfloat16)
    layer_out = (
        embedded.astype(jnp.float32) + jnp.dot(mixed, w_out, preferred_element_type=jnp.float32)
    ).astype(jnp.bfloat16)
    grad_mixed = jnp.dot(cotangent, w_out.T, preferred_element_type=jnp.float32)
    grad_gate = grad_mixed * att_norm
    grad_norm = grad_mixed * gate.astype(jnp.float32)
    grad_att = norm_back(grad_norm, att_norm, att_inverse).astype(jnp.bfloat16)
    key_piece = lax.all_gather(keys_in, "ctx", axis=0, tiled=True)
    value_piece = lax.all_gather(values, "ctx", axis=0, tiled=True)
    seg_piece = lax.all_gather(own_seg, "ctx", axis=0, tiled=True)
    count = key_piece.shape[0]
    key_pos = jnp.arange(count, dtype=jnp.int32)
    raw = (
        jnp.einsum(
            "qhd,khd->hqk",
            split_heads(queries),
            split_heads(key_piece),
            preferred_element_type=jnp.float32,
        )
        * scale
    )
    mask = visible(own_pos, own_seg, key_pos, seg_piece)[None]
    grad_weights = jnp.einsum(
        "qhd,khd->hqk",
        split_heads(grad_att),
        split_heads(value_piece),
        preferred_element_type=jnp.float32,
    )
    grad_raw = (jnp.where(mask, grad_weights * silu_grad(raw), 0.0) * scale).astype(jnp.bfloat16)
    added = jnp.einsum(
        "hqk,khd->qhd", grad_raw, split_heads(key_piece), preferred_element_type=jnp.float32
    )
    grad_queries = added.reshape(events, width)
    query_piece = lax.all_gather(queries, "ctx", axis=0, tiled=True)
    grad_piece = lax.all_gather(grad_att, "ctx", axis=0, tiled=True)
    seg_piece = lax.all_gather(own_seg, "ctx", axis=0, tiled=True)
    count = query_piece.shape[0]
    query_pos = jnp.arange(count, dtype=jnp.int32)
    raw = (
        jnp.einsum(
            "qhd,khd->hqk",
            split_heads(query_piece),
            split_heads(keys_in),
            preferred_element_type=jnp.float32,
        )
        * scale
    )
    mask = visible(query_pos, seg_piece, own_pos, own_seg)[None]
    weights = jnp.where(mask, jax.nn.silu(raw), 0.0).astype(jnp.bfloat16)
    grad_weights = jnp.einsum(
        "qhd,khd->hqk",
        split_heads(grad_piece),
        split_heads(values),
        preferred_element_type=jnp.float32,
    )
    grad_raw = (jnp.where(mask, grad_weights * silu_grad(raw), 0.0) * scale).astype(jnp.bfloat16)
    key_added = jnp.einsum(
        "hqk,qhd->khd", grad_raw, split_heads(query_piece), preferred_element_type=jnp.float32
    )
    value_added = jnp.einsum(
        "hqk,qhd->khd", weights, split_heads(grad_piece), preferred_element_type=jnp.float32
    )
    grad_keys = key_added.reshape(events, width)
    grad_values = value_added.reshape(events, width)
    joined = jnp.concatenate([grad_gate, grad_values, grad_queries, grad_keys], 1)
    grad_proj = (joined * silu_grad(before)).astype(jnp.bfloat16)
    grad_normed = jnp.dot(grad_proj, w_in.T, preferred_element_type=jnp.float32)
    grad_embedded = norm_back(grad_normed, normed, inverse) + cotangent.astype(jnp.float32)
    spread = jnp.broadcast_to(
        grad_embedded.reshape(events, 1, width), (events, NIDS, width)
    ).reshape(id_count, width)
    slot_grad = jnp.zeros((owners * capacity, width), jnp.float32).at[slots].set(spread)
    returned = lax.all_to_all(
        slot_grad.reshape(owners, capacity, width),
        ("table", "ctx"),
        split_axis=0,
        concat_axis=0,
        tiled=True,
    )
    row_grad = jax.ops.segment_sum(
        returned.reshape(owners * capacity, width), asked.reshape(-1), num_segments=table.shape[0]
    )
    return (layer_out, row_grad)


def solution(mesh):
    placed = (
        P(("table", "ctx"), None),
        P(("table", "ctx"), None),
        P(("table", "ctx"), None),
        P("table", "ctx"),
        P(),
        P(),
        P(("table", "ctx"), None),
    )
    return jax.shard_map(
        local,
        mesh=mesh,
        in_specs=placed,
        out_specs=(P(("table", "ctx"), None), P(("table", "ctx"), None)),
        check_vma=False,
    )
```

profile of v0, /device:TPU:0, one launch (start us, length us, event | category | flops | bytes accessed | tf_op | source)
XLA Modules:
  0.0 237.5 jit_solution(7931483103832293130)
XLA Ops:
  7.2 0.8 broadcast_multiply_fusion
  8.0 0.8 copy.22
  9.4 1.2 reduce-window.6
  10.9 0.8 copy.25
  12.0 2.4 %scatter_custom_fusion = s32[1024]{0:T(1024)S(1)} fusion(s32[512]{0:T(512)S(1)} %bitcast.117, s32[512]{0:T(512)S(1)} %reshape.334, s32[]{:T(128)} %constant.16.clone.1), kind=kCustom, calls=%fused_computation.84 | custom fusion | bytes 4100 | tf_op jit(solution)/shard_map/scatter | solution.py:54
  14.5 14.3 %all_to_all.22 = s32[32,1,32]{2,1,0:T(1,128)S(1)} all-to-all(s32[32,1,32]{2,1,0:T(1,128)S(1)} %all_to_all.14), channel_id=1, replica_groups=mesh['table'=8,'ctx'=4] {'table','ctx'}, dimensions={0} | all-to-all | bytes 8192 | tf_op jit(solution)/shard_map/all_to_all | solution.py:55
  28.9 5.1 %gather_fusion = bf16[1024,512]{1,0:T(8,128)(2,1)} fusion(bf16[512,512]{1,0:T(8,128)(2,1)S(1)} %copy-done.1, s32[1024]{0:T(1024)S(1)} %broadcast_clamp_fusion), kind=kCustom, calls=%fused_computation | custom fusion | bytes 2101248 | tf_op jit(solution)/shard_map/gather | solution.py:59
  33.9 2.6 %all-to-all-start.1 = ((bf16[32,32,512]{2,1,0:T(8,128)(2,1)}), bf16[32,32,512]{2,1,0:T(8,128)(2,1)S(1)}, u32[]{:S(2)}, u32[]{:S(2)}) async-start(bf16[32,32,512]{2,1,0:T(8,128)(2,1)} %bitcast.100), calls=%async_computation.1 | async-start | bytes 2097152 | tf_op jit(solution)/shard_map/all_to_all | solution.py:58
  36.6 26.2 %all-to-all-done.1 = bf16[32,32,512]{2,1,0:T(8,128)(2,1)S(1)} async-done(((bf16[32,32,512]{2,1,0:T(8,128)(2,1)}), bf16[32,32,512]{2,1,0:T(8,128)(2,1)S(1)}, u32[]{:S(2)}, u32[]{:S(2)}) %all-to-all-start.1) | async-done | bytes 1048608 | tf_op jit(solution)/shard_map/all_to_all | solution.py:58
  62.8 2.6 %gather_fusion.1 = bf16[512,512]{1,0:T(8,128)(2,1)} fusion(bf16[1024,512]{1,0:T(8,128)(2,1)S(1)} %bitcast.98, s32[1024]{0:T(1024)S(1)} %pad_clamp_fusion), kind=kCustom, calls=%fused_computation.1 | custom fusion | bytes 1050624 | tf_op jit(solution)/shard_map/gather | solution.py:62
  65.4 1.2 gather.10
  66.7 1.4 reduce_sum.97
  68.4 2.1 multiply_convert_fusion.2
  70.5 1.0 copy-done.4
  71.5 1.1 slice_bitcast_fusion
  72.7 0.7 all-gather.6.cloned.1.call-update
  73.5 5.1 %all-gather = s32[1,1024]{1,0:T(1,128)S(1)} all-gather(s32[1,256]{1,0:T(1,128)S(1)} %copy-done.10), channel_id=2, replica_groups=mesh['table'=8,'ctx'=4] {'ctx'}, dimensions={1}, use_global_device_ids=true | all-gather | bytes 5120 | tf_op jit(solution)/shard_map/all_gather | solution.py:78
  78.6 1.1 fusion.11
  79.9 8.6 %all-gather.8.cloned.1.call-done = bf16[1024,512]{1,0:T(8,128)(2,1)} async-done(((bf16[256,512]{1,0:T(8,128)(2,1)}), bf16[1024,512]{1,0:T(8,128)(2,1)}) %all-gather.8.cloned.1.call-update) | async-done | bytes 1048592 | tf_op jit(solution)/shard_map/all_gather | solution.py:76
  88.5 1.5 copy.47
  90.0 3.8 %fusion.44 = f32[4,256,1024]{2,1,0:T(8,128)} fusion(bf16[1024,4,128]{0,2,1:T(8,128)(2,1)S(1)} %bitcast.101, bf16[32,4,8,128]{3,2,1,0:T(8,128)(2,1)} %get-tuple-element.9), kind=kOutput, calls=%fused_computation.62 | convolution fusion | flops 268435456 | bytes 5505024 | tf_op jit(solution)/shard_map/qhd,khd->hqk/dot_general | solution.py:82
  93.8 13.1 %all-gather.6.cloned.1.call-done = bf16[1024,512]{1,0:T(8,128)(2,1)} async-done(((bf16[256,512]{1,0:T(8,128)(2,1)}), bf16[1024,512]{1,0:T(8,128)(2,1)}) %all-gather.6.cloned.1.call-update) | async-done | bytes 1048592 | tf_op jit(solution)/shard_map/all_gather | solution.py:77
  106.8 2.3 copy.41
  109.1 4.7 %fusion.74 = (f32[256]{0:T(256)S(1)}, f32[4,128,256]{2,1,0:T(8,128)}) fusion(bf16[1024,4,128]{0,2,1:T(8,128)(2,1)} %bitcast.106, f32[4,256,1024]{2,1,0:T(8,128)} %fusion.44, pred[256,1024]{1,0:T(8,128)(4,1)} %fusion.11), kind=kOutput, calls=%fused_computation.113 | convolution fusion | flops 275906304 | bytes 6030336 | tf_op jit(solution)/shard_map/hqk,khd->qhd/dot_general | solution.py:92
  113.8 1.3 copy.42
  115.2 1.2 fusion.30
  116.4 1.7 fusion.52
  118.0 2.1 fusion.33
  120.2 0.9 fusion.12
  121.1 0.8 copy.45
  122.0 6.5 %fusion.3 = f32[4,128,256]{2,1,0:T(8,128)} fusion(bf16[1024,4,128]{0,2,1:T(8,128)(2,1)} %bitcast.102, f32[4,256,1024]{2,1,0:T(8,128)} %fusion.44, bf16[1024,4,128]{0,2,1:T(8,128)(2,1)} %bitcast.107, pred[256,1024]{1,0:T(8,128)(4,1)S(1)} %copy-done.9, bf16[256,512]{1,0:T(8,128)(2,1)} %get-tuple-element.7), kind=kOutput, calls=%fused_computation.17 | convolution fusion | flops 549453824 | bytes 7340032 | tf_op jit(solution)/shard_map/hqk,khd->qhd/dot_general | solution.py:127
  128.5 2.0 copy.44
  130.5 2.3 copy.48
  132.8 3.9 %fusion.41 = f32[4,1024,256]{2,1,0:T(8,128)} fusion(bf16[1024,4,128]{0,2,1:T(8,128)(2,1)} %bitcast.103, bf16[32,4,8,128]{3,2,1,0:T(8,128)(2,1)S(1)} %copy-done.7), kind=kOutput, calls=%fused_computation.59 | convolution fusion | flops 268435456 | bytes 5505024 | tf_op jit(solution)/shard_map/qhd,khd->hqk/dot_general | solution.py:137
  136.8 6.6 %all-gather.10.cloned.1.call-done = bf16[1024,512]{1,0:T(8,128)(2,1)} async-done(((bf16[256,512]{1,0:T(8,128)(2,1)}), bf16[1024,512]{1,0:T(8,128)(2,1)}) %all-gather.10.cloned.1.call-update) | async-done | bytes 1048592 | tf_op jit(solution)/shard_map/all_gather | solution.py:132
  143.3 4.0 %fusion.2 = f32[4,128,256]{2,1,0:T(8,128)S(1)} fusion(f32[4,1024,256]{2,1,0:T(8,128)} %fusion.41, pred[1024,256]{1,0:T(8,128)(4,1)} %fusion.12, bf16[1024,512]{1,0:T(8,128)(2,1)} %all-gather.10.cloned.1.call-done), kind=kOutput, calls=%fused_computation.16 | convolution fusion | flops 275775488 | bytes 6029312 | tf_op jit(solution)/shard_map/hqk,qhd->khd/dot_general | solution.py:157
  147.4 1.0 copy.43
  148.3 6.2 %fusion.4 = f32[4,128,256]{2,1,0:T(8,128)} fusion(bf16[1024,4,128]{0,2,1:T(8,128)(2,1)} %bitcast.104, f32[4,1024,256]{2,1,0:T(8,128)} %fusion.41, bf16[256,4,128]{0,2,1:T(8,128)(2,1)} %bitcast.111, pred[1024,256]{1,0:T(8,128)(4,1)} %fusion.12, bf16[1024,512]{1,0:T(8,128)(2,1)} %all-gather.10.cloned.1.call-done), kind=kOutput, calls=%fused_computation.18 | convolution fusion | flops 549453824 | bytes 7340032 | tf_op jit(solution)/shard_map/hqk,qhd->khd/dot_general | solution.py:154
  154.5 2.0 copy.46
  156.6 3.2 %fusion.73 = (f32[256]{0:T(256)S(1)}, f32[256]{0:T(256)S(1)}, f32[256,512]{1,0:T(8,128)S(1)}) fusion(f32[256]{0:T(256)S(1)} %add_rsqrt_fusion.1, f32[256]{0:T(256)S(1)} %broadcast_multiply_fusion.6, bf16[256,512]{1,0:T(8,128)(2,1)S(1)} %reduce_sum.97, bf16[512,2048]{1,0:T(8,128)(2,1)S(1)} %copy-done, f32[256,512]{1,0:T(8,128)} %copy.46, ...), kind=kOutput, calls=%fused_computation.112 | convolution fusion | flops 543948288 | bytes 7081984 | tf_op jit(solution)/shard_map/dot_general | solution.py:164
  160.1 1.3 broadcast_in_dim.78
  161.4 3.0 %reshape.342 = f32[512,512]{1,0:T(8,128)} reshape(f32[256,2,512]{2,1,0:T(2,128)} %broadcast_in_dim.78) | data formatting | bytes 2097152 | tf_op jit(solution)/shard_map/reshape | solution.py:168
  164.4 4.3 %scatter_custom_fusion.1 = f32[1024,512]{1,0:T(8,128)} fusion(s32[512]{0:T(512)S(1)} %bitcast.119, f32[512,512]{1,0:T(8,128)} %reshape.342, f32[]{:T(128)} %constant.22.clone.1), kind=kCustom, calls=%fused_computation.24 | custom fusion | bytes 2097664 | tf_op jit(solution)/shard_map/scatter | solution.py:169
  168.7 5.0 %all-to-all-start.2 = ((f32[32,32,512]{2,1,0:T(8,128)}), f32[32,32,512]{2,1,0:T(8,128)}, u32[]{:S(2)}, u32[]{:S(2)}) async-start(f32[32,32,512]{2,1,0:T(8,128)} %bitcast.99), calls=%async_computation.2 | async-start | bytes 4194304 | tf_op jit(solution)/shard_map/all_to_all | solution.py:170
  174.3 0.7 reduce.9
  175.0 2.0 fusion.5
  177.0 45.5 %all-to-all-done.2 = f32[32,32,512]{2,1,0:T(8,128)} async-done(((f32[32,32,512]{2,1,0:T(8,128)}), f32[32,32,512]{2,1,0:T(8,128)}, u32[]{:S(2)}, u32[]{:S(2)}) %all-to-all-start.2) | async-done | bytes 2097184 | tf_op jit(solution)/shard_map/all_to_all | solution.py:170
  222.5 8.5 %scatter_custom_fusion.2 = f32[512,512]{1,0:T(8,128)} fusion(s32[1024]{0:T(1024)S(1)} %reshape.348, f32[1024,512]{1,0:T(8,128)} %bitcast.19, f32[]{:T(128)} %constant.22.clone.1), kind=kCustom, calls=%fused_computation.52 | custom fusion | flops 524288 | bytes 1049088 | tf_op jit(solution)/shard_map/scatter-add | solution.py:177
  (58 shorter events, 2.9 us)
Async XLA Ops:
  7.2 61.2 %copy-start = (bf16[512,2048]{1,0:T(8,128)(2,1)S(1)}, bf16[512,2048]{1,0:T(8,128)(2,1)}, u32[]{:S(2)}) copy-start(bf16[512,2048]{1,0:T(8,128)(2,1)} %param.11) | copy-start | bytes 6291460
  7.2 21.7 %copy-start.1 = (bf16[512,512]{1,0:T(8,128)(2,1)S(1)}, bf16[512,512]{1,0:T(8,128)(2,1)}, u32[]{:S(2)}) copy-start(bf16[512,512]{1,0:T(8,128)(2,1)} %param.7) | copy-start | bytes 1572868
  33.9 28.9 %all-to-all-start.1 = ((bf16[32,32,512]{2,1,0:T(8,128)(2,1)}), bf16[32,32,512]{2,1,0:T(8,128)(2,1)S(1)}, u32[]{:S(2)}, u32[]{:S(2)}) async-start(bf16[32,32,512]{2,1,0:T(8,128)(2,1)} %bitcast.100), calls=%async_computation.1 | async-start | bytes 2097152 | tf_op jit(solution)/shard_map/all_to_all | solution.py:58
  36.6 51.9 %all-gather.8.cloned.1.call-start = ((), (), s32[]{:S(2)}) async-start(), calls=%async_computation.4 | async-start | bytes 1310720 | tf_op jit(solution)/shard_map/all_gather | solution.py:76
  68.4 5.1 %copy-start.10 = (s32[1,256]{1,0:T(1,128)S(1)}, s32[1,256]{1,0:T(1,128)}, u32[]{:S(2)}) copy-start(s32[1,256]{1,0:T(1,128)} %param.10) | copy-start | bytes 3076
  70.5 1.0 copy-start.4
  72.7 34.1 %all-gather.6.cloned.1.call-start = ((), (), s32[]{:S(2)}) async-start(), calls=%async_computation.3 | async-start | bytes 1310720 | tf_op jit(solution)/shard_map/all_gather | solution.py:77
  73.4 57.1 %all-gather.12.cloned.1.call-start = ((), (), s32[]{:S(2)}) async-start(), calls=%async_computation.6 | async-start | bytes 1310720 | tf_op jit(solution)/shard_map/all_gather | solution.py:131
  79.7 63.7 %all-gather.10.cloned.1.call-start = ((), (), s32[]{:S(2)}) async-start(), calls=%async_computation.5 | async-start | bytes 1310720 | tf_op jit(solution)/shard_map/all_gather | solution.py:132
  90.0 23.8 %copy-start.2 = (bf16[1024,512]{0,1:T(8,128)(2,1)}, bf16[1024,512]{0,1:T(8,128)(2,1)S(1)}, u32[]{:S(2)}) copy-start(bf16[1024,512]{0,1:T(8,128)(2,1)S(1)} %copy.47) | copy-start | bytes 3145732
  113.8 7.3 %copy-start.3 = (bf16[256,512]{1,0:T(8,128)(2,1)S(1)}, bf16[256,512]{1,0:T(8,128)(2,1)}, u32[]{:S(2)}) copy-start(bf16[256,512]{1,0:T(8,128)(2,1)} %get-tuple-element.12) | copy-start | bytes 786436
  113.8 8.1 %copy-start.9 = (pred[256,1024]{1,0:T(8,128)(4,1)S(1)}, pred[256,1024]{1,0:T(8,128)(4,1)}, u32[]{:S(2)}) copy-start(pred[256,1024]{1,0:T(8,128)(4,1)} %fusion.11) | copy-start | bytes 786436
  122.0 10.9 %copy-start.7 = (bf16[32,4,8,128]{3,2,1,0:T(8,128)(2,1)S(1)}, bf16[32,4,8,128]{3,2,1,0:T(8,128)(2,1)}, u32[]{:S(2)}) copy-start(bf16[32,4,8,128]{3,2,1,0:T(8,128)(2,1)} %get-tuple-element.8) | copy-start | bytes 786436
  148.3 8.2 %copy-start.8 = (f32[256,512]{1,0:T(8,128)S(1)}, f32[256,512]{1,0:T(8,128)}, u32[]{:S(2)}) copy-start(f32[256,512]{1,0:T(8,128)} %copy.44) | copy-start | bytes 1572868
  156.6 3.2 %copy-start.6 = (bf16[256,512]{1,0:T(8,128)(2,1)S(1)}, bf16[256,512]{1,0:T(8,128)(2,1)}, u32[]{:S(2)}) copy-start(bf16[256,512]{1,0:T(8,128)(2,1)} %param.13) | copy-start | bytes 786436
  161.4 13.6 %copy-start.5 = (bf16[512,512]{1,0:T(8,128)(2,1)S(1)}, bf16[512,512]{1,0:T(8,128)(2,1)}, u32[]{:S(2)}) copy-start(bf16[512,512]{1,0:T(8,128)(2,1)} %param.12) | copy-start | bytes 1572868
  168.7 53.8 %all-to-all-start.2 = ((f32[32,32,512]{2,1,0:T(8,128)}), f32[32,32,512]{2,1,0:T(8,128)}, u32[]{:S(2)}, u32[]{:S(2)}) async-start(f32[32,32,512]{2,1,0:T(8,128)} %bitcast.99), calls=%async_computation.2 | async-start | bytes 4194304 | tf_op jit(solution)/shard_map/all_to_all | solution.py:170
Sparse Core Ops, SparseCore 0:
  72.8 15.6 all-gather.7
  90.1 16.7 all-gather.5
  108.4 16.7 all-gather.11
  126.6 16.7 all-gather.9
where the time goes:
time: 238 us
  waiting for transfers between devices  101 us (42%)
  local copies, waits for them, and re-layouts  38.7 us (16%)
  matrix products  38.2 us (16%)
  blocking collectives  19.3 us (8%)
  other arithmetic  18.6 us (8%)
  between operations  14 us (6%)
  starting transfers between devices  7.98 us (3%)
    all_to_all x1, waiting for transfers between devices, local(): lax.all_to_all(slot_grad.reshape(owners, capacity, width), ('table', 'ctx...  45.5 us
    all_to_all x1, waiting for transfers between devices, local(): lax.all_to_all(table[asked], ('table', 'ctx'), split_axis=0, concat_axis=...  26.2 us
    all_to_all x1, blocking collectives, local(): lax.all_to_all(wanted.reshape(owners, capacity), ('table', 'ctx'), split_...  14.3 us
    all_gather x1, waiting for transfers between devices, local(): value_piece = lax.all_gather(values, 'ctx', axis=0, tiled=True)  13.1 us
    all_gather x1, waiting for transfers between devices, local(): key_piece = lax.all_gather(keys_in, 'ctx', axis=0, tiled=True)  8.61 us
    scatter-add x1, other arithmetic, local(): jax.ops.segment_sum(returned.reshape(owners * capacity, width), asked.res...  8.47 us
    reshape x4, local copies, waits for them, and re-layouts, split_heads(): return values.reshape(values.shape[0], HEADS, HEAD_DIM)  6.85 us
    all_gather x1, waiting for transfers between devices, local(): grad_piece = lax.all_gather(grad_att, 'ctx', axis=0, tiled=True)  6.57 us
  transfers between devices with their start and end apart: 6, of which 5 were waited for; matrix products, arithmetic and copies ran while one was open for 17% of the time, Pallas kernels for 0%

commit v1 on v0

v1 whole, which is shorter than its diff:
```python
import functools

import jax
import jax.numpy as jnp
from jax import lax
from jax.experimental import pallas as pl
from jax.experimental.pallas import tpu as pltpu
from jax.sharding import PartitionSpec as P

HEADS = 4
HEAD_DIM = 128
NIDS = 2
EPS = 1e-06
VMEM_LIMIT = 50 * 1024 * 1024

F32 = jnp.float32
BF16 = jnp.bfloat16


def dot(a, b):
    return jnp.dot(a, b, preferred_element_type=F32)


def dot_nt(a, b):
    return lax.dot_general(a, b, (((1,), (1,)), ((), ())), preferred_element_type=F32)


def iota(shape, dim):
    return lax.broadcasted_iota(jnp.int32, shape, dim)


def normalize(values):
    centred = values - jnp.mean(values, -1, keepdims=True)
    inverse = lax.rsqrt(jnp.mean(centred * centred, -1, keepdims=True) + EPS)
    return centred * inverse, inverse


def norm_back(grad_norm, normed, inverse):
    mean_grad = jnp.mean(grad_norm, -1, keepdims=True)
    mean_cross = jnp.mean(grad_norm * normed, -1, keepdims=True)
    return (grad_norm - mean_grad - normed * mean_cross) * inverse


def split_exact(values):
    return (values >> 4).astype(F32).astype(BF16), (values & 15).astype(F32).astype(BF16)


def slots_kernel(capacity, owner_ref, row_ref, slots_ref, wanted_ref):
    events = owner_ref.shape[1]
    owners = wanted_ref.shape[0]
    owner = jnp.concatenate([owner_ref[k : k + 1, :] for k in range(NIDS)], 1)
    row = jnp.concatenate([row_ref[k : k + 1, :] for k in range(NIDS)], 1)
    ids = owner.shape[1]
    named = iota((owners, ids), 0) == owner
    named_f = jnp.where(named, 1.0, 0.0)
    before = jnp.where(iota((ids, ids), 0) < iota((ids, ids), 1), 1.0, 0.0).astype(BF16)
    earlier = dot(named_f.astype(BF16), before)
    rank = jnp.sum(earlier * named_f, 0, keepdims=True).astype(jnp.int32)
    slot = owner * capacity + rank
    slots_ref[...] = jnp.full(slots_ref.shape, -1, jnp.int32)
    for k in range(NIDS):
        slots_ref[k : k + 1, :] = slot[:, k * events : (k + 1) * events]
    ranked = jnp.where(iota((capacity, ids), 0) == rank, 1.0, 0.0).astype(BF16)
    high, low = (row >> 4).astype(F32), (row & 15).astype(F32)
    wanted = 16.0 * dot_nt((named_f * high).astype(BF16), ranked) + dot_nt(
        (named_f * low).astype(BF16), ranked
    )
    wanted_ref[...] = wanted.astype(jnp.int32)


def select_kernel(asked_ref, table_ref, out_ref):
    owners, capacity = asked_ref.shape
    rows = table_ref.shape[0]
    slots = owners * capacity
    high, low = split_exact(asked_ref[...])
    source = jnp.where(
        iota((slots, owners), 0) // capacity == iota((slots, owners), 1), 1.0, 0.0
    ).astype(BF16)
    spread = 16.0 * dot(source, high) + dot(source, low)
    mine = iota((slots, capacity), 0) % capacity == iota((slots, capacity), 1)
    asked = jnp.sum(jnp.where(mine, spread, 0.0), 1, keepdims=True).astype(jnp.int32)
    chosen = jnp.where(iota((slots, rows), 1) == asked, 1.0, 0.0).astype(BF16)
    out_ref[...] = dot(chosen, table_ref[...]).astype(BF16)


def embed_kernel(slots_ref, fetched_ref, out_ref):
    events = out_ref.shape[0]
    slots = fetched_ref.shape[0]
    column = jnp.transpose(slots_ref[...])
    lane = iota((events, slots), 1)
    hit = lane == column[:, 0:1]
    for k in range(1, NIDS):
        hit = hit | (lane == column[:, k : k + 1])
    picked = jnp.where(hit, 1.0, 0.0).astype(BF16)
    out_ref[...] = dot(picked, fetched_ref[...]).astype(BF16)


def collect_kernel(asked_ref, returned_ref, out_ref):
    owners, capacity = asked_ref.shape
    rows = out_ref.shape[0]
    slots = owners * capacity
    high, low = split_exact(asked_ref[...])
    place = jnp.where(
        iota((capacity, slots), 1) % capacity == iota((capacity, slots), 0), 1.0, 0.0
    ).astype(BF16)
    spread = 16.0 * dot(high, place) + dot(low, place)
    mine = iota((owners, slots), 1) // capacity == iota((owners, slots), 0)
    asked = jnp.sum(jnp.where(mine, spread, 0.0), 0, keepdims=True).astype(jnp.int32)
    chosen = jnp.where(iota((rows, slots), 0) == asked, 1.0, 0.0).astype(BF16)
    out_ref[...] = dot(chosen, returned_ref[...])


def layer_kernel(count, *refs):
    index_ref = refs[0]
    slots_ref = refs[1]
    emb_refs = refs[2 : 2 + count]
    cot_refs = refs[2 + count : 2 + 2 * count]
    seg_refs = refs[2 + 2 * count : 2 + 3 * count]
    w_in_ref, w_out_ref = refs[2 + 3 * count : 4 + 3 * count]
    out_ref, grad_ref = refs[4 + 3 * count : 6 + 3 * count]
    (
        proj_ref,
        slope_ref,
        cot_ref,
        segc_ref,
        segr_ref,
        att_ref,
        gatt_ref,
        join_ref,
    ) = refs[6 + 3 * count :]
    events, width = out_ref.shape
    half_scale = 0.5 * HEAD_DIM ** (-0.5)
    scale = HEAD_DIM ** (-0.5)
    own = index_ref[0]

    for t in range(count):
        place = index_ref[t]
        normed, _ = normalize(emb_refs[t][...].astype(F32))
        normed = normed.astype(BF16)
        for block in range(4):
            columns = slice(block * width, (block + 1) * width)
            before = dot(normed, w_in_ref[:, columns])
            half = 0.5 * before
            bend = jnp.tanh(half)
            value = half + half * bend
            proj_ref[place, :, columns] = value.astype(BF16)
            if t == 0:
                sigma = 0.5 + 0.5 * bend
                slope_ref[:, columns] = sigma + value - value * sigma
        cot_ref[place] = cot_refs[t][...]
        seg = jnp.broadcast_to(seg_refs[t][...], (8, events))
        segr_ref[place] = seg
        segc_ref[place] = jnp.broadcast_to(jnp.transpose(seg)[:, 0:1], segc_ref.shape[1:])

    def head(part, h):
        return slice(part * width + h * HEAD_DIM, part * width + (h + 1) * HEAD_DIM)

    def forward(i, _):
        att_ref[...] = jnp.zeros_like(att_ref)

        def pair(j, _):
            mask = (segc_ref[i][:, 0:1] == segr_ref[j][0:1, :]) & (
                iota((events, events), 0) + (i - j) * events >= iota((events, events), 1)
            )
            for h in range(HEADS):
                raw = dot_nt(proj_ref[i, :, head(2, h)], proj_ref[j, :, head(3, h)])
                half = raw * half_scale
                value = half + half * jnp.tanh(half)
                weights = jnp.where(mask, value, 0.0).astype(BF16)
                columns = slice(h * HEAD_DIM, (h + 1) * HEAD_DIM)
                att_ref[:, columns] += dot(weights, proj_ref[j, :, head(1, h)])
            return 0

        lax.fori_loop(0, i + 1, pair, 0)
        att_norm, att_inverse = normalize(att_ref[...])
        gate = proj_ref[i, :, 0:width].astype(F32)
        grad_mixed = dot_nt(cot_ref[i], w_out_ref[...])
        grad_norm = grad_mixed * gate
        gatt_ref[i] = norm_back(grad_norm, att_norm, att_inverse).astype(BF16)

        @pl.when(i == own)
        def _():
            mixed = (att_norm * gate).astype(BF16)
            out_ref[...] = (emb_refs[0][...].astype(F32) + dot(mixed, w_out_ref[...])).astype(BF16)
            join_ref[:, 0:width] = grad_mixed * att_norm

        return 0

    lax.fori_loop(own, count, forward, 0)
    join_ref[:, width:] = jnp.zeros((events, 3 * width), F32)

    def query_side(j, _):
        mask = (segc_ref[own][:, 0:1] == segr_ref[j][0:1, :]) & (
            iota((events, events), 0) + (own - j) * events >= iota((events, events), 1)
        )
        for h in range(HEADS):
            keys = proj_ref[j, :, head(3, h)]
            raw = dot_nt(proj_ref[own, :, head(2, h)], keys)
            half = raw * half_scale
            bend = jnp.tanh(half)
            value = half + half * bend
            sigma = 0.5 + 0.5 * bend
            slope = sigma + value - value * sigma
            columns = slice(h * HEAD_DIM, (h + 1) * HEAD_DIM)
            grad_weights = dot_nt(gatt_ref[own, :, columns], proj_ref[j, :, head(1, h)])
            grad_raw = jnp.where(mask, grad_weights * slope * scale, 0.0).astype(BF16)
            join_ref[:, head(2, h)] += dot(grad_raw, keys)
        return 0

    lax.fori_loop(0, own + 1, query_side, 0)

    def key_side(i, _):
        mask = (segc_ref[own][:, 0:1] == segr_ref[i][0:1, :]) & (
            iota((events, events), 0) <= iota((events, events), 1) + (i - own) * events
        )
        for h in range(HEADS):
            queries = proj_ref[i, :, head(2, h)]
            raw = dot_nt(proj_ref[own, :, head(3, h)], queries)
            half = raw * half_scale
            bend = jnp.tanh(half)
            value = half + half * bend
            sigma = 0.5 + 0.5 * bend
            slope = sigma + value - value * sigma
            columns = slice(h * HEAD_DIM, (h + 1) * HEAD_DIM)
            grad_att = gatt_ref[i, :, columns]
            grad_weights = dot_nt(proj_ref[own, :, head(1, h)], grad_att)
            grad_raw = jnp.where(mask, grad_weights * slope * scale, 0.0).astype(BF16)
            weights = jnp.where(mask, value, 0.0).astype(BF16)
            join_ref[:, head(3, h)] += dot(grad_raw, queries)
            join_ref[:, head(1, h)] += dot(weights, grad_att)
        return 0

    lax.fori_loop(own, count, key_side, 0)

    grad_proj = (join_ref[...] * slope_ref[...]).astype(BF16)
    grad_normed = dot_nt(grad_proj, w_in_ref[...])
    normed, inverse = normalize(emb_refs[0][...].astype(F32))
    grad = norm_back(grad_normed, normed, inverse) + cot_refs[0][...].astype(F32)
    slot = iota((grad_ref.shape[0], events), 0)
    hit = slot == slots_ref[0:1, :]
    for k in range(1, NIDS):
        hit = hit | (slot == slots_ref[k : k + 1, :])
    spread = jnp.where(hit, 1.0, 0.0).astype(BF16)
    grad_ref[...] = dot(spread, grad.astype(BF16)).astype(BF16)


def params():
    return pltpu.CompilerParams(vmem_limit_bytes=VMEM_LIMIT)


def gather_blocks(value, axis):
    count = lax.axis_size(axis)
    if count & (count - 1):
        return [value] + [
            lax.ppermute(value, axis, [((i + t) % count, i) for i in range(count)])
            for t in range(1, count)
        ]
    blocks = {0: value}
    bit = count // 2
    while bit:
        pairs = [(i, i ^ bit) for i in range(count)]
        for t in list(blocks):
            blocks[t | bit] = lax.ppermute(blocks[t], axis, pairs)
        bit //= 2
    return [blocks[t] for t in range(count)]


def block_index(axis):
    count = lax.axis_size(axis)
    own = lax.axis_index(axis).astype(jnp.int32)
    steps = jnp.arange(count, dtype=jnp.int32)
    if count & (count - 1):
        return (own + steps) % count
    return own ^ steps


def local(table, item_owner, item_row, segment_ids, w_in, w_out, cotangent):
    owners = lax.axis_size("table") * lax.axis_size("ctx")
    count = lax.axis_size("ctx")
    events, width = cotangent.shape
    id_count = events * NIDS
    capacity = 2 * ((id_count + owners - 1) // owners)
    slot_count = owners * capacity
    axes = ("table", "ctx")
    vmem = pl.BlockSpec(memory_space=pltpu.VMEM)

    def exchange(value):
        return lax.all_to_all(value, axes, split_axis=0, concat_axis=0, tiled=True)

    slots, wanted = pl.pallas_call(
        functools.partial(slots_kernel, capacity),
        out_shape=(
            jax.ShapeDtypeStruct((8, events), jnp.int32),
            jax.ShapeDtypeStruct((owners, capacity), jnp.int32),
        ),
        compiler_params=params(),
        name="slots",
    )(item_owner.T, item_row.T)
    asked = exchange(wanted)
    rows = pl.pallas_call(
        select_kernel,
        out_shape=jax.ShapeDtypeStruct((slot_count, width), BF16),
        compiler_params=params(),
        name="select",
    )(asked, table)
    fetched = exchange(rows.reshape(owners, capacity, width)).reshape(slot_count, width)
    embedded = pl.pallas_call(
        embed_kernel,
        out_shape=jax.ShapeDtypeStruct((events, width), BF16),
        compiler_params=params(),
        name="embed",
    )(slots, fetched)
    emb_blocks = gather_blocks(embedded, "ctx")
    cot_blocks = gather_blocks(cotangent, "ctx")
    seg_blocks = gather_blocks(segment_ids.reshape(1, events), "ctx")
    layer_out, slot_grad = pl.pallas_call(
        functools.partial(layer_kernel, count),
        out_shape=(
            jax.ShapeDtypeStruct((events, width), BF16),
            jax.ShapeDtypeStruct((slot_count, width), BF16),
        ),
        in_specs=[pl.BlockSpec(memory_space=pltpu.SMEM)] + [vmem] * (3 + 3 * count),
        out_specs=(vmem, vmem),
        scratch_shapes=[
            pltpu.VMEM((count, events, 4 * width), BF16),
            pltpu.VMEM((events, 4 * width), F32),
            pltpu.VMEM((count, events, width), BF16),
            pltpu.VMEM((count, events, 128), jnp.int32),
            pltpu.VMEM((count, 8, events), jnp.int32),
            pltpu.VMEM((events, width), F32),
            pltpu.VMEM((count, events, width), BF16),
            pltpu.VMEM((events, 4 * width), F32),
        ],
        compiler_params=params(),
        name="layer",
    )(block_index("ctx"), slots, *emb_blocks, *cot_blocks, *seg_blocks, w_in, w_out)
    returned = exchange(slot_grad.reshape(owners, capacity, width)).reshape(slot_count, width)
    row_grad = pl.pallas_call(
        collect_kernel,
        out_shape=jax.ShapeDtypeStruct(table.shape, F32),
        compiler_params=params(),
        name="collect",
    )(asked, returned)
    return layer_out, row_grad


def solution(mesh):
    rows = P(("table", "ctx"), None)
    return jax.shard_map(
        local,
        mesh=mesh,
        in_specs=(rows, rows, rows, P("table", "ctx"), P(), P(), rows),
        out_specs=(rows, rows),
        check_vma=False,
    )
```

time: 238 us -> 117 us (0.49)
  waiting for transfers between devices: 101 us -> 34.3 us
  matrix products: 38.2 us -> 0 us
  local copies, waits for them, and re-layouts: 38.7 us -> 2.41 us
  Pallas kernels: 0 us -> 26.5 us
  blocking collectives: 19.3 us -> 43.5 us
  other arithmetic: 18.6 us -> 0.01 us
  between operations: 14 us -> 0.71 us
    all_to_all x2 -> x1, waiting for transfers between devices: 71.6 us -> 24.5 us  [exchange(): return lax.all_to_all(value, axes, split_axis=0, concat_axis=0, tiled=True)]
    dot_general x10 -> x0, matrix products: 38.2 us -> none  [the longest x1 6.55 us: local(): jnp.einsum('hqk,khd->qhd', grad_raw, split_heads(key_piece), preferred_el...]
    all_to_all x1 -> x2, blocking collectives: 14.3 us -> 43.5 us  [exchange(): return lax.all_to_all(value, axes, split_axis=0, concat_axis=0, tiled=True)]
    all_gather x4 -> x0, waiting for transfers between devices: 28.2 us -> none  [the longest x1 13.1 us: local(): value_piece = lax.all_gather(values, 'ctx', axis=0, tiled=True)]
    pallas_call x0 -> x5, Pallas kernels: none -> 26.5 us  [the longest x1 21.8 us: local(): pl.pallas_call(functools.partial(layer_kernel, count), out_shape=(jax.Sha...]
    reshape x10 -> x0, local copies, waits for them, and re-layouts: 16.3 us -> none  [the longest x4 6.85 us: split_heads(): return values.reshape(values.shape[0], HEADS, HEAD_DIM)]
    ppermute x0 -> x9, waiting for transfers between devices: none -> 9.77 us  [gather_blocks(): blocks[t | bit] = lax.ppermute(blocks[t], axis, pairs)]
    gather x3 -> x0, local copies, waits for them, and re-layouts: 8.93 us -> none  [the longest x1 5.08 us: local(): table[asked]]
  transfers between devices with their start and end apart: 6 -> 10, of which waited for: 5 -> 5; matrix products, arithmetic and copies ran while one was open for 17% -> 0% of each run, Pallas kernels for 0% -> 1%
where the time goes in v1:
time: 117 us; the launch traced here: 116 us
  blocking collectives  43.5 us (37%)
  waiting for transfers between devices  34.3 us (29%)
  Pallas kernels  26.5 us (23%)
  starting transfers between devices  8.79 us (8%)
  local copies, waits for them, and re-layouts  2.41 us (2%)
    all_to_all x2, blocking collectives, exchange(): return lax.all_to_all(value, axes, split_axis=0, concat_axis=0, tiled=True)  43.5 us
    all_to_all x1, waiting for transfers between devices, exchange(): return lax.all_to_all(value, axes, split_axis=0, concat_axis=0, tiled=True)  24.5 us
    pallas_call x1, Pallas kernels, local(): pl.pallas_call(functools.partial(layer_kernel, count), out_shape=(jax.Sha...  21.8 us
    ppermute x9, waiting for transfers between devices, gather_blocks(): blocks[t | bit] = lax.ppermute(blocks[t], axis, pairs)  9.77 us
    ppermute x9, starting transfers between devices, gather_blocks(): blocks[t | bit] = lax.ppermute(blocks[t], axis, pairs)  6.01 us
    all_to_all x1, starting transfers between devices, exchange(): return lax.all_to_all(value, axes, split_axis=0, concat_axis=0, tiled=True)  2.78 us
    unnamed x12, local copies, waits for them, and re-layouts  2.41 us
  transfers between devices with their start and end apart: 10, of which 5 were waited for; matrix products, arithmetic and copies ran while one was open for 0% of the time, Pallas kernels for 1%

profile of v1, /device:TPU:0, one launch (start us, length us, event | category | flops | bytes accessed | tf_op | source)
XLA Modules:
  0.0 116.2 jit_solution(9483881844202179396)
XLA Ops:
  0.6 0.0 copy-start.3
  0.6 0.7 copy-done.3
  1.3 0.0 copy-start.4
  1.3 0.7 copy-done.4
  2.0 0.3 slots.1
  2.3 14.3 %all_to_all.21 = s32[32,1,32]{2,1,0:T(1,128)S(1)} all-to-all(s32[32,1,32]{2,1,0:T(1,128)S(1)} %bitcast.15), channel_id=1, replica_groups=mesh['table'=8,'ctx'=4] {'table','ctx'}, dimensions={0} | all-to-all | bytes 8192 | tf_op jit(solution)/shard_map/all_to_all | solution.py:288
  16.6 0.0 copy-start
  16.6 1.0 copy-done
  17.6 0.0 copy-start.2
  17.6 1.9 %select.1 = bf16[1024,512]{1,0:T(8,128)(2,1)} custom-call(s32[32,32]{1,0:T(8,128)S(1)} %bitcast.13, bf16[512,512]{1,0:T(8,128)(2,1)S(1)} %copy-done), custom_call_target="tpu_custom_call" | custom-call | tf_op jit(solution)/shard_map/select/pallas_call | solution.py:300
  19.6 0.0 copy-start.5
  19.6 0.0 copy-start.1
  19.6 2.8 %all-to-all-start.1 = ((bf16[32,32,512]{2,1,0:T(8,128)(2,1)}), bf16[32,32,512]{2,1,0:T(8,128)(2,1)S(1)}, u32[]{:S(2)}, u32[]{:S(2)}) async-start(bf16[32,32,512]{2,1,0:T(8,128)(2,1)} %bitcast.5), calls=%async_computation.1 | async-start | bytes 2097152 | tf_op jit(solution)/shard_map/all_to_all | solution.py:288
  22.3 0.0 copy-done.2
  22.4 1.7 %collective-permute-start.4 = (bf16[256,512]{1,0:T(8,128)(2,1)S(1)}, bf16[256,512]{1,0:T(8,128)(2,1)S(1)}, u32[]{:S(2)}, u32[]{:S(2)}) collective-permute-start(bf16[256,512]{1,0:T(8,128)(2,1)S(1)} %copy-done.2), channel_id=1, source_target_pairs={{0,2},{1,3},{2,0},{3,1},{4,6},{5,7},{6,4},{7,5},{8,10},{9,11},{10,... | collective-permute-start | bytes 786440 | tf_op jit(solution)/shard_map/ppermute | solution.py:263
  24.1 24.5 %all-to-all-done.1 = bf16[32,32,512]{2,1,0:T(8,128)(2,1)S(1)} async-done(((bf16[32,32,512]{2,1,0:T(8,128)(2,1)}), bf16[32,32,512]{2,1,0:T(8,128)(2,1)S(1)}, u32[]{:S(2)}, u32[]{:S(2)}) %all-to-all-start.1) | async-done | bytes 1048608 | tf_op jit(solution)/shard_map/all_to_all | solution.py:288
  48.6 0.7 embed.1.refs_2_
  49.3 1.5 %collective-permute-start.1 = (bf16[256,512]{1,0:T(8,128)(2,1)S(1)}, bf16[256,512]{1,0:T(8,128)(2,1)S(1)}, u32[]{:S(2)}, u32[]{:S(2)}) collective-permute-start(bf16[256,512]{1,0:T(8,128)(2,1)S(1)} %embed.1.refs_2_), channel_id=1, source_target_pairs={{0,2},{1,3},{2,0},{3,1},{4,6},{5,7},{6,4},{7,5},{8,10},{9,11},{10,... | collective-permute-start | bytes 786440 | tf_op jit(solution)/shard_map/ppermute | solution.py:263
  50.8 0.0 collective-permute-start.3
  50.8 0.0 collective-permute-done.4.refs_8_
  50.8 0.5 collective-permute-start.5
  51.3 0.0 collective-permute-start
  51.4 5.8 %collective-permute-done.1.refs_4_ = bf16[256,512]{1,0:T(8,128)(2,1)S(1)} collective-permute-done((bf16[256,512]{1,0:T(8,128)(2,1)S(1)}, bf16[256,512]{1,0:T(8,128)(2,1)S(1)}, u32[]{:S(2)}, u32[]{:S(2)}) %collective-permute-start.1) | collective-permute-done | bytes 262176 | tf_op jit(solution)/shard_map/ppermute | solution.py:263
  57.1 0.0 collective-permute-start.2
  57.1 0.0 copy-done.5
  57.1 0.5 collective-permute-start.6
  57.6 1.0 collective-permute-done.6.refs_11_
  58.7 1.7 %collective-permute-start.7 = (s32[1,256]{1,0:T(1,128)S(1)}, s32[1,256]{1,0:T(1,128)S(1)}, u32[]{:S(2)}, u32[]{:S(2)}) collective-permute-start(s32[1,256]{1,0:T(1,128)S(1)} %copy-done.5), channel_id=1, source_target_pairs={{0,2},{1,3},{2,0},{3,1},{4,6},{5,7},{6,4},{7,5},{8,10},{9,11},{10,... | collective-permute-start | bytes 3080 | tf_op jit(solution)/shard_map/ppermute | solution.py:263
  60.4 1.8 %collective-permute-done.7.refs_12_ = s32[1,256]{1,0:T(1,128)S(1)} collective-permute-done((s32[1,256]{1,0:T(1,128)S(1)}, s32[1,256]{1,0:T(1,128)S(1)}, u32[]{:S(2)}, u32[]{:S(2)}) %collective-permute-start.7) | collective-permute-done | bytes 1056 | tf_op jit(solution)/shard_map/ppermute | solution.py:263
  62.2 0.0 collective-permute-start.8
  62.2 1.1 collective-permute-done.8.refs_13_
  63.4 0.0 collective-permute-done.3.refs_7_
  63.4 0.0 collective-permute-done.5.refs_9_
  63.4 0.0 collective-permute-done.refs_3_
  63.4 0.0 collective-permute-done.2.refs_5_
  63.4 0.0 copy-done.1
  63.4 21.8 %layer.1 = (bf16[256,512]{1,0:T(8,128)(2,1)}, bf16[1024,512]{1,0:T(8,128)(2,1)S(1)}) custom-call(s32[4]{0:T(128)S(1)} %iota_xor_fusion.refs_0_, s32[8,256]{1,0:T(8,128)S(1)} %get-tuple-element.6.slots_ref.refs_1_, bf16[256,512]{1,0:T(8,128)(2,1)S(1)} %embed.1.refs_2_, bf16[256,512]{1,0:T(8,128)(2,1)S(1)} %collective-permute-done.refs_3_, ...), custom_call_target="tpu_custom_call" | custom-call | tf_op jit(solution)/shard_map/layer/pallas_call | solution.py:316
  85.2 29.2 %all_to_all.22 = bf16[32,32,512]{2,1,0:T(8,128)(2,1)S(1)} all-to-all(bf16[32,32,512]{2,1,0:T(8,128)(2,1)S(1)} %bitcast.12), channel_id=1, replica_groups=mesh['table'=8,'ctx'=4] {'table','ctx'}, dimensions={0} | all-to-all | bytes 2097152 | tf_op jit(solution)/shard_map/all_to_all | solution.py:288
  114.4 1.8 %collect.1 = f32[512,512]{1,0:T(8,128)} custom-call(s32[32,32]{1,0:T(8,128)S(1)} %bitcast.14, bf16[1024,512]{1,0:T(8,128)(2,1)S(1)} %bitcast.11), custom_call_target="tpu_custom_call" | custom-call | tf_op jit(solution)/shard_map/collect/pallas_call | solution.py:338
  (1 shorter events, 0.0 us)
Async XLA Ops:
  0.6 0.7 copy-start.3
  1.3 0.7 copy-start.4
  16.6 1.0 copy-start
  17.6 4.7 %copy-start.2 = (bf16[256,512]{1,0:T(8,128)(2,1)S(1)}, bf16[256,512]{1,0:T(8,128)(2,1)}, u32[]{:S(2)}) copy-start(bf16[256,512]{1,0:T(8,128)(2,1)} %refs_6_.1) | copy-start | bytes 786436
  19.6 37.6 %copy-start.5 = (s32[1,256]{1,0:T(1,128)S(1)}, s32[1,256]{1,0:T(1,128)}, u32[]{:S(2)}) copy-start(s32[1,256]{1,0:T(1,128)} %refs_10_.1) | copy-start | bytes 3076
  19.6 43.8 %copy-start.1 = (bf16[512,512]{1,0:T(8,128)(2,1)S(1)}, bf16[512,512]{1,0:T(8,128)(2,1)}, u32[]{:S(2)}) copy-start(bf16[512,512]{1,0:T(8,128)(2,1)} %refs_15_.1) | copy-start | bytes 1572868
  19.6 29.0 %all-to-all-start.1 = ((bf16[32,32,512]{2,1,0:T(8,128)(2,1)}), bf16[32,32,512]{2,1,0:T(8,128)(2,1)S(1)}, u32[]{:S(2)}, u32[]{:S(2)}) async-start(bf16[32,32,512]{2,1,0:T(8,128)(2,1)} %bitcast.5), calls=%async_computation.1 | async-start | bytes 2097152 | tf_op jit(solution)/shard_map/all_to_all | solution.py:288
  22.4 28.5 %collective-permute-start.4 = (bf16[256,512]{1,0:T(8,128)(2,1)S(1)}, bf16[256,512]{1,0:T(8,128)(2,1)S(1)}, u32[]{:S(2)}, u32[]{:S(2)}) collective-permute-start(bf16[256,512]{1,0:T(8,128)(2,1)S(1)} %copy-done.2), channel_id=1, source_target_pairs={{0,2},{1,3},{2,0},{3,1},{4,6},{5,7},{6,4},{7,5},{8,10},{9,11},{10,... | collective-permute-start | bytes 786440 | tf_op jit(solution)/shard_map/ppermute | solution.py:263
  49.3 7.8 %collective-permute-start.1 = (bf16[256,512]{1,0:T(8,128)(2,1)S(1)}, bf16[256,512]{1,0:T(8,128)(2,1)S(1)}, u32[]{:S(2)}, u32[]{:S(2)}) collective-permute-start(bf16[256,512]{1,0:T(8,128)(2,1)S(1)} %embed.1.refs_2_), channel_id=1, source_target_pairs={{0,2},{1,3},{2,0},{3,1},{4,6},{5,7},{6,4},{7,5},{8,10},{9,11},{10,... | collective-permute-start | bytes 786440 | tf_op jit(solution)/shard_map/ppermute | solution.py:263
  50.8 12.5 %collective-permute-start.3 = (bf16[256,512]{1,0:T(8,128)(2,1)S(1)}, bf16[256,512]{1,0:T(8,128)(2,1)S(1)}, u32[]{:S(2)}, u32[]{:S(2)}) collective-permute-start(bf16[256,512]{1,0:T(8,128)(2,1)S(1)} %copy-done.2), channel_id=1, source_target_pairs={{0,1},{1,0},{2,3},{3,2},{4,5},{5,4},{6,7},{7,6},{8,9},{9,8},{10,11... | collective-permute-start | bytes 786440 | tf_op jit(solution)/shard_map/ppermute | solution.py:263
  50.8 12.5 %collective-permute-start.5 = (bf16[256,512]{1,0:T(8,128)(2,1)S(1)}, bf16[256,512]{1,0:T(8,128)(2,1)S(1)}, u32[]{:S(2)}, u32[]{:S(2)}) collective-permute-start(bf16[256,512]{1,0:T(8,128)(2,1)S(1)} %collective-permute-done.4.refs_8_), channel_id=1, source_target_pairs={{0,1},{1,0},{2,3},{3,2},{4,5},{5,4},{6,7},{7,6},{8,9},{9,8},{10,11... | collective-permute-start | bytes 786440 | tf_op jit(solution)/shard_map/ppermute | solution.py:263
  51.3 12.0 %collective-permute-start = (bf16[256,512]{1,0:T(8,128)(2,1)S(1)}, bf16[256,512]{1,0:T(8,128)(2,1)S(1)}, u32[]{:S(2)}, u32[]{:S(2)}) collective-permute-start(bf16[256,512]{1,0:T(8,128)(2,1)S(1)} %embed.1.refs_2_), channel_id=1, source_target_pairs={{0,1},{1,0},{2,3},{3,2},{4,5},{5,4},{6,7},{7,6},{8,9},{9,8},{10,11... | collective-permute-start | bytes 786440 | tf_op jit(solution)/shard_map/ppermute | solution.py:263
  57.1 6.3 %collective-permute-start.2 = (bf16[256,512]{1,0:T(8,128)(2,1)S(1)}, bf16[256,512]{1,0:T(8,128)(2,1)S(1)}, u32[]{:S(2)}, u32[]{:S(2)}) collective-permute-start(bf16[256,512]{1,0:T(8,128)(2,1)S(1)} %collective-permute-done.1.refs_4_), channel_id=1, source_target_pairs={{0,1},{1,0},{2,3},{3,2},{4,5},{5,4},{6,7},{7,6},{8,9},{9,8},{10,11... | collective-permute-start | bytes 786440 | tf_op jit(solution)/shard_map/ppermute | solution.py:263
  57.1 1.5 %collective-permute-start.6 = (s32[1,256]{1,0:T(1,128)S(1)}, s32[1,256]{1,0:T(1,128)S(1)}, u32[]{:S(2)}, u32[]{:S(2)}) collective-permute-start(s32[1,256]{1,0:T(1,128)S(1)} %copy-done.5), channel_id=1, source_target_pairs={{0,1},{1,0},{2,3},{3,2},{4,5},{5,4},{6,7},{7,6},{8,9},{9,8},{10,11... | collective-permute-start | bytes 3080 | tf_op jit(solution)/shard_map/ppermute | solution.py:263
  58.7 3.6 %collective-permute-start.7 = (s32[1,256]{1,0:T(1,128)S(1)}, s32[1,256]{1,0:T(1,128)S(1)}, u32[]{:S(2)}, u32[]{:S(2)}) collective-permute-start(s32[1,256]{1,0:T(1,128)S(1)} %copy-done.5), channel_id=1, source_target_pairs={{0,2},{1,3},{2,0},{3,1},{4,6},{5,7},{6,4},{7,5},{8,10},{9,11},{10,... | collective-permute-start | bytes 3080 | tf_op jit(solution)/shard_map/ppermute | solution.py:263
  62.2 1.1 collective-permute-start.8

commit v2 on v1

--- a/solution.py
+++ b/solution.py
@@ -68,46 +68,64 @@
     wanted_ref[...] = wanted.astype(jnp.int32)
 
 
-def select_kernel(asked_ref, table_ref, out_ref):
+def select_kernel(where_ref, asked_ref, own_ref, mate_ref, out_ref):
     owners, capacity = asked_ref.shape
-    rows = table_ref.shape[0]
-    slots = owners * capacity
+    rows = own_ref.shape[0]
+    slots = out_ref.shape[0]
+    first, parity = where_ref[0], where_ref[1]
     high, low = split_exact(asked_ref[...])
-    source = jnp.where(
-        iota((slots, owners), 0) // capacity == iota((slots, owners), 1), 1.0, 0.0
-    ).astype(BF16)
+    place = iota((slots, owners), 0) // capacity + first
+    source = jnp.where(place == iota((slots, owners), 1), 1.0, 0.0).astype(BF16)
     spread = 16.0 * dot(source, high) + dot(source, low)
     mine = iota((slots, capacity), 0) % capacity == iota((slots, capacity), 1)
     asked = jnp.sum(jnp.where(mine, spread, 0.0), 1, keepdims=True).astype(jnp.int32)
-    chosen = jnp.where(iota((slots, rows), 1) == asked, 1.0, 0.0).astype(BF16)
-    out_ref[...] = dot(chosen, table_ref[...]).astype(BF16)
-
-
-def embed_kernel(slots_ref, fetched_ref, out_ref):
-    events = out_ref.shape[0]
+    member = (iota((slots, 1), 0) // capacity) % 2
+    lane = iota((slots, rows), 1)
+    ours = jnp.where(lane == jnp.where(member == parity, asked, -1), 1.0, 0.0).astype(BF16)
+    theirs = jnp.where(lane == jnp.where(member == parity, -1, asked), 1.0, 0.0).astype(BF16)
+    out_ref[...] = (dot(ours, own_ref[...]) + dot(theirs, mate_ref[...])).astype(BF16)
+
+
+def gather_events(slots_ref, base, fetched_ref, events):
     slots = fetched_ref.shape[0]
-    column = jnp.transpose(slots_ref[...])
+    column = jnp.transpose(slots_ref[...]) - base
     lane = iota((events, slots), 1)
     hit = lane == column[:, 0:1]
     for k in range(1, NIDS):
         hit = hit | (lane == column[:, k : k + 1])
     picked = jnp.where(hit, 1.0, 0.0).astype(BF16)
-    out_ref[...] = dot(picked, fetched_ref[...]).astype(BF16)
-
-
-def collect_kernel(asked_ref, returned_ref, out_ref):
-    owners, capacity = asked_ref.shape
+    return dot(picked, fetched_ref[...])
+
+
+def scatter_events(slots_ref, base, grad, slots):
+    events = grad.shape[0]
+    slot = iota((slots, events), 0) + base
+    hit = slot == slots_ref[0:1, :]
+    for k in range(1, NIDS):
+        hit = hit | (slot == slots_ref[k : k + 1, :])
+    return dot(jnp.where(hit, 1.0, 0.0).astype(BF16), grad).astype(BF16)
+
+
+def far_kernel(base_ref, slots_ref, fetched_ref, out_ref):
+    out_ref[...] = gather_events(slots_ref, base_ref[0], fetched_ref, out_ref.shape[0]).astype(BF16)
+
+
+def embed_kernel(base_ref, slots_ref, fetched_ref, far_ref, out_ref):
+    near = gather_events(slots_ref, base_ref[0], fetched_ref, out_ref.shape[0])
+    out_ref[...] = (near + far_ref[...].astype(F32)).astype(BF16)
+
+
+def spread_kernel(base_ref, slots_ref, grad_ref, out_ref):
+    out_ref[...] = scatter_events(slots_ref, base_ref[0], grad_ref[...], out_ref.shape[0])
+
+
+def collect_kernel(asked_ref, near_ref, far_ref, out_ref):
     rows = out_ref.shape[0]
-    slots = owners * capacity
-    high, low = split_exact(asked_ref[...])
-    place = jnp.where(
-        iota((capacity, slots), 1) % capacity == iota((capacity, slots), 0), 1.0, 0.0
-    ).astype(BF16)
-    spread = 16.0 * dot(high, place) + dot(low, place)
-    mine = iota((owners, slots), 1) // capacity == iota((owners, slots), 0)
-    asked = jnp.sum(jnp.where(mine, spread, 0.0), 0, keepdims=True).astype(jnp.int32)
-    chosen = jnp.where(iota((rows, slots), 0) == asked, 1.0, 0.0).astype(BF16)
-    out_ref[...] = dot(chosen, returned_ref[...])
+    slots = near_ref.shape[0]
+    row = iota((rows, slots), 0)
+    near = jnp.where(row == asked_ref[:, 0:slots], 1.0, 0.0).astype(BF16)
+    far = jnp.where(row == asked_ref[:, slots:], 1.0, 0.0).astype(BF16)
+    out_ref[...] = dot(near, near_ref[...]) + dot(far, far_ref[...])
 
 
 def layer_kernel(count, *refs):
@@ -117,7 +135,7 @@
     cot_refs = refs[2 + count : 2 + 2 * count]
     seg_refs = refs[2 + 2 * count : 2 + 3 * count]
     w_in_ref, w_out_ref = refs[2 + 3 * count : 4 + 3 * count]
-    out_ref, grad_ref = refs[4 + 3 * count : 6 + 3 * count]
+    out_ref, grad_ref, near_ref = refs[4 + 3 * count : 7 + 3 * count]
     (
         proj_ref,
         slope_ref,
@@ -127,7 +145,7 @@
         att_ref,
         gatt_ref,
         join_ref,
-    ) = refs[6 + 3 * count :]
+    ) = refs[7 + 3 * count :]
     events, width = out_ref.shape
     half_scale = 0.5 * HEAD_DIM ** (-0.5)
     scale = HEAD_DIM ** (-0.5)
@@ -236,12 +254,8 @@
     grad_normed = dot_nt(grad_proj, w_in_ref[...])
     normed, inverse = normalize(emb_refs[0][...].astype(F32))
     grad = norm_back(grad_normed, normed, inverse) + cot_refs[0][...].astype(F32)
-    slot = iota((grad_ref.shape[0], events), 0)
-    hit = slot == slots_ref[0:1, :]
-    for k in range(1, NIDS):
-        hit = hit | (slot == slots_ref[k : k + 1, :])
-    spread = jnp.where(hit, 1.0, 0.0).astype(BF16)
-    grad_ref[...] = dot(spread, grad.astype(BF16)).astype(BF16)
+    grad_ref[...] = grad.astype(BF16)
+    near_ref[...] = scatter_events(slots_ref, index_ref[count], grad.astype(BF16), near_ref.shape[0])
 
 
 def params():
@@ -275,18 +289,48 @@
 
 
 def local(table, item_owner, item_row, segment_ids, w_in, w_out, cotangent):
-    owners = lax.axis_size("table") * lax.axis_size("ctx")
-    count = lax.axis_size("ctx")
+    tables, count = lax.axis_size("table"), lax.axis_size("ctx")
+    owners = tables * count
+    half = owners // 2
     events, width = cotangent.shape
     id_count = events * NIDS
     capacity = 2 * ((id_count + owners - 1) // owners)
-    slot_count = owners * capacity
+    half_slots = half * capacity
     axes = ("table", "ctx")
     vmem = pl.BlockSpec(memory_space=pltpu.VMEM)
-
-    def exchange(value):
-        return lax.all_to_all(value, axes, split_axis=0, concat_axis=0, tiled=True)
-
+    smem = pl.BlockSpec(memory_space=pltpu.SMEM)
+
+    parities = [[d for d in range(owners) if d % 2 == m] for m in range(2)]
+    halves = [list(range(h * half, (h + 1) * half)) for h in range(2)]
+    half_parities = [[d for d in group if d % 2 == m] for group in halves for m in range(2)]
+    partners = [(t, t ^ (tables // 2)) for t in range(tables)]
+    mates = [(c, c ^ 1) for c in range(count)]
+    side = lax.axis_index("table").astype(jnp.int32) // (tables // 2)
+    parity = lax.axis_index("ctx").astype(jnp.int32) % 2
+    base = (side * half_slots).reshape(1)
+
+    def exchange(value, groups):
+        return lax.all_to_all(
+            value, axes, split_axis=0, concat_axis=0, tiled=True, axis_index_groups=groups
+        )
+
+    def to_partner(value):
+        return lax.ppermute(value, "table", partners)
+
+    def to_mate(value):
+        return lax.ppermute(value, "ctx", mates)
+
+    def call(kernel, shape, name, smems, *operands):
+        return pl.pallas_call(
+            kernel,
+            out_shape=jax.ShapeDtypeStruct(shape, F32 if name == "collect" else BF16),
+            in_specs=[smem] * smems + [vmem] * (len(operands) - smems),
+            out_specs=vmem,
+            compiler_params=params(),
+            name=name,
+        )(*operands)
+
+    table_mate = to_mate(table)
     slots, wanted = pl.pallas_call(
         functools.partial(slots_kernel, capacity),
         out_shape=(
@@ -296,31 +340,44 @@
         compiler_params=params(),
         name="slots",
     )(item_owner.T, item_row.T)
-    asked = exchange(wanted)
-    rows = pl.pallas_call(
-        select_kernel,
-        out_shape=jax.ShapeDtypeStruct((slot_count, width), BF16),
-        compiler_params=params(),
-        name="select",
-    )(asked, table)
-    fetched = exchange(rows.reshape(owners, capacity, width)).reshape(slot_count, width)
-    embedded = pl.pallas_call(
-        embed_kernel,
-        out_shape=jax.ShapeDtypeStruct((events, width), BF16),
-        compiler_params=params(),
-        name="embed",
-    )(slots, fetched)
-    emb_blocks = gather_blocks(embedded, "ctx")
+    partner_slots = to_partner(slots)
+    asked = exchange(wanted, parities)
     cot_blocks = gather_blocks(cotangent, "ctx")
     seg_blocks = gather_blocks(segment_ids.reshape(1, events), "ctx")
-    layer_out, slot_grad = pl.pallas_call(
+
+    def select(first, name):
+        where = jnp.stack([first, parity])
+        return call(select_kernel, (half_slots, width), name, 1, where, asked, table, table_mate)
+
+    far_rows = select((1 - side) * half, "select_far")
+    near_rows = select(side * half, "select_near")
+    far_fetched = exchange(far_rows, half_parities)
+    far_sum = call(far_kernel, (events, width), "far_sum", 1, base, partner_slots, far_fetched)
+    near_rows, far_sum = lax.optimization_barrier((near_rows, far_sum))
+    far_part = to_partner(far_sum)
+    near_fetched = exchange(near_rows, half_parities)
+    slots, cot_blocks, seg_blocks = lax.optimization_barrier((slots, cot_blocks, seg_blocks))
+    embedded = call(
+        embed_kernel, (events, width), "embed", 1, base, slots, near_fetched, far_part
+    )
+    emb_blocks = gather_blocks(embedded, "ctx")
+
+    asked_mate = to_mate(asked)
+    lists = jnp.stack(
+        [jnp.where(parity == m, asked, asked_mate).reshape(half, 2, capacity) for m in range(2)], 1
+    )
+    lists = jnp.where(parity == 0, lists[:, :, 0], lists[:, :, 1]).reshape(2, half_slots)
+    lists = jnp.where(side == 0, lists, lists[::-1]).reshape(1, 2 * half_slots)
+
+    layer_out, grad, near_grad = pl.pallas_call(
         functools.partial(layer_kernel, count),
         out_shape=(
             jax.ShapeDtypeStruct((events, width), BF16),
-            jax.ShapeDtypeStruct((slot_count, width), BF16),
+            jax.ShapeDtypeStruct((events, width), BF16),
+            jax.ShapeDtypeStruct((half_slots, width), BF16),
         ),
-        in_specs=[pl.BlockSpec(memory_space=pltpu.SMEM)] + [vmem] * (3 + 3 * count),
-        out_specs=(vmem, vmem),
+        in_specs=[smem] + [vmem] * (3 + 3 * count),
+        out_specs=(vmem, vmem, vmem),
         scratch_shapes=[
             pltpu.VMEM((count, events, 4 * width), BF16),
             pltpu.VMEM((events, 4 * width), F32),
@@ -333,14 +390,22 @@
         ],
         compiler_params=params(),
         name="layer",
-    )(block_index("ctx"), slots, *emb_blocks, *cot_blocks, *seg_blocks, w_in, w_out)
-    returned = exchange(slot_grad.reshape(owners, capacity, width)).reshape(slot_count, width)
-    row_grad = pl.pallas_call(
-        collect_kernel,
-        out_shape=jax.ShapeDtypeStruct(table.shape, F32),
-        compiler_params=params(),
-        name="collect",
-    )(asked, returned)
+    )(
+        jnp.concatenate([block_index("ctx"), base]),
+        slots,
+        *emb_blocks,
+        *cot_blocks,
+        *seg_blocks,
+        w_in,
+        w_out,
+    )
+    far_grad = to_partner(grad)
+    near_returned = exchange(near_grad, halves)
+    far_slots = call(
+        spread_kernel, (half_slots, width), "spread_far", 1, base, partner_slots, far_grad
+    )
+    far_returned = exchange(far_slots, halves)
+    row_grad = call(collect_kernel, table.shape, "collect", 0, lists, near_returned, far_returned)
     return layer_out, row_grad
 
 

time: 117 us -> 136 us (1.16)
  blocking collectives: 43.5 us -> 0 us
  waiting for transfers between devices: 34.3 us -> 70.2 us
  starting transfers between devices: 8.79 us -> 29 us
  Pallas kernels: 26.5 us -> 32.2 us
    all_to_all x2 -> x0, blocking collectives: 43.5 us -> none  [exchange(): return lax.all_to_all(value, axes, split_axis=0, concat_axis=0, tiled=True)]
    ppermute x0 -> x5, waiting for transfers between devices: none -> 23.8 us  [the longest x3 23 us: to_partner(): return lax.ppermute(value, 'table', partners)]
    all_to_all x1 -> x5, starting transfers between devices: 2.78 us -> 22.7 us  [exchange(): lax.all_to_all(value, axes, split_axis=0, concat_axis=0, tiled=True, axis...]
    ppermute x9, waiting for transfers between devices: 9.77 us -> 24.2 us  [gather_blocks(): blocks[t | bit] = lax.ppermute(blocks[t], axis, pairs)]
    pallas_call x3 -> x6, Pallas kernels: 4.44 us -> 8.59 us  [call(): pl.pallas_call(kernel, out_shape=jax.ShapeDtypeStruct(shape, F32 if name...]
    ppermute x0 -> x5, starting transfers between devices: none -> 3.65 us  [the longest x3 2.72 us: to_partner(): return lax.ppermute(value, 'table', partners)]
    ppermute x9, starting transfers between devices: 6.01 us -> 2.56 us  [gather_blocks(): blocks[t | bit] = lax.ppermute(blocks[t], axis, pairs)]
    all_to_all x1 -> x5, waiting for transfers between devices: 24.5 us -> 22.2 us  [exchange(): lax.all_to_all(value, axes, split_axis=0, concat_axis=0, tiled=True, axis...]
  transfers between devices with their start and end apart: 10 -> 19, of which waited for: 5 -> 13; matrix products, arithmetic and copies ran while one was open for 0% -> 0% of each run, Pallas kernels for 1% -> 3%
where the time goes in v2:
time: 136 us; the launch traced here: 135 us
  waiting for transfers between devices  70.2 us (52%)
  Pallas kernels  32.2 us (24%)
  starting transfers between devices  29 us (21%)
  local copies, waits for them, and re-layouts  2.62 us (2%)
    ppermute x9, waiting for transfers between devices, gather_blocks(): blocks[t | bit] = lax.ppermute(blocks[t], axis, pairs)  24.2 us
    ppermute x3, waiting for transfers between devices, to_partner(): return lax.ppermute(value, 'table', partners)  23 us
    all_to_all x5, starting transfers between devices, exchange(): lax.all_to_all(value, axes, split_axis=0, concat_axis=0, tiled=True, axis...  22.7 us
    pallas_call x1, Pallas kernels, local(): pl.pallas_call(functools.partial(layer_kernel, count), out_shape=(jax.Sha...  22.6 us
    all_to_all x5, waiting for transfers between devices, exchange(): lax.all_to_all(value, axes, split_axis=0, concat_axis=0, tiled=True, axis...  22.2 us
    pallas_call x6, Pallas kernels, call(): pl.pallas_call(kernel, out_shape=jax.ShapeDtypeStruct(shape, F32 if name...  8.59 us
    ppermute x3, starting transfers between devices, to_partner(): return lax.ppermute(value, 'table', partners)  2.72 us
  transfers between devices with their start and end apart: 19, of which 13 were waited for; matrix products, arithmetic and copies ran while one was open for 0% of the time, Pallas kernels for 3%

profile of v2, /device:TPU:0, one launch (start us, length us, event | category | flops | bytes accessed | tf_op | source)
XLA Modules:
  0.0 135.0 jit_solution(9981854868182894766)
XLA Ops:
  0.6 0.5 collective-permute-start.6
  1.1 0.7 copy-done.4
  1.8 0.7 copy-done.5
  2.5 1.0 slots.1
  3.5 7.9 %all-to-all-start = ((s32[16,2,32]{2,1,0:T(2,128)}), s32[16,2,32]{2,1,0:T(2,128)S(1)}, u32[]{:S(2)}, u32[]{:S(2)}) async-start(s32[16,2,32]{2,1,0:T(2,128)} %bitcast.5), calls=%async_computation | async-start | bytes 32768 | tf_op jit(solution)/shard_map/all_to_all | solution.py:313
  11.4 0.1 pad_add_fusion.3.where_ref
  11.5 7.2 %all-to-all-done = s32[16,2,32]{2,1,0:T(2,128)S(1)} async-done(((s32[16,2,32]{2,1,0:T(2,128)}), s32[16,2,32]{2,1,0:T(2,128)S(1)}, u32[]{:S(2)}, u32[]{:S(2)}) %all-to-all-start) | async-done | bytes 4128 | tf_op jit(solution)/shard_map/all_to_all | solution.py:313
  18.7 0.0 collective-permute-done.6.mate_ref
  18.7 1.0 copy-done
  19.7 2.3 %select_far.1 = bf16[512,512]{1,0:T(8,128)(2,1)} custom-call(s32[2]{0:T(128)S(1)} %pad_add_fusion.3.where_ref, s32[32,32]{1,0:T(8,128)S(1)} %bitcast.28, bf16[512,512]{1,0:T(8,128)(2,1)S(1)} %copy-done, bf16[512,512]{1,0:T(8,128)(2,1)S(1)} %collective-permute-done.6.mate_ref), custom_call_target="tpu_custom_call" | custom-call | tf_op jit(solution)/shard_map/select_far/pallas_call | solution.py:324
  22.1 3.6 %all-to-all-start.1 = ((bf16[8,64,512]{2,1,0:T(8,128)(2,1)}), bf16[8,64,512]{2,1,0:T(8,128)(2,1)S(1)}, u32[]{:S(2)}, u32[]{:S(2)}) async-start(bf16[8,64,512]{2,1,0:T(8,128)(2,1)} %bitcast.8), calls=%async_computation.1 | async-start | bytes 1048576 | tf_op jit(solution)/shard_map/all_to_all | solution.py:313
  25.7 0.7 collective-permute-start.7
  26.4 0.1 pad_add_fusion.2.where_ref
  26.5 2.4 %select_near.1 = bf16[512,512]{1,0:T(8,128)(2,1)} custom-call(s32[2]{0:T(128)S(1)} %pad_add_fusion.2.where_ref, s32[32,32]{1,0:T(8,128)S(1)} %bitcast.29, bf16[512,512]{1,0:T(8,128)(2,1)S(1)} %copy-done.1, bf16[512,512]{1,0:T(8,128)(2,1)S(1)} %collective-permute-done.6.mate_ref), custom_call_target="tpu_custom_call" | custom-call | tf_op jit(solution)/shard_map/select_near/pallas_call | solution.py:324
  28.8 2.4 %collective-permute-done.7.slots_ref = s32[8,256]{1,0:T(8,128)S(1)} collective-permute-done((s32[8,256]{1,0:T(8,128)S(1)}, s32[8,256]{1,0:T(8,128)S(1)}, u32[]{:S(2)}, u32[]{:S(2)}) %collective-permute-start.7) | collective-permute-done | bytes 8224 | tf_op jit(solution)/shard_map/ppermute | solution.py:318
  31.2 3.2 %all-to-all-done.1 = bf16[8,64,512]{2,1,0:T(8,128)(2,1)S(1)} async-done(((bf16[8,64,512]{2,1,0:T(8,128)(2,1)}), bf16[8,64,512]{2,1,0:T(8,128)(2,1)S(1)}, u32[]{:S(2)}, u32[]{:S(2)}) %all-to-all-start.1) | async-done | bytes 524320 | tf_op jit(solution)/shard_map/all_to_all | solution.py:313
  34.4 0.6 far_sum.1
  35.0 3.5 %all-to-all-start.2 = ((bf16[8,64,512]{2,1,0:T(8,128)(2,1)}), bf16[8,64,512]{2,1,0:T(8,128)(2,1)S(1)}, u32[]{:S(2)}, u32[]{:S(2)}) async-start(bf16[8,64,512]{2,1,0:T(8,128)(2,1)} %bitcast.10), calls=%async_computation.2 | async-start | bytes 1048576 | tf_op jit(solution)/shard_map/all_to_all | solution.py:313
  38.5 1.9 %collective-permute-start.1 = (bf16[256,512]{1,0:T(8,128)(2,1)S(1)}, bf16[256,512]{1,0:T(8,128)(2,1)S(1)}, u32[]{:S(2)}, u32[]{:S(2)}) collective-permute-start(bf16[256,512]{1,0:T(8,128)(2,1)S(1)} %copy-done.3), channel_id=1, source_target_pairs={{0,2},{1,3},{2,0},{3,1},{4,6},{5,7},{6,4},{7,5},{8,10},{9,11},{10,... | collective-permute-start | bytes 786440 | tf_op jit(solution)/shard_map/ppermute | solution.py:277
  40.4 0.0 collective-permute-start
  40.4 10.7 %collective-permute-done.1.refs_8_ = bf16[256,512]{1,0:T(8,128)(2,1)S(1)} collective-permute-done((bf16[256,512]{1,0:T(8,128)(2,1)S(1)}, bf16[256,512]{1,0:T(8,128)(2,1)S(1)}, u32[]{:S(2)}, u32[]{:S(2)}) %collective-permute-start.1) | collective-permute-done | bytes 262176 | tf_op jit(solution)/shard_map/ppermute | solution.py:277
  51.1 0.0 collective-permute-start.2
  51.1 0.7 collective-permute-start.8
  51.8 0.3 collective-permute-start.4
  52.1 0.0 collective-permute-start.3
  52.1 3.3 %collective-permute-done.4.refs_12_ = s32[1,256]{1,0:T(1,128)S(1)} collective-permute-done((s32[1,256]{1,0:T(1,128)S(1)}, s32[1,256]{1,0:T(1,128)S(1)}, u32[]{:S(2)}, u32[]{:S(2)}) %collective-permute-start.4) | collective-permute-done | bytes 1056 | tf_op jit(solution)/shard_map/ppermute | solution.py:277
  55.4 1.1 collective-permute-done.5.refs_13_
  56.5 9.8 %collective-permute-done.8.far_ref = bf16[256,512]{1,0:T(8,128)(2,1)S(1)} collective-permute-done((bf16[256,512]{1,0:T(8,128)(2,1)S(1)}, bf16[256,512]{1,0:T(8,128)(2,1)S(1)}, u32[]{:S(2)}, u32[]{:S(2)}) %collective-permute-start.8) | collective-permute-done | bytes 262176 | tf_op jit(solution)/shard_map/ppermute | solution.py:318
  66.3 0.6 embed.1.refs_2_
  66.9 0.3 collective-permute-start.10
  67.2 0.0 collective-permute-start.9
  67.2 7.6 %collective-permute-done.10.refs_4_ = bf16[256,512]{1,0:T(8,128)(2,1)S(1)} collective-permute-done((bf16[256,512]{1,0:T(8,128)(2,1)S(1)}, bf16[256,512]{1,0:T(8,128)(2,1)S(1)}, u32[]{:S(2)}, u32[]{:S(2)}) %collective-permute-start.10) | collective-permute-done | bytes 262176 | tf_op jit(solution)/shard_map/ppermute | solution.py:277
  74.9 0.0 collective-permute-start.11
  74.9 0.1 pad_add_fusion.1.refs_0_
  75.0 1.4 %collective-permute-done.11.refs_5_ = bf16[256,512]{1,0:T(8,128)(2,1)S(1)} collective-permute-done((bf16[256,512]{1,0:T(8,128)(2,1)S(1)}, bf16[256,512]{1,0:T(8,128)(2,1)S(1)}, u32[]{:S(2)}, u32[]{:S(2)}) %collective-permute-start.11) | collective-permute-done | bytes 262176 | tf_op jit(solution)/shard_map/ppermute | solution.py:277
  76.4 22.6 %layer.1 = (bf16[256,512]{1,0:T(8,128)(2,1)}, bf16[256,512]{1,0:T(8,128)(2,1)S(1)}, bf16[512,512]{1,0:T(8,128)(2,1)}) custom-call(s32[5]{0:T(128)S(1)} %pad_add_fusion.1.refs_0_, s32[8,256]{1,0:T(8,128)S(1)} %get-tuple-element.19.slots_ref.refs_1_, bf16[256,512]{1,0:T(8,128)(2,1)S(1)} %embed.1.refs_2_, bf16[256,512]{1,0:T(8,128)(2,1)S(1)} %collective-permute-done.9.refs_3_, ...), custom_call_target="tpu_custom_call" | custom-call | tf_op jit(solution)/shard_map/layer/pallas_call | solution.py:372
  99.0 3.6 %all-to-all-start.3 = ((bf16[16,32,512]{2,1,0:T(8,128)(2,1)}), bf16[16,32,512]{2,1,0:T(8,128)(2,1)S(1)}, u32[]{:S(2)}, u32[]{:S(2)}) async-start(bf16[16,32,512]{2,1,0:T(8,128)(2,1)} %bitcast.14), calls=%async_computation.3 | async-start | bytes 1048576 | tf_op jit(solution)/shard_map/all_to_all | solution.py:313
  102.6 1.3 collective-permute-start.13
  103.9 10.8 %collective-permute-done.13.grad_ref = bf16[256,512]{1,0:T(8,128)(2,1)S(1)} collective-permute-done((bf16[256,512]{1,0:T(8,128)(2,1)S(1)}, bf16[256,512]{1,0:T(8,128)(2,1)S(1)}, u32[]{:S(2)}, u32[]{:S(2)}) %collective-permute-start.13) | collective-permute-done | bytes 262176 | tf_op jit(solution)/shard_map/ppermute | solution.py:318
  114.8 1.1 spread_far.1
  115.9 2.7 %all-to-all-done.3 = bf16[16,32,512]{2,1,0:T(8,128)(2,1)S(1)} async-done(((bf16[16,32,512]{2,1,0:T(8,128)(2,1)}), bf16[16,32,512]{2,1,0:T(8,128)(2,1)S(1)}, u32[]{:S(2)}, u32[]{:S(2)}) %all-to-all-start.3) | async-done | bytes 524320 | tf_op jit(solution)/shard_map/all_to_all | solution.py:313
  118.6 4.2 %all-to-all-start.4 = ((bf16[16,32,512]{2,1,0:T(8,128)(2,1)}), bf16[16,32,512]{2,1,0:T(8,128)(2,1)S(1)}, u32[]{:S(2)}, u32[]{:S(2)}) async-start(bf16[16,32,512]{2,1,0:T(8,128)(2,1)} %bitcast.16), calls=%async_computation.4 | async-start | bytes 1048576 | tf_op jit(solution)/shard_map/all_to_all | solution.py:313
  122.8 0.4 collective-permute-start.12
  123.2 0.8 collective-permute-done.12
  124.1 0.1 select_n.54
  124.2 0.1 rev.3
  124.3 9.0 %all-to-all-done.4 = bf16[16,32,512]{2,1,0:T(8,128)(2,1)S(1)} async-done(((bf16[16,32,512]{2,1,0:T(8,128)(2,1)}), bf16[16,32,512]{2,1,0:T(8,128)(2,1)S(1)}, u32[]{:S(2)}, u32[]{:S(2)}) %all-to-all-start.4) | async-done | bytes 524320 | tf_op jit(solution)/shard_map/all_to_all | solution.py:313
  133.3 1.7 %collect.1 = f32[512,512]{1,0:T(8,128)} custom-call(s32[1,1024]{1,0:T(1,128)S(1)} %bitcast.32, bf16[512,512]{1,0:T(8,128)(2,1)S(1)} %bitcast.26, bf16[512,512]{1,0:T(8,128)(2,1)S(1)} %bitcast.27), custom_call_target="tpu_custom_call" | custom-call | tf_op jit(solution)/shard_map/collect/pallas_call | solution.py:324
  (23 shorter events, 0.1 us)
Async XLA Ops:
  0.6 18.1 %collective-permute-start.6 = (bf16[512,512]{1,0:T(8,128)(2,1)}, bf16[512,512]{1,0:T(8,128)(2,1)S(1)}, u32[]{:S(2)}, u32[]{:S(2)}) collective-permute-start(bf16[512,512]{1,0:T(8,128)(2,1)} %own_ref.3), channel_id=1, source_target_pairs={{0,1},{1,0},{2,3},{3,2},{4,5},{5,4},{6,7},{7,6},{8,9},{9,8},{10,11... | collective-permute-start | bytes 1572872 | tf_op jit(solution)/shard_map/ppermute | solution.py:321
  1.1 0.7 copy-start.4
  1.8 0.7 copy-start.5
  3.5 15.2 %all-to-all-start = ((s32[16,2,32]{2,1,0:T(2,128)}), s32[16,2,32]{2,1,0:T(2,128)S(1)}, u32[]{:S(2)}, u32[]{:S(2)}) async-start(s32[16,2,32]{2,1,0:T(2,128)} %bitcast.5), calls=%async_computation | async-start | bytes 32768 | tf_op jit(solution)/shard_map/all_to_all | solution.py:313
  18.7 1.0 copy-start
  19.7 6.7 %copy-start.1 = (bf16[512,512]{1,0:T(8,128)(2,1)S(1)}, bf16[512,512]{1,0:T(8,128)(2,1)}, u32[]{:S(2)}) copy-start(bf16[512,512]{1,0:T(8,128)(2,1)} %own_ref.3) | copy-start | bytes 1572868
  22.1 16.4 %copy-start.3 = (bf16[256,512]{1,0:T(8,128)(2,1)S(1)}, bf16[256,512]{1,0:T(8,128)(2,1)}, u32[]{:S(2)}) copy-start(bf16[256,512]{1,0:T(8,128)(2,1)} %refs_6_) | copy-start | bytes 786436
  22.1 29.7 %copy-start.6 = (s32[1,256]{1,0:T(1,128)S(1)}, s32[1,256]{1,0:T(1,128)}, u32[]{:S(2)}) copy-start(s32[1,256]{1,0:T(1,128)} %refs_10_) | copy-start | bytes 3076
  22.1 12.3 %all-to-all-start.1 = ((bf16[8,64,512]{2,1,0:T(8,128)(2,1)}), bf16[8,64,512]{2,1,0:T(8,128)(2,1)S(1)}, u32[]{:S(2)}, u32[]{:S(2)}) async-start(bf16[8,64,512]{2,1,0:T(8,128)(2,1)} %bitcast.8), calls=%async_computation.1 | async-start | bytes 1048576 | tf_op jit(solution)/shard_map/all_to_all | solution.py:313
  25.7 5.5 %collective-permute-start.7 = (s32[8,256]{1,0:T(8,128)S(1)}, s32[8,256]{1,0:T(8,128)S(1)}, u32[]{:S(2)}, u32[]{:S(2)}) collective-permute-start(s32[8,256]{1,0:T(8,128)S(1)} %get-tuple-element.19.slots_ref.refs_1_), channel_id=1, source_target_pairs={{0,16},{4,20},{8,24},{12,28},{16,0},{20,4},{24,8},{28,12},{1,17},{... | collective-permute-start | bytes 24584 | tf_op jit(solution)/shard_map/ppermute | solution.py:318
  26.5 49.9 %copy-start.2 = (bf16[512,512]{1,0:T(8,128)(2,1)S(1)}, bf16[512,512]{1,0:T(8,128)(2,1)}, u32[]{:S(2)}) copy-start(bf16[512,512]{1,0:T(8,128)(2,1)} %refs_15_.1) | copy-start | bytes 1572868
  35.0 31.3 %all-to-all-start.2 = ((bf16[8,64,512]{2,1,0:T(8,128)(2,1)}), bf16[8,64,512]{2,1,0:T(8,128)(2,1)S(1)}, u32[]{:S(2)}, u32[]{:S(2)}) async-start(bf16[8,64,512]{2,1,0:T(8,128)(2,1)} %bitcast.10), calls=%async_computation.2 | async-start | bytes 1048576 | tf_op jit(solution)/shard_map/all_to_all | solution.py:313
  38.5 12.6 %collective-permute-start.1 = (bf16[256,512]{1,0:T(8,128)(2,1)S(1)}, bf16[256,512]{1,0:T(8,128)(2,1)S(1)}, u32[]{:S(2)}, u32[]{:S(2)}) collective-permute-start(bf16[256,512]{1,0:T(8,128)(2,1)S(1)} %copy-done.3), channel_id=1, source_target_pairs={{0,2},{1,3},{2,0},{3,1},{4,6},{5,7},{6,4},{7,5},{8,10},{9,11},{10,... | collective-permute-start | bytes 786440 | tf_op jit(solution)/shard_map/ppermute | solution.py:277
  40.4 16.1 %collective-permute-start = (bf16[256,512]{1,0:T(8,128)(2,1)S(1)}, bf16[256,512]{1,0:T(8,128)(2,1)S(1)}, u32[]{:S(2)}, u32[]{:S(2)}) collective-permute-start(bf16[256,512]{1,0:T(8,128)(2,1)S(1)} %copy-done.3), channel_id=1, source_target_pairs={{0,1},{1,0},{2,3},{3,2},{4,5},{5,4},{6,7},{7,6},{8,9},{9,8},{10,11... | collective-permute-start | bytes 786440 | tf_op jit(solution)/shard_map/ppermute | solution.py:277
  51.1 5.5 %collective-permute-start.2 = (bf16[256,512]{1,0:T(8,128)(2,1)S(1)}, bf16[256,512]{1,0:T(8,128)(2,1)S(1)}, u32[]{:S(2)}, u32[]{:S(2)}) collective-permute-start(bf16[256,512]{1,0:T(8,128)(2,1)S(1)} %collective-permute-done.1.refs_8_), channel_id=1, source_target_pairs={{0,1},{1,0},{2,3},{3,2},{4,5},{5,4},{6,7},{7,6},{8,9},{9,8},{10,11... | collective-permute-start | bytes 786440 | tf_op jit(solution)/shard_map/ppermute | solution.py:277
  51.1 15.2 %collective-permute-start.8 = (bf16[256,512]{1,0:T(8,128)(2,1)S(1)}, bf16[256,512]{1,0:T(8,128)(2,1)S(1)}, u32[]{:S(2)}, u32[]{:S(2)}) collective-permute-start(bf16[256,512]{1,0:T(8,128)(2,1)S(1)} %far_sum.1), channel_id=1, source_target_pairs={{0,16},{4,20},{8,24},{12,28},{16,0},{20,4},{24,8},{28,12},{1,17},{... | collective-permute-start | bytes 786440 | tf_op jit(solution)/shard_map/ppermute | solution.py:318
  51.8 3.6 %collective-permute-start.4 = (s32[1,256]{1,0:T(1,128)S(1)}, s32[1,256]{1,0:T(1,128)S(1)}, u32[]{:S(2)}, u32[]{:S(2)}) collective-permute-start(s32[1,256]{1,0:T(1,128)S(1)} %copy-done.6), channel_id=1, source_target_pairs={{0,2},{1,3},{2,0},{3,1},{4,6},{5,7},{6,4},{7,5},{8,10},{9,11},{10,... | collective-permute-start | bytes 3080 | tf_op jit(solution)/shard_map/ppermute | solution.py:277
  52.1 3.3 %collective-permute-start.3 = (s32[1,256]{1,0:T(1,128)S(1)}, s32[1,256]{1,0:T(1,128)S(1)}, u32[]{:S(2)}, u32[]{:S(2)}) collective-permute-start(s32[1,256]{1,0:T(1,128)S(1)} %copy-done.6), channel_id=1, source_target_pairs={{0,1},{1,0},{2,3},{3,2},{4,5},{5,4},{6,7},{7,6},{8,9},{9,8},{10,11... | collective-permute-start | bytes 3080 | tf_op jit(solution)/shard_map/ppermute | solution.py:277
  55.4 1.1 collective-permute-start.5
  66.9 8.0 %collective-permute-start.10 = (bf16[256,512]{1,0:T(8,128)(2,1)S(1)}, bf16[256,512]{1,0:T(8,128)(2,1)S(1)}, u32[]{:S(2)}, u32[]{:S(2)}) collective-permute-start(bf16[256,512]{1,0:T(8,128)(2,1)S(1)} %embed.1.refs_2_), channel_id=1, source_target_pairs={{0,2},{1,3},{2,0},{3,1},{4,6},{5,7},{6,4},{7,5},{8,10},{9,11},{10,... | collective-permute-start | bytes 786440 | tf_op jit(solution)/shard_map/ppermute | solution.py:277
  67.2 7.7 %collective-permute-start.9 = (bf16[256,512]{1,0:T(8,128)(2,1)S(1)}, bf16[256,512]{1,0:T(8,128)(2,1)S(1)}, u32[]{:S(2)}, u32[]{:S(2)}) collective-permute-start(bf16[256,512]{1,0:T(8,128)(2,1)S(1)} %embed.1.refs_2_), channel_id=1, source_target_pairs={{0,1},{1,0},{2,3},{3,2},{4,5},{5,4},{6,7},{7,6},{8,9},{9,8},{10,11... | collective-permute-start | bytes 786440 | tf_op jit(solution)/shard_map/ppermute | solution.py:277
  74.9 1.5 %collective-permute-start.11 = (bf16[256,512]{1,0:T(8,128)(2,1)S(1)}, bf16[256,512]{1,0:T(8,128)(2,1)S(1)}, u32[]{:S(2)}, u32[]{:S(2)}) collective-permute-start(bf16[256,512]{1,0:T(8,128)(2,1)S(1)} %collective-permute-done.10.refs_4_), channel_id=1, source_target_pairs={{0,1},{1,0},{2,3},{3,2},{4,5},{5,4},{6,7},{7,6},{8,9},{9,8},{10,11... | collective-permute-start | bytes 786440 | tf_op jit(solution)/shard_map/ppermute | solution.py:277
  99.0 19.6 %all-to-all-start.3 = ((bf16[16,32,512]{2,1,0:T(8,128)(2,1)}), bf16[16,32,512]{2,1,0:T(8,128)(2,1)S(1)}, u32[]{:S(2)}, u32[]{:S(2)}) async-start(bf16[16,32,512]{2,1,0:T(8,128)(2,1)} %bitcast.14), calls=%async_computation.3 | async-start | bytes 1048576 | tf_op jit(solution)/shard_map/all_to_all | solution.py:313
  102.6 12.2 %collective-permute-start.13 = (bf16[256,512]{1,0:T(8,128)(2,1)S(1)}, bf16[256,512]{1,0:T(8,128)(2,1)S(1)}, u32[]{:S(2)}, u32[]{:S(2)}) collective-permute-start(bf16[256,512]{1,0:T(8,128)(2,1)S(1)} %get-tuple-element.33), channel_id=1, source_target_pairs={{0,16},{4,20},{8,24},{12,28},{16,0},{20,4},{24,8},{28,12},{1,17},{... | collective-permute-start | bytes 786440 | tf_op jit(solution)/shard_map/ppermute | solution.py:318
  118.6 14.7 %all-to-all-start.4 = ((bf16[16,32,512]{2,1,0:T(8,128)(2,1)}), bf16[16,32,512]{2,1,0:T(8,128)(2,1)S(1)}, u32[]{:S(2)}, u32[]{:S(2)}) async-start(bf16[16,32,512]{2,1,0:T(8,128)(2,1)} %bitcast.16), calls=%async_computation.4 | async-start | bytes 1048576 | tf_op jit(solution)/shard_map/all_to_all | solution.py:313
  122.8 1.2 collective-permute-start.12

commit v3 on v1

v3 whole, which is shorter than its diff:
```python
import functools

import jax
import jax.numpy as jnp
from jax import lax
from jax.experimental import pallas as pl
from jax.experimental.pallas import tpu as pltpu
from jax.sharding import PartitionSpec as P

HEADS = 4
HEAD_DIM = 128
NIDS = 2
EPS = 1e-06
VMEM_LIMIT = 40 * 1024 * 1024

F32 = jnp.float32
BF16 = jnp.bfloat16


def dot(a, b):
    return jnp.dot(a, b, preferred_element_type=F32)


def dot_nt(a, b):
    return lax.dot_general(a, b, (((1,), (1,)), ((), ())), preferred_element_type=F32)


def iota(shape, dim):
    return lax.broadcasted_iota(jnp.int32, shape, dim)


def normalize(values):
    centred = values - jnp.mean(values, -1, keepdims=True)
    inverse = lax.rsqrt(jnp.mean(centred * centred, -1, keepdims=True) + EPS)
    return centred * inverse, inverse


def norm_back(grad_norm, normed, inverse):
    mean_grad = jnp.mean(grad_norm, -1, keepdims=True)
    mean_cross = jnp.mean(grad_norm * normed, -1, keepdims=True)
    return (grad_norm - mean_grad - normed * mean_cross) * inverse


def split_exact(values):
    return (values >> 4).astype(F32).astype(BF16), (values & 15).astype(F32).astype(BF16)


EXTRA = 16


def slots_kernel(
    capacity, owner_ref, row_ref, seg_ref, cot_ref, slots_ref, wanted_ref, side_ref
):
    side_ref[0 : cot_ref.shape[0], :] = cot_ref[...]
    side_ref[cot_ref.shape[0] :, :] = jnp.zeros((EXTRA, side_ref.shape[1]), BF16)
    segments = seg_ref[...].astype(F32)
    side_ref[cot_ref.shape[0] :, 0 : seg_ref.shape[1]] = jnp.broadcast_to(
        segments, (EXTRA, seg_ref.shape[1])
    ).astype(BF16)
    events = owner_ref.shape[1]
    owners = wanted_ref.shape[0]
    owner = jnp.concatenate([owner_ref[k : k + 1, :] for k in range(NIDS)], 1)
    row = jnp.concatenate([row_ref[k : k + 1, :] for k in range(NIDS)], 1)
    ids = owner.shape[1]
    named = iota((owners, ids), 0) == owner
    named_f = jnp.where(named, 1.0, 0.0)
    before = jnp.where(iota((ids, ids), 0) < iota((ids, ids), 1), 1.0, 0.0).astype(BF16)
    earlier = dot(named_f.astype(BF16), before)
    rank = jnp.sum(earlier * named_f, 0, keepdims=True).astype(jnp.int32)
    slot = owner * capacity + rank
    slots_ref[...] = jnp.full(slots_ref.shape, -1, jnp.int32)
    for k in range(NIDS):
        slots_ref[k : k + 1, :] = slot[:, k * events : (k + 1) * events]
    ranked = jnp.where(iota((capacity, ids), 0) == rank, 1.0, 0.0).astype(BF16)
    high, low = (row >> 4).astype(F32), (row & 15).astype(F32)
    wanted = 16.0 * dot_nt((named_f * high).astype(BF16), ranked) + dot_nt(
        (named_f * low).astype(BF16), ranked
    )
    wanted_ref[...] = wanted.astype(jnp.int32)


def select_kernel(asked_ref, table_ref, out_ref):
    owners, capacity = asked_ref.shape
    rows = table_ref.shape[0]
    columns = jnp.transpose(asked_ref[...])
    lane = iota((capacity, rows), 1)
    chosen = jnp.concatenate(
        [jnp.where(lane == columns[:, s : s + 1], 1.0, 0.0) for s in range(owners)], 0
    )
    out_ref[...] = dot(chosen.astype(BF16), table_ref[...]).astype(BF16)


def embed_kernel(slots_ref, fetched_ref, out_ref):
    events = out_ref.shape[0]
    slots = fetched_ref.shape[0]
    column = jnp.transpose(slots_ref[...])
    lane = iota((events, slots), 1)
    hit = lane == column[:, 0:1]
    for k in range(1, NIDS):
        hit = hit | (lane == column[:, k : k + 1])
    picked = jnp.where(hit, 1.0, 0.0).astype(BF16)
    out_ref[...] = dot(picked, fetched_ref[...]).astype(BF16)


def collect_kernel(asked_ref, returned_ref, out_ref):
    owners, capacity = asked_ref.shape
    rows = out_ref.shape[0]
    slots = owners * capacity
    high, low = split_exact(asked_ref[...])
    place = jnp.where(
        iota((capacity, slots), 1) % capacity == iota((capacity, slots), 0), 1.0, 0.0
    ).astype(BF16)
    spread = 16.0 * dot(high, place) + dot(low, place)
    mine = iota((owners, slots), 1) // capacity == iota((owners, slots), 0)
    asked = jnp.sum(jnp.where(mine, spread, 0.0), 0, keepdims=True).astype(jnp.int32)
    chosen = jnp.where(iota((rows, slots), 0) == asked, 1.0, 0.0).astype(BF16)
    out_ref[...] = dot(chosen, returned_ref[...])


SCALE = HEAD_DIM ** (-0.5)


def head(part, h, width):
    return slice(part * width + h * HEAD_DIM, part * width + (h + 1) * HEAD_DIM)


def visible(query_chunk, key_chunk, segc_ref, segr_ref, flip):
    events = segr_ref.shape[2]
    first, second = iota((events, events), 0), iota((events, events), 1)
    if flip:
        same = segc_ref[key_chunk][:, 0:1] == segr_ref[query_chunk][0:1, :]
        return same & (first <= second + (query_chunk - key_chunk) * events)
    same = segc_ref[query_chunk][:, 0:1] == segr_ref[key_chunk][0:1, :]
    return same & (first + (query_chunk - key_chunk) * events >= second)


def project(emb, w_in_ref, write, slope_ref):
    width = emb.shape[1]
    normed = normalize(emb.astype(F32))[0].astype(BF16)
    for block in range(4):
        columns = slice(block * width, (block + 1) * width)
        half = 0.5 * dot(normed, w_in_ref[:, columns])
        bend = jnp.tanh(half)
        value = half + half * bend
        write(columns, value.astype(BF16))
        if slope_ref is not None:
            sigma = 0.5 + 0.5 * bend
            slope_ref[:, columns] = sigma + value - value * sigma


def hold_side(side_ref, place, cots_ref, segc_ref, segr_ref):
    events = cots_ref.shape[1]
    cots_ref[place] = side_ref[0:events, :]
    seg = side_ref[events : events + EXTRA, 0:events].astype(F32)[0:8]
    segr_ref[place] = seg
    segc_ref[place] = jnp.broadcast_to(jnp.transpose(seg)[:, 0:1], segc_ref.shape[1:])


class Chunks:
    def __init__(self, first, proj_ref, gatt_ref, segc_ref, segr_ref, join_ref):
        self.first, self.proj, self.gatt = first, proj_ref, gatt_ref
        self.segc, self.segr, self.join = segc_ref, segr_ref, join_ref
        self.width = gatt_ref.shape[2]

    def attend(self, i, start, stop, att_ref):
        def pair(j, _):
            mask = visible(i, j, self.segc, self.segr, False)
            qi, kj = i - self.first, j - self.first
            for h in range(HEADS):
                queries = self.proj[qi, :, head(2, h, self.width)]
                raw = dot_nt(queries, self.proj[kj, :, head(3, h, self.width)])
                half = raw * (0.5 * SCALE)
                value = half + half * jnp.tanh(half)
                weights = jnp.where(mask, value, 0.0).astype(BF16)
                added = dot(weights, self.proj[kj, :, head(1, h, self.width)])
                att_ref[:, head(0, h, self.width)] += added
            return 0

        lax.fori_loop(start, stop, pair, 0)

    def finish(self, i, own, att, cot, emb_ref, w_out_ref, out_ref):
        att_norm, att_inverse = normalize(att)
        gate = self.proj[i - self.first, :, 0 : self.width].astype(F32)
        grad_mixed = dot_nt(cot, w_out_ref[...])
        grad_att = norm_back(grad_mixed * gate, att_norm, att_inverse)
        self.gatt[i - self.first] = grad_att.astype(BF16)

        @pl.when(i == own)
        def _():
            mixed = (att_norm * gate).astype(BF16)
            out = emb_ref[...].astype(F32) + dot(mixed, w_out_ref[...])
            out_ref[...] = out.astype(BF16)
            self.join[:, 0 : self.width] = grad_mixed * att_norm

    def query_side(self, own, start, stop):
        def pair(j, _):
            mask = visible(own, j, self.segc, self.segr, False)
            me, kj = own - self.first, j - self.first
            for h in range(HEADS):
                keys = self.proj[kj, :, head(3, h, self.width)]
                half = dot_nt(self.proj[me, :, head(2, h, self.width)], keys) * (0.5 * SCALE)
                bend = jnp.tanh(half)
                value = half + half * bend
                sigma = 0.5 + 0.5 * bend
                slope = sigma + value - value * sigma
                grad_weights = dot_nt(
                    self.gatt[me, :, head(0, h, self.width)],
                    self.proj[kj, :, head(1, h, self.width)],
                )
                grad_raw = jnp.where(mask, grad_weights * slope * SCALE, 0.0).astype(BF16)
                self.join[:, head(2, h, self.width)] += dot(grad_raw, keys)
            return 0

        lax.fori_loop(start, stop, pair, 0)

    def key_side(self, own, start, stop):
        def pair(i, _):
            mask = visible(i, own, self.segc, self.segr, True)
            me, qi = own - self.first, i - self.first
            for h in range(HEADS):
                queries = self.proj[qi, :, head(2, h, self.width)]
                half = dot_nt(self.proj[me, :, head(3, h, self.width)], queries) * (0.5 * SCALE)
                bend = jnp.tanh(half)
                value = half + half * bend
                sigma = 0.5 + 0.5 * bend
                slope = sigma + value - value * sigma
                grad_att = self.gatt[qi, :, head(0, h, self.width)]
                grad_weights = dot_nt(self.proj[me, :, head(1, h, self.width)], grad_att)
                grad_raw = jnp.where(mask, grad_weights * slope * SCALE, 0.0).astype(BF16)
                weights = jnp.where(mask, value, 0.0).astype(BF16)
                self.join[:, head(3, h, self.width)] += dot(grad_raw, queries)
                self.join[:, head(1, h, self.width)] += dot(weights, grad_att)
            return 0

        lax.fori_loop(start, stop, pair, 0)


def early_kernel(
    index_ref,
    emb_ref,
    mate_ref,
    side_ref,
    side_mate_ref,
    w_in_ref,
    w_out_ref,
    proj_ref,
    att_ref,
    gatt_ref,
    join_ref,
    slope_ref,
    out_ref,
    segc_ref,
    segr_ref,
    cots_ref,
):
    own = index_ref[0]
    mate = index_ref[1]
    base = jnp.minimum(own, mate)
    last = jnp.maximum(own, mate)

    def write_to(place):
        def write(columns, value):
            proj_ref[place - base, :, columns] = value

        return write

    project(emb_ref[...], w_in_ref, write_to(own), slope_ref)
    project(mate_ref[...], w_in_ref, write_to(mate), None)
    hold_side(side_ref, own - base, cots_ref, segc_ref, segr_ref)
    hold_side(side_mate_ref, mate - base, cots_ref, segc_ref, segr_ref)
    att_ref[...] = jnp.zeros_like(att_ref)
    join_ref[...] = jnp.zeros_like(join_ref)
    chunks = Chunks(0, proj_ref, gatt_ref, segc_ref, segr_ref, join_ref)

    def forward(i, _):
        chunks.attend(i, 0, i + 1, att_ref.at[i])
        return 0

    lax.fori_loop(own - base, last - base + 1, forward, 0)

    @pl.when(base == 0)
    def _():
        def finish(i, _):
            chunks.finish(i, own, att_ref[i], cots_ref[i], emb_ref, w_out_ref, out_ref)
            return 0

        lax.fori_loop(own, last + 1, finish, 0)
        chunks.query_side(own, 0, own + 1)
        chunks.key_side(own, own, last + 1)


def late_kernel(count, *refs):
    index_ref, slots_ref = refs[:2]
    emb_refs = refs[2 : 2 + count]
    side_refs = refs[2 + count : 2 + 2 * count]
    (
        w_in_ref,
        w_out_ref,
        proj_pair_ref,
        att_pair_ref,
        gatt_pair_ref,
        join_early_ref,
        slope_ref,
        out_early_ref,
        out_ref,
        grad_ref,
        proj_ref,
        cot_ref,
        segc_ref,
        segr_ref,
        att_ref,
        gatt_ref,
        join_ref,
    ) = refs[2 + 2 * count :]
    own = index_ref[0]
    base = jnp.minimum(own, index_ref[1])
    last = jnp.maximum(own, index_ref[1])
    closed = base == 0

    for t in range(count):
        place = index_ref[t]
        hold_side(side_refs[t], place, cot_ref, segc_ref, segr_ref)
    for t in range(2):
        proj_ref[base + t] = proj_pair_ref[t]
        gatt_ref[base + t] = gatt_pair_ref[t]

    def write_to(place):
        def write(columns, value):
            proj_ref[place, :, columns] = value

        return write

    for t in range(2, count):
        project(emb_refs[t][...], w_in_ref, write_to(index_ref[t]), None)
    join_ref[...] = jnp.zeros_like(join_ref)
    chunks = Chunks(0, proj_ref, gatt_ref, segc_ref, segr_ref, join_ref)

    @pl.when(closed)
    def _():
        out_ref[...] = out_early_ref[...]

    def forward(i, _):
        begun = i <= last

        @pl.when(begun)
        def _():
            att_ref[...] = att_pair_ref[jnp.minimum(i - base, 1)]

        @pl.when(jnp.logical_not(begun))
        def _():
            att_ref[...] = jnp.zeros_like(att_ref)

        chunks.attend(i, 0, jnp.where(begun, base, i + 1), att_ref)
        chunks.finish(i, own, att_ref[...], cot_ref[i], emb_refs[0], w_out_ref, out_ref)
        return 0

    lax.fori_loop(jnp.where(closed, last + 1, own), count, forward, 0)
    chunks.query_side(own, jnp.where(closed, own + 1, 0), own + 1)
    chunks.key_side(own, jnp.where(closed, last + 1, own), count)

    grad_proj = ((join_ref[...] + join_early_ref[...]) * slope_ref[...]).astype(BF16)
    grad_normed = dot_nt(grad_proj, w_in_ref[...])
    normed, inverse = normalize(emb_refs[0][...].astype(F32))
    grad = norm_back(grad_normed, normed, inverse) + cot_ref[own].astype(F32)
    slot = iota((grad_ref.shape[0], grad.shape[0]), 0)
    hit = slot == slots_ref[0:1, :]
    for k in range(1, NIDS):
        hit = hit | (slot == slots_ref[k : k + 1, :])
    spread = jnp.where(hit, 1.0, 0.0).astype(BF16)
    grad_ref[...] = dot(spread, grad.astype(BF16)).astype(BF16)


def params():
    return pltpu.CompilerParams(vmem_limit_bytes=VMEM_LIMIT)


def flip(value, axis, offset):
    count = lax.axis_size(axis)
    return lax.ppermute(value, axis, [(i, i ^ offset) for i in range(count)])


def gather_blocks(value, axis, known):
    bit = lax.axis_size(axis)
    blocks = {0: value}
    while bit > 1:
        bit //= 2
        for t in list(blocks):
            blocks[t | bit] = known.get(t | bit)
            if blocks[t | bit] is None:
                blocks[t | bit] = flip(blocks[t], axis, bit)
    return [blocks[t] for t in range(lax.axis_size(axis))]


def after(value, earlier):
    return lax.optimization_barrier((value, earlier))[0]


def local(table, item_owner, item_row, segment_ids, w_in, w_out, cotangent):
    owners = lax.axis_size("table") * lax.axis_size("ctx")
    count = lax.axis_size("ctx")
    events, width = cotangent.shape
    id_count = events * NIDS
    capacity = 2 * ((id_count + owners - 1) // owners)
    slot_count = owners * capacity
    axes = ("table", "ctx")
    vmem = pl.BlockSpec(memory_space=pltpu.VMEM)
    smem = pl.BlockSpec(memory_space=pltpu.SMEM)

    def exchange(value):
        return lax.all_to_all(value, axes, split_axis=0, concat_axis=0, tiled=True)

    slots, wanted, side = pl.pallas_call(
        functools.partial(slots_kernel, capacity),
        out_shape=(
            jax.ShapeDtypeStruct((8, events), jnp.int32),
            jax.ShapeDtypeStruct((owners, capacity), jnp.int32),
            jax.ShapeDtypeStruct((events + EXTRA, width), BF16),
        ),
        compiler_params=params(),
        name="slots",
    )(item_owner.T, item_row.T, segment_ids.reshape(1, events), cotangent)
    asked = exchange(wanted)
    rows = pl.pallas_call(
        select_kernel,
        out_shape=jax.ShapeDtypeStruct((slot_count, width), BF16),
        compiler_params=params(),
        name="select",
    )(asked, table)
    fetched = exchange(rows.reshape(owners, capacity, width)).reshape(slot_count, width)
    held = after(side, rows)
    side_blocks = [side] + [flip(held, "ctx", t) for t in range(1, count)]
    slots, side_blocks = lax.optimization_barrier((slots, side_blocks))
    embedded = pl.pallas_call(
        embed_kernel,
        out_shape=jax.ShapeDtypeStruct((events, width), BF16),
        compiler_params=params(),
        name="embed",
    )(slots, fetched)
    emb_far = flip(embedded, "ctx", count // 2)
    emb_mate = flip(embedded, "ctx", 1)
    index = lax.axis_index("ctx").astype(jnp.int32) ^ jnp.arange(count, dtype=jnp.int32)
    event_shape = jax.ShapeDtypeStruct((events, width), BF16)
    early = pl.pallas_call(
        early_kernel,
        out_shape=(
            jax.ShapeDtypeStruct((2, events, 4 * width), BF16),
            jax.ShapeDtypeStruct((2, events, width), F32),
            jax.ShapeDtypeStruct((2, events, width), BF16),
            jax.ShapeDtypeStruct((events, 4 * width), F32),
            jax.ShapeDtypeStruct((events, 4 * width), F32),
            event_shape,
        ),
        in_specs=[smem] + [vmem] * 6,
        out_specs=(vmem,) * 6,
        scratch_shapes=[
            pltpu.VMEM((2, events, 128), F32),
            pltpu.VMEM((2, 8, events), F32),
            pltpu.VMEM((2, events, width), BF16),
        ],
        compiler_params=params(),
        name="early",
    )(index, embedded, emb_mate, *side_blocks[:2], w_in, w_out)
    emb_blocks = gather_blocks(embedded, "ctx", {1: emb_mate, count // 2: after(emb_far, early)})
    layer_out, slot_grad = pl.pallas_call(
        functools.partial(late_kernel, count),
        out_shape=(event_shape, jax.ShapeDtypeStruct((slot_count, width), BF16)),
        in_specs=[smem] + [vmem] * (9 + 2 * count),
        out_specs=(vmem, vmem),
        scratch_shapes=[
            pltpu.VMEM((count, events, 4 * width), BF16),
            pltpu.VMEM((count, events, width), BF16),
            pltpu.VMEM((count, events, 128), F32),
            pltpu.VMEM((count, 8, events), F32),
            pltpu.VMEM((events, width), F32),
            pltpu.VMEM((count, events, width), BF16),
            pltpu.VMEM((events, 4 * width), F32),
        ],
        compiler_params=params(),
        name="late",
    )(index, slots, *emb_blocks, *side_blocks, w_in, w_out, *early)
    returned = exchange(slot_grad.reshape(owners, capacity, width)).reshape(slot_count, width)
    row_grad = pl.pallas_call(
        collect_kernel,
        out_shape=jax.ShapeDtypeStruct(table.shape, F32),
        compiler_params=params(),
        name="collect",
    )(asked, returned)
    return layer_out, row_grad


def solution(mesh):
    rows = P(("table", "ctx"), None)
    return jax.shard_map(
        local,
        mesh=mesh,
        in_specs=(rows, rows, rows, P("table", "ctx"), P(), P(), rows),
        out_specs=(rows, rows),
        check_vma=False,
    )
```

time: 117 us -> 117 us (level)
  local copies, waits for them, and re-layouts: 2.41 us -> 14 us
  waiting for transfers between devices: 34.3 us -> 25.9 us
  starting transfers between devices: 8.79 us -> 5.28 us
  blocking collectives: 43.5 us -> 45 us
    all_to_all x1, waiting for transfers between devices: 24.5 us -> 0.01 us  [exchange(): return lax.all_to_all(value, axes, split_axis=0, concat_axis=0, tiled=True)]
    ppermute x9 -> x6, waiting for transfers between devices: 9.77 us -> 25.9 us  [flip(): return lax.ppermute(value, axis, [(i, i ^ offset) for i in range(count)])]
    unnamed x12 -> x38, local copies, waits for them, and re-layouts: 2.41 us -> 14 us
    ppermute x9 -> x6, starting transfers between devices: 6.01 us -> 2.5 us  [flip(): return lax.ppermute(value, axis, [(i, i ^ offset) for i in range(count)])]
    all_to_all x2, blocking collectives: 43.5 us -> 45 us  [exchange(): return lax.all_to_all(value, axes, split_axis=0, concat_axis=0, tiled=True)]
    pallas_call x1 -> x2, Pallas kernels: 21.8 us -> 22.3 us  [the longest x1 12.5 us: local(): pl.pallas_call(functools.partial(late_kernel, count), out_shape=(event_sh...]
  transfers between devices with their start and end apart: 10 -> 7, of which waited for: 5 -> 4; matrix products, arithmetic and copies ran while one was open for 0% -> 0% of each run, Pallas kernels for 1% -> 8%
where the time goes in v3:
time: 117 us
  blocking collectives  45 us (38%)
  Pallas kernels  26 us (22%)
  waiting for transfers between devices  25.9 us (22%)
  local copies, waits for them, and re-layouts  14 us (12%)
  starting transfers between devices  5.28 us (5%)
    all_to_all x2, blocking collectives, exchange(): return lax.all_to_all(value, axes, split_axis=0, concat_axis=0, tiled=True)  45 us
    ppermute x6, waiting for transfers between devices, flip(): return lax.ppermute(value, axis, [(i, i ^ offset) for i in range(count)])  25.9 us
    unnamed x38, local copies, waits for them, and re-layouts  14 us
    pallas_call x1, Pallas kernels, local(): pl.pallas_call(functools.partial(late_kernel, count), out_shape=(event_sh...  12.5 us
    pallas_call x1, Pallas kernels, local(): pl.pallas_call(early_kernel, out_shape=(jax.ShapeDtypeStruct((2, events,...  9.74 us
    all_to_all x1, starting transfers between devices, exchange(): return lax.all_to_all(value, axes, split_axis=0, concat_axis=0, tiled=True)  2.78 us
    ppermute x6, starting transfers between devices, flip(): return lax.ppermute(value, axis, [(i, i ^ offset) for i in range(count)])  2.5 us
  transfers between devices with their start and end apart: 7, of which 4 were waited for; matrix products, arithmetic and copies ran while one was open for 0% of the time, Pallas kernels for 8%

profile of v3, /device:TPU:0, one launch (start us, length us, event | category | flops | bytes accessed | tf_op | source)
XLA Modules:
  0.0 116.9 jit_solution(12088767186041904007)
XLA Ops:
  0.6 0.0 copy-start.15
  0.6 0.9 copy-done.15
  1.6 0.0 copy-start.16
  1.6 0.7 copy-done.16
  2.3 0.0 copy-start.17
  2.3 0.7 copy-done.17
  2.9 0.0 copy-start.18
  2.9 0.7 copy-done.18
  3.6 0.4 slots.1
  4.0 0.0 copy-start.4
  4.0 14.3 %all_to_all.21 = s32[32,1,32]{2,1,0:T(1,128)S(1)} all-to-all(s32[32,1,32]{2,1,0:T(1,128)S(1)} %bitcast.16), channel_id=1, replica_groups=mesh['table'=8,'ctx'=4] {'table','ctx'}, dimensions={0} | all-to-all | bytes 8192 | tf_op jit(solution)/shard_map/all_to_all | solution.py:410
  18.3 0.0 copy-start.10
  18.3 1.0 copy-done.10
  19.3 0.8 select.1
  20.1 0.0 copy-start.1
  20.1 1.0 copy-done.1
  21.1 2.8 %all-to-all-start.1 = ((bf16[32,32,512]{2,1,0:T(8,128)(2,1)}), bf16[32,32,512]{2,1,0:T(8,128)(2,1)S(1)}, u32[]{:S(2)}, u32[]{:S(2)}) async-start(bf16[32,32,512]{2,1,0:T(8,128)(2,1)} %bitcast.11), calls=%async_computation.1 | async-start | bytes 2097152 | tf_op jit(solution)/shard_map/all_to_all | solution.py:410
  23.9 1.5 %collective-permute-start.2 = (bf16[272,512]{1,0:T(8,128)(2,1)S(1)}, bf16[272,512]{1,0:T(8,128)(2,1)S(1)}, u32[]{:S(2)}, u32[]{:S(2)}) collective-permute-start(bf16[272,512]{1,0:T(8,128)(2,1)S(1)} %get-tuple-element.25.side_ref.refs_6_), channel_id=1, source_target_pairs={{0,3},{1,2},{2,1},{3,0},{4,7},{5,6},{6,5},{7,4},{8,11},{9,10},{10,... | collective-permute-start | bytes 835592 | tf_op jit(solution)/shard_map/ppermute | solution.py:379
  25.3 0.4 collective-permute-start.1
  25.7 0.1 collective-permute-start
  25.8 15.7 %collective-permute-done.2.refs_9_ = bf16[272,512]{1,0:T(8,128)(2,1)S(1)} collective-permute-done((bf16[272,512]{1,0:T(8,128)(2,1)S(1)}, bf16[272,512]{1,0:T(8,128)(2,1)S(1)}, u32[]{:S(2)}, u32[]{:S(2)}) %collective-permute-start.2) | collective-permute-done | bytes 278560 | tf_op jit(solution)/shard_map/ppermute | solution.py:379
  41.6 0.7 copy-done.11
  42.3 7.5 %collective-permute-done.1.refs_8_ = bf16[272,512]{1,0:T(8,128)(2,1)S(1)} collective-permute-done((bf16[272,512]{1,0:T(8,128)(2,1)S(1)}, bf16[272,512]{1,0:T(8,128)(2,1)S(1)}, u32[]{:S(2)}, u32[]{:S(2)}) %collective-permute-start.1) | collective-permute-done | bytes 278560 | tf_op jit(solution)/shard_map/ppermute | solution.py:379
  49.8 0.7 copy-done.13
  50.5 0.0 collective-permute-done.side_mate_ref.refs_7_
  50.5 0.7 copy-done.7
  51.2 0.0 all-to-all-done.1
  51.2 0.0 copy-done.4
  51.2 0.7 embed.1.emb_ref.refs_2_
  52.0 0.1 collective-permute-start.3
  52.0 0.4 collective-permute-start.4
  52.5 1.1 collective-permute-done.3.mate_ref.refs_3_
  53.6 0.0 copy-done
  53.6 1.0 copy-done.2
  54.6 1.0 copy-done.5
  55.6 1.0 copy-done.8
  56.5 9.7 %early.1 = (bf16[2,256,2048]{2,1,0:T(8,128)(2,1)S(1)}, f32[2,256,512]{2,1,0:T(8,128)S(1)}, bf16[2,256,512]{2,1,0:T(8,128)(2,1)S(1)}, f32[256,2048]{1,0:T(8,128)S...) custom-call(s32[4]{0:T(128)S(1)} %iota_xor_fusion.index_ref.refs_0_, ...), custom_call_target="tpu_custom_call" | custom-call | tf_op jit(solution)/shard_map/early/pallas_call | solution.py:443
  66.3 0.0 collective-permute-done.4.refs_4_
  66.3 0.1 collective-permute-start.5
  66.4 1.5 %collective-permute-done.5.refs_5_ = bf16[256,512]{1,0:T(8,128)(2,1)S(1)} collective-permute-done((bf16[256,512]{1,0:T(8,128)(2,1)S(1)}, bf16[256,512]{1,0:T(8,128)(2,1)S(1)}, u32[]{:S(2)}, u32[]{:S(2)}) %collective-permute-start.5) | collective-permute-done | bytes 262176 | tf_op jit(solution)/shard_map/ppermute | solution.py:379
  67.9 0.0 copy-done.6
  67.9 1.0 copy-done.3
  68.9 1.0 copy-done.9
  69.9 1.0 copy-done.12
  70.9 1.0 copy-done.14
  71.8 12.5 %late.1 = (bf16[256,512]{1,0:T(8,128)(2,1)}, bf16[1024,512]{1,0:T(8,128)(2,1)S(1)}) custom-call(s32[4]{0:T(128)S(1)} %iota_xor_fusion.index_ref.refs_0_, s32[8,256]{1,0:T(8,128)S(1)} %get-tuple-element.24.slots_ref.refs_1_, bf16[256,512]{1,0:T(8,128)(2,1)S(1)} %embed.1.emb_ref.refs_2_, bf16[256,512]{1,0:T(8,128)(2,1)S(1)} %collective-permute-done.3.mate_ref.refs_3_, ...), custom_call_target="tpu_custom_call" | custom-call | tf_op jit(solution)/shard_map/late/pallas_call | solution.py:464
  84.3 30.8 %all_to_all.22 = bf16[32,32,512]{2,1,0:T(8,128)(2,1)S(1)} all-to-all(bf16[32,32,512]{2,1,0:T(8,128)(2,1)S(1)} %bitcast.13), channel_id=1, replica_groups=mesh['table'=8,'ctx'=4] {'table','ctx'}, dimensions={0} | all-to-all | bytes 2097152 | tf_op jit(solution)/shard_map/all_to_all | solution.py:410
  115.1 1.8 %collect.1 = f32[512,512]{1,0:T(8,128)} custom-call(s32[32,32]{1,0:T(8,128)S(1)} %bitcast.15, bf16[1024,512]{1,0:T(8,128)(2,1)S(1)} %bitcast.12), custom_call_target="tpu_custom_call" | custom-call | tf_op jit(solution)/shard_map/collect/pallas_call | solution.py:482
  (13 shorter events, 0.0 us)
Async XLA Ops:
  0.6 1.0 copy-start.15
  1.6 0.7 copy-start.16
  2.3 0.7 copy-start.17
  2.9 0.7 copy-start.18
  4.0 47.2 %copy-start.4 = (bf16[272,512]{1,0:T(8,128)(2,1)}, bf16[272,512]{1,0:T(8,128)(2,1)S(1)}, u32[]{:S(2)}) copy-start(bf16[272,512]{1,0:T(8,128)(2,1)S(1)} %get-tuple-element.25.side_ref.refs_6_) | copy-start | bytes 835588
  18.3 1.0 copy-start.10
  20.1 1.0 copy-start.1
  21.1 32.5 %copy-start = (bf16[512,2048]{1,0:T(8,128)(2,1)S(1)}, bf16[512,2048]{1,0:T(8,128)(2,1)}, u32[]{:S(2)}) copy-start(bf16[512,2048]{1,0:T(8,128)(2,1)} %refs_10_.1) | copy-start | bytes 6291460
  21.1 30.1 %all-to-all-start.1 = ((bf16[32,32,512]{2,1,0:T(8,128)(2,1)}), bf16[32,32,512]{2,1,0:T(8,128)(2,1)S(1)}, u32[]{:S(2)}, u32[]{:S(2)}) async-start(bf16[32,32,512]{2,1,0:T(8,128)(2,1)} %bitcast.11), calls=%async_computation.1 | async-start | bytes 2097152 | tf_op jit(solution)/shard_map/all_to_all | solution.py:410
  23.9 17.7 %collective-permute-start.2 = (bf16[272,512]{1,0:T(8,128)(2,1)S(1)}, bf16[272,512]{1,0:T(8,128)(2,1)S(1)}, u32[]{:S(2)}, u32[]{:S(2)}) collective-permute-start(bf16[272,512]{1,0:T(8,128)(2,1)S(1)} %get-tuple-element.25.side_ref.refs_6_), channel_id=1, source_target_pairs={{0,3},{1,2},{2,1},{3,0},{4,7},{5,6},{6,5},{7,4},{8,11},{9,10},{10,... | collective-permute-start | bytes 835592 | tf_op jit(solution)/shard_map/ppermute | solution.py:379
  25.3 24.4 %collective-permute-start.1 = (bf16[272,512]{1,0:T(8,128)(2,1)S(1)}, bf16[272,512]{1,0:T(8,128)(2,1)S(1)}, u32[]{:S(2)}, u32[]{:S(2)}) collective-permute-start(bf16[272,512]{1,0:T(8,128)(2,1)S(1)} %get-tuple-element.25.side_ref.refs_6_), channel_id=1, source_target_pairs={{0,2},{1,3},{2,0},{3,1},{4,6},{5,7},{6,4},{7,5},{8,10},{9,11},{10,... | collective-permute-start | bytes 835592 | tf_op jit(solution)/shard_map/ppermute | solution.py:379
  25.7 24.8 %collective-permute-start = (bf16[272,512]{1,0:T(8,128)(2,1)S(1)}, bf16[272,512]{1,0:T(8,128)(2,1)S(1)}, u32[]{:S(2)}, u32[]{:S(2)}) collective-permute-start(bf16[272,512]{1,0:T(8,128)(2,1)S(1)} %get-tuple-element.25.side_ref.refs_6_), channel_id=1, source_target_pairs={{0,1},{1,0},{2,3},{3,2},{4,5},{5,4},{6,7},{7,6},{8,9},{9,8},{10,11... | collective-permute-start | bytes 835592 | tf_op jit(solution)/shard_map/ppermute | solution.py:379
  41.6 0.7 copy-start.11
  49.8 0.7 copy-start.13
  50.5 0.7 copy-start.7
  52.0 1.6 %collective-permute-start.3 = (bf16[256,512]{1,0:T(8,128)(2,1)S(1)}, bf16[256,512]{1,0:T(8,128)(2,1)S(1)}, u32[]{:S(2)}, u32[]{:S(2)}) collective-permute-start(bf16[256,512]{1,0:T(8,128)(2,1)S(1)} %embed.1.emb_ref.refs_2_), channel_id=1, source_target_pairs={{0,1},{1,0},{2,3},{3,2},{4,5},{5,4},{6,7},{7,6},{8,9},{9,8},{10,11... | collective-permute-start | bytes 786440 | tf_op jit(solution)/shard_map/ppermute | solution.py:379
  52.0 14.2 %collective-permute-start.4 = (bf16[256,512]{1,0:T(8,128)(2,1)S(1)}, bf16[256,512]{1,0:T(8,128)(2,1)S(1)}, u32[]{:S(2)}, u32[]{:S(2)}) collective-permute-start(bf16[256,512]{1,0:T(8,128)(2,1)S(1)} %embed.1.emb_ref.refs_2_), channel_id=1, source_target_pairs={{0,2},{1,3},{2,0},{3,1},{4,6},{5,7},{6,4},{7,5},{8,10},{9,11},{10,... | collective-permute-start | bytes 786440 | tf_op jit(solution)/shard_map/ppermute | solution.py:379
  53.6 1.0 copy-start.2
  54.6 1.0 copy-start.5
  55.6 1.0 copy-start.8
  56.5 11.4 %copy-start.6 = (bf16[272,512]{1,0:T(8,128)(2,1)S(1)}, bf16[272,512]{1,0:T(8,128)(2,1)}, u32[]{:S(2)}) copy-start(bf16[272,512]{1,0:T(8,128)(2,1)} %copy-done.4) | copy-start | bytes 835588
  66.3 1.6 %collective-permute-start.5 = (bf16[256,512]{1,0:T(8,128)(2,1)S(1)}, bf16[256,512]{1,0:T(8,128)(2,1)S(1)}, u32[]{:S(2)}, u32[]{:S(2)}) collective-permute-start(bf16[256,512]{1,0:T(8,128)(2,1)S(1)} %collective-permute-done.4.refs_4_), channel_id=1, source_target_pairs={{0,1},{1,0},{2,3},{3,2},{4,5},{5,4},{6,7},{7,6},{8,9},{9,8},{10,11... | collective-permute-start | bytes 786440 | tf_op jit(solution)/shard_map/ppermute | solution.py:379
  67.9 1.0 copy-start.3
  68.9 1.0 copy-start.9
  69.9 1.0 copy-start.12
  70.8 1.0 copy-start.14

commit v4 on v3

--- a/solution.py
+++ b/solution.py
@@ -11,7 +11,6 @@
 HEAD_DIM = 128
 NIDS = 2
 EPS = 1e-06
-VMEM_LIMIT = 40 * 1024 * 1024
 
 F32 = jnp.float32
 BF16 = jnp.bfloat16
@@ -46,18 +45,38 @@
 
 
 EXTRA = 16
+WHOLE = 61
 
 
 def slots_kernel(
-    capacity, owner_ref, row_ref, seg_ref, cot_ref, slots_ref, wanted_ref, side_ref
+    capacity,
+    owner_in,
+    row_in,
+    seg_in,
+    cot_in,
+    slots_ref,
+    wanted_ref,
+    side_ref,
+    owner_ref,
+    row_ref,
+    seg_ref,
+    sems,
 ):
-    side_ref[0 : cot_ref.shape[0], :] = cot_ref[...]
-    side_ref[cot_ref.shape[0] :, :] = jnp.zeros((EXTRA, side_ref.shape[1]), BF16)
-    segments = seg_ref[...].astype(F32)
-    side_ref[cot_ref.shape[0] :, 0 : seg_ref.shape[1]] = jnp.broadcast_to(
-        segments, (EXTRA, seg_ref.shape[1])
-    ).astype(BF16)
-    events = owner_ref.shape[1]
+    events, width = cot_in.shape
+    pairs = (
+        (owner_in, owner_ref),
+        (row_in, row_ref),
+        (seg_in, seg_ref),
+        (cot_in, side_ref.at[0:events]),
+    )
+    copies = [pltpu.make_async_copy(a, b, sems.at[i]) for i, (a, b) in enumerate(pairs)]
+    for copy in copies:
+        copy.start()
+    for copy in copies[:3]:
+        copy.wait()
+    side_ref[events:, :] = jnp.zeros((EXTRA, width), BF16)
+    segments = jnp.broadcast_to(seg_ref[...].astype(F32), (EXTRA, events))
+    side_ref[events:, 0:events] = segments.astype(BF16)
     owners = wanted_ref.shape[0]
     owner = jnp.concatenate([owner_ref[k : k + 1, :] for k in range(NIDS)], 1)
     row = jnp.concatenate([row_ref[k : k + 1, :] for k in range(NIDS)], 1)
@@ -77,9 +96,16 @@
         (named_f * low).astype(BF16), ranked
     )
     wanted_ref[...] = wanted.astype(jnp.int32)
-
-
-def select_kernel(asked_ref, table_ref, out_ref):
+    for copy in copies[3:]:
+        copy.wait()
+
+
+def select_kernel(asked_in, table_in, out_ref, asked_ref, table_ref, sems):
+    pairs = ((asked_in, asked_ref), (table_in, table_ref))
+    copies = [pltpu.make_async_copy(a, b, sems.at[i]) for i, (a, b) in enumerate(pairs)]
+    for copy in copies:
+        copy.start()
+    copies[0].wait()
     owners, capacity = asked_ref.shape
     rows = table_ref.shape[0]
     columns = jnp.transpose(asked_ref[...])
@@ -87,7 +113,9 @@
     chosen = jnp.concatenate(
         [jnp.where(lane == columns[:, s : s + 1], 1.0, 0.0) for s in range(owners)], 0
     )
-    out_ref[...] = dot(chosen.astype(BF16), table_ref[...]).astype(BF16)
+    chosen = chosen.astype(BF16)
+    copies[1].wait()
+    out_ref[...] = dot(chosen, table_ref[...]).astype(BF16)
 
 
 def embed_kernel(slots_ref, fetched_ref, out_ref):
@@ -370,8 +398,8 @@
     grad_ref[...] = dot(spread, grad.astype(BF16)).astype(BF16)
 
 
-def params():
-    return pltpu.CompilerParams(vmem_limit_bytes=VMEM_LIMIT)
+def params(mebibytes=12):
+    return pltpu.CompilerParams(vmem_limit_bytes=mebibytes * 1024 * 1024)
 
 
 def flip(value, axis, offset):
@@ -409,6 +437,7 @@
     def exchange(value):
         return lax.all_to_all(value, axes, split_axis=0, concat_axis=0, tiled=True)
 
+    anywhere = pl.BlockSpec(memory_space=pl.ANY)
     slots, wanted, side = pl.pallas_call(
         functools.partial(slots_kernel, capacity),
         out_shape=(
@@ -416,19 +445,35 @@
             jax.ShapeDtypeStruct((owners, capacity), jnp.int32),
             jax.ShapeDtypeStruct((events + EXTRA, width), BF16),
         ),
-        compiler_params=params(),
+        in_specs=[anywhere] * 4,
+        out_specs=(vmem,) * 3,
+        scratch_shapes=[
+            pltpu.VMEM((NIDS, events), jnp.int32),
+            pltpu.VMEM((NIDS, events), jnp.int32),
+            pltpu.VMEM((1, events), jnp.int32),
+            pltpu.SemaphoreType.DMA((4,)),
+        ],
+        compiler_params=params(WHOLE),
         name="slots",
     )(item_owner.T, item_row.T, segment_ids.reshape(1, events), cotangent)
     asked = exchange(wanted)
     rows = pl.pallas_call(
         select_kernel,
         out_shape=jax.ShapeDtypeStruct((slot_count, width), BF16),
-        compiler_params=params(),
+        in_specs=[anywhere] * 2,
+        out_specs=vmem,
+        scratch_shapes=[
+            pltpu.VMEM((owners, capacity), jnp.int32),
+            pltpu.VMEM(table.shape, BF16),
+            pltpu.SemaphoreType.DMA((2,)),
+        ],
+        compiler_params=params(WHOLE),
         name="select",
     )(asked, table)
     fetched = exchange(rows.reshape(owners, capacity, width)).reshape(slot_count, width)
-    held = after(side, rows)
-    side_blocks = [side] + [flip(held, "ctx", t) for t in range(1, count)]
+    side_far = flip(side, "ctx", count // 2)
+    side_mate = flip(side, "ctx", 1)
+    side_blocks = gather_blocks(side, "ctx", {1: side_mate, count // 2: after(side_far, rows)})
     slots, side_blocks = lax.optimization_barrier((slots, side_blocks))
     embedded = pl.pallas_call(
         embed_kernel,
@@ -457,7 +502,7 @@
             pltpu.VMEM((2, 8, events), F32),
             pltpu.VMEM((2, events, width), BF16),
         ],
-        compiler_params=params(),
+        compiler_params=params(20),
         name="early",
     )(index, embedded, emb_mate, *side_blocks[:2], w_in, w_out)
     emb_blocks = gather_blocks(embedded, "ctx", {1: emb_mate, count // 2: after(emb_far, early)})
@@ -475,7 +520,7 @@
             pltpu.VMEM((count, events, width), BF16),
             pltpu.VMEM((events, 4 * width), F32),
         ],
-        compiler_params=params(),
+        compiler_params=params(28),
         name="late",
     )(index, slots, *emb_blocks, *side_blocks, w_in, w_out, *early)
     returned = exchange(slot_grad.reshape(owners, capacity, width)).reshape(slot_count, width)

time: 117 us -> 115 us (0.983)
  Pallas kernels: 26 us -> 30 us
  local copies, waits for them, and re-layouts: 14 us -> 10.6 us
  blocking collectives: 45 us -> 43.2 us
  waiting for transfers between devices: 25.9 us -> 24.1 us
    ppermute x6, waiting for transfers between devices: 25.9 us -> 18.7 us  [flip(): return lax.ppermute(value, axis, [(i, i ^ offset) for i in range(count)])]
    all_to_all x1, waiting for transfers between devices: 0.01 us -> 5.41 us  [exchange(): return lax.all_to_all(value, axes, split_axis=0, concat_axis=0, tiled=True)]
    unnamed x38 -> x32, local copies, waits for them, and re-layouts: 14 us -> 10.6 us
    pallas_call x1, Pallas kernels: 0.82 us -> 2.78 us  [local(): pl.pallas_call(select_kernel, out_shape=jax.ShapeDtypeStruct((slot_count,...]
    all_to_all x2, blocking collectives: 45 us -> 43.2 us  [exchange(): return lax.all_to_all(value, axes, split_axis=0, concat_axis=0, tiled=True)]
    pallas_call x1, Pallas kernels: 0.36 us -> 1.82 us  [local(): pl.pallas_call(functools.partial(slots_kernel, capacity), out_shape=(jax....]
  transfers between devices with their start and end apart: 7 -> 7, of which waited for: 4 -> 4; matrix products, arithmetic and copies ran while one was open for 0% -> 0% of each run, Pallas kernels for 8% -> 9%
where the time goes in v4:
time: 115 us
  blocking collectives  43.2 us (38%)
  Pallas kernels  30 us (26%)
  waiting for transfers between devices  24.1 us (21%)
  local copies, waits for them, and re-layouts  10.6 us (9%)
  starting transfers between devices  6.19 us (5%)
    all_to_all x2, blocking collectives, exchange(): return lax.all_to_all(value, axes, split_axis=0, concat_axis=0, tiled=True)  43.2 us
    ppermute x6, waiting for transfers between devices, flip(): return lax.ppermute(value, axis, [(i, i ^ offset) for i in range(count)])  18.7 us
    pallas_call x1, Pallas kernels, local(): pl.pallas_call(functools.partial(late_kernel, count), out_shape=(event_sh...  13.1 us
    unnamed x32, local copies, waits for them, and re-layouts  10.6 us
    pallas_call x1, Pallas kernels, local(): pl.pallas_call(early_kernel, out_shape=(jax.ShapeDtypeStruct((2, events,...  9.86 us
    all_to_all x1, waiting for transfers between devices, exchange(): return lax.all_to_all(value, axes, split_axis=0, concat_axis=0, tiled=True)  5.41 us
    ppermute x6, starting transfers between devices, flip(): return lax.ppermute(value, axis, [(i, i ^ offset) for i in range(count)])  3.39 us
    all_to_all x1, starting transfers between devices, exchange(): return lax.all_to_all(value, axes, split_axis=0, concat_axis=0, tiled=True)  2.8 us
  transfers between devices with their start and end apart: 7, of which 4 were waited for; matrix products, arithmetic and copies ran while one was open for 0% of the time, Pallas kernels for 9%

profile of v4, /device:TPU:0, one launch (start us, length us, event | category | flops | bytes accessed | tf_op | source)
XLA Modules:
  0.0 114.8 jit_solution(6311291915737226157)
XLA Ops:
  0.6 1.8 %slots.1 = (s32[8,256]{1,0:T(8,128)}, s32[32,32]{1,0:T(8,128)}, bf16[272,512]{1,0:T(8,128)(2,1)}) custom-call(s32[2,256]{1,0:T(2,128)} %bitcast.17, s32[2,256]{1,0:T(2,128)} %bitcast.18, s32[1,256]{1,0:T(1,128)} %seg_in.1, bf16[256,512]{1,0:T(8,128)(2,1)} %cot_in.1), custom_call_target="tpu_custom_call" | custom-call | tf_op jit(solution)/shard_map/slots/pallas_call | solution.py:441
  2.5 0.0 copy-start.2
  2.5 0.0 copy-start.15
  2.5 14.5 %all_to_all.21 = s32[32,1,32]{2,1,0:T(1,128)} all-to-all(s32[32,1,32]{2,1,0:T(1,128)} %bitcast.16), channel_id=1, replica_groups=mesh['table'=8,'ctx'=4] {'table','ctx'}, dimensions={0} | all-to-all | bytes 8192 | tf_op jit(solution)/shard_map/all_to_all | solution.py:438
  17.0 2.8 %select.1 = bf16[1024,512]{1,0:T(8,128)(2,1)} custom-call(s32[32,32]{1,0:T(8,128)} %bitcast.13, bf16[512,512]{1,0:T(8,128)(2,1)} %table_in.1), custom_call_target="tpu_custom_call" | custom-call | tf_op jit(solution)/shard_map/select/pallas_call | solution.py:460
  19.8 0.0 copy-start
  19.8 2.8 %all-to-all-start.1 = ((bf16[32,32,512]{2,1,0:T(8,128)(2,1)}), bf16[32,32,512]{2,1,0:T(8,128)(2,1)S(1)}, u32[]{:S(2)}, u32[]{:S(2)}) async-start(bf16[32,32,512]{2,1,0:T(8,128)(2,1)} %bitcast.15), calls=%async_computation.1 | async-start | bytes 2097152 | tf_op jit(solution)/shard_map/all_to_all | solution.py:438
  22.6 0.0 copy-done.2
  22.6 1.7 %collective-permute-start.1 = (bf16[272,512]{1,0:T(8,128)(2,1)S(1)}, bf16[272,512]{1,0:T(8,128)(2,1)S(1)}, u32[]{:S(2)}, u32[]{:S(2)}) collective-permute-start(bf16[272,512]{1,0:T(8,128)(2,1)S(1)} %copy-done.2), channel_id=1, source_target_pairs={{0,2},{1,3},{2,0},{3,1},{4,6},{5,7},{6,4},{7,5},{8,10},{9,11},{10,... | collective-permute-start | bytes 835592 | tf_op jit(solution)/shard_map/ppermute | solution.py:407
  24.3 0.0 collective-permute-start
  24.3 16.8 %collective-permute-done.1.refs_8_ = bf16[272,512]{1,0:T(8,128)(2,1)S(1)} collective-permute-done((bf16[272,512]{1,0:T(8,128)(2,1)S(1)}, bf16[272,512]{1,0:T(8,128)(2,1)S(1)}, u32[]{:S(2)}, u32[]{:S(2)}) %collective-permute-start.1) | collective-permute-done | bytes 278560 | tf_op jit(solution)/shard_map/ppermute | solution.py:407
  41.1 0.0 collective-permute-start.2
  41.1 0.0 copy-start.10
  41.1 0.7 copy-done.10
  41.8 0.0 collective-permute-done.side_mate_ref.refs_7_
  41.8 0.0 copy-start.4
  41.8 0.7 copy-done.4
  42.5 0.1 collective-permute-done.2.refs_9_
  42.7 0.0 copy-start.12
  42.7 0.7 copy-done.12
  43.4 5.4 %all-to-all-done.1 = bf16[32,32,512]{2,1,0:T(8,128)(2,1)S(1)} async-done(((bf16[32,32,512]{2,1,0:T(8,128)(2,1)}), bf16[32,32,512]{2,1,0:T(8,128)(2,1)S(1)}, u32[]{:S(2)}, u32[]{:S(2)}) %all-to-all-start.1) | async-done | bytes 1048608 | tf_op jit(solution)/shard_map/all_to_all | solution.py:438
  48.8 0.0 copy-done.15
  48.8 0.7 embed.1.emb_ref.refs_2_
  49.5 0.1 collective-permute-start.3
  49.6 1.5 %collective-permute-start.4 = (bf16[256,512]{1,0:T(8,128)(2,1)S(1)}, bf16[256,512]{1,0:T(8,128)(2,1)}, u32[]{:S(2)}, u32[]{:S(2)}) collective-permute-start(bf16[256,512]{1,0:T(8,128)(2,1)S(1)} %embed.1.emb_ref.refs_2_), channel_id=1, source_target_pairs={{0,2},{1,3},{2,0},{3,1},{4,6},{5,7},{6,4},{7,5},{8,10},{9,11},{10,... | collective-permute-start | bytes 786440 | tf_op jit(solution)/shard_map/ppermute | solution.py:407
  51.1 0.0 collective-permute-done.3.mate_ref.refs_3_
  51.1 0.0 copy-start.7
  51.1 0.7 copy-done.7
  51.8 0.0 copy-done
  51.9 0.0 copy-start.1
  51.9 1.0 copy-done.1
  52.9 0.0 copy-start.3
  52.9 1.0 copy-done.3
  53.9 1.0 copy-done.5
  54.8 0.9 copy-done.8
  55.8 9.9 %early.1 = (bf16[2,256,2048]{2,1,0:T(8,128)(2,1)S(1)}, f32[2,256,512]{2,1,0:T(8,128)S(1)}, bf16[2,256,512]{2,1,0:T(8,128)(2,1)S(1)}, f32[256,2048]{1,0:T(8,128)S...) custom-call(s32[4]{0:T(128)S(1)} %iota_xor_fusion.index_ref.refs_0_, ...), custom_call_target="tpu_custom_call" | custom-call | tf_op jit(solution)/shard_map/early/pallas_call | solution.py:488
  65.6 0.0 collective-permute-done.4.refs_4_
  65.6 0.1 collective-permute-start.5
  65.7 1.7 %collective-permute-done.5.refs_5_ = bf16[256,512]{1,0:T(8,128)(2,1)S(1)} collective-permute-done((bf16[256,512]{1,0:T(8,128)(2,1)}, bf16[256,512]{1,0:T(8,128)(2,1)S(1)}, u32[]{:S(2)}, u32[]{:S(2)}) %collective-permute-start.5) | collective-permute-done | bytes 262176 | tf_op jit(solution)/shard_map/ppermute | solution.py:407
  67.5 1.0 copy-done.6
  68.4 0.9 copy-done.9
  69.4 1.0 copy-done.11
  70.3 1.0 copy-done.13
  71.3 13.1 %late.1 = (bf16[256,512]{1,0:T(8,128)(2,1)}, bf16[1024,512]{1,0:T(8,128)(2,1)S(1)}) custom-call(s32[4]{0:T(128)S(1)} %iota_xor_fusion.index_ref.refs_0_, s32[8,256]{1,0:T(8,128)S(1)} %copy-done.15, bf16[256,512]{1,0:T(8,128)(2,1)S(1)} %embed.1.emb_ref.refs_2_, bf16[256,512]{1,0:T(8,128)(2,1)S(1)} %copy-done.9, ...), custom_call_target="tpu_custom_call" | custom-call | tf_op jit(solution)/shard_map/late/pallas_call | solution.py:509
  84.3 0.0 copy-start.14
  84.3 28.7 %all_to_all.22 = bf16[32,32,512]{2,1,0:T(8,128)(2,1)S(1)} all-to-all(bf16[32,32,512]{2,1,0:T(8,128)(2,1)S(1)} %bitcast.12), channel_id=1, replica_groups=mesh['table'=8,'ctx'=4] {'table','ctx'}, dimensions={0} | all-to-all | bytes 2097152 | tf_op jit(solution)/shard_map/all_to_all | solution.py:438
  113.0 0.0 copy-done.14
  113.0 1.8 %collect.1 = f32[512,512]{1,0:T(8,128)} custom-call(s32[32,32]{1,0:T(8,128)S(1)} %bitcast.14, bf16[1024,512]{1,0:T(8,128)(2,1)S(1)} %bitcast.11), custom_call_target="tpu_custom_call" | custom-call | tf_op jit(solution)/shard_map/collect/pallas_call | solution.py:527
  (7 shorter events, 0.0 us)
Async XLA Ops:
  2.5 20.1 %copy-start.2 = (bf16[272,512]{1,0:T(8,128)(2,1)S(1)}, bf16[272,512]{1,0:T(8,128)(2,1)}, u32[]{:S(2)}) copy-start(bf16[272,512]{1,0:T(8,128)(2,1)} %get-tuple-element.25.side_ref.refs_6_) | copy-start | bytes 835588
  2.5 46.3 %copy-start.15 = (s32[8,256]{1,0:T(8,128)S(1)}, s32[8,256]{1,0:T(8,128)}, u32[]{:S(2)}) copy-start(s32[8,256]{1,0:T(8,128)} %get-tuple-element.24.slots_ref.refs_1_) | copy-start | bytes 24580
  19.8 32.1 %copy-start = (bf16[512,2048]{1,0:T(8,128)(2,1)S(1)}, bf16[512,2048]{1,0:T(8,128)(2,1)}, u32[]{:S(2)}) copy-start(bf16[512,2048]{1,0:T(8,128)(2,1)} %refs_10_.1) | copy-start | bytes 6291460
  19.8 29.0 %all-to-all-start.1 = ((bf16[32,32,512]{2,1,0:T(8,128)(2,1)}), bf16[32,32,512]{2,1,0:T(8,128)(2,1)S(1)}, u32[]{:S(2)}, u32[]{:S(2)}) async-start(bf16[32,32,512]{2,1,0:T(8,128)(2,1)} %bitcast.15), calls=%async_computation.1 | async-start | bytes 2097152 | tf_op jit(solution)/shard_map/all_to_all | solution.py:438
  22.6 18.5 %collective-permute-start.1 = (bf16[272,512]{1,0:T(8,128)(2,1)S(1)}, bf16[272,512]{1,0:T(8,128)(2,1)S(1)}, u32[]{:S(2)}, u32[]{:S(2)}) collective-permute-start(bf16[272,512]{1,0:T(8,128)(2,1)S(1)} %copy-done.2), channel_id=1, source_target_pairs={{0,2},{1,3},{2,0},{3,1},{4,6},{5,7},{6,4},{7,5},{8,10},{9,11},{10,... | collective-permute-start | bytes 835592 | tf_op jit(solution)/shard_map/ppermute | solution.py:407
  24.3 17.5 %collective-permute-start = (bf16[272,512]{1,0:T(8,128)(2,1)S(1)}, bf16[272,512]{1,0:T(8,128)(2,1)S(1)}, u32[]{:S(2)}, u32[]{:S(2)}) collective-permute-start(bf16[272,512]{1,0:T(8,128)(2,1)S(1)} %copy-done.2), channel_id=1, source_target_pairs={{0,1},{1,0},{2,3},{3,2},{4,5},{5,4},{6,7},{7,6},{8,9},{9,8},{10,11... | collective-permute-start | bytes 835592 | tf_op jit(solution)/shard_map/ppermute | solution.py:407
  41.1 1.6 %collective-permute-start.2 = (bf16[272,512]{1,0:T(8,128)(2,1)S(1)}, bf16[272,512]{1,0:T(8,128)(2,1)S(1)}, u32[]{:S(2)}, u32[]{:S(2)}) collective-permute-start(bf16[272,512]{1,0:T(8,128)(2,1)S(1)} %collective-permute-done.1.refs_8_), channel_id=1, source_target_pairs={{0,1},{1,0},{2,3},{3,2},{4,5},{5,4},{6,7},{7,6},{8,9},{9,8},{10,11... | collective-permute-start | bytes 835592 | tf_op jit(solution)/shard_map/ppermute | solution.py:407
  41.1 0.7 copy-start.10
  41.8 0.7 copy-start.4
  42.7 0.7 copy-start.12
  49.5 1.6 %collective-permute-start.3 = (bf16[256,512]{1,0:T(8,128)(2,1)S(1)}, bf16[256,512]{1,0:T(8,128)(2,1)S(1)}, u32[]{:S(2)}, u32[]{:S(2)}) collective-permute-start(bf16[256,512]{1,0:T(8,128)(2,1)S(1)} %embed.1.emb_ref.refs_2_), channel_id=1, source_target_pairs={{0,1},{1,0},{2,3},{3,2},{4,5},{5,4},{6,7},{7,6},{8,9},{9,8},{10,11... | collective-permute-start | bytes 786440 | tf_op jit(solution)/shard_map/ppermute | solution.py:407
  49.6 16.0 %collective-permute-start.4 = (bf16[256,512]{1,0:T(8,128)(2,1)S(1)}, bf16[256,512]{1,0:T(8,128)(2,1)}, u32[]{:S(2)}, u32[]{:S(2)}) collective-permute-start(bf16[256,512]{1,0:T(8,128)(2,1)S(1)} %embed.1.emb_ref.refs_2_), channel_id=1, source_target_pairs={{0,2},{1,3},{2,0},{3,1},{4,6},{5,7},{6,4},{7,5},{8,10},{9,11},{10,... | collective-permute-start | bytes 786440 | tf_op jit(solution)/shard_map/ppermute | solution.py:407
  51.1 0.7 copy-start.7
  51.9 1.0 copy-start.1
  52.9 1.0 copy-start.3
  53.8 1.0 copy-start.5
  54.8 0.9 copy-start.8
  65.6 1.8 %collective-permute-start.5 = (bf16[256,512]{1,0:T(8,128)(2,1)}, bf16[256,512]{1,0:T(8,128)(2,1)S(1)}, u32[]{:S(2)}, u32[]{:S(2)}) collective-permute-start(bf16[256,512]{1,0:T(8,128)(2,1)} %collective-permute-done.4.refs_4_), channel_id=1, source_target_pairs={{0,1},{1,0},{2,3},{3,2},{4,5},{5,4},{6,7},{7,6},{8,9},{9,8},{10,11... | collective-permute-start | bytes 786440 | tf_op jit(solution)/shard_map/ppermute | solution.py:407
  67.4 1.0 copy-start.6
  68.4 0.9 copy-start.9
  69.4 1.0 copy-start.11
  70.3 1.0 copy-start.13
  84.3 28.7 %copy-start.14 = (s32[32,1,32]{2,1,0:T(1,128)S(1)}, s32[32,1,32]{2,1,0:T(1,128)}, u32[]{:S(2)}) copy-start(s32[32,1,32]{2,1,0:T(1,128)} %all_to_all.21) | copy-start | bytes 12292

commit v5 on v4

--- a/solution.py
+++ b/solution.py
@@ -118,9 +118,22 @@
     out_ref[...] = dot(chosen, table_ref[...]).astype(BF16)
 
 
-def embed_kernel(slots_ref, fetched_ref, out_ref):
+def start_copies(pairs, sems):
+    copies = [pltpu.make_async_copy(a, b, sems.at[i]) for i, (a, b) in enumerate(pairs)]
+    for copy in copies:
+        copy.start()
+    return copies
+
+
+def embed_kernel(count, slots_in, fetched_ref, w_in_in, w_out_in, *refs):
+    side_ins = refs[:count]
+    out_ref, slots_ref, w_in_ref, w_out_ref, sides_ref, sems = refs[count:]
+    pairs = [(slots_in, slots_ref), (w_in_in, w_in_ref), (w_out_in, w_out_ref)]
+    pairs += [(side_ins[t], sides_ref.at[t]) for t in range(count)]
+    copies = start_copies(pairs, sems)
     events = out_ref.shape[0]
     slots = fetched_ref.shape[0]
+    copies[0].wait()
     column = jnp.transpose(slots_ref[...])
     lane = iota((events, slots), 1)
     hit = lane == column[:, 0:1]
@@ -128,6 +141,8 @@
         hit = hit | (lane == column[:, k : k + 1])
     picked = jnp.where(hit, 1.0, 0.0).astype(BF16)
     out_ref[...] = dot(picked, fetched_ref[...]).astype(BF16)
+    for copy in copies[1:]:
+        copy.wait()
 
 
 def collect_kernel(asked_ref, returned_ref, out_ref):
@@ -267,20 +282,29 @@
     index_ref,
     emb_ref,
     mate_ref,
-    side_ref,
-    side_mate_ref,
+    slots_ref,
     w_in_ref,
     w_out_ref,
+    sides_ref,
     proj_ref,
     att_ref,
     gatt_ref,
     join_ref,
     slope_ref,
     out_ref,
+    slots_on,
+    w_in_on,
+    w_out_on,
+    sides_on,
     segc_ref,
     segr_ref,
     cots_ref,
+    sems,
 ):
+    copies = start_copies(
+        ((slots_ref, slots_on), (w_in_ref, w_in_on), (w_out_ref, w_out_on), (sides_ref, sides_on)),
+        sems,
+    )
     own = index_ref[0]
     mate = index_ref[1]
     base = jnp.minimum(own, mate)
@@ -294,8 +318,8 @@
 
     project(emb_ref[...], w_in_ref, write_to(own), slope_ref)
     project(mate_ref[...], w_in_ref, write_to(mate), None)
-    hold_side(side_ref, own - base, cots_ref, segc_ref, segr_ref)
-    hold_side(side_mate_ref, mate - base, cots_ref, segc_ref, segr_ref)
+    hold_side(sides_ref.at[0], own - base, cots_ref, segc_ref, segr_ref)
+    hold_side(sides_ref.at[1], mate - base, cots_ref, segc_ref, segr_ref)
     att_ref[...] = jnp.zeros_like(att_ref)
     join_ref[...] = jnp.zeros_like(join_ref)
     chunks = Chunks(0, proj_ref, gatt_ref, segc_ref, segr_ref, join_ref)
@@ -316,20 +340,24 @@
         chunks.query_side(own, 0, own + 1)
         chunks.key_side(own, own, last + 1)
 
+    for copy in copies:
+        copy.wait()
+
 
 def late_kernel(count, *refs):
-    index_ref, slots_ref = refs[:2]
-    emb_refs = refs[2 : 2 + count]
-    side_refs = refs[2 + count : 2 + 2 * count]
+    index_ref = refs[0]
+    emb_refs = refs[1 : 1 + count]
     (
-        w_in_ref,
-        w_out_ref,
         proj_pair_ref,
         att_pair_ref,
         gatt_pair_ref,
         join_early_ref,
         slope_ref,
         out_early_ref,
+        slots_ref,
+        w_in_ref,
+        w_out_ref,
+        sides_ref,
         out_ref,
         grad_ref,
         proj_ref,
@@ -339,7 +367,7 @@
         att_ref,
         gatt_ref,
         join_ref,
-    ) = refs[2 + 2 * count :]
+    ) = refs[1 + count :]
     own = index_ref[0]
     base = jnp.minimum(own, index_ref[1])
     last = jnp.maximum(own, index_ref[1])
@@ -347,7 +375,7 @@
 
     for t in range(count):
         place = index_ref[t]
-        hold_side(side_refs[t], place, cot_ref, segc_ref, segr_ref)
+        hold_side(sides_ref.at[t], place, cot_ref, segc_ref, segr_ref)
     for t in range(2):
         proj_ref[base + t] = proj_pair_ref[t]
         gatt_ref[base + t] = gatt_pair_ref[t]
@@ -474,13 +502,21 @@
     side_far = flip(side, "ctx", count // 2)
     side_mate = flip(side, "ctx", 1)
     side_blocks = gather_blocks(side, "ctx", {1: side_mate, count // 2: after(side_far, rows)})
-    slots, side_blocks = lax.optimization_barrier((slots, side_blocks))
-    embedded = pl.pallas_call(
-        embed_kernel,
-        out_shape=jax.ShapeDtypeStruct((events, width), BF16),
+    held_shapes = (
+        jax.ShapeDtypeStruct(slots.shape, jnp.int32),
+        jax.ShapeDtypeStruct(w_in.shape, BF16),
+        jax.ShapeDtypeStruct(w_out.shape, BF16),
+        jax.ShapeDtypeStruct((count, events + EXTRA, width), BF16),
+    )
+    embedded, *held = pl.pallas_call(
+        functools.partial(embed_kernel, count),
+        out_shape=(jax.ShapeDtypeStruct((events, width), BF16),) + held_shapes,
+        in_specs=[anywhere, vmem] + [anywhere] * (2 + count),
+        out_specs=(vmem,) * 5,
+        scratch_shapes=[pltpu.SemaphoreType.DMA((3 + count,))],
         compiler_params=params(),
         name="embed",
-    )(slots, fetched)
+    )(slots, fetched, w_in, w_out, *side_blocks)
     emb_far = flip(embedded, "ctx", count // 2)
     emb_mate = flip(embedded, "ctx", 1)
     index = lax.axis_index("ctx").astype(jnp.int32) ^ jnp.arange(count, dtype=jnp.int32)
@@ -494,22 +530,24 @@
             jax.ShapeDtypeStruct((events, 4 * width), F32),
             jax.ShapeDtypeStruct((events, 4 * width), F32),
             event_shape,
-        ),
+        )
+        + held_shapes,
         in_specs=[smem] + [vmem] * 6,
-        out_specs=(vmem,) * 6,
+        out_specs=(vmem,) * 10,
         scratch_shapes=[
             pltpu.VMEM((2, events, 128), F32),
             pltpu.VMEM((2, 8, events), F32),
             pltpu.VMEM((2, events, width), BF16),
+            pltpu.SemaphoreType.DMA((4,)),
         ],
         compiler_params=params(20),
         name="early",
-    )(index, embedded, emb_mate, *side_blocks[:2], w_in, w_out)
+    )(index, embedded, emb_mate, *held)
     emb_blocks = gather_blocks(embedded, "ctx", {1: emb_mate, count // 2: after(emb_far, early)})
     layer_out, slot_grad = pl.pallas_call(
         functools.partial(late_kernel, count),
         out_shape=(event_shape, jax.ShapeDtypeStruct((slot_count, width), BF16)),
-        in_specs=[smem] + [vmem] * (9 + 2 * count),
+        in_specs=[smem] + [vmem] * (10 + count),
         out_specs=(vmem, vmem),
         scratch_shapes=[
             pltpu.VMEM((count, events, 4 * width), BF16),
@@ -522,7 +560,7 @@
         ],
         compiler_params=params(28),
         name="late",
-    )(index, slots, *emb_blocks, *side_blocks, w_in, w_out, *early)
+    )(index, *emb_blocks, *early)
     returned = exchange(slot_grad.reshape(owners, capacity, width)).reshape(slot_count, width)
     row_grad = pl.pallas_call(
         collect_kernel,

time: 115 us -> 119 us (1.035)
  local copies, waits for them, and re-layouts: 10.6 us -> 14 us
    unnamed x32 -> x36, local copies, waits for them, and re-layouts: 10.6 us -> 14 us
where the time goes in v5:
time: 119 us; the launch traced here: 118 us
  blocking collectives  43.1 us (36%)
  Pallas kernels  30.6 us (26%)
  waiting for transfers between devices  23.9 us (20%)
  local copies, waits for them, and re-layouts  14 us (12%)
  starting transfers between devices  5.93 us (5%)
    all_to_all x2, blocking collectives, exchange(): return lax.all_to_all(value, axes, split_axis=0, concat_axis=0, tiled=True)  43.1 us
    ppermute x6, waiting for transfers between devices, flip(): return lax.ppermute(value, axis, [(i, i ^ offset) for i in range(count)])  18.5 us
    unnamed x36, local copies, waits for them, and re-layouts  14 us
    pallas_call x1, Pallas kernels, local(): pl.pallas_call(functools.partial(late_kernel, count), out_shape=(event_sh...  12.7 us
    pallas_call x1, Pallas kernels, local(): pl.pallas_call(early_kernel, out_shape=(jax.ShapeDtypeStruct((2, events,...  10.2 us
    all_to_all x1, waiting for transfers between devices, exchange(): return lax.all_to_all(value, axes, split_axis=0, concat_axis=0, tiled=True)  5.4 us
    ppermute x6, starting transfers between devices, flip(): return lax.ppermute(value, axis, [(i, i ^ offset) for i in range(count)])  3.26 us
    pallas_call x1, Pallas kernels, local(): pl.pallas_call(select_kernel, out_shape=jax.ShapeDtypeStruct((slot_count,...  2.78 us
  transfers between devices with their start and end apart: 7, of which 4 were waited for; matrix products, arithmetic and copies ran while one was open for 0% of the time, Pallas kernels for 9%

profile of v5, /device:TPU:0, one launch (start us, length us, event | category | flops | bytes accessed | tf_op | source)
XLA Modules:
  0.0 118.4 jit_solution(3625694324686980769)
XLA Ops:
  0.6 0.0 copy-start
  0.6 2.0 %slots.1 = (s32[8,256]{1,0:T(8,128)}, s32[32,32]{1,0:T(8,128)}, bf16[272,512]{1,0:T(8,128)(2,1)}) custom-call(s32[2,256]{1,0:T(2,128)} %bitcast.17, s32[2,256]{1,0:T(2,128)} %bitcast.18, s32[1,256]{1,0:T(1,128)} %seg_in.1, bf16[256,512]{1,0:T(8,128)(2,1)} %cot_in.1), custom_call_target="tpu_custom_call" | custom-call | tf_op jit(solution)/shard_map/slots/pallas_call | solution.py:469
  2.6 0.0 copy-start.8
  2.6 0.0 copy-start.17
  2.7 14.3 %all_to_all.21 = s32[32,1,32]{2,1,0:T(1,128)} all-to-all(s32[32,1,32]{2,1,0:T(1,128)} %bitcast.16), channel_id=1, replica_groups=mesh['table'=8,'ctx'=4] {'table','ctx'}, dimensions={0} | all-to-all | bytes 8192 | tf_op jit(solution)/shard_map/all_to_all | solution.py:466
  17.0 2.8 %select.1 = bf16[1024,512]{1,0:T(8,128)(2,1)} custom-call(s32[32,32]{1,0:T(8,128)} %bitcast.13, bf16[512,512]{1,0:T(8,128)(2,1)} %table_in.1), custom_call_target="tpu_custom_call" | custom-call | tf_op jit(solution)/shard_map/select/pallas_call | solution.py:488
  19.8 2.7 %all-to-all-start.1 = ((bf16[32,32,512]{2,1,0:T(8,128)(2,1)}), bf16[32,32,512]{2,1,0:T(8,128)(2,1)S(1)}, u32[]{:S(2)}, u32[]{:S(2)}) async-start(bf16[32,32,512]{2,1,0:T(8,128)(2,1)} %bitcast.15), calls=%async_computation.1 | async-start | bytes 2097152 | tf_op jit(solution)/shard_map/all_to_all | solution.py:466
  22.5 0.0 copy-done.8
  22.5 1.7 %collective-permute-start.1 = (bf16[272,512]{1,0:T(8,128)(2,1)S(1)}, bf16[272,512]{1,0:T(8,128)(2,1)S(1)}, u32[]{:S(2)}, u32[]{:S(2)}) collective-permute-start(bf16[272,512]{1,0:T(8,128)(2,1)S(1)} %copy-done.8), channel_id=1, source_target_pairs={{0,2},{1,3},{2,0},{3,1},{4,6},{5,7},{6,4},{7,5},{8,10},{9,11},{10,... | collective-permute-start | bytes 835592 | tf_op jit(solution)/shard_map/ppermute | solution.py:435
  24.2 0.0 collective-permute-start
  24.2 16.8 %collective-permute-done.1.refs_2_ = bf16[272,512]{1,0:T(8,128)(2,1)S(1)} collective-permute-done((bf16[272,512]{1,0:T(8,128)(2,1)S(1)}, bf16[272,512]{1,0:T(8,128)(2,1)S(1)}, u32[]{:S(2)}, u32[]{:S(2)}) %collective-permute-start.1) | collective-permute-done | bytes 278560 | tf_op jit(solution)/shard_map/ppermute | solution.py:435
  41.0 0.0 collective-permute-start.2
  41.0 0.0 copy-start.10
  41.0 0.7 copy-done.10
  41.7 0.0 collective-permute-done.refs_1_
  41.7 0.0 copy-start.12
  41.7 0.7 copy-done.12
  42.4 0.1 collective-permute-done.2.refs_3_
  42.5 0.7 copy-done.14
  43.3 5.4 %all-to-all-done.1 = bf16[32,32,512]{2,1,0:T(8,128)(2,1)S(1)} async-done(((bf16[32,32,512]{2,1,0:T(8,128)(2,1)}), bf16[32,32,512]{2,1,0:T(8,128)(2,1)S(1)}, u32[]{:S(2)}, u32[]{:S(2)}) %all-to-all-start.1) | async-done | bytes 1048608 | tf_op jit(solution)/shard_map/all_to_all | solution.py:466
  48.7 0.0 copy-done
  48.7 0.0 copy-done.17
  48.7 0.0 copy-start.5
  48.7 1.0 copy-done.5
  49.7 1.0 copy-done.9
  50.7 1.0 copy-done.11
  51.6 1.0 copy-done.13
  52.6 1.0 copy-done.15
  53.5 1.1 embed.1
  54.7 0.0 copy-start.1
  54.7 1.3 %copy-done.1 = bf16[512,2048]{1,0:T(8,128)(2,1)} copy-done((bf16[512,2048]{1,0:T(8,128)(2,1)}, bf16[512,2048]{1,0:T(8,128)(2,1)S(1)}, u32[]{:S(2)}) %copy-start.1) | copy-done | bytes 2097176
  56.0 1.0 copy-done.3
  57.0 0.8 copy-done.6
  57.8 0.0 collective-permute-start.3
  57.8 1.5 %collective-permute-start.4 = (bf16[256,512]{1,0:T(8,128)(2,1)S(1)}, bf16[256,512]{1,0:T(8,128)(2,1)S(1)}, u32[]{:S(2)}, u32[]{:S(2)}) collective-permute-start(bf16[256,512]{1,0:T(8,128)(2,1)S(1)} %get-tuple-element.28.emb_ref.refs_1_), channel_id=1, source_target_pairs={{0,2},{1,3},{2,0},{3,1},{4,6},{5,7},{6,4},{7,5},{8,10},{9,11},{10,... | collective-permute-start | bytes 786440 | tf_op jit(solution)/shard_map/ppermute | solution.py:435
  59.3 0.0 collective-permute-done.3.mate_ref.refs_2_
  59.3 1.6 %copy-done.2 = bf16[512,2048]{1,0:T(8,128)(2,1)S(1)} copy-done((bf16[512,2048]{1,0:T(8,128)(2,1)S(1)}, bf16[512,2048]{1,0:T(8,128)(2,1)}, u32[]{:S(2)}) %copy-start.2) | copy-done | bytes 2097176
  60.9 1.2 %copy-done.4 = bf16[4,272,512]{2,1,0:T(8,128)(2,1)S(1)} copy-done((bf16[4,272,512]{2,1,0:T(8,128)(2,1)S(1)}, bf16[4,272,512]{2,1,0:T(8,128)(2,1)}, u32[]{:S(2)}) %copy-start.4) | copy-done | bytes 1114136
  62.2 1.0 copy-done.7
  63.2 10.2 %early.1 = (bf16[2,256,2048]{2,1,0:T(8,128)(2,1)S(1)}, f32[2,256,512]{2,1,0:T(8,128)S(1)}, bf16[2,256,512]{2,1,0:T(8,128)(2,1)S(1)}, f32[256,2048]{1,0:T(8,128)S...) custom-call(s32[4]{0:T(128)S(1)} %iota_xor_fusion.index_ref.refs_0_,, ...), custom_call_target="tpu_custom_call" | custom-call | tf_op jit(solution)/shard_map/early/pallas_call | solution.py:524
  73.5 0.0 collective-permute-done.4.refs_3_
  73.5 0.1 collective-permute-start.5
  73.6 1.5 %collective-permute-done.5.refs_4_ = bf16[256,512]{1,0:T(8,128)(2,1)S(1)} collective-permute-done((bf16[256,512]{1,0:T(8,128)(2,1)S(1)}, bf16[256,512]{1,0:T(8,128)(2,1)S(1)}, u32[]{:S(2)}, u32[]{:S(2)}) %collective-permute-start.5) | collective-permute-done | bytes 262176 | tf_op jit(solution)/shard_map/ppermute | solution.py:435
  75.1 12.7 %late.1 = (bf16[256,512]{1,0:T(8,128)(2,1)}, bf16[1024,512]{1,0:T(8,128)(2,1)S(1)}) custom-call(s32[4]{0:T(128)S(1)} %iota_xor_fusion.index_ref.refs_0_, bf16[256,512]{1,0:T(8,128)(2,1)S(1)} %get-tuple-element.28.emb_ref.refs_1_, bf16[256,512]{1,0:T(8,128)(2,1)S(1)} %collective-permute-done.3.mate_ref.refs_2_, ...), custom_call_target="tpu_custom_call" | custom-call | tf_op jit(solution)/shard_map/late/pallas_call | solution.py:547
  87.8 0.0 copy-start.16
  87.8 28.7 %all_to_all.22 = bf16[32,32,512]{2,1,0:T(8,128)(2,1)S(1)} all-to-all(bf16[32,32,512]{2,1,0:T(8,128)(2,1)S(1)} %bitcast.12), channel_id=1, replica_groups=mesh['table'=8,'ctx'=4] {'table','ctx'}, dimensions={0} | all-to-all | bytes 2097152 | tf_op jit(solution)/shard_map/all_to_all | solution.py:466
  116.5 0.0 copy-done.16
  116.5 1.8 %collect.1 = f32[512,512]{1,0:T(8,128)} custom-call(s32[32,32]{1,0:T(8,128)S(1)} %bitcast.14, bf16[1024,512]{1,0:T(8,128)(2,1)S(1)} %bitcast.10), custom_call_target="tpu_custom_call" | custom-call | tf_op jit(solution)/shard_map/collect/pallas_call | solution.py:565
  (11 shorter events, 0.0 us)
Async XLA Ops:
  0.6 48.0 %copy-start = (bf16[512,2048]{1,0:T(8,128)(2,1)S(1)}, bf16[512,2048]{1,0:T(8,128)(2,1)}, u32[]{:S(2)}) copy-start(bf16[512,2048]{1,0:T(8,128)(2,1)} %w_in_in.1) | copy-start | bytes 6291460
  2.6 19.8 %copy-start.8 = (bf16[272,512]{1,0:T(8,128)(2,1)S(1)}, bf16[272,512]{1,0:T(8,128)(2,1)}, u32[]{:S(2)}) copy-start(bf16[272,512]{1,0:T(8,128)(2,1)} %get-tuple-element.26.refs_0_) | copy-start | bytes 835588
  2.6 46.0 %copy-start.17 = (s32[8,256]{1,0:T(8,128)S(1)}, s32[8,256]{1,0:T(8,128)}, u32[]{:S(2)}) copy-start(s32[8,256]{1,0:T(8,128)} %get-tuple-element.24.slots_in) | copy-start | bytes 24580
  19.8 28.9 %all-to-all-start.1 = ((bf16[32,32,512]{2,1,0:T(8,128)(2,1)}), bf16[32,32,512]{2,1,0:T(8,128)(2,1)S(1)}, u32[]{:S(2)}, u32[]{:S(2)}) async-start(bf16[32,32,512]{2,1,0:T(8,128)(2,1)} %bitcast.15), calls=%async_computation.1 | async-start | bytes 2097152 | tf_op jit(solution)/shard_map/all_to_all | solution.py:466
  22.5 18.5 %collective-permute-start.1 = (bf16[272,512]{1,0:T(8,128)(2,1)S(1)}, bf16[272,512]{1,0:T(8,128)(2,1)S(1)}, u32[]{:S(2)}, u32[]{:S(2)}) collective-permute-start(bf16[272,512]{1,0:T(8,128)(2,1)S(1)} %copy-done.8), channel_id=1, source_target_pairs={{0,2},{1,3},{2,0},{3,1},{4,6},{5,7},{6,4},{7,5},{8,10},{9,11},{10,... | collective-permute-start | bytes 835592 | tf_op jit(solution)/shard_map/ppermute | solution.py:435
  24.2 17.5 %collective-permute-start = (bf16[272,512]{1,0:T(8,128)(2,1)S(1)}, bf16[272,512]{1,0:T(8,128)(2,1)S(1)}, u32[]{:S(2)}, u32[]{:S(2)}) collective-permute-start(bf16[272,512]{1,0:T(8,128)(2,1)S(1)} %copy-done.8), channel_id=1, source_target_pairs={{0,1},{1,0},{2,3},{3,2},{4,5},{5,4},{6,7},{7,6},{8,9},{9,8},{10,11... | collective-permute-start | bytes 835592 | tf_op jit(solution)/shard_map/ppermute | solution.py:435
  41.0 1.6 %collective-permute-start.2 = (bf16[272,512]{1,0:T(8,128)(2,1)S(1)}, bf16[272,512]{1,0:T(8,128)(2,1)S(1)}, u32[]{:S(2)}, u32[]{:S(2)}) collective-permute-start(bf16[272,512]{1,0:T(8,128)(2,1)S(1)} %collective-permute-done.1.refs_2_), channel_id=1, source_target_pairs={{0,1},{1,0},{2,3},{3,2},{4,5},{5,4},{6,7},{7,6},{8,9},{9,8},{10,11... | collective-permute-start | bytes 835592 | tf_op jit(solution)/shard_map/ppermute | solution.py:435
  41.0 0.7 copy-start.10
  41.7 0.7 copy-start.12
  42.5 0.7 copy-start.14
  48.7 1.0 copy-start.5
  49.7 1.0 copy-start.9
  50.7 1.0 copy-start.11
  51.6 1.0 copy-start.13
  52.6 1.0 copy-start.15
  54.7 1.3 %copy-start.1 = (bf16[512,2048]{1,0:T(8,128)(2,1)}, bf16[512,2048]{1,0:T(8,128)(2,1)S(1)}, u32[]{:S(2)}) copy-start(bf16[512,2048]{1,0:T(8,128)(2,1)S(1)} %get-tuple-element.30.w_in_ref) | copy-start | bytes 6291460
  56.0 1.0 copy-start.3
  57.0 0.8 copy-start.6
  57.8 1.5 %collective-permute-start.3 = (bf16[256,512]{1,0:T(8,128)(2,1)S(1)}, bf16[256,512]{1,0:T(8,128)(2,1)S(1)}, u32[]{:S(2)}, u32[]{:S(2)}) collective-permute-start(bf16[256,512]{1,0:T(8,128)(2,1)S(1)} %get-tuple-element.28.emb_ref.refs_1_), channel_id=1, source_target_pairs={{0,1},{1,0},{2,3},{3,2},{4,5},{5,4},{6,7},{7,6},{8,9},{9,8},{10,11... | collective-permute-start | bytes 786440 | tf_op jit(solution)/shard_map/ppermute | solution.py:435
  57.8 15.7 %collective-permute-start.4 = (bf16[256,512]{1,0:T(8,128)(2,1)S(1)}, bf16[256,512]{1,0:T(8,128)(2,1)S(1)}, u32[]{:S(2)}, u32[]{:S(2)}) collective-permute-start(bf16[256,512]{1,0:T(8,128)(2,1)S(1)} %get-tuple-element.28.emb_ref.refs_1_), channel_id=1, source_target_pairs={{0,2},{1,3},{2,0},{3,1},{4,6},{5,7},{6,4},{7,5},{8,10},{9,11},{10,... | collective-permute-start | bytes 786440 | tf_op jit(solution)/shard_map/ppermute | solution.py:435
  59.3 1.6 %copy-start.2 = (bf16[512,2048]{1,0:T(8,128)(2,1)S(1)}, bf16[512,2048]{1,0:T(8,128)(2,1)}, u32[]{:S(2)}) copy-start(bf16[512,2048]{1,0:T(8,128)(2,1)} %copy-done.1) | copy-start | bytes 6291460
  60.9 1.2 %copy-start.4 = (bf16[4,272,512]{2,1,0:T(8,128)(2,1)S(1)}, bf16[4,272,512]{2,1,0:T(8,128)(2,1)}, u32[]{:S(2)}) copy-start(bf16[4,272,512]{2,1,0:T(8,128)(2,1)} %copy-done.3) | copy-start | bytes 3342340
  62.2 1.0 copy-start.7
  73.5 1.6 %collective-permute-start.5 = (bf16[256,512]{1,0:T(8,128)(2,1)S(1)}, bf16[256,512]{1,0:T(8,128)(2,1)S(1)}, u32[]{:S(2)}, u32[]{:S(2)}) collective-permute-start(bf16[256,512]{1,0:T(8,128)(2,1)S(1)} %collective-permute-done.4.refs_3_), channel_id=1, source_target_pairs={{0,1},{1,0},{2,3},{3,2},{4,5},{5,4},{6,7},{7,6},{8,9},{9,8},{10,11... | collective-permute-start | bytes 786440 | tf_op jit(solution)/shard_map/ppermute | solution.py:435
  87.8 28.7 %copy-start.16 = (s32[32,1,32]{2,1,0:T(1,128)S(1)}, s32[32,1,32]{2,1,0:T(1,128)}, u32[]{:S(2)}) copy-start(s32[32,1,32]{2,1,0:T(1,128)} %all_to_all.21) | copy-start | bytes 12292

commit v6 on v4

--- a/solution.py
+++ b/solution.py
@@ -44,8 +44,14 @@
     return (values >> 4).astype(F32).astype(BF16), (values & 15).astype(F32).astype(BF16)
 
 
+def start_copies(pairs, sems):
+    copies = [pltpu.make_async_copy(a, b, sems.at[i]) for i, (a, b) in enumerate(pairs)]
+    for copy in copies:
+        copy.start()
+    return copies
+
+
 EXTRA = 16
-WHOLE = 61
 
 
 def slots_kernel(
@@ -56,10 +62,11 @@
     cot_in,
     slots_ref,
     wanted_ref,
-    side_ref,
+    side_out,
     owner_ref,
     row_ref,
     seg_ref,
+    mark_ref,
     sems,
 ):
     events, width = cot_in.shape
@@ -67,16 +74,17 @@
         (owner_in, owner_ref),
         (row_in, row_ref),
         (seg_in, seg_ref),
-        (cot_in, side_ref.at[0:events]),
+        (cot_in, side_out.at[0:events]),
     )
-    copies = [pltpu.make_async_copy(a, b, sems.at[i]) for i, (a, b) in enumerate(pairs)]
-    for copy in copies:
-        copy.start()
+    copies = start_copies(pairs, sems)
     for copy in copies[:3]:
         copy.wait()
-    side_ref[events:, :] = jnp.zeros((EXTRA, width), BF16)
+    mark_ref[...] = jnp.zeros((EXTRA, width), BF16)
     segments = jnp.broadcast_to(seg_ref[...].astype(F32), (EXTRA, events))
-    side_ref[events:, 0:events] = segments.astype(BF16)
+    mark_ref[:, 0:events] = segments.astype(BF16)
+    mark = pltpu.make_async_copy(mark_ref, side_out.at[events : events + EXTRA], sems.at[4])
+    mark.start()
+    copies.append(mark)
     owners = wanted_ref.shape[0]
     owner = jnp.concatenate([owner_ref[k : k + 1, :] for k in range(NIDS)], 1)
     row = jnp.concatenate([row_ref[k : k + 1, :] for k in range(NIDS)], 1)
@@ -100,22 +108,28 @@
         copy.wait()
 
 
-def select_kernel(asked_in, table_in, out_ref, asked_ref, table_ref, sems):
-    pairs = ((asked_in, asked_ref), (table_in, table_ref))
-    copies = [pltpu.make_async_copy(a, b, sems.at[i]) for i, (a, b) in enumerate(pairs)]
-    for copy in copies:
-        copy.start()
-    copies[0].wait()
+def select_kernel(asked_ref, table_in, out_ref, table_ref, rows_ref, sems):
+    (table_copy,) = start_copies(((table_in, table_ref),), sems)
     owners, capacity = asked_ref.shape
     rows = table_ref.shape[0]
+    parts = sems.shape[0] - 1
+    step = owners // parts
     columns = jnp.transpose(asked_ref[...])
     lane = iota((capacity, rows), 1)
-    chosen = jnp.concatenate(
-        [jnp.where(lane == columns[:, s : s + 1], 1.0, 0.0) for s in range(owners)], 0
-    )
-    chosen = chosen.astype(BF16)
-    copies[1].wait()
-    out_ref[...] = dot(chosen, table_ref[...]).astype(BF16)
+    copies = []
+    for part in range(parts):
+        sources = range(part * step, (part + 1) * step)
+        chosen = [jnp.where(lane == columns[:, s : s + 1], 1.0, 0.0) for s in sources]
+        chosen = jnp.concatenate(chosen, 0).astype(BF16)
+        if part == 0:
+            table_copy.wait()
+        place = pl.ds(part * step * capacity, step * capacity)
+        rows_ref[place, :] = dot(chosen, table_ref[...]).astype(BF16)
+        copy = pltpu.make_async_copy(rows_ref.at[place], out_ref.at[place], sems.at[1 + part])
+        copy.start()
+        copies.append(copy)
+    for copy in copies:
+        copy.wait()
 
 
 def embed_kernel(slots_ref, fetched_ref, out_ref):
@@ -263,24 +277,27 @@
         lax.fori_loop(start, stop, pair, 0)
 
 
-def early_kernel(
-    index_ref,
-    emb_ref,
-    mate_ref,
-    side_ref,
-    side_mate_ref,
-    w_in_ref,
-    w_out_ref,
-    proj_ref,
-    att_ref,
-    gatt_ref,
-    join_ref,
-    slope_ref,
-    out_ref,
-    segc_ref,
-    segr_ref,
-    cots_ref,
-):
+def early_kernel(count, index_ref, emb_ref, mate_ref, slots_in, w_in_in, w_out_in, *refs):
+    (
+        proj_ref,
+        att_ref,
+        gatt_ref,
+        join_ref,
+        slope_ref,
+        out_ref,
+        slots_ref,
+        w_in_ref,
+        w_out_ref,
+        sides_ref,
+        segc_ref,
+        segr_ref,
+        cots_ref,
+        sems,
+    ) = refs[count:]
+    pairs = [(w_in_in, w_in_ref), (w_out_in, w_out_ref), (slots_in, slots_ref)]
+    pairs += [(refs[t], sides_ref.at[t]) for t in range(count)]
+    copies = start_copies(pairs, sems)
+    copies[0].wait()
     own = index_ref[0]
     mate = index_ref[1]
     base = jnp.minimum(own, mate)
@@ -294,8 +311,10 @@
 
     project(emb_ref[...], w_in_ref, write_to(own), slope_ref)
     project(mate_ref[...], w_in_ref, write_to(mate), None)
-    hold_side(side_ref, own - base, cots_ref, segc_ref, segr_ref)
-    hold_side(side_mate_ref, mate - base, cots_ref, segc_ref, segr_ref)
+    for copy in copies[1:]:
+        copy.wait()
+    hold_side(sides_ref.at[0], own - base, cots_ref, segc_ref, segr_ref)
+    hold_side(sides_ref.at[1], mate - base, cots_ref, segc_ref, segr_ref)
     att_ref[...] = jnp.zeros_like(att_ref)
     join_ref[...] = jnp.zeros_like(join_ref)
     chunks = Chunks(0, proj_ref, gatt_ref, segc_ref, segr_ref, join_ref)
@@ -318,18 +337,19 @@
 
 
 def late_kernel(count, *refs):
-    index_ref, slots_ref = refs[:2]
-    emb_refs = refs[2 : 2 + count]
-    side_refs = refs[2 + count : 2 + 2 * count]
+    index_ref = refs[0]
+    emb_refs = refs[1 : 1 + count]
     (
-        w_in_ref,
-        w_out_ref,
         proj_pair_ref,
         att_pair_ref,
         gatt_pair_ref,
         join_early_ref,
         slope_ref,
         out_early_ref,
+        slots_ref,
+        w_in_ref,
+        w_out_ref,
+        sides_ref,
         out_ref,
         grad_ref,
         proj_ref,
@@ -339,7 +359,7 @@
         att_ref,
         gatt_ref,
         join_ref,
-    ) = refs[2 + 2 * count :]
+    ) = refs[1 + count :]
     own = index_ref[0]
     base = jnp.minimum(own, index_ref[1])
     last = jnp.maximum(own, index_ref[1])
@@ -347,7 +367,7 @@
 
     for t in range(count):
         place = index_ref[t]
-        hold_side(side_refs[t], place, cot_ref, segc_ref, segr_ref)
+        hold_side(sides_ref.at[t], place, cot_ref, segc_ref, segr_ref)
     for t in range(2):
         proj_ref[base + t] = proj_pair_ref[t]
         gatt_ref[base + t] = gatt_pair_ref[t]
@@ -398,6 +418,10 @@
     grad_ref[...] = dot(spread, grad.astype(BF16)).astype(BF16)
 
 
+def in_hbm(*arrays):
+    return [pltpu.with_memory_space_constraint(a, pltpu.HBM) for a in arrays]
+
+
 def params(mebibytes=12):
     return pltpu.CompilerParams(vmem_limit_bytes=mebibytes * 1024 * 1024)
 
@@ -437,44 +461,52 @@
     def exchange(value):
         return lax.all_to_all(value, axes, split_axis=0, concat_axis=0, tiled=True)
 
-    anywhere = pl.BlockSpec(memory_space=pl.ANY)
+    hbm = pl.BlockSpec(memory_space=pltpu.HBM)
     slots, wanted, side = pl.pallas_call(
         functools.partial(slots_kernel, capacity),
         out_shape=(
             jax.ShapeDtypeStruct((8, events), jnp.int32),
             jax.ShapeDtypeStruct((owners, capacity), jnp.int32),
-            jax.ShapeDtypeStruct((events + EXTRA, width), BF16),
+            pltpu.HBM((events + EXTRA, width), BF16),
         ),
-        in_specs=[anywhere] * 4,
-        out_specs=(vmem,) * 3,
+        in_specs=[hbm] * 4,
+        out_specs=(vmem, vmem, hbm),
         scratch_shapes=[
             pltpu.VMEM((NIDS, events), jnp.int32),
             pltpu.VMEM((NIDS, events), jnp.int32),
             pltpu.VMEM((1, events), jnp.int32),
-            pltpu.SemaphoreType.DMA((4,)),
+            pltpu.VMEM((EXTRA, width), BF16),
+            pltpu.SemaphoreType.DMA((5,)),
         ],
-        compiler_params=params(WHOLE),
+        compiler_params=params(),
         name="slots",
-    )(item_owner.T, item_row.T, segment_ids.reshape(1, events), cotangent)
+    )(*in_hbm(item_owner.T, item_row.T, segment_ids.reshape(1, events), cotangent))
     asked = exchange(wanted)
     rows = pl.pallas_call(
         select_kernel,
-        out_shape=jax.ShapeDtypeStruct((slot_count, width), BF16),
-        in_specs=[anywhere] * 2,
-        out_specs=vmem,
+        out_shape=pltpu.HBM((slot_count, width), BF16),
+        in_specs=[vmem, hbm],
+        out_specs=hbm,
         scratch_shapes=[
-            pltpu.VMEM((owners, capacity), jnp.int32),
             pltpu.VMEM(table.shape, BF16),
-            pltpu.SemaphoreType.DMA((2,)),
+            pltpu.VMEM((slot_count, width), BF16),
+            pltpu.SemaphoreType.DMA((5,)),
         ],
-        compiler_params=params(WHOLE),
+        compiler_params=params(),
         name="select",
-    )(asked, table)
+    )(asked, *in_hbm(table))
     fetched = exchange(rows.reshape(owners, capacity, width)).reshape(slot_count, width)
     side_far = flip(side, "ctx", count // 2)
     side_mate = flip(side, "ctx", 1)
     side_blocks = gather_blocks(side, "ctx", {1: side_mate, count // 2: after(side_far, rows)})
-    slots, side_blocks = lax.optimization_barrier((slots, side_blocks))
+    held_shapes = (
+        jax.ShapeDtypeStruct(slots.shape, jnp.int32),
+        jax.ShapeDtypeStruct(w_in.shape, BF16),
+        jax.ShapeDtypeStruct(w_out.shape, BF16),
+        jax.ShapeDtypeStruct((count, events + EXTRA, width), BF16),
+    )
+    side_blocks = in_hbm(*side_blocks)
+    fetched, side_blocks = lax.optimization_barrier((fetched, side_blocks))
     embedded = pl.pallas_call(
         embed_kernel,
         out_shape=jax.ShapeDtypeStruct((events, width), BF16),
@@ -486,7 +518,7 @@
     index = lax.axis_index("ctx").astype(jnp.int32) ^ jnp.arange(count, dtype=jnp.int32)
     event_shape = jax.ShapeDtypeStruct((events, width), BF16)
     early = pl.pallas_call(
-        early_kernel,
+        functools.partial(early_kernel, count),
         out_shape=(
             jax.ShapeDtypeStruct((2, events, 4 * width), BF16),
             jax.ShapeDtypeStruct((2, events, width), F32),
@@ -494,22 +526,24 @@
             jax.ShapeDtypeStruct((events, 4 * width), F32),
             jax.ShapeDtypeStruct((events, 4 * width), F32),
             event_shape,
-        ),
-        in_specs=[smem] + [vmem] * 6,
-        out_specs=(vmem,) * 6,
+        )
+        + held_shapes,
+        in_specs=[smem, vmem, vmem] + [hbm] * (3 + count),
+        out_specs=(vmem,) * 10,
         scratch_shapes=[
             pltpu.VMEM((2, events, 128), F32),
             pltpu.VMEM((2, 8, events), F32),
             pltpu.VMEM((2, events, width), BF16),
+            pltpu.SemaphoreType.DMA((3 + count,)),
         ],
         compiler_params=params(20),
         name="early",
-    )(index, embedded, emb_mate, *side_blocks[:2], w_in, w_out)
+    )(index, embedded, emb_mate, *in_hbm(slots, w_in, w_out), *side_blocks)
     emb_blocks = gather_blocks(embedded, "ctx", {1: emb_mate, count // 2: after(emb_far, early)})
     layer_out, slot_grad = pl.pallas_call(
         functools.partial(late_kernel, count),
         out_shape=(event_shape, jax.ShapeDtypeStruct((slot_count, width), BF16)),
-        in_specs=[smem] + [vmem] * (9 + 2 * count),
+        in_specs=[smem] + [vmem] * (10 + count),
         out_specs=(vmem, vmem),
         scratch_shapes=[
             pltpu.VMEM((count, events, 4 * width), BF16),
@@ -522,7 +556,7 @@
         ],
         compiler_params=params(28),
         name="late",
-    )(index, slots, *emb_blocks, *side_blocks, w_in, w_out, *early)
+    )(index, *emb_blocks, *early)
     returned = exchange(slot_grad.reshape(owners, capacity, width)).reshape(slot_count, width)
     row_grad = pl.pallas_call(
         collect_kernel,

time: 115 us -> 114 us (level)
  local copies, waits for them, and re-layouts: 10.6 us -> 0.02 us
  Pallas kernels: 30 us -> 38.3 us
  waiting for transfers between devices: 24.1 us -> 26 us
    unnamed x32 -> x10, local copies, waits for them, and re-layouts: 10.6 us -> 0.02 us
    pallas_call x1, Pallas kernels: 1.82 us -> 9.09 us  [local(): pl.pallas_call(functools.partial(slots_kernel, capacity), out_shape=(jax....]
    pallas_call x2, Pallas kernels: 12.6 us -> 14.1 us  [the longest x1 11.6 us: local(): pl.pallas_call(functools.partial(early_kernel, count), out_shape=(jax.Sha...]
    ppermute x6, waiting for transfers between devices: 18.7 us -> 19.9 us  [flip(): return lax.ppermute(value, axis, [(i, i ^ offset) for i in range(count)])]
  transfers between devices with their start and end apart: 7 -> 7, of which waited for: 4 -> 4; matrix products, arithmetic and copies ran while one was open for 0% -> 0% of each run, Pallas kernels for 9% -> 10%
where the time goes in v6:
time: 114 us
  blocking collectives  42.9 us (38%)
  Pallas kernels  38.3 us (34%)
  waiting for transfers between devices  26 us (23%)
  starting transfers between devices  6.06 us (5%)
    all_to_all x2, blocking collectives, exchange(): return lax.all_to_all(value, axes, split_axis=0, concat_axis=0, tiled=True)  42.9 us
    ppermute x6, waiting for transfers between devices, flip(): return lax.ppermute(value, axis, [(i, i ^ offset) for i in range(count)])  19.9 us
    pallas_call x1, Pallas kernels, local(): pl.pallas_call(functools.partial(late_kernel, count), out_shape=(event_sh...  12.6 us
    pallas_call x1, Pallas kernels, local(): pl.pallas_call(functools.partial(early_kernel, count), out_shape=(jax.Sha...  11.6 us
    pallas_call x1, Pallas kernels, local(): pl.pallas_call(functools.partial(slots_kernel, capacity), out_shape=(jax....  9.09 us
    all_to_all x1, waiting for transfers between devices, exchange(): return lax.all_to_all(value, axes, split_axis=0, concat_axis=0, tiled=True)  6.12 us
    ppermute x6, starting transfers between devices, flip(): return lax.ppermute(value, axis, [(i, i ^ offset) for i in range(count)])  3.39 us
    all_to_all x1, starting transfers between devices, exchange(): return lax.all_to_all(value, axes, split_axis=0, concat_axis=0, tiled=True)  2.66 us
  transfers between devices with their start and end apart: 7, of which 4 were waited for; matrix products, arithmetic and copies ran while one was open for 0% of the time, Pallas kernels for 10%

profile of v6, /device:TPU:0, one launch (start us, length us, event | category | flops | bytes accessed | tf_op | source)
XLA Modules:
  0.0 114.1 jit_solution(1740779775956643042)
XLA Ops:
  0.6 9.1 %slots.1 = (s32[8,256]{1,0:T(8,128)S(1)}, s32[32,32]{1,0:T(8,128)S(1)}, bf16[272,512]{1,0:T(8,128)(2,1)}) custom-call(s32[2,256]{1,0:T(2,128)} %bitcast.17, s32[2,256]{1,0:T(2,128)} %bitcast.18, s32[1,256]{1,0:T(1,128)} %seg_in.1, bf16[256,512]{1,0:T(8,128)(2,1)} %cot_in.1), custom_call_target="tpu_custom_call" | custom-call | tf_op jit(solution)/shard_map/slots/pallas_call | solution.py:465
  9.7 0.0 copy-start
  9.7 0.0 copy-start.1
  9.8 14.3 %all_to_all.21 = s32[32,1,32]{2,1,0:T(1,128)S(1)} all-to-all(s32[32,1,32]{2,1,0:T(1,128)S(1)} %bitcast.15), channel_id=1, replica_groups=mesh['table'=8,'ctx'=4] {'table','ctx'}, dimensions={0} | all-to-all | bytes 8192 | tf_op jit(solution)/shard_map/all_to_all | solution.py:462
  24.0 2.5 %select.1 = bf16[1024,512]{1,0:T(8,128)(2,1)} custom-call(s32[32,32]{1,0:T(8,128)S(1)} %bitcast.13, bf16[512,512]{1,0:T(8,128)(2,1)} %table_in.1), custom_call_target="tpu_custom_call" | custom-call | tf_op jit(solution)/shard_map/select/pallas_call | solution.py:485
  26.5 2.7 %all-to-all-start.1 = ((bf16[32,32,512]{2,1,0:T(8,128)(2,1)}), bf16[32,32,512]{2,1,0:T(8,128)(2,1)S(1)}, u32[]{:S(2)}, u32[]{:S(2)}) async-start(bf16[32,32,512]{2,1,0:T(8,128)(2,1)} %bitcast.16), calls=%async_computation.1 | async-start | bytes 2097152 | tf_op jit(solution)/shard_map/all_to_all | solution.py:462
  29.2 0.0 copy-done.1
  29.2 1.7 %collective-permute-start.1 = (bf16[272,512]{1,0:T(8,128)(2,1)S(1)}, bf16[272,512]{1,0:T(8,128)(2,1)S(1)}, u32[]{:S(2)}, u32[]{:S(2)}) collective-permute-start(bf16[272,512]{1,0:T(8,128)(2,1)S(1)} %copy-done.1), channel_id=1, source_target_pairs={{0,2},{1,3},{2,0},{3,1},{4,6},{5,7},{6,4},{7,5},{8,10},{9,11},{10,... | collective-permute-start | bytes 835592 | tf_op jit(solution)/shard_map/ppermute | solution.py:431
  30.9 0.0 collective-permute-start
  30.9 16.8 %collective-permute-done.1.refs_2_ = bf16[272,512]{1,0:T(8,128)(2,1)S(1)} collective-permute-done((bf16[272,512]{1,0:T(8,128)(2,1)S(1)}, bf16[272,512]{1,0:T(8,128)(2,1)S(1)}, u32[]{:S(2)}, u32[]{:S(2)}) %collective-permute-start.1) | collective-permute-done | bytes 278560 | tf_op jit(solution)/shard_map/ppermute | solution.py:431
  47.7 0.0 copy-start.2
  47.7 0.0 collective-permute-start.2
  47.7 0.0 collective-permute-done.refs_1_
  47.7 0.0 copy-start.3
  47.7 1.5 %collective-permute-done.2.refs_3_ = bf16[272,512]{1,0:T(8,128)(2,1)S(1)} collective-permute-done((bf16[272,512]{1,0:T(8,128)(2,1)S(1)}, bf16[272,512]{1,0:T(8,128)(2,1)S(1)}, u32[]{:S(2)}, u32[]{:S(2)}) %collective-permute-start.2) | collective-permute-done | bytes 278560 | tf_op jit(solution)/shard_map/ppermute | solution.py:431
  49.3 0.0 copy-start.4
  49.3 6.1 %all-to-all-done.1 = bf16[32,32,512]{2,1,0:T(8,128)(2,1)S(1)} async-done(((bf16[32,32,512]{2,1,0:T(8,128)(2,1)}), bf16[32,32,512]{2,1,0:T(8,128)(2,1)S(1)}, u32[]{:S(2)}, u32[]{:S(2)}) %all-to-all-start.1) | async-done | bytes 1048608 | tf_op jit(solution)/shard_map/all_to_all | solution.py:462
  55.4 0.7 embed.1.emb_ref.refs_1_
  56.1 0.0 copy-done
  56.1 0.1 collective-permute-start.3
  56.2 1.5 %collective-permute-start.4 = (bf16[256,512]{1,0:T(8,128)(2,1)S(1)}, bf16[256,512]{1,0:T(8,128)(2,1)S(1)}, u32[]{:S(2)}, u32[]{:S(2)}) collective-permute-start(bf16[256,512]{1,0:T(8,128)(2,1)S(1)} %embed.1.emb_ref.refs_1_), channel_id=1, source_target_pairs={{0,2},{1,3},{2,0},{3,1},{4,6},{5,7},{6,4},{7,5},{8,10},{9,11},{10,... | collective-permute-start | bytes 786440 | tf_op jit(solution)/shard_map/ppermute | solution.py:431
  57.8 0.0 collective-permute-done.3.mate_ref.refs_2_
  57.8 0.0 copy-done.2
  57.8 0.0 copy-done.3
  57.8 0.0 copy-done.4
  57.8 11.6 %early.1 = (bf16[2,256,2048]{2,1,0:T(8,128)(2,1)S(1)}, f32[2,256,512]{2,1,0:T(8,128)S(1)}, bf16[2,256,512]{2,1,0:T(8,128)(2,1)S(1)}, f32[256,2048]{1,0:T(8,128)S...) custom-call(s32[4]{0:T(128)S(1)} %iota_xor_fusion.index_ref.refs_0_,, ...), custom_call_target="tpu_custom_call" | custom-call | tf_op jit(solution)/shard_map/early/pallas_call | solution.py:520
  69.4 0.0 collective-permute-done.4.refs_3_
  69.4 0.1 collective-permute-start.5
  69.5 1.5 %collective-permute-done.5.refs_4_ = bf16[256,512]{1,0:T(8,128)(2,1)S(1)} collective-permute-done((bf16[256,512]{1,0:T(8,128)(2,1)S(1)}, bf16[256,512]{1,0:T(8,128)(2,1)S(1)}, u32[]{:S(2)}, u32[]{:S(2)}) %collective-permute-start.5) | collective-permute-done | bytes 262176 | tf_op jit(solution)/shard_map/ppermute | solution.py:431
  71.0 12.6 %late.1 = (bf16[256,512]{1,0:T(8,128)(2,1)}, bf16[1024,512]{1,0:T(8,128)(2,1)S(1)}) custom-call(s32[4]{0:T(128)S(1)} %iota_xor_fusion.index_ref.refs_0_, bf16[256,512]{1,0:T(8,128)(2,1)S(1)} %embed.1.emb_ref.refs_1_, bf16[256,512]{1,0:T(8,128)(2,1)S(1)} %collective-permute-done.3.mate_ref.refs_2_, bf16[256,512]{1,0:T(8,128)(2,1)S(1)} %collective-permute-done.4.refs_3_, ...), custom_call_target="tpu_custom_call" | custom-call | tf_op jit(solution)/shard_map/late/pallas_call | solution.py:543
  83.6 28.7 %all_to_all.22 = bf16[32,32,512]{2,1,0:T(8,128)(2,1)S(1)} all-to-all(bf16[32,32,512]{2,1,0:T(8,128)(2,1)S(1)} %bitcast.12), channel_id=1, replica_groups=mesh['table'=8,'ctx'=4] {'table','ctx'}, dimensions={0} | all-to-all | bytes 2097152 | tf_op jit(solution)/shard_map/all_to_all | solution.py:462
  112.3 1.8 %collect.1 = f32[512,512]{1,0:T(8,128)} custom-call(s32[32,32]{1,0:T(8,128)S(1)} %bitcast.14, bf16[1024,512]{1,0:T(8,128)(2,1)S(1)} %bitcast.11), custom_call_target="tpu_custom_call" | custom-call | tf_op jit(solution)/shard_map/collect/pallas_call | solution.py:561
  (1 shorter events, 0.0 us)
Async XLA Ops:
  9.7 46.4 %copy-start = (s32[8,256]{1,0:T(8,128)}, s32[8,256]{1,0:T(8,128)S(1)}, u32[]{:S(2)}) copy-start(s32[8,256]{1,0:T(8,128)S(1)} %get-tuple-element.24.slots_ref.slots_in) | copy-start | bytes 24580
  9.7 19.5 %copy-start.1 = (bf16[272,512]{1,0:T(8,128)(2,1)S(1)}, bf16[272,512]{1,0:T(8,128)(2,1)}, u32[]{:S(2)}) copy-start(bf16[272,512]{1,0:T(8,128)(2,1)} %get-tuple-element.29.refs_0_) | copy-start | bytes 835588
  26.5 28.9 %all-to-all-start.1 = ((bf16[32,32,512]{2,1,0:T(8,128)(2,1)}), bf16[32,32,512]{2,1,0:T(8,128)(2,1)S(1)}, u32[]{:S(2)}, u32[]{:S(2)}) async-start(bf16[32,32,512]{2,1,0:T(8,128)(2,1)} %bitcast.16), calls=%async_computation.1 | async-start | bytes 2097152 | tf_op jit(solution)/shard_map/all_to_all | solution.py:462
  29.2 18.5 %collective-permute-start.1 = (bf16[272,512]{1,0:T(8,128)(2,1)S(1)}, bf16[272,512]{1,0:T(8,128)(2,1)S(1)}, u32[]{:S(2)}, u32[]{:S(2)}) collective-permute-start(bf16[272,512]{1,0:T(8,128)(2,1)S(1)} %copy-done.1), channel_id=1, source_target_pairs={{0,2},{1,3},{2,0},{3,1},{4,6},{5,7},{6,4},{7,5},{8,10},{9,11},{10,... | collective-permute-start | bytes 835592 | tf_op jit(solution)/shard_map/ppermute | solution.py:431
  30.9 16.8 %collective-permute-start = (bf16[272,512]{1,0:T(8,128)(2,1)S(1)}, bf16[272,512]{1,0:T(8,128)(2,1)S(1)}, u32[]{:S(2)}, u32[]{:S(2)}) collective-permute-start(bf16[272,512]{1,0:T(8,128)(2,1)S(1)} %copy-done.1), channel_id=1, source_target_pairs={{0,1},{1,0},{2,3},{3,2},{4,5},{5,4},{6,7},{7,6},{8,9},{9,8},{10,11... | collective-permute-start | bytes 835592 | tf_op jit(solution)/shard_map/ppermute | solution.py:431
  47.7 10.1 %copy-start.2 = (bf16[272,512]{1,0:T(8,128)(2,1)}, bf16[272,512]{1,0:T(8,128)(2,1)S(1)}, u32[]{:S(2)}) copy-start(bf16[272,512]{1,0:T(8,128)(2,1)S(1)} %collective-permute-done.1.refs_2_) | copy-start | bytes 835588
  47.7 1.6 %collective-permute-start.2 = (bf16[272,512]{1,0:T(8,128)(2,1)S(1)}, bf16[272,512]{1,0:T(8,128)(2,1)S(1)}, u32[]{:S(2)}, u32[]{:S(2)}) collective-permute-start(bf16[272,512]{1,0:T(8,128)(2,1)S(1)} %collective-permute-done.1.refs_2_), channel_id=1, source_target_pairs={{0,1},{1,0},{2,3},{3,2},{4,5},{5,4},{6,7},{7,6},{8,9},{9,8},{10,11... | collective-permute-start | bytes 835592 | tf_op jit(solution)/shard_map/ppermute | solution.py:431
  47.7 10.0 %copy-start.3 = (bf16[272,512]{1,0:T(8,128)(2,1)}, bf16[272,512]{1,0:T(8,128)(2,1)S(1)}, u32[]{:S(2)}) copy-start(bf16[272,512]{1,0:T(8,128)(2,1)S(1)} %collective-permute-done.refs_1_) | copy-start | bytes 835588
  49.3 8.5 %copy-start.4 = (bf16[272,512]{1,0:T(8,128)(2,1)}, bf16[272,512]{1,0:T(8,128)(2,1)S(1)}, u32[]{:S(2)}) copy-start(bf16[272,512]{1,0:T(8,128)(2,1)S(1)} %collective-permute-done.2.refs_3_) | copy-start | bytes 835588
  56.1 1.6 %collective-permute-start.3 = (bf16[256,512]{1,0:T(8,128)(2,1)S(1)}, bf16[256,512]{1,0:T(8,128)(2,1)S(1)}, u32[]{:S(2)}, u32[]{:S(2)}) collective-permute-start(bf16[256,512]{1,0:T(8,128)(2,1)S(1)} %embed.1.emb_ref.refs_1_), channel_id=1, source_target_pairs={{0,1},{1,0},{2,3},{3,2},{4,5},{5,4},{6,7},{7,6},{8,9},{9,8},{10,11... | collective-permute-start | bytes 786440 | tf_op jit(solution)/shard_map/ppermute | solution.py:431
  56.2 13.2 %collective-permute-start.4 = (bf16[256,512]{1,0:T(8,128)(2,1)S(1)}, bf16[256,512]{1,0:T(8,128)(2,1)S(1)}, u32[]{:S(2)}, u32[]{:S(2)}) collective-permute-start(bf16[256,512]{1,0:T(8,128)(2,1)S(1)} %embed.1.emb_ref.refs_1_), channel_id=1, source_target_pairs={{0,2},{1,3},{2,0},{3,1},{4,6},{5,7},{6,4},{7,5},{8,10},{9,11},{10,... | collective-permute-start | bytes 786440 | tf_op jit(solution)/shard_map/ppermute | solution.py:431
  69.4 1.6 %collective-permute-start.5 = (bf16[256,512]{1,0:T(8,128)(2,1)S(1)}, bf16[256,512]{1,0:T(8,128)(2,1)S(1)}, u32[]{:S(2)}, u32[]{:S(2)}) collective-permute-start(bf16[256,512]{1,0:T(8,128)(2,1)S(1)} %collective-permute-done.4.refs_3_), channel_id=1, source_target_pairs={{0,1},{1,0},{2,3},{3,2},{4,5},{5,4},{6,7},{7,6},{8,9},{9,8},{10,11... | collective-permute-start | bytes 786440 | tf_op jit(solution)/shard_map/ppermute | solution.py:431

commit v7 on v6

--- a/solution.py
+++ b/solution.py
@@ -62,11 +62,10 @@
     cot_in,
     slots_ref,
     wanted_ref,
-    side_out,
+    side_ref,
     owner_ref,
     row_ref,
     seg_ref,
-    mark_ref,
     sems,
 ):
     events, width = cot_in.shape
@@ -74,17 +73,14 @@
         (owner_in, owner_ref),
         (row_in, row_ref),
         (seg_in, seg_ref),
-        (cot_in, side_out.at[0:events]),
+        (cot_in, side_ref.at[0:events]),
     )
     copies = start_copies(pairs, sems)
     for copy in copies[:3]:
         copy.wait()
-    mark_ref[...] = jnp.zeros((EXTRA, width), BF16)
+    side_ref[events:, :] = jnp.zeros((EXTRA, width), BF16)
     segments = jnp.broadcast_to(seg_ref[...].astype(F32), (EXTRA, events))
-    mark_ref[:, 0:events] = segments.astype(BF16)
-    mark = pltpu.make_async_copy(mark_ref, side_out.at[events : events + EXTRA], sems.at[4])
-    mark.start()
-    copies.append(mark)
+    side_ref[events:, 0:events] = segments.astype(BF16)
     owners = wanted_ref.shape[0]
     owner = jnp.concatenate([owner_ref[k : k + 1, :] for k in range(NIDS)], 1)
     row = jnp.concatenate([row_ref[k : k + 1, :] for k in range(NIDS)], 1)
@@ -176,11 +172,13 @@
     return same & (first + (query_chunk - key_chunk) * events >= second)
 
 
-def project(emb, w_in_ref, write, slope_ref):
+def project(emb, w_in_ref, write, slope_ref, copies=()):
     width = emb.shape[1]
     normed = normalize(emb.astype(F32))[0].astype(BF16)
     for block in range(4):
         columns = slice(block * width, (block + 1) * width)
+        if copies:
+            copies[block].wait()
         half = 0.5 * dot(normed, w_in_ref[:, columns])
         bend = jnp.tanh(half)
         value = half + half * bend
@@ -198,6 +196,16 @@
     segc_ref[place] = jnp.broadcast_to(jnp.transpose(seg)[:, 0:1], segc_ref.shape[1:])
 
 
+HIDDEN = -1e4
+
+
+def bent(raw, mask):
+    half = jnp.where(mask, raw * (0.5 * SCALE), HIDDEN)
+    bend = jnp.tanh(half)
+    product = half * bend
+    return half + product, (1.0 + bend) * (1.0 + (half - product))
+
+
 class Chunks:
     def __init__(self, first, proj_ref, gatt_ref, segc_ref, segr_ref, join_ref):
         self.first, self.proj, self.gatt = first, proj_ref, gatt_ref
@@ -208,14 +216,19 @@
         def pair(j, _):
             mask = visible(i, j, self.segc, self.segr, False)
             qi, kj = i - self.first, j - self.first
+
+            def scores(h):
+                queries = self.proj[qi, :, head(2, h, self.width)]
+                return dot_nt(queries, self.proj[kj, :, head(3, h, self.width)])
+
+            raw = scores(0)
             for h in range(HEADS):
-                queries = self.proj[qi, :, head(2, h, self.width)]
-                raw = dot_nt(queries, self.proj[kj, :, head(3, h, self.width)])
-                half = raw * (0.5 * SCALE)
-                value = half + half * jnp.tanh(half)
-                weights = jnp.where(mask, value, 0.0).astype(BF16)
+                later = scores(h + 1) if h + 1 < HEADS else None
+                half = jnp.where(mask, raw * (0.5 * SCALE), HIDDEN)
+                weights = (half + half * jnp.tanh(half)).astype(BF16)
                 added = dot(weights, self.proj[kj, :, head(1, h, self.width)])
                 att_ref[:, head(0, h, self.width)] += added
+                raw = later
             return 0
 
         lax.fori_loop(start, stop, pair, 0)
@@ -238,19 +251,26 @@
         def pair(j, _):
             mask = visible(own, j, self.segc, self.segr, False)
             me, kj = own - self.first, j - self.first
-            for h in range(HEADS):
-                keys = self.proj[kj, :, head(3, h, self.width)]
-                half = dot_nt(self.proj[me, :, head(2, h, self.width)], keys) * (0.5 * SCALE)
-                bend = jnp.tanh(half)
-                value = half + half * bend
-                sigma = 0.5 + 0.5 * bend
-                slope = sigma + value - value * sigma
+
+            def scores(h):
+                raw = dot_nt(
+                    self.proj[me, :, head(2, h, self.width)],
+                    self.proj[kj, :, head(3, h, self.width)],
+                )
                 grad_weights = dot_nt(
                     self.gatt[me, :, head(0, h, self.width)],
                     self.proj[kj, :, head(1, h, self.width)],
                 )
-                grad_raw = jnp.where(mask, grad_weights * slope * SCALE, 0.0).astype(BF16)
-                self.join[:, head(2, h, self.width)] += dot(grad_raw, keys)
+                return raw, grad_weights
+
+            raw, grad_weights = scores(0)
+            for h in range(HEADS):
+                later = scores(h + 1) if h + 1 < HEADS else (None, None)
+                _, slope = bent(raw, mask)
+                grad_raw = (grad_weights * slope).astype(BF16)
+                added = dot(grad_raw, self.proj[kj, :, head(3, h, self.width)])
+                self.join[:, head(2, h, self.width)] += added
+                raw, grad_weights = later
             return 0
 
         lax.fori_loop(start, stop, pair, 0)
@@ -259,19 +279,28 @@
         def pair(i, _):
             mask = visible(i, own, self.segc, self.segr, True)
             me, qi = own - self.first, i - self.first
+
+            def scores(h):
+                raw = dot_nt(
+                    self.proj[me, :, head(3, h, self.width)],
+                    self.proj[qi, :, head(2, h, self.width)],
+                )
+                grad_weights = dot_nt(
+                    self.proj[me, :, head(1, h, self.width)],
+                    self.gatt[qi, :, head(0, h, self.width)],
+                )
+                return raw, grad_weights
+
+            raw, grad_weights = scores(0)
             for h in range(HEADS):
+                later = scores(h + 1) if h + 1 < HEADS else (None, None)
+                value, slope = bent(raw, mask)
+                grad_raw = (grad_weights * slope).astype(BF16)
                 queries = self.proj[qi, :, head(2, h, self.width)]
-                half = dot_nt(self.proj[me, :, head(3, h, self.width)], queries) * (0.5 * SCALE)
-                bend = jnp.tanh(half)
-                value = half + half * bend
-                sigma = 0.5 + 0.5 * bend
-                slope = sigma + value - value * sigma
                 grad_att = self.gatt[qi, :, head(0, h, self.width)]
-                grad_weights = dot_nt(self.proj[me, :, head(1, h, self.width)], grad_att)
-                grad_raw = jnp.where(mask, grad_weights * slope * SCALE, 0.0).astype(BF16)
-                weights = jnp.where(mask, value, 0.0).astype(BF16)
                 self.join[:, head(3, h, self.width)] += dot(grad_raw, queries)
-                self.join[:, head(1, h, self.width)] += dot(weights, grad_att)
+                self.join[:, head(1, h, self.width)] += dot(value.astype(BF16), grad_att)
+                raw, grad_weights = later
             return 0
 
         lax.fori_loop(start, stop, pair, 0)
@@ -294,10 +323,12 @@
         cots_ref,
         sems,
     ) = refs[count:]
-    pairs = [(w_in_in, w_in_ref), (w_out_in, w_out_ref), (slots_in, slots_ref)]
+    width = emb_ref.shape[1]
+    blocks = [pl.ds(block * width, width) for block in range(4)]
+    pairs = [(w_in_in.at[:, block], w_in_ref.at[:, block]) for block in blocks]
+    pairs += [(w_out_in, w_out_ref), (slots_in, slots_ref)]
     pairs += [(refs[t], sides_ref.at[t]) for t in range(count)]
     copies = start_copies(pairs, sems)
-    copies[0].wait()
     own = index_ref[0]
     mate = index_ref[1]
     base = jnp.minimum(own, mate)
@@ -309,9 +340,9 @@
 
         return write
 
-    project(emb_ref[...], w_in_ref, write_to(own), slope_ref)
+    project(emb_ref[...], w_in_ref, write_to(own), slope_ref, copies[:4])
     project(mate_ref[...], w_in_ref, write_to(mate), None)
-    for copy in copies[1:]:
+    for copy in copies[4:]:
         copy.wait()
     hold_side(sides_ref.at[0], own - base, cots_ref, segc_ref, segr_ref)
     hold_side(sides_ref.at[1], mate - base, cots_ref, segc_ref, segr_ref)
@@ -406,7 +437,10 @@
     chunks.query_side(own, jnp.where(closed, own + 1, 0), own + 1)
     chunks.key_side(own, jnp.where(closed, last + 1, own), count)
 
-    grad_proj = ((join_ref[...] + join_early_ref[...]) * slope_ref[...]).astype(BF16)
+    width = gatt_ref.shape[2]
+    scaled = jnp.where(iota((1, 4 * width), 1) < 2 * width, 1.0, 0.5 * SCALE)
+    joined = (join_ref[...] + join_early_ref[...]) * scaled
+    grad_proj = (joined * slope_ref[...]).astype(BF16)
     grad_normed = dot_nt(grad_proj, w_in_ref[...])
     normed, inverse = normalize(emb_refs[0][...].astype(F32))
     grad = norm_back(grad_normed, normed, inverse) + cot_ref[own].astype(F32)
@@ -467,16 +501,15 @@
         out_shape=(
             jax.ShapeDtypeStruct((8, events), jnp.int32),
             jax.ShapeDtypeStruct((owners, capacity), jnp.int32),
-            pltpu.HBM((events + EXTRA, width), BF16),
+            jax.ShapeDtypeStruct((events + EXTRA, width), BF16),
         ),
         in_specs=[hbm] * 4,
-        out_specs=(vmem, vmem, hbm),
+        out_specs=(vmem, vmem, vmem),
         scratch_shapes=[
             pltpu.VMEM((NIDS, events), jnp.int32),
             pltpu.VMEM((NIDS, events), jnp.int32),
             pltpu.VMEM((1, events), jnp.int32),
-            pltpu.VMEM((EXTRA, width), BF16),
-            pltpu.SemaphoreType.DMA((5,)),
+            pltpu.SemaphoreType.DMA((4,)),
         ],
         compiler_params=params(),
         name="slots",
@@ -534,7 +567,7 @@
             pltpu.VMEM((2, events, 128), F32),
             pltpu.VMEM((2, 8, events), F32),
             pltpu.VMEM((2, events, width), BF16),
-            pltpu.SemaphoreType.DMA((3 + count,)),
+            pltpu.SemaphoreType.DMA((6 + count,)),
         ],
         compiler_params=params(20),
         name="early",

time: 114 us -> 104 us (0.912)
  Pallas kernels: 38.3 us -> 27.7 us
    pallas_call x1, Pallas kernels: 9.09 us -> 1.11 us  [local(): pl.pallas_call(functools.partial(slots_kernel, capacity), out_shape=(jax....]
    pallas_call x1, Pallas kernels: 12.6 us -> 11.3 us  [local(): pl.pallas_call(functools.partial(late_kernel, count), out_shape=(event_sh...]
    pallas_call x1, Pallas kernels: 11.6 us -> 10.2 us  [local(): pl.pallas_call(functools.partial(early_kernel, count), out_shape=(jax.Sha...]
where the time goes in v7:
time: 104 us; the launch traced here: 103 us
  blocking collectives  42.9 us (41%)
  Pallas kernels  27.7 us (27%)
  waiting for transfers between devices  26 us (25%)
  starting transfers between devices  6.06 us (6%)
    all_to_all x2, blocking collectives, exchange(): return lax.all_to_all(value, axes, split_axis=0, concat_axis=0, tiled=True)  42.9 us
    ppermute x6, waiting for transfers between devices, flip(): return lax.ppermute(value, axis, [(i, i ^ offset) for i in range(count)])  19.9 us
    pallas_call x1, Pallas kernels, local(): pl.pallas_call(functools.partial(late_kernel, count), out_shape=(event_sh...  11.3 us
    pallas_call x1, Pallas kernels, local(): pl.pallas_call(functools.partial(early_kernel, count), out_shape=(jax.Sha...  10.2 us
    all_to_all x1, waiting for transfers between devices, exchange(): return lax.all_to_all(value, axes, split_axis=0, concat_axis=0, tiled=True)  6.12 us
    ppermute x6, starting transfers between devices, flip(): return lax.ppermute(value, axis, [(i, i ^ offset) for i in range(count)])  3.39 us
    all_to_all x1, starting transfers between devices, exchange(): return lax.all_to_all(value, axes, split_axis=0, concat_axis=0, tiled=True)  2.66 us
    pallas_call x1, Pallas kernels, local(): pl.pallas_call(select_kernel, out_shape=pltpu.HBM((slot_count, width), BF...  2.51 us
  transfers between devices with their start and end apart: 7, of which 4 were waited for; matrix products, arithmetic and copies ran while one was open for 0% of the time, Pallas kernels for 10%

profile of v7, /device:TPU:0, one launch (start us, length us, event | category | flops | bytes accessed | tf_op | source)
XLA Modules:
  0.0 103.5 jit_solution(16958261820491048038)
XLA Ops:
  0.6 1.1 %slots.1 = (s32[8,256]{1,0:T(8,128)S(1)}, s32[32,32]{1,0:T(8,128)S(1)}, bf16[272,512]{1,0:T(8,128)(2,1)S(1)}) custom-call(s32[2,256]{1,0:T(2,128)} %bitcast.17, s32[2,256]{1,0:T(2,128)} %bitcast.18, s32[1,256]{1,0:T(1,128)} %seg_in.1, bf16[256,512]{1,0:T(8,128)(2,1)} %cot_in.1), custom_call_target="tpu_custom_call" | custom-call | tf_op jit(solution)/shard_map/slots/pallas_call | solution.py:499
  1.7 0.0 copy-start
  1.8 0.0 copy-start.1
  1.8 14.3 %all_to_all.21 = s32[32,1,32]{2,1,0:T(1,128)S(1)} all-to-all(s32[32,1,32]{2,1,0:T(1,128)S(1)} %bitcast.15), channel_id=1, replica_groups=mesh['table'=8,'ctx'=4] {'table','ctx'}, dimensions={0} | all-to-all | bytes 8192 | tf_op jit(solution)/shard_map/all_to_all | solution.py:496
  16.0 2.5 %select.1 = bf16[1024,512]{1,0:T(8,128)(2,1)} custom-call(s32[32,32]{1,0:T(8,128)S(1)} %bitcast.13, bf16[512,512]{1,0:T(8,128)(2,1)} %table_in.1), custom_call_target="tpu_custom_call" | custom-call | tf_op jit(solution)/shard_map/select/pallas_call | solution.py:518
  18.5 2.7 %all-to-all-start.1 = ((bf16[32,32,512]{2,1,0:T(8,128)(2,1)}), bf16[32,32,512]{2,1,0:T(8,128)(2,1)S(1)}, u32[]{:S(2)}, u32[]{:S(2)}) async-start(bf16[32,32,512]{2,1,0:T(8,128)(2,1)} %bitcast.16), calls=%async_computation.1 | async-start | bytes 2097152 | tf_op jit(solution)/shard_map/all_to_all | solution.py:496
  21.2 1.7 %collective-permute-start.1 = (bf16[272,512]{1,0:T(8,128)(2,1)S(1)}, bf16[272,512]{1,0:T(8,128)(2,1)S(1)}, u32[]{:S(2)}, u32[]{:S(2)}) collective-permute-start(bf16[272,512]{1,0:T(8,128)(2,1)S(1)} %get-tuple-element.29.refs_0_), channel_id=1, source_target_pairs={{0,2},{1,3},{2,0},{3,1},{4,6},{5,7},{6,4},{7,5},{8,10},{9,11},{10,... | collective-permute-start | bytes 835592 | tf_op jit(solution)/shard_map/ppermute | solution.py:465
  22.9 0.0 collective-permute-start
  22.9 16.8 %collective-permute-done.1.refs_2_ = bf16[272,512]{1,0:T(8,128)(2,1)S(1)} collective-permute-done((bf16[272,512]{1,0:T(8,128)(2,1)S(1)}, bf16[272,512]{1,0:T(8,128)(2,1)S(1)}, u32[]{:S(2)}, u32[]{:S(2)}) %collective-permute-start.1) | collective-permute-done | bytes 278560 | tf_op jit(solution)/shard_map/ppermute | solution.py:465
  39.7 0.0 copy-start.2
  39.7 0.0 collective-permute-start.2
  39.7 0.0 collective-permute-done.refs_1_
  39.8 0.0 copy-start.3
  39.8 1.5 %collective-permute-done.2.refs_3_ = bf16[272,512]{1,0:T(8,128)(2,1)S(1)} collective-permute-done((bf16[272,512]{1,0:T(8,128)(2,1)S(1)}, bf16[272,512]{1,0:T(8,128)(2,1)S(1)}, u32[]{:S(2)}, u32[]{:S(2)}) %collective-permute-start.2) | collective-permute-done | bytes 278560 | tf_op jit(solution)/shard_map/ppermute | solution.py:465
  41.3 0.0 copy-start.4
  41.3 6.1 %all-to-all-done.1 = bf16[32,32,512]{2,1,0:T(8,128)(2,1)S(1)} async-done(((bf16[32,32,512]{2,1,0:T(8,128)(2,1)}), bf16[32,32,512]{2,1,0:T(8,128)(2,1)S(1)}, u32[]{:S(2)}, u32[]{:S(2)}) %all-to-all-start.1) | async-done | bytes 1048608 | tf_op jit(solution)/shard_map/all_to_all | solution.py:496
  47.4 0.7 embed.1.emb_ref.refs_1_
  48.2 0.0 copy-done
  48.2 0.0 copy-done.1
  48.2 0.1 collective-permute-start.3
  48.3 1.5 %collective-permute-start.4 = (bf16[256,512]{1,0:T(8,128)(2,1)S(1)}, bf16[256,512]{1,0:T(8,128)(2,1)S(1)}, u32[]{:S(2)}, u32[]{:S(2)}) collective-permute-start(bf16[256,512]{1,0:T(8,128)(2,1)S(1)} %embed.1.emb_ref.refs_1_), channel_id=1, source_target_pairs={{0,2},{1,3},{2,0},{3,1},{4,6},{5,7},{6,4},{7,5},{8,10},{9,11},{10,... | collective-permute-start | bytes 786440 | tf_op jit(solution)/shard_map/ppermute | solution.py:465
  49.8 0.0 collective-permute-done.3.mate_ref.refs_2_
  49.8 0.0 copy-done.2
  49.8 0.0 copy-done.3
  49.8 0.0 copy-done.4
  49.8 10.2 %early.1 = (bf16[2,256,2048]{2,1,0:T(8,128)(2,1)S(1)}, f32[2,256,512]{2,1,0:T(8,128)S(1)}, bf16[2,256,512]{2,1,0:T(8,128)(2,1)S(1)}, f32[256,2048]{1,0:T(8,128)S...) custom-call(s32[4]{0:T(128)S(1)} %iota_xor_fusion.index_ref.refs_0_,, ...), custom_call_target="tpu_custom_call" | custom-call | tf_op jit(solution)/shard_map/early/pallas_call | solution.py:553
  60.1 0.0 collective-permute-done.4.refs_3_
  60.1 0.1 collective-permute-start.5
  60.2 1.5 %collective-permute-done.5.refs_4_ = bf16[256,512]{1,0:T(8,128)(2,1)S(1)} collective-permute-done((bf16[256,512]{1,0:T(8,128)(2,1)S(1)}, bf16[256,512]{1,0:T(8,128)(2,1)S(1)}, u32[]{:S(2)}, u32[]{:S(2)}) %collective-permute-start.5) | collective-permute-done | bytes 262176 | tf_op jit(solution)/shard_map/ppermute | solution.py:465
  61.7 11.3 %late.1 = (bf16[256,512]{1,0:T(8,128)(2,1)}, bf16[1024,512]{1,0:T(8,128)(2,1)S(1)}) custom-call(s32[4]{0:T(128)S(1)} %iota_xor_fusion.index_ref.refs_0_, bf16[256,512]{1,0:T(8,128)(2,1)S(1)} %embed.1.emb_ref.refs_1_, bf16[256,512]{1,0:T(8,128)(2,1)S(1)} %collective-permute-done.3.mate_ref.refs_2_, bf16[256,512]{1,0:T(8,128)(2,1)S(1)} %collective-permute-done.4.refs_3_, ...), custom_call_target="tpu_custom_call" | custom-call | tf_op jit(solution)/shard_map/late/pallas_call | solution.py:576
  73.0 28.7 %all_to_all.22 = bf16[32,32,512]{2,1,0:T(8,128)(2,1)S(1)} all-to-all(bf16[32,32,512]{2,1,0:T(8,128)(2,1)S(1)} %bitcast.12), channel_id=1, replica_groups=mesh['table'=8,'ctx'=4] {'table','ctx'}, dimensions={0} | all-to-all | bytes 2097152 | tf_op jit(solution)/shard_map/all_to_all | solution.py:496
  101.7 1.8 %collect.1 = f32[512,512]{1,0:T(8,128)} custom-call(s32[32,32]{1,0:T(8,128)S(1)} %bitcast.14, bf16[1024,512]{1,0:T(8,128)(2,1)S(1)} %bitcast.11), custom_call_target="tpu_custom_call" | custom-call | tf_op jit(solution)/shard_map/collect/pallas_call | solution.py:594
  (1 shorter events, 0.0 us)
Async XLA Ops:
  1.7 46.4 %copy-start = (bf16[272,512]{1,0:T(8,128)(2,1)}, bf16[272,512]{1,0:T(8,128)(2,1)S(1)}, u32[]{:S(2)}) copy-start(bf16[272,512]{1,0:T(8,128)(2,1)S(1)} %get-tuple-element.29.refs_0_) | copy-start | bytes 835588
  1.8 46.4 %copy-start.1 = (s32[8,256]{1,0:T(8,128)}, s32[8,256]{1,0:T(8,128)S(1)}, u32[]{:S(2)}) copy-start(s32[8,256]{1,0:T(8,128)S(1)} %get-tuple-element.24.slots_ref.slots_in) | copy-start | bytes 24580
  18.5 28.9 %all-to-all-start.1 = ((bf16[32,32,512]{2,1,0:T(8,128)(2,1)}), bf16[32,32,512]{2,1,0:T(8,128)(2,1)S(1)}, u32[]{:S(2)}, u32[]{:S(2)}) async-start(bf16[32,32,512]{2,1,0:T(8,128)(2,1)} %bitcast.16), calls=%async_computation.1 | async-start | bytes 2097152 | tf_op jit(solution)/shard_map/all_to_all | solution.py:496
  21.2 18.5 %collective-permute-start.1 = (bf16[272,512]{1,0:T(8,128)(2,1)S(1)}, bf16[272,512]{1,0:T(8,128)(2,1)S(1)}, u32[]{:S(2)}, u32[]{:S(2)}) collective-permute-start(bf16[272,512]{1,0:T(8,128)(2,1)S(1)} %get-tuple-element.29.refs_0_), channel_id=1, source_target_pairs={{0,2},{1,3},{2,0},{3,1},{4,6},{5,7},{6,4},{7,5},{8,10},{9,11},{10,... | collective-permute-start | bytes 835592 | tf_op jit(solution)/shard_map/ppermute | solution.py:465
  22.9 16.8 %collective-permute-start = (bf16[272,512]{1,0:T(8,128)(2,1)S(1)}, bf16[272,512]{1,0:T(8,128)(2,1)S(1)}, u32[]{:S(2)}, u32[]{:S(2)}) collective-permute-start(bf16[272,512]{1,0:T(8,128)(2,1)S(1)} %get-tuple-element.29.refs_0_), channel_id=1, source_target_pairs={{0,1},{1,0},{2,3},{3,2},{4,5},{5,4},{6,7},{7,6},{8,9},{9,8},{10,11... | collective-permute-start | bytes 835592 | tf_op jit(solution)/shard_map/ppermute | solution.py:465
  39.7 10.1 %copy-start.2 = (bf16[272,512]{1,0:T(8,128)(2,1)}, bf16[272,512]{1,0:T(8,128)(2,1)S(1)}, u32[]{:S(2)}) copy-start(bf16[272,512]{1,0:T(8,128)(2,1)S(1)} %collective-permute-done.1.refs_2_) | copy-start | bytes 835588
  39.7 1.6 %collective-permute-start.2 = (bf16[272,512]{1,0:T(8,128)(2,1)S(1)}, bf16[272,512]{1,0:T(8,128)(2,1)S(1)}, u32[]{:S(2)}, u32[]{:S(2)}) collective-permute-start(bf16[272,512]{1,0:T(8,128)(2,1)S(1)} %collective-permute-done.1.refs_2_), channel_id=1, source_target_pairs={{0,1},{1,0},{2,3},{3,2},{4,5},{5,4},{6,7},{7,6},{8,9},{9,8},{10,11... | collective-permute-start | bytes 835592 | tf_op jit(solution)/shard_map/ppermute | solution.py:465
  39.8 10.1 %copy-start.3 = (bf16[272,512]{1,0:T(8,128)(2,1)}, bf16[272,512]{1,0:T(8,128)(2,1)S(1)}, u32[]{:S(2)}) copy-start(bf16[272,512]{1,0:T(8,128)(2,1)S(1)} %collective-permute-done.refs_1_) | copy-start | bytes 835588
  41.3 8.5 %copy-start.4 = (bf16[272,512]{1,0:T(8,128)(2,1)}, bf16[272,512]{1,0:T(8,128)(2,1)S(1)}, u32[]{:S(2)}) copy-start(bf16[272,512]{1,0:T(8,128)(2,1)S(1)} %collective-permute-done.2.refs_3_) | copy-start | bytes 835588
  48.2 1.6 %collective-permute-start.3 = (bf16[256,512]{1,0:T(8,128)(2,1)S(1)}, bf16[256,512]{1,0:T(8,128)(2,1)S(1)}, u32[]{:S(2)}, u32[]{:S(2)}) collective-permute-start(bf16[256,512]{1,0:T(8,128)(2,1)S(1)} %embed.1.emb_ref.refs_1_), channel_id=1, source_target_pairs={{0,1},{1,0},{2,3},{3,2},{4,5},{5,4},{6,7},{7,6},{8,9},{9,8},{10,11... | collective-permute-start | bytes 786440 | tf_op jit(solution)/shard_map/ppermute | solution.py:465
  48.3 11.8 %collective-permute-start.4 = (bf16[256,512]{1,0:T(8,128)(2,1)S(1)}, bf16[256,512]{1,0:T(8,128)(2,1)S(1)}, u32[]{:S(2)}, u32[]{:S(2)}) collective-permute-start(bf16[256,512]{1,0:T(8,128)(2,1)S(1)} %embed.1.emb_ref.refs_1_), channel_id=1, source_target_pairs={{0,2},{1,3},{2,0},{3,1},{4,6},{5,7},{6,4},{7,5},{8,10},{9,11},{10,... | collective-permute-start | bytes 786440 | tf_op jit(solution)/shard_map/ppermute | solution.py:465
  60.1 1.6 %collective-permute-start.5 = (bf16[256,512]{1,0:T(8,128)(2,1)S(1)}, bf16[256,512]{1,0:T(8,128)(2,1)S(1)}, u32[]{:S(2)}, u32[]{:S(2)}) collective-permute-start(bf16[256,512]{1,0:T(8,128)(2,1)S(1)} %collective-permute-done.4.refs_3_), channel_id=1, source_target_pairs={{0,1},{1,0},{2,3},{3,2},{4,5},{5,4},{6,7},{7,6},{8,9},{9,8},{10,11... | collective-permute-start | bytes 786440 | tf_op jit(solution)/shard_map/ppermute | solution.py:465

commit v8 on v7

--- a/solution.py
+++ b/solution.py
@@ -140,19 +140,18 @@
     out_ref[...] = dot(picked, fetched_ref[...]).astype(BF16)
 
 
-def collect_kernel(asked_ref, returned_ref, out_ref):
-    owners, capacity = asked_ref.shape
-    rows = out_ref.shape[0]
-    slots = owners * capacity
-    high, low = split_exact(asked_ref[...])
-    place = jnp.where(
-        iota((capacity, slots), 1) % capacity == iota((capacity, slots), 0), 1.0, 0.0
-    ).astype(BF16)
-    spread = 16.0 * dot(high, place) + dot(low, place)
-    mine = iota((owners, slots), 1) // capacity == iota((owners, slots), 0)
-    asked = jnp.sum(jnp.where(mine, spread, 0.0), 0, keepdims=True).astype(jnp.int32)
-    chosen = jnp.where(iota((rows, slots), 0) == asked, 1.0, 0.0).astype(BF16)
-    out_ref[...] = dot(chosen, returned_ref[...])
+def collect_kernel(chosen_ref, returned_ref, out_ref, rows_ref, sems):
+    parts = sems.shape[0]
+    step = rows_ref.shape[0] // parts
+    copies = []
+    for part in range(parts):
+        place = pl.ds(part * step, step)
+        rows_ref[place, :] = dot(chosen_ref[place, :], returned_ref[...])
+        copy = pltpu.make_async_copy(rows_ref.at[place], out_ref.at[place], sems.at[part])
+        copy.start()
+        copies.append(copy)
+    for copy in copies:
+        copy.wait()
 
 
 SCALE = HEAD_DIM ** (-0.5)
@@ -174,12 +173,12 @@
 
 def project(emb, w_in_ref, write, slope_ref, copies=()):
     width = emb.shape[1]
-    normed = normalize(emb.astype(F32))[0].astype(BF16)
+    normed = (0.5 * normalize(emb.astype(F32))[0]).astype(BF16)
     for block in range(4):
         columns = slice(block * width, (block + 1) * width)
         if copies:
             copies[block].wait()
-        half = 0.5 * dot(normed, w_in_ref[:, columns])
+        half = dot(normed, w_in_ref[:, columns])
         bend = jnp.tanh(half)
         value = half + half * bend
         write(columns, value.astype(BF16))
@@ -188,12 +187,30 @@
             slope_ref[:, columns] = sigma + value - value * sigma
 
 
-def hold_side(side_ref, place, cots_ref, segc_ref, segr_ref):
-    events = cots_ref.shape[1]
-    cots_ref[place] = side_ref[0:events, :]
-    seg = side_ref[events : events + EXTRA, 0:events].astype(F32)[0:8]
-    segr_ref[place] = seg
-    segc_ref[place] = jnp.broadcast_to(jnp.transpose(seg)[:, 0:1], segc_ref.shape[1:])
+def prep_kernel(count, index_ref, slots_ref, asked_ref, w_out_ref, *refs):
+    mixed_ref, segc_ref, segr_ref, spread_ref, chosen_ref = refs[count:]
+    events = spread_ref.shape[1]
+    for t in range(count):
+        place = index_ref[t]
+        mixed_ref[place] = dot_nt(refs[t][0:events, :], w_out_ref[...])
+        seg = refs[t][events : events + EXTRA, 0:events].astype(F32)[0:8]
+        segr_ref[place] = seg
+        segc_ref[place] = jnp.broadcast_to(jnp.transpose(seg)[:, 0:1], segc_ref.shape[1:])
+    slot = iota(spread_ref.shape, 0)
+    hit = slot == slots_ref[0:1, :]
+    for k in range(1, NIDS):
+        hit = hit | (slot == slots_ref[k : k + 1, :])
+    spread_ref[...] = jnp.where(hit, 1.0, 0.0).astype(BF16)
+    owners, capacity = asked_ref.shape
+    slots = owners * capacity
+    high, low = split_exact(asked_ref[...])
+    place = jnp.where(
+        iota((capacity, slots), 1) % capacity == iota((capacity, slots), 0), 1.0, 0.0
+    ).astype(BF16)
+    values = 16.0 * dot(high, place) + dot(low, place)
+    mine = iota((owners, slots), 1) // capacity == iota((owners, slots), 0)
+    asked = jnp.sum(jnp.where(mine, values, 0.0), 0, keepdims=True).astype(jnp.int32)
+    chosen_ref[...] = jnp.where(iota(chosen_ref.shape, 0) == asked, 1.0, 0.0).astype(BF16)
 
 
 HIDDEN = -1e4
@@ -201,9 +218,10 @@
 
 def bent(raw, mask):
     half = jnp.where(mask, raw * (0.5 * SCALE), HIDDEN)
-    bend = jnp.tanh(half)
-    product = half * bend
-    return half + product, (1.0 + bend) * (1.0 + (half - product))
+    raised = (1.0 + jnp.tanh(half)).astype(BF16)
+    half = half.astype(BF16)
+    one, two = BF16(1.0), BF16(2.0)
+    return half * raised, raised * (one + half * (two - raised))
 
 
 class Chunks:
@@ -233,10 +251,9 @@
 
         lax.fori_loop(start, stop, pair, 0)
 
-    def finish(self, i, own, att, cot, emb_ref, w_out_ref, out_ref):
+    def finish(self, i, own, att, grad_mixed, emb_ref, w_out_ref, out_ref):
         att_norm, att_inverse = normalize(att)
         gate = self.proj[i - self.first, :, 0 : self.width].astype(F32)
-        grad_mixed = dot_nt(cot, w_out_ref[...])
         grad_att = norm_back(grad_mixed * gate, att_norm, att_inverse)
         self.gatt[i - self.first] = grad_att.astype(BF16)
 
@@ -267,7 +284,7 @@
             for h in range(HEADS):
                 later = scores(h + 1) if h + 1 < HEADS else (None, None)
                 _, slope = bent(raw, mask)
-                grad_raw = (grad_weights * slope).astype(BF16)
+                grad_raw = grad_weights.astype(BF16) * slope
                 added = dot(grad_raw, self.proj[kj, :, head(3, h, self.width)])
                 self.join[:, head(2, h, self.width)] += added
                 raw, grad_weights = later
@@ -295,39 +312,26 @@
             for h in range(HEADS):
                 later = scores(h + 1) if h + 1 < HEADS else (None, None)
                 value, slope = bent(raw, mask)
-                grad_raw = (grad_weights * slope).astype(BF16)
+                grad_raw = grad_weights.astype(BF16) * slope
                 queries = self.proj[qi, :, head(2, h, self.width)]
                 grad_att = self.gatt[qi, :, head(0, h, self.width)]
                 self.join[:, head(3, h, self.width)] += dot(grad_raw, queries)
-                self.join[:, head(1, h, self.width)] += dot(value.astype(BF16), grad_att)
+                self.join[:, head(1, h, self.width)] += dot(value, grad_att)
                 raw, grad_weights = later
             return 0
 
         lax.fori_loop(start, stop, pair, 0)
 
 
-def early_kernel(count, index_ref, emb_ref, mate_ref, slots_in, w_in_in, w_out_in, *refs):
-    (
-        proj_ref,
-        att_ref,
-        gatt_ref,
-        join_ref,
-        slope_ref,
-        out_ref,
-        slots_ref,
-        w_in_ref,
-        w_out_ref,
-        sides_ref,
-        segc_ref,
-        segr_ref,
-        cots_ref,
-        sems,
-    ) = refs[count:]
+def early_kernel(index_ref, emb_ref, mate_ref, *refs):
+    w_in_in, w_out_in, mixed_in, segc_in, segr_in, spread_in, side_in = refs[:7]
+    proj_ref, att_ref, gatt_ref, join_ref, slope_ref, out_ref = refs[7:13]
+    w_in_ref, w_out_ref, mixed_ref, segc_ref, segr_ref, spread_ref, side_ref, sems = refs[13:]
     width = emb_ref.shape[1]
     blocks = [pl.ds(block * width, width) for block in range(4)]
     pairs = [(w_in_in.at[:, block], w_in_ref.at[:, block]) for block in blocks]
-    pairs += [(w_out_in, w_out_ref), (slots_in, slots_ref)]
-    pairs += [(refs[t], sides_ref.at[t]) for t in range(count)]
+    pairs += [(segc_in, segc_ref), (segr_in, segr_ref), (mixed_in, mixed_ref)]
+    pairs += [(w_out_in, w_out_ref), (spread_in, spread_ref), (side_in, side_ref)]
     copies = start_copies(pairs, sems)
     own = index_ref[0]
     mate = index_ref[1]
@@ -344,11 +348,12 @@
     project(mate_ref[...], w_in_ref, write_to(mate), None)
     for copy in copies[4:]:
         copy.wait()
-    hold_side(sides_ref.at[0], own - base, cots_ref, segc_ref, segr_ref)
-    hold_side(sides_ref.at[1], mate - base, cots_ref, segc_ref, segr_ref)
     att_ref[...] = jnp.zeros_like(att_ref)
     join_ref[...] = jnp.zeros_like(join_ref)
-    chunks = Chunks(0, proj_ref, gatt_ref, segc_ref, segr_ref, join_ref)
+    pair_rows = pl.ds(base, 2)
+    chunks = Chunks(
+        0, proj_ref, gatt_ref, segc_ref.at[pair_rows], segr_ref.at[pair_rows], join_ref
+    )
 
     def forward(i, _):
         chunks.attend(i, 0, i + 1, att_ref.at[i])
@@ -359,7 +364,7 @@
     @pl.when(base == 0)
     def _():
         def finish(i, _):
-            chunks.finish(i, own, att_ref[i], cots_ref[i], emb_ref, w_out_ref, out_ref)
+            chunks.finish(i, own, att_ref[i], mixed_ref[i], emb_ref, w_out_ref, out_ref)
             return 0
 
         lax.fori_loop(own, last + 1, finish, 0)
@@ -377,16 +382,16 @@
         join_early_ref,
         slope_ref,
         out_early_ref,
-        slots_ref,
         w_in_ref,
         w_out_ref,
-        sides_ref,
+        mixed_ref,
+        segc_ref,
+        segr_ref,
+        spread_ref,
+        side_ref,
         out_ref,
         grad_ref,
         proj_ref,
-        cot_ref,
-        segc_ref,
-        segr_ref,
         att_ref,
         gatt_ref,
         join_ref,
@@ -396,9 +401,6 @@
     last = jnp.maximum(own, index_ref[1])
     closed = base == 0
 
-    for t in range(count):
-        place = index_ref[t]
-        hold_side(sides_ref.at[t], place, cot_ref, segc_ref, segr_ref)
     for t in range(2):
         proj_ref[base + t] = proj_pair_ref[t]
         gatt_ref[base + t] = gatt_pair_ref[t]
@@ -430,7 +432,7 @@
             att_ref[...] = jnp.zeros_like(att_ref)
 
         chunks.attend(i, 0, jnp.where(begun, base, i + 1), att_ref)
-        chunks.finish(i, own, att_ref[...], cot_ref[i], emb_refs[0], w_out_ref, out_ref)
+        chunks.finish(i, own, att_ref[...], mixed_ref[i], emb_refs[0], w_out_ref, out_ref)
         return 0
 
     lax.fori_loop(jnp.where(closed, last + 1, own), count, forward, 0)
@@ -443,13 +445,8 @@
     grad_proj = (joined * slope_ref[...]).astype(BF16)
     grad_normed = dot_nt(grad_proj, w_in_ref[...])
     normed, inverse = normalize(emb_refs[0][...].astype(F32))
-    grad = norm_back(grad_normed, normed, inverse) + cot_ref[own].astype(F32)
-    slot = iota((grad_ref.shape[0], grad.shape[0]), 0)
-    hit = slot == slots_ref[0:1, :]
-    for k in range(1, NIDS):
-        hit = hit | (slot == slots_ref[k : k + 1, :])
-    spread = jnp.where(hit, 1.0, 0.0).astype(BF16)
-    grad_ref[...] = dot(spread, grad.astype(BF16)).astype(BF16)
+    grad = norm_back(grad_normed, normed, inverse) + side_ref[0 : emb_refs[0].shape[0], :].astype(F32)
+    grad_ref[...] = dot(spread_ref[...], grad.astype(BF16)).astype(BF16)
 
 
 def in_hbm(*arrays):
@@ -532,14 +529,24 @@
     side_far = flip(side, "ctx", count // 2)
     side_mate = flip(side, "ctx", 1)
     side_blocks = gather_blocks(side, "ctx", {1: side_mate, count // 2: after(side_far, rows)})
-    held_shapes = (
-        jax.ShapeDtypeStruct(slots.shape, jnp.int32),
-        jax.ShapeDtypeStruct(w_in.shape, BF16),
-        jax.ShapeDtypeStruct(w_out.shape, BF16),
-        jax.ShapeDtypeStruct((count, events + EXTRA, width), BF16),
+    index = lax.axis_index("ctx").astype(jnp.int32) ^ jnp.arange(count, dtype=jnp.int32)
+    prep_shapes = (
+        jax.ShapeDtypeStruct((count, events, width), F32),
+        jax.ShapeDtypeStruct((count, events, 128), F32),
+        jax.ShapeDtypeStruct((count, 8, events), F32),
+        jax.ShapeDtypeStruct((slot_count, events), BF16),
     )
-    side_blocks = in_hbm(*side_blocks)
-    fetched, side_blocks = lax.optimization_barrier((fetched, side_blocks))
+    *prepared, chosen = pl.pallas_call(
+        functools.partial(prep_kernel, count),
+        out_shape=tuple(pltpu.HBM(a.shape, a.dtype) for a in prep_shapes)
+        + (jax.ShapeDtypeStruct((table.shape[0], slot_count), BF16),),
+        in_specs=[smem] + [vmem] * (3 + count),
+        out_specs=(vmem,) * 5,
+        compiler_params=params(20),
+        name="prep",
+    )(index, slots, asked, w_out, *side_blocks)
+    prepared = in_hbm(*prepared)
+    fetched, prepared = lax.optimization_barrier((fetched, prepared))
     embedded = pl.pallas_call(
         embed_kernel,
         out_shape=jax.ShapeDtypeStruct((events, width), BF16),
@@ -548,10 +555,9 @@
     )(slots, fetched)
     emb_far = flip(embedded, "ctx", count // 2)
     emb_mate = flip(embedded, "ctx", 1)
-    index = lax.axis_index("ctx").astype(jnp.int32) ^ jnp.arange(count, dtype=jnp.int32)
     event_shape = jax.ShapeDtypeStruct((events, width), BF16)
     early = pl.pallas_call(
-        functools.partial(early_kernel, count),
+        early_kernel,
         out_shape=(
             jax.ShapeDtypeStruct((2, events, 4 * width), BF16),
             jax.ShapeDtypeStruct((2, events, width), F32),
@@ -560,29 +566,23 @@
             jax.ShapeDtypeStruct((events, 4 * width), F32),
             event_shape,
         )
-        + held_shapes,
-        in_specs=[smem, vmem, vmem] + [hbm] * (3 + count),
-        out_specs=(vmem,) * 10,
-        scratch_shapes=[
-            pltpu.VMEM((2, events, 128), F32),
-            pltpu.VMEM((2, 8, events), F32),
-            pltpu.VMEM((2, events, width), BF16),
-            pltpu.SemaphoreType.DMA((6 + count,)),
-        ],
+        + tuple(jax.ShapeDtypeStruct(a.shape, BF16) for a in (w_in, w_out))
+        + prep_shapes
+        + (jax.ShapeDtypeStruct(side.shape, BF16),),
+        in_specs=[smem, vmem, vmem] + [hbm] * 7,
+        out_specs=(vmem,) * 13,
+        scratch_shapes=[pltpu.SemaphoreType.DMA((10,))],
         compiler_params=params(20),
         name="early",
-    )(index, embedded, emb_mate, *in_hbm(slots, w_in, w_out), *side_blocks)
+    )(index, embedded, emb_mate, *in_hbm(w_in, w_out), *prepared, *in_hbm(side))
     emb_blocks = gather_blocks(embedded, "ctx", {1: emb_mate, count // 2: after(emb_far, early)})
     layer_out, slot_grad = pl.pallas_call(
         functools.partial(late_kernel, count),
         out_shape=(event_shape, jax.ShapeDtypeStruct((slot_count, width), BF16)),
-        in_specs=[smem] + [vmem] * (10 + count),
+        in_specs=[smem] + [vmem] * (13 + count),
         out_specs=(vmem, vmem),
         scratch_shapes=[
             pltpu.VMEM((count, events, 4 * width), BF16),
-            pltpu.VMEM((count, events, width), BF16),
-            pltpu.VMEM((count, events, 128), F32),
-            pltpu.VMEM((count, 8, events), F32),
             pltpu.VMEM((events, width), F32),
             pltpu.VMEM((count, events, width), BF16),
             pltpu.VMEM((events, 4 * width), F32),
@@ -593,10 +593,13 @@
     returned = exchange(slot_grad.reshape(owners, capacity, width)).reshape(slot_count, width)
     row_grad = pl.pallas_call(
         collect_kernel,
-        out_shape=jax.ShapeDtypeStruct(table.shape, F32),
+        out_shape=pltpu.HBM(table.shape, F32),
+        in_specs=[vmem, vmem],
+        out_specs=hbm,
+        scratch_shapes=[pltpu.VMEM(table.shape, F32), pltpu.SemaphoreType.DMA((4,))],
         compiler_params=params(),
         name="collect",
-    )(asked, returned)
+    )(chosen, returned)
     return layer_out, row_grad
 
 

time: 104 us -> 103 us (level)
  waiting for transfers between devices: 26 us -> 21.1 us
  local copies, waits for them, and re-layouts: 0.02 us -> 1.67 us
  Pallas kernels: 27.7 us -> 29.2 us
    all_to_all x1, waiting for transfers between devices: 6.12 us -> 1.22 us  [exchange(): return lax.all_to_all(value, axes, split_axis=0, concat_axis=0, tiled=True)]
    pallas_call x2 -> x3, Pallas kernels: 12.1 us -> 14.1 us  [the longest x1 9.35 us: local(): pl.pallas_call(early_kernel, out_shape=(jax.ShapeDtypeStruct((2, events,...]
    unnamed x10 -> x8, local copies, waits for them, and re-layouts: 0.02 us -> 1.67 us
  transfers between devices with their start and end apart: 7 -> 7, of which waited for: 4 -> 4; matrix products, arithmetic and copies ran while one was open for 0% -> 0% of each run, Pallas kernels for 10% -> 12%
where the time goes in v8:
time: 103 us
  blocking collectives  43.7 us (42%)
  Pallas kernels  29.2 us (28%)
  waiting for transfers between devices  21.1 us (20%)
  starting transfers between devices  6.06 us (6%)
  local copies, waits for them, and re-layouts  1.67 us (2%)
    all_to_all x2, blocking collectives, exchange(): return lax.all_to_all(value, axes, split_axis=0, concat_axis=0, tiled=True)  43.7 us
    ppermute x6, waiting for transfers between devices, flip(): return lax.ppermute(value, axis, [(i, i ^ offset) for i in range(count)])  19.9 us
    pallas_call x1, Pallas kernels, local(): pl.pallas_call(functools.partial(late_kernel, count), out_shape=(event_sh...  10.7 us
    pallas_call x1, Pallas kernels, local(): pl.pallas_call(early_kernel, out_shape=(jax.ShapeDtypeStruct((2, events,...  9.35 us
    ppermute x6, starting transfers between devices, flip(): return lax.ppermute(value, axis, [(i, i ^ offset) for i in range(count)])  3.39 us
    pallas_call x1, Pallas kernels, local(): pl.pallas_call(functools.partial(prep_kernel, count), out_shape=tuple((pl...  3.25 us
    all_to_all x1, starting transfers between devices, exchange(): return lax.all_to_all(value, axes, split_axis=0, concat_axis=0, tiled=True)  2.66 us
    pallas_call x1, Pallas kernels, local(): pl.pallas_call(select_kernel, out_shape=pltpu.HBM((slot_count, width), BF...  2.51 us
  transfers between devices with their start and end apart: 7, of which 4 were waited for; matrix products, arithmetic and copies ran while one was open for 0% of the time, Pallas kernels for 12%

profile of v8, /device:TPU:0, one launch (start us, length us, event | category | flops | bytes accessed | tf_op | source)
XLA Modules:
  0.0 102.7 jit_solution(10505839335953930763)
XLA Ops:
  0.6 0.0 copy-start
  0.6 1.2 %slots.1 = (s32[8,256]{1,0:T(8,128)S(1)}, s32[32,32]{1,0:T(8,128)S(1)}, bf16[272,512]{1,0:T(8,128)(2,1)S(1)}) custom-call(s32[2,256]{1,0:T(2,128)} %bitcast.17, s32[2,256]{1,0:T(2,128)} %bitcast.18, s32[1,256]{1,0:T(1,128)} %seg_in.1, bf16[256,512]{1,0:T(8,128)(2,1)} %cot_in.1), custom_call_target="tpu_custom_call" | custom-call | tf_op jit(solution)/shard_map/slots/pallas_call | solution.py:496
  1.8 0.0 copy-start.1
  1.8 14.3 %all_to_all.21 = s32[32,1,32]{2,1,0:T(1,128)S(1)} all-to-all(s32[32,1,32]{2,1,0:T(1,128)S(1)} %bitcast.15), channel_id=1, replica_groups=mesh['table'=8,'ctx'=4] {'table','ctx'}, dimensions={0} | all-to-all | bytes 8192 | tf_op jit(solution)/shard_map/all_to_all | solution.py:493
  16.1 2.5 %select.1 = bf16[1024,512]{1,0:T(8,128)(2,1)} custom-call(s32[32,32]{1,0:T(8,128)S(1)} %bitcast.13, bf16[512,512]{1,0:T(8,128)(2,1)} %table_in.1), custom_call_target="tpu_custom_call" | custom-call | tf_op jit(solution)/shard_map/select/pallas_call | solution.py:515
  18.6 2.7 %all-to-all-start.1 = ((bf16[32,32,512]{2,1,0:T(8,128)(2,1)}), bf16[32,32,512]{2,1,0:T(8,128)(2,1)S(1)}, u32[]{:S(2)}, u32[]{:S(2)}) async-start(bf16[32,32,512]{2,1,0:T(8,128)(2,1)} %bitcast.16), calls=%async_computation.1 | async-start | bytes 2097152 | tf_op jit(solution)/shard_map/all_to_all | solution.py:493
  21.3 1.7 %collective-permute-start.1 = (bf16[272,512]{1,0:T(8,128)(2,1)S(1)}, bf16[272,512]{1,0:T(8,128)(2,1)S(1)}, u32[]{:S(2)}, u32[]{:S(2)}) collective-permute-start(bf16[272,512]{1,0:T(8,128)(2,1)S(1)} %get-tuple-element.34.refs_0_.refs_6_), channel_id=1, source_target_pairs={{0,2},{1,3},{2,0},{3,1},{4,6},{5,7},{6,4},{7,5},{8,10},{9,11},{10,... | collective-permute-start | bytes 835592 | tf_op jit(solution)/shard_map/ppermute | solution.py:462
  23.0 0.0 collective-permute-start
  23.0 16.8 %collective-permute-done.1.refs_2_ = bf16[272,512]{1,0:T(8,128)(2,1)S(1)} collective-permute-done((bf16[272,512]{1,0:T(8,128)(2,1)S(1)}, bf16[272,512]{1,0:T(8,128)(2,1)S(1)}, u32[]{:S(2)}, u32[]{:S(2)}) %collective-permute-start.1) | collective-permute-done | bytes 278560 | tf_op jit(solution)/shard_map/ppermute | solution.py:462
  39.8 0.0 collective-permute-start.2
  39.8 0.0 collective-permute-done.refs_1_
  39.8 1.5 %collective-permute-done.2.refs_3_ = bf16[272,512]{1,0:T(8,128)(2,1)S(1)} collective-permute-done((bf16[272,512]{1,0:T(8,128)(2,1)S(1)}, bf16[272,512]{1,0:T(8,128)(2,1)S(1)}, u32[]{:S(2)}, u32[]{:S(2)}) %collective-permute-start.2) | collective-permute-done | bytes 278560 | tf_op jit(solution)/shard_map/ppermute | solution.py:462
  41.4 0.0 copy-start.2
  41.4 0.7 copy-done.2
  42.1 0.0 copy-done
  42.1 0.0 copy-start.3
  42.1 1.0 copy-done.3
  43.0 3.2 %prep.1 = (f32[4,256,512]{2,1,0:T(8,128)}, f32[4,256,128]{2,1,0:T(8,128)}, f32[4,8,256]{2,1,0:T(8,128)}, bf16[1024,256]{1,0:T(8,128)(2,1)}, bf16[512,1024]{1,0:T(8,128)(2,1)S(1)}) custom-call(s32[4]{0:T(128)S(1)} %iota_xor_fusion.index_ref.refs_0_, s32[8,256]{1,0:T(8,128)S(1)} %get-tuple-element.32.slots_ref, s32[32,32]{1,0:T(8,128)S(1)} %bitcast.14, ...), custom_call_target="tpu_custom_call" | custom-call | tf_op jit(solution)/shard_map/prep/pallas_call | solution.py:539
  46.3 0.0 copy-done.1
  46.3 1.2 %all-to-all-done.1 = bf16[32,32,512]{2,1,0:T(8,128)(2,1)S(1)} async-done(((bf16[32,32,512]{2,1,0:T(8,128)(2,1)}), bf16[32,32,512]{2,1,0:T(8,128)(2,1)S(1)}, u32[]{:S(2)}, u32[]{:S(2)}) %all-to-all-start.1) | async-done | bytes 1048608 | tf_op jit(solution)/shard_map/all_to_all | solution.py:493
  47.5 0.7 embed.1.emb_ref.refs_1_
  48.2 0.1 collective-permute-start.3
  48.3 1.5 %collective-permute-start.4 = (bf16[256,512]{1,0:T(8,128)(2,1)S(1)}, bf16[256,512]{1,0:T(8,128)(2,1)S(1)}, u32[]{:S(2)}, u32[]{:S(2)}) collective-permute-start(bf16[256,512]{1,0:T(8,128)(2,1)S(1)} %embed.1.emb_ref.refs_1_), channel_id=1, source_target_pairs={{0,2},{1,3},{2,0},{3,1},{4,6},{5,7},{6,4},{7,5},{8,10},{9,11},{10,... | collective-permute-start | bytes 786440 | tf_op jit(solution)/shard_map/ppermute | solution.py:462
  49.8 0.0 collective-permute-done.3.mate_ref.refs_2_
  49.8 9.4 %early.1 = (bf16[2,256,2048]{2,1,0:T(8,128)(2,1)S(1)}, f32[2,256,512]{2,1,0:T(8,128)S(1)}, bf16[2,256,512]{2,1,0:T(8,128)(2,1)S(1)}, f32[256,2048]{1,0:T(8,128)S...) custom-call(s32[4]{0:T(128)S(1)} %iota_xor_fusion.index_ref.refs_0_,, ...), custom_call_target="tpu_custom_call" | custom-call | tf_op jit(solution)/shard_map/early/pallas_call | solution.py:559
  59.2 0.0 collective-permute-done.4.refs_3_
  59.2 0.1 collective-permute-start.5
  59.3 1.5 %collective-permute-done.5.refs_4_ = bf16[256,512]{1,0:T(8,128)(2,1)S(1)} collective-permute-done((bf16[256,512]{1,0:T(8,128)(2,1)S(1)}, bf16[256,512]{1,0:T(8,128)(2,1)S(1)}, u32[]{:S(2)}, u32[]{:S(2)}) %collective-permute-start.5) | collective-permute-done | bytes 262176 | tf_op jit(solution)/shard_map/ppermute | solution.py:462
  60.8 10.7 %late.1 = (bf16[256,512]{1,0:T(8,128)(2,1)}, bf16[1024,512]{1,0:T(8,128)(2,1)S(1)}) custom-call(s32[4]{0:T(128)S(1)} %iota_xor_fusion.index_ref.refs_0_, bf16[256,512]{1,0:T(8,128)(2,1)S(1)} %embed.1.emb_ref.refs_1_, bf16[256,512]{1,0:T(8,128)(2,1)S(1)} %collective-permute-done.3.mate_ref.refs_2_, bf16[256,512]{1,0:T(8,128)(2,1)S(1)} %collective-permute-done.4.refs_3_, ...), custom_call_target="tpu_custom_call" | custom-call | tf_op jit(solution)/shard_map/late/pallas_call | solution.py:579
  71.6 29.5 %all_to_all.22 = bf16[32,32,512]{2,1,0:T(8,128)(2,1)S(1)} all-to-all(bf16[32,32,512]{2,1,0:T(8,128)(2,1)S(1)} %bitcast.12), channel_id=1, replica_groups=mesh['table'=8,'ctx'=4] {'table','ctx'}, dimensions={0} | all-to-all | bytes 2097152 | tf_op jit(solution)/shard_map/all_to_all | solution.py:493
  101.1 1.5 %collect.1 = f32[512,512]{1,0:T(8,128)} custom-call(bf16[512,1024]{1,0:T(8,128)(2,1)S(1)} %get-tuple-element.60.chosen_ref, bf16[1024,512]{1,0:T(8,128)(2,1)S(1)} %bitcast.10), custom_call_target="tpu_custom_call" | custom-call | tf_op jit(solution)/shard_map/collect/pallas_call | solution.py:594
  (1 shorter events, 0.0 us)
Async XLA Ops:
  0.6 41.4 %copy-start = (bf16[512,512]{1,0:T(8,128)(2,1)S(1)}, bf16[512,512]{1,0:T(8,128)(2,1)}, u32[]{:S(2)}) copy-start(bf16[512,512]{1,0:T(8,128)(2,1)} %refs_1_.1) | copy-start | bytes 1572868
  1.8 44.5 %copy-start.1 = (bf16[272,512]{1,0:T(8,128)(2,1)}, bf16[272,512]{1,0:T(8,128)(2,1)S(1)}, u32[]{:S(2)}) copy-start(bf16[272,512]{1,0:T(8,128)(2,1)S(1)} %get-tuple-element.34.refs_0_.refs_6_) | copy-start | bytes 835588
  18.6 28.9 %all-to-all-start.1 = ((bf16[32,32,512]{2,1,0:T(8,128)(2,1)}), bf16[32,32,512]{2,1,0:T(8,128)(2,1)S(1)}, u32[]{:S(2)}, u32[]{:S(2)}) async-start(bf16[32,32,512]{2,1,0:T(8,128)(2,1)} %bitcast.16), calls=%async_computation.1 | async-start | bytes 2097152 | tf_op jit(solution)/shard_map/all_to_all | solution.py:493
  21.3 18.5 %collective-permute-start.1 = (bf16[272,512]{1,0:T(8,128)(2,1)S(1)}, bf16[272,512]{1,0:T(8,128)(2,1)S(1)}, u32[]{:S(2)}, u32[]{:S(2)}) collective-permute-start(bf16[272,512]{1,0:T(8,128)(2,1)S(1)} %get-tuple-element.34.refs_0_.refs_6_), channel_id=1, source_target_pairs={{0,2},{1,3},{2,0},{3,1},{4,6},{5,7},{6,4},{7,5},{8,10},{9,11},{10,... | collective-permute-start | bytes 835592 | tf_op jit(solution)/shard_map/ppermute | solution.py:462
  23.0 16.8 %collective-permute-start = (bf16[272,512]{1,0:T(8,128)(2,1)S(1)}, bf16[272,512]{1,0:T(8,128)(2,1)S(1)}, u32[]{:S(2)}, u32[]{:S(2)}) collective-permute-start(bf16[272,512]{1,0:T(8,128)(2,1)S(1)} %get-tuple-element.34.refs_0_.refs_6_), channel_id=1, source_target_pairs={{0,1},{1,0},{2,3},{3,2},{4,5},{5,4},{6,7},{7,6},{8,9},{9,8},{10,11... | collective-permute-start | bytes 835592 | tf_op jit(solution)/shard_map/ppermute | solution.py:462
  39.8 1.6 %collective-permute-start.2 = (bf16[272,512]{1,0:T(8,128)(2,1)S(1)}, bf16[272,512]{1,0:T(8,128)(2,1)S(1)}, u32[]{:S(2)}, u32[]{:S(2)}) collective-permute-start(bf16[272,512]{1,0:T(8,128)(2,1)S(1)} %collective-permute-done.1.refs_2_), channel_id=1, source_target_pairs={{0,1},{1,0},{2,3},{3,2},{4,5},{5,4},{6,7},{7,6},{8,9},{9,8},{10,11... | collective-permute-start | bytes 835592 | tf_op jit(solution)/shard_map/ppermute | solution.py:462
  41.4 0.7 copy-start.2
  42.1 1.0 copy-start.3
  48.2 1.6 %collective-permute-start.3 = (bf16[256,512]{1,0:T(8,128)(2,1)S(1)}, bf16[256,512]{1,0:T(8,128)(2,1)S(1)}, u32[]{:S(2)}, u32[]{:S(2)}) collective-permute-start(bf16[256,512]{1,0:T(8,128)(2,1)S(1)} %embed.1.emb_ref.refs_1_), channel_id=1, source_target_pairs={{0,1},{1,0},{2,3},{3,2},{4,5},{5,4},{6,7},{7,6},{8,9},{9,8},{10,11... | collective-permute-start | bytes 786440 | tf_op jit(solution)/shard_map/ppermute | solution.py:462
  48.3 10.9 %collective-permute-start.4 = (bf16[256,512]{1,0:T(8,128)(2,1)S(1)}, bf16[256,512]{1,0:T(8,128)(2,1)S(1)}, u32[]{:S(2)}, u32[]{:S(2)}) collective-permute-start(bf16[256,512]{1,0:T(8,128)(2,1)S(1)} %embed.1.emb_ref.refs_1_), channel_id=1, source_target_pairs={{0,2},{1,3},{2,0},{3,1},{4,6},{5,7},{6,4},{7,5},{8,10},{9,11},{10,... | collective-permute-start | bytes 786440 | tf_op jit(solution)/shard_map/ppermute | solution.py:462
  59.2 1.6 %collective-permute-start.5 = (bf16[256,512]{1,0:T(8,128)(2,1)S(1)}, bf16[256,512]{1,0:T(8,128)(2,1)S(1)}, u32[]{:S(2)}, u32[]{:S(2)}) collective-permute-start(bf16[256,512]{1,0:T(8,128)(2,1)S(1)} %collective-permute-done.4.refs_3_), channel_id=1, source_target_pairs={{0,1},{1,0},{2,3},{3,2},{4,5},{5,4},{6,7},{7,6},{8,9},{9,8},{10,11... | collective-permute-start | bytes 786440 | tf_op jit(solution)/shard_map/ppermute | solution.py:462

commit v9 on v8

--- a/solution.py
+++ b/solution.py
@@ -224,38 +224,62 @@
     return half * raised, raised * (one + half * (two - raised))
 
 
+def by_twos(start, stop, work):
+    twos = (stop - start) // 2
+
+    def step(k, _):
+        work([start + 2 * k, start + 2 * k + 1])
+        return 0
+
+    lax.fori_loop(0, twos, step, 0)
+
+    @pl.when(stop - start > 2 * twos)
+    def _():
+        work([stop - 1])
+
+
+def pipelined(numbers, mask_of, scores, finish):
+    masks = {}
+    items = [(n, h) for n in range(len(numbers)) for h in range(HEADS)]
+    ready = scores(numbers[0], 0)
+    for at, (n, h) in enumerate(items):
+        now = ready
+        if at + 1 < len(items):
+            later, later_head = items[at + 1]
+            ready = scores(numbers[later], later_head)
+        if n not in masks:
+            masks[n] = mask_of(numbers[n])
+        finish(numbers[n], h, now, masks[n])
+
+
 class Chunks:
-    def __init__(self, first, proj_ref, gatt_ref, segc_ref, segr_ref, join_ref):
-        self.first, self.proj, self.gatt = first, proj_ref, gatt_ref
+    def __init__(self, proj_ref, gatt_ref, segc_ref, segr_ref, join_ref):
+        self.proj, self.gatt = proj_ref, gatt_ref
         self.segc, self.segr, self.join = segc_ref, segr_ref, join_ref
         self.width = gatt_ref.shape[2]
 
+    def cut(self, chunk, part, h):
+        return self.proj[chunk, :, head(part, h, self.width)]
+
     def attend(self, i, start, stop, att_ref):
-        def pair(j, _):
-            mask = visible(i, j, self.segc, self.segr, False)
-            qi, kj = i - self.first, j - self.first
-
-            def scores(h):
-                queries = self.proj[qi, :, head(2, h, self.width)]
-                return dot_nt(queries, self.proj[kj, :, head(3, h, self.width)])
-
-            raw = scores(0)
-            for h in range(HEADS):
-                later = scores(h + 1) if h + 1 < HEADS else None
-                half = jnp.where(mask, raw * (0.5 * SCALE), HIDDEN)
-                weights = (half + half * jnp.tanh(half)).astype(BF16)
-                added = dot(weights, self.proj[kj, :, head(1, h, self.width)])
-                att_ref[:, head(0, h, self.width)] += added
-                raw = later
-            return 0
-
-        lax.fori_loop(start, stop, pair, 0)
+        def scores(j, h):
+            return dot_nt(self.cut(i, 2, h), self.cut(j, 3, h))
+
+        def finish(j, h, raw, mask):
+            half = jnp.where(mask, raw * (0.5 * SCALE), HIDDEN)
+            weights = (half + half * jnp.tanh(half)).astype(BF16)
+            att_ref[:, head(0, h, self.width)] += dot(weights, self.cut(j, 1, h))
+
+        def mask_of(j):
+            return visible(i, j, self.segc, self.segr, False)
+
+        by_twos(start, stop, lambda js: pipelined(js, mask_of, scores, finish))
 
     def finish(self, i, own, att, grad_mixed, emb_ref, w_out_ref, out_ref):
         att_norm, att_inverse = normalize(att)
-        gate = self.proj[i - self.first, :, 0 : self.width].astype(F32)
+        gate = self.proj[i, :, 0 : self.width].astype(F32)
         grad_att = norm_back(grad_mixed * gate, att_norm, att_inverse)
-        self.gatt[i - self.first] = grad_att.astype(BF16)
+        self.gatt[i] = grad_att.astype(BF16)
 
         @pl.when(i == own)
         def _():
@@ -265,62 +289,44 @@
             self.join[:, 0 : self.width] = grad_mixed * att_norm
 
     def query_side(self, own, start, stop):
-        def pair(j, _):
-            mask = visible(own, j, self.segc, self.segr, False)
-            me, kj = own - self.first, j - self.first
-
-            def scores(h):
-                raw = dot_nt(
-                    self.proj[me, :, head(2, h, self.width)],
-                    self.proj[kj, :, head(3, h, self.width)],
-                )
-                grad_weights = dot_nt(
-                    self.gatt[me, :, head(0, h, self.width)],
-                    self.proj[kj, :, head(1, h, self.width)],
-                )
-                return raw, grad_weights
-
-            raw, grad_weights = scores(0)
-            for h in range(HEADS):
-                later = scores(h + 1) if h + 1 < HEADS else (None, None)
-                _, slope = bent(raw, mask)
-                grad_raw = grad_weights.astype(BF16) * slope
-                added = dot(grad_raw, self.proj[kj, :, head(3, h, self.width)])
-                self.join[:, head(2, h, self.width)] += added
-                raw, grad_weights = later
-            return 0
-
-        lax.fori_loop(start, stop, pair, 0)
+        def scores(j, h):
+            grad_att = self.gatt[own, :, head(0, h, self.width)]
+            return (
+                dot_nt(self.cut(own, 2, h), self.cut(j, 3, h)),
+                dot_nt(grad_att, self.cut(j, 1, h)),
+            )
+
+        def finish(j, h, pair, mask):
+            raw, grad_weights = pair
+            _, slope = bent(raw, mask)
+            grad_raw = grad_weights.astype(BF16) * slope
+            self.join[:, head(2, h, self.width)] += dot(grad_raw, self.cut(j, 3, h))
+
+        def mask_of(j):
+            return visible(own, j, self.segc, self.segr, False)
+
+        by_twos(start, stop, lambda js: pipelined(js, mask_of, scores, finish))
 
     def key_side(self, own, start, stop):
-        def pair(i, _):
-            mask = visible(i, own, self.segc, self.segr, True)
-            me, qi = own - self.first, i - self.first
-
-            def scores(h):
-                raw = dot_nt(
-                    self.proj[me, :, head(3, h, self.width)],
-                    self.proj[qi, :, head(2, h, self.width)],
-                )
-                grad_weights = dot_nt(
-                    self.proj[me, :, head(1, h, self.width)],
-                    self.gatt[qi, :, head(0, h, self.width)],
-                )
-                return raw, grad_weights
-
-            raw, grad_weights = scores(0)
-            for h in range(HEADS):
-                later = scores(h + 1) if h + 1 < HEADS else (None, None)
-                value, slope = bent(raw, mask)
-                grad_raw = grad_weights.astype(BF16) * slope
-                queries = self.proj[qi, :, head(2, h, self.width)]
-                grad_att = self.gatt[qi, :, head(0, h, self.width)]
-                self.join[:, head(3, h, self.width)] += dot(grad_raw, queries)
-                self.join[:, head(1, h, self.width)] += dot(value, grad_att)
-                raw, grad_weights = later
-            return 0
-
-        lax.fori_loop(start, stop, pair, 0)
+        def scores(i, h):
+            grad_att = self.gatt[i, :, head(0, h, self.width)]
+            return (
+                dot_nt(self.cut(own, 3, h), self.cut(i, 2, h)),
+                dot_nt(self.cut(own, 1, h), grad_att),
+            )
+
+        def finish(i, h, pair, mask):
+            raw, grad_weights = pair
+            value, slope = bent(raw, mask)
+            grad_raw = grad_weights.astype(BF16) * slope
+            self.join[:, head(3, h, self.width)] += dot(grad_raw, self.cut(i, 2, h))
+            grad_att = self.gatt[i, :, head(0, h, self.width)]
+            self.join[:, head(1, h, self.width)] += dot(value, grad_att)
+
+        def mask_of(i):
+            return visible(i, own, self.segc, self.segr, True)
+
+        by_twos(start, stop, lambda chunks: pipelined(chunks, mask_of, scores, finish))
 
 
 def early_kernel(index_ref, emb_ref, mate_ref, *refs):
@@ -352,7 +358,7 @@
     join_ref[...] = jnp.zeros_like(join_ref)
     pair_rows = pl.ds(base, 2)
     chunks = Chunks(
-        0, proj_ref, gatt_ref, segc_ref.at[pair_rows], segr_ref.at[pair_rows], join_ref
+        proj_ref, gatt_ref, segc_ref.at[pair_rows], segr_ref.at[pair_rows], join_ref
     )
 
     def forward(i, _):
@@ -395,15 +401,22 @@
         att_ref,
         gatt_ref,
         join_ref,
+        sems,
     ) = refs[1 + count :]
     own = index_ref[0]
     base = jnp.minimum(own, index_ref[1])
     last = jnp.maximum(own, index_ref[1])
     closed = base == 0
 
-    for t in range(2):
-        proj_ref[base + t] = proj_pair_ref[t]
-        gatt_ref[base + t] = gatt_pair_ref[t]
+    pair_rows = pl.ds(base, 2)
+    copies = start_copies(
+        (
+            (join_early_ref, join_ref),
+            (proj_pair_ref, proj_ref.at[pair_rows]),
+            (gatt_pair_ref, gatt_ref.at[pair_rows]),
+        ),
+        sems,
+    )
 
     def write_to(place):
         def write(columns, value):
@@ -413,8 +426,9 @@
 
     for t in range(2, count):
         project(emb_refs[t][...], w_in_ref, write_to(index_ref[t]), None)
-    join_ref[...] = jnp.zeros_like(join_ref)
-    chunks = Chunks(0, proj_ref, gatt_ref, segc_ref, segr_ref, join_ref)
+    for copy in copies:
+        copy.wait()
+    chunks = Chunks(proj_ref, gatt_ref, segc_ref, segr_ref, join_ref)
 
     @pl.when(closed)
     def _():
@@ -440,10 +454,14 @@
     chunks.key_side(own, jnp.where(closed, last + 1, own), count)
 
     width = gatt_ref.shape[2]
-    scaled = jnp.where(iota((1, 4 * width), 1) < 2 * width, 1.0, 0.5 * SCALE)
-    joined = (join_ref[...] + join_early_ref[...]) * scaled
-    grad_proj = (joined * slope_ref[...]).astype(BF16)
-    grad_normed = dot_nt(grad_proj, w_in_ref[...])
+    grad_normed = None
+    for block in range(4):
+        columns = slice(block * width, (block + 1) * width)
+        joined = join_ref[:, columns] * slope_ref[:, columns]
+        if block >= 2:
+            joined = joined * (0.5 * SCALE)
+        part = dot_nt(joined.astype(BF16), w_in_ref[:, columns])
+        grad_normed = part if block == 0 else grad_normed + part
     normed, inverse = normalize(emb_refs[0][...].astype(F32))
     grad = norm_back(grad_normed, normed, inverse) + side_ref[0 : emb_refs[0].shape[0], :].astype(F32)
     grad_ref[...] = dot(spread_ref[...], grad.astype(BF16)).astype(BF16)
@@ -586,6 +604,7 @@
             pltpu.VMEM((events, width), F32),
             pltpu.VMEM((count, events, width), BF16),
             pltpu.VMEM((events, 4 * width), F32),
+            pltpu.SemaphoreType.DMA((3,)),
         ],
         compiler_params=params(28),
         name="late",

time: 103 us -> 102 us (level)
  Pallas kernels: 29.2 us -> 28.1 us
where the time goes in v9:
time: 102 us
  blocking collectives  43.7 us (43%)
  Pallas kernels  28.1 us (28%)
  waiting for transfers between devices  21.1 us (21%)
  starting transfers between devices  6.06 us (6%)
  local copies, waits for them, and re-layouts  1.67 us (2%)
    all_to_all x2, blocking collectives, exchange(): return lax.all_to_all(value, axes, split_axis=0, concat_axis=0, tiled=True)  43.7 us
    ppermute x6, waiting for transfers between devices, flip(): return lax.ppermute(value, axis, [(i, i ^ offset) for i in range(count)])  19.9 us
    pallas_call x1, Pallas kernels, local(): pl.pallas_call(functools.partial(late_kernel, count), out_shape=(event_sh...  9.91 us
    pallas_call x1, Pallas kernels, local(): pl.pallas_call(early_kernel, out_shape=(jax.ShapeDtypeStruct((2, events,...  9.05 us
    ppermute x6, starting transfers between devices, flip(): return lax.ppermute(value, axis, [(i, i ^ offset) for i in range(count)])  3.39 us
    pallas_call x1, Pallas kernels, local(): pl.pallas_call(functools.partial(prep_kernel, count), out_shape=tuple((pl...  3.25 us
    all_to_all x1, starting transfers between devices, exchange(): return lax.all_to_all(value, axes, split_axis=0, concat_axis=0, tiled=True)  2.66 us
    pallas_call x1, Pallas kernels, local(): pl.pallas_call(select_kernel, out_shape=pltpu.HBM((slot_count, width), BF...  2.51 us
  transfers between devices with their start and end apart: 7, of which 4 were waited for; matrix products, arithmetic and copies ran while one was open for 0% of the time, Pallas kernels for 12%

profile of v9, /device:TPU:0, one launch (start us, length us, event | category | flops | bytes accessed | tf_op | source)
XLA Modules:
  0.0 101.5 jit_solution(17668720006824703830)
XLA Ops:
  0.6 0.0 copy-start
  0.6 1.2 %slots.1 = (s32[8,256]{1,0:T(8,128)S(1)}, s32[32,32]{1,0:T(8,128)S(1)}, bf16[272,512]{1,0:T(8,128)(2,1)S(1)}) custom-call(s32[2,256]{1,0:T(2,128)} %bitcast.17, s32[2,256]{1,0:T(2,128)} %bitcast.18, s32[1,256]{1,0:T(1,128)} %seg_in.1, bf16[256,512]{1,0:T(8,128)(2,1)} %cot_in.1), custom_call_target="tpu_custom_call" | custom-call | tf_op jit(solution)/shard_map/slots/pallas_call | solution.py:514
  1.8 0.0 copy-start.1
  1.8 14.3 %all_to_all.21 = s32[32,1,32]{2,1,0:T(1,128)S(1)} all-to-all(s32[32,1,32]{2,1,0:T(1,128)S(1)} %bitcast.15), channel_id=1, replica_groups=mesh['table'=8,'ctx'=4] {'table','ctx'}, dimensions={0} | all-to-all | bytes 8192 | tf_op jit(solution)/shard_map/all_to_all | solution.py:511
  16.1 2.5 %select.1 = bf16[1024,512]{1,0:T(8,128)(2,1)} custom-call(s32[32,32]{1,0:T(8,128)S(1)} %bitcast.13, bf16[512,512]{1,0:T(8,128)(2,1)} %table_in.1), custom_call_target="tpu_custom_call" | custom-call | tf_op jit(solution)/shard_map/select/pallas_call | solution.py:533
  18.6 2.7 %all-to-all-start.1 = ((bf16[32,32,512]{2,1,0:T(8,128)(2,1)}), bf16[32,32,512]{2,1,0:T(8,128)(2,1)S(1)}, u32[]{:S(2)}, u32[]{:S(2)}) async-start(bf16[32,32,512]{2,1,0:T(8,128)(2,1)} %bitcast.16), calls=%async_computation.1 | async-start | bytes 2097152 | tf_op jit(solution)/shard_map/all_to_all | solution.py:511
  21.3 1.7 %collective-permute-start.1 = (bf16[272,512]{1,0:T(8,128)(2,1)S(1)}, bf16[272,512]{1,0:T(8,128)(2,1)S(1)}, u32[]{:S(2)}, u32[]{:S(2)}) collective-permute-start(bf16[272,512]{1,0:T(8,128)(2,1)S(1)} %get-tuple-element.34.refs_0_.refs_6_), channel_id=1, source_target_pairs={{0,2},{1,3},{2,0},{3,1},{4,6},{5,7},{6,4},{7,5},{8,10},{9,11},{10,... | collective-permute-start | bytes 835592 | tf_op jit(solution)/shard_map/ppermute | solution.py:480
  23.0 0.0 collective-permute-start
  23.0 16.8 %collective-permute-done.1.refs_2_ = bf16[272,512]{1,0:T(8,128)(2,1)S(1)} collective-permute-done((bf16[272,512]{1,0:T(8,128)(2,1)S(1)}, bf16[272,512]{1,0:T(8,128)(2,1)S(1)}, u32[]{:S(2)}, u32[]{:S(2)}) %collective-permute-start.1) | collective-permute-done | bytes 278560 | tf_op jit(solution)/shard_map/ppermute | solution.py:480
  39.8 0.0 collective-permute-start.2
  39.8 0.0 collective-permute-done.refs_1_
  39.8 1.5 %collective-permute-done.2.refs_3_ = bf16[272,512]{1,0:T(8,128)(2,1)S(1)} collective-permute-done((bf16[272,512]{1,0:T(8,128)(2,1)S(1)}, bf16[272,512]{1,0:T(8,128)(2,1)S(1)}, u32[]{:S(2)}, u32[]{:S(2)}) %collective-permute-start.2) | collective-permute-done | bytes 278560 | tf_op jit(solution)/shard_map/ppermute | solution.py:480
  41.4 0.0 copy-start.2
  41.4 0.7 copy-done.2
  42.1 0.0 copy-done
  42.1 0.0 copy-start.3
  42.1 1.0 copy-done.3
  43.0 3.2 %prep.1 = (f32[4,256,512]{2,1,0:T(8,128)}, f32[4,256,128]{2,1,0:T(8,128)}, f32[4,8,256]{2,1,0:T(8,128)}, bf16[1024,256]{1,0:T(8,128)(2,1)}, bf16[512,1024]{1,0:T(8,128)(2,1)S(1)}) custom-call(s32[4]{0:T(128)S(1)} %iota_xor_fusion.index_ref.refs_0_, s32[8,256]{1,0:T(8,128)S(1)} %get-tuple-element.32.slots_ref, s32[32,32]{1,0:T(8,128)S(1)} %bitcast.14, ...), custom_call_target="tpu_custom_call" | custom-call | tf_op jit(solution)/shard_map/prep/pallas_call | solution.py:557
  46.3 0.0 copy-done.1
  46.3 1.2 %all-to-all-done.1 = bf16[32,32,512]{2,1,0:T(8,128)(2,1)S(1)} async-done(((bf16[32,32,512]{2,1,0:T(8,128)(2,1)}), bf16[32,32,512]{2,1,0:T(8,128)(2,1)S(1)}, u32[]{:S(2)}, u32[]{:S(2)}) %all-to-all-start.1) | async-done | bytes 1048608 | tf_op jit(solution)/shard_map/all_to_all | solution.py:511
  47.5 0.7 embed.1.emb_ref.refs_1_
  48.2 0.1 collective-permute-start.3
  48.3 1.5 %collective-permute-start.4 = (bf16[256,512]{1,0:T(8,128)(2,1)S(1)}, bf16[256,512]{1,0:T(8,128)(2,1)S(1)}, u32[]{:S(2)}, u32[]{:S(2)}) collective-permute-start(bf16[256,512]{1,0:T(8,128)(2,1)S(1)} %embed.1.emb_ref.refs_1_), channel_id=1, source_target_pairs={{0,2},{1,3},{2,0},{3,1},{4,6},{5,7},{6,4},{7,5},{8,10},{9,11},{10,... | collective-permute-start | bytes 786440 | tf_op jit(solution)/shard_map/ppermute | solution.py:480
  49.8 0.0 collective-permute-done.3.mate_ref.refs_2_
  49.8 9.0 %early.1 = (bf16[2,256,2048]{2,1,0:T(8,128)(2,1)S(1)}, f32[2,256,512]{2,1,0:T(8,128)S(1)}, bf16[2,256,512]{2,1,0:T(8,128)(2,1)S(1)}, f32[256,2048]{1,0:T(8,128)S...) custom-call(s32[4]{0:T(128)S(1)} %iota_xor_fusion.index_ref.refs_0_,, ...), custom_call_target="tpu_custom_call" | custom-call | tf_op jit(solution)/shard_map/early/pallas_call | solution.py:577
  58.9 0.0 collective-permute-done.4.refs_3_
  58.9 0.1 collective-permute-start.5
  59.0 1.5 %collective-permute-done.5.refs_4_ = bf16[256,512]{1,0:T(8,128)(2,1)S(1)} collective-permute-done((bf16[256,512]{1,0:T(8,128)(2,1)S(1)}, bf16[256,512]{1,0:T(8,128)(2,1)S(1)}, u32[]{:S(2)}, u32[]{:S(2)}) %collective-permute-start.5) | collective-permute-done | bytes 262176 | tf_op jit(solution)/shard_map/ppermute | solution.py:480
  60.5 9.9 %late.1 = (bf16[256,512]{1,0:T(8,128)(2,1)}, bf16[1024,512]{1,0:T(8,128)(2,1)S(1)}) custom-call(s32[4]{0:T(128)S(1)} %iota_xor_fusion.index_ref.refs_0_, bf16[256,512]{1,0:T(8,128)(2,1)S(1)} %embed.1.emb_ref.refs_1_, bf16[256,512]{1,0:T(8,128)(2,1)S(1)} %collective-permute-done.3.mate_ref.refs_2_, bf16[256,512]{1,0:T(8,128)(2,1)S(1)} %collective-permute-done.4.refs_3_, ...), custom_call_target="tpu_custom_call" | custom-call | tf_op jit(solution)/shard_map/late/pallas_call | solution.py:597
  70.4 29.5 %all_to_all.22 = bf16[32,32,512]{2,1,0:T(8,128)(2,1)S(1)} all-to-all(bf16[32,32,512]{2,1,0:T(8,128)(2,1)S(1)} %bitcast.12), channel_id=1, replica_groups=mesh['table'=8,'ctx'=4] {'table','ctx'}, dimensions={0} | all-to-all | bytes 2097152 | tf_op jit(solution)/shard_map/all_to_all | solution.py:511
  99.9 1.5 %collect.1 = f32[512,512]{1,0:T(8,128)} custom-call(bf16[512,1024]{1,0:T(8,128)(2,1)S(1)} %get-tuple-element.60.chosen_ref, bf16[1024,512]{1,0:T(8,128)(2,1)S(1)} %bitcast.10), custom_call_target="tpu_custom_call" | custom-call | tf_op jit(solution)/shard_map/collect/pallas_call | solution.py:613
  (1 shorter events, 0.0 us)
Async XLA Ops:
  0.6 41.4 %copy-start = (bf16[512,512]{1,0:T(8,128)(2,1)S(1)}, bf16[512,512]{1,0:T(8,128)(2,1)}, u32[]{:S(2)}) copy-start(bf16[512,512]{1,0:T(8,128)(2,1)} %refs_1_.1) | copy-start | bytes 1572868
  1.8 44.5 %copy-start.1 = (bf16[272,512]{1,0:T(8,128)(2,1)}, bf16[272,512]{1,0:T(8,128)(2,1)S(1)}, u32[]{:S(2)}) copy-start(bf16[272,512]{1,0:T(8,128)(2,1)S(1)} %get-tuple-element.34.refs_0_.refs_6_) | copy-start | bytes 835588
  18.6 28.9 %all-to-all-start.1 = ((bf16[32,32,512]{2,1,0:T(8,128)(2,1)}), bf16[32,32,512]{2,1,0:T(8,128)(2,1)S(1)}, u32[]{:S(2)}, u32[]{:S(2)}) async-start(bf16[32,32,512]{2,1,0:T(8,128)(2,1)} %bitcast.16), calls=%async_computation.1 | async-start | bytes 2097152 | tf_op jit(solution)/shard_map/all_to_all | solution.py:511
  21.3 18.5 %collective-permute-start.1 = (bf16[272,512]{1,0:T(8,128)(2,1)S(1)}, bf16[272,512]{1,0:T(8,128)(2,1)S(1)}, u32[]{:S(2)}, u32[]{:S(2)}) collective-permute-start(bf16[272,512]{1,0:T(8,128)(2,1)S(1)} %get-tuple-element.34.refs_0_.refs_6_), channel_id=1, source_target_pairs={{0,2},{1,3},{2,0},{3,1},{4,6},{5,7},{6,4},{7,5},{8,10},{9,11},{10,... | collective-permute-start | bytes 835592 | tf_op jit(solution)/shard_map/ppermute | solution.py:480
  23.0 16.8 %collective-permute-start = (bf16[272,512]{1,0:T(8,128)(2,1)S(1)}, bf16[272,512]{1,0:T(8,128)(2,1)S(1)}, u32[]{:S(2)}, u32[]{:S(2)}) collective-permute-start(bf16[272,512]{1,0:T(8,128)(2,1)S(1)} %get-tuple-element.34.refs_0_.refs_6_), channel_id=1, source_target_pairs={{0,1},{1,0},{2,3},{3,2},{4,5},{5,4},{6,7},{7,6},{8,9},{9,8},{10,11... | collective-permute-start | bytes 835592 | tf_op jit(solution)/shard_map/ppermute | solution.py:480
  39.8 1.6 %collective-permute-start.2 = (bf16[272,512]{1,0:T(8,128)(2,1)S(1)}, bf16[272,512]{1,0:T(8,128)(2,1)S(1)}, u32[]{:S(2)}, u32[]{:S(2)}) collective-permute-start(bf16[272,512]{1,0:T(8,128)(2,1)S(1)} %collective-permute-done.1.refs_2_), channel_id=1, source_target_pairs={{0,1},{1,0},{2,3},{3,2},{4,5},{5,4},{6,7},{7,6},{8,9},{9,8},{10,11... | collective-permute-start | bytes 835592 | tf_op jit(solution)/shard_map/ppermute | solution.py:480
  41.4 0.7 copy-start.2
  42.1 1.0 copy-start.3
  48.2 1.6 %collective-permute-start.3 = (bf16[256,512]{1,0:T(8,128)(2,1)S(1)}, bf16[256,512]{1,0:T(8,128)(2,1)S(1)}, u32[]{:S(2)}, u32[]{:S(2)}) collective-permute-start(bf16[256,512]{1,0:T(8,128)(2,1)S(1)} %embed.1.emb_ref.refs_1_), channel_id=1, source_target_pairs={{0,1},{1,0},{2,3},{3,2},{4,5},{5,4},{6,7},{7,6},{8,9},{9,8},{10,11... | collective-permute-start | bytes 786440 | tf_op jit(solution)/shard_map/ppermute | solution.py:480
  48.3 10.6 %collective-permute-start.4 = (bf16[256,512]{1,0:T(8,128)(2,1)S(1)}, bf16[256,512]{1,0:T(8,128)(2,1)S(1)}, u32[]{:S(2)}, u32[]{:S(2)}) collective-permute-start(bf16[256,512]{1,0:T(8,128)(2,1)S(1)} %embed.1.emb_ref.refs_1_), channel_id=1, source_target_pairs={{0,2},{1,3},{2,0},{3,1},{4,6},{5,7},{6,4},{7,5},{8,10},{9,11},{10,... | collective-permute-start | bytes 786440 | tf_op jit(solution)/shard_map/ppermute | solution.py:480
  58.9 1.6 %collective-permute-start.5 = (bf16[256,512]{1,0:T(8,128)(2,1)S(1)}, bf16[256,512]{1,0:T(8,128)(2,1)S(1)}, u32[]{:S(2)}, u32[]{:S(2)}) collective-permute-start(bf16[256,512]{1,0:T(8,128)(2,1)S(1)} %collective-permute-done.4.refs_3_), channel_id=1, source_target_pairs={{0,1},{1,0},{2,3},{3,2},{4,5},{5,4},{6,7},{7,6},{8,9},{9,8},{10,11... | collective-permute-start | bytes 786440 | tf_op jit(solution)/shard_map/ppermute | solution.py:480

commit v10 on v9

--- a/solution.py
+++ b/solution.py
@@ -171,13 +171,11 @@
     return same & (first + (query_chunk - key_chunk) * events >= second)
 
 
-def project(emb, w_in_ref, write, slope_ref, copies=()):
+def project(emb, w_in_ref, write, slope_ref):
     width = emb.shape[1]
     normed = (0.5 * normalize(emb.astype(F32))[0]).astype(BF16)
     for block in range(4):
         columns = slice(block * width, (block + 1) * width)
-        if copies:
-            copies[block].wait()
         half = dot(normed, w_in_ref[:, columns])
         bend = jnp.tanh(half)
         value = half + half * bend
@@ -333,11 +331,9 @@
     w_in_in, w_out_in, mixed_in, segc_in, segr_in, spread_in, side_in = refs[:7]
     proj_ref, att_ref, gatt_ref, join_ref, slope_ref, out_ref = refs[7:13]
     w_in_ref, w_out_ref, mixed_ref, segc_ref, segr_ref, spread_ref, side_ref, sems = refs[13:]
-    width = emb_ref.shape[1]
-    blocks = [pl.ds(block * width, width) for block in range(4)]
-    pairs = [(w_in_in.at[:, block], w_in_ref.at[:, block]) for block in blocks]
-    pairs += [(segc_in, segc_ref), (segr_in, segr_ref), (mixed_in, mixed_ref)]
+    pairs = [(segc_in, segc_ref), (segr_in, segr_ref), (mixed_in, mixed_ref)]
     pairs += [(w_out_in, w_out_ref), (spread_in, spread_ref), (side_in, side_ref)]
+    pairs += [(w_in_in, w_in_ref)]
     copies = start_copies(pairs, sems)
     own = index_ref[0]
     mate = index_ref[1]
@@ -350,9 +346,9 @@
 
         return write
 
-    project(emb_ref[...], w_in_ref, write_to(own), slope_ref, copies[:4])
-    project(mate_ref[...], w_in_ref, write_to(mate), None)
-    for copy in copies[4:]:
+    project(emb_ref[...], w_in_in, write_to(own), slope_ref)
+    project(mate_ref[...], w_in_in, write_to(mate), None)
+    for copy in copies:
         copy.wait()
     att_ref[...] = jnp.zeros_like(att_ref)
     join_ref[...] = jnp.zeros_like(join_ref)
@@ -378,9 +374,17 @@
         chunks.key_side(own, own, last + 1)
 
 
+def project_kernel(emb_ref, w_in_ref, proj_ref):
+    def write(columns, value):
+        proj_ref[:, columns] = value
+
+    project(emb_ref[...], w_in_ref, write, None)
+
+
 def late_kernel(count, *refs):
     index_ref = refs[0]
     emb_refs = refs[1 : 1 + count]
+    proj_far_ref = refs[1 + count]
     (
         proj_pair_ref,
         att_pair_ref,
@@ -402,7 +406,7 @@
         gatt_ref,
         join_ref,
         sems,
-    ) = refs[1 + count :]
+    ) = refs[2 + count :]
     own = index_ref[0]
     base = jnp.minimum(own, index_ref[1])
     last = jnp.maximum(own, index_ref[1])
@@ -414,6 +418,7 @@
             (join_early_ref, join_ref),
             (proj_pair_ref, proj_ref.at[pair_rows]),
             (gatt_pair_ref, gatt_ref.at[pair_rows]),
+            (proj_far_ref, proj_ref.at[index_ref[count // 2]]),
         ),
         sems,
     )
@@ -425,6 +430,8 @@
         return write
 
     for t in range(2, count):
+        if t == count // 2:
+            continue
         project(emb_refs[t][...], w_in_ref, write_to(index_ref[t]), None)
     for copy in copies:
         copy.wait()
@@ -587,28 +594,35 @@
         + tuple(jax.ShapeDtypeStruct(a.shape, BF16) for a in (w_in, w_out))
         + prep_shapes
         + (jax.ShapeDtypeStruct(side.shape, BF16),),
-        in_specs=[smem, vmem, vmem] + [hbm] * 7,
+        in_specs=[smem, vmem, vmem, vmem] + [hbm] * 6,
         out_specs=(vmem,) * 13,
-        scratch_shapes=[pltpu.SemaphoreType.DMA((10,))],
+        scratch_shapes=[pltpu.SemaphoreType.DMA((7,))],
         compiler_params=params(20),
         name="early",
-    )(index, embedded, emb_mate, *in_hbm(w_in, w_out), *prepared, *in_hbm(side))
-    emb_blocks = gather_blocks(embedded, "ctx", {1: emb_mate, count // 2: after(emb_far, early)})
+    )(index, embedded, emb_mate, w_in, *in_hbm(w_out), *prepared, *in_hbm(side))
+    emb_far = after(emb_far, early[0])
+    proj_far = pl.pallas_call(
+        project_kernel,
+        out_shape=jax.ShapeDtypeStruct((events, 4 * width), BF16),
+        compiler_params=params(),
+        name="project_far",
+    )(emb_far, early[6])
+    emb_blocks = gather_blocks(embedded, "ctx", {1: emb_mate, count // 2: emb_far})
     layer_out, slot_grad = pl.pallas_call(
         functools.partial(late_kernel, count),
         out_shape=(event_shape, jax.ShapeDtypeStruct((slot_count, width), BF16)),
-        in_specs=[smem] + [vmem] * (13 + count),
+        in_specs=[smem] + [vmem] * (14 + count),
         out_specs=(vmem, vmem),
         scratch_shapes=[
             pltpu.VMEM((count, events, 4 * width), BF16),
             pltpu.VMEM((events, width), F32),
             pltpu.VMEM((count, events, width), BF16),
             pltpu.VMEM((events, 4 * width), F32),
-            pltpu.SemaphoreType.DMA((3,)),
+            pltpu.SemaphoreType.DMA((4,)),
         ],
         compiler_params=params(28),
         name="late",
-    )(index, *emb_blocks, *early)
+    )(index, *emb_blocks, proj_far, *early)
     returned = exchange(slot_grad.reshape(owners, capacity, width)).reshape(slot_count, width)
     row_grad = pl.pallas_call(
         collect_kernel,

time: 102 us -> 102 us (level)
  waiting for transfers between devices: 21.1 us -> 19.6 us
  blocking collectives: 43.7 us -> 45 us
    pallas_call x1, Pallas kernels: 9.05 us -> 7.72 us  [local(): pl.pallas_call(early_kernel, out_shape=(jax.ShapeDtypeStruct((2, events,...]
    all_to_all x2, blocking collectives: 43.7 us -> 45 us  [exchange(): return lax.all_to_all(value, axes, split_axis=0, concat_axis=0, tiled=True)]
    all_to_all x1, waiting for transfers between devices: 1.22 us -> 0.01 us  [exchange(): return lax.all_to_all(value, axes, split_axis=0, concat_axis=0, tiled=True)]
where the time goes in v10:
time: 102 us; the launch traced here: 101 us
  blocking collectives  45 us (44%)
  Pallas kernels  27.7 us (27%)
  waiting for transfers between devices  19.6 us (19%)
  starting transfers between devices  6.02 us (6%)
  local copies, waits for them, and re-layouts  2.02 us (2%)
    all_to_all x2, blocking collectives, exchange(): return lax.all_to_all(value, axes, split_axis=0, concat_axis=0, tiled=True)  45 us
    ppermute x6, waiting for transfers between devices, flip(): return lax.ppermute(value, axis, [(i, i ^ offset) for i in range(count)])  19.6 us
    pallas_call x1, Pallas kernels, local(): pl.pallas_call(functools.partial(late_kernel, count), out_shape=(event_sh...  9.39 us
    pallas_call x1, Pallas kernels, local(): pl.pallas_call(early_kernel, out_shape=(jax.ShapeDtypeStruct((2, events,...  7.72 us
    pallas_call x1, Pallas kernels, local(): pl.pallas_call(functools.partial(prep_kernel, count), out_shape=tuple((pl...  3.84 us
    ppermute x6, starting transfers between devices, flip(): return lax.ppermute(value, axis, [(i, i ^ offset) for i in range(count)])  3.23 us
    all_to_all x1, starting transfers between devices, exchange(): return lax.all_to_all(value, axes, split_axis=0, concat_axis=0, tiled=True)  2.8 us
    pallas_call x1, Pallas kernels, local(): pl.pallas_call(select_kernel, out_shape=pltpu.HBM((slot_count, width), BF...  2.51 us
  transfers between devices with their start and end apart: 7, of which 4 were waited for; matrix products, arithmetic and copies ran while one was open for 0% of the time, Pallas kernels for 12%

profile of v10, /device:TPU:0, one launch (start us, length us, event | category | flops | bytes accessed | tf_op | source)
XLA Modules:
  0.0 101.2 jit_solution(445275613760450133)
XLA Ops:
  0.6 1.1 %slots.1 = (s32[8,256]{1,0:T(8,128)S(1)}, s32[32,32]{1,0:T(8,128)S(1)}, bf16[272,512]{1,0:T(8,128)(2,1)S(1)}) custom-call(s32[2,256]{1,0:T(2,128)} %bitcast.17, s32[2,256]{1,0:T(2,128)} %bitcast.18, s32[1,256]{1,0:T(1,128)} %seg_in.1, bf16[256,512]{1,0:T(8,128)(2,1)} %cot_in.1), custom_call_target="tpu_custom_call" | custom-call | tf_op jit(solution)/shard_map/slots/pallas_call | solution.py:521
  1.7 0.0 copy-start.2
  1.8 14.3 %all_to_all.21 = s32[32,1,32]{2,1,0:T(1,128)S(1)} all-to-all(s32[32,1,32]{2,1,0:T(1,128)S(1)} %bitcast.15), channel_id=1, replica_groups=mesh['table'=8,'ctx'=4] {'table','ctx'}, dimensions={0} | all-to-all | bytes 8192 | tf_op jit(solution)/shard_map/all_to_all | solution.py:518
  16.0 2.5 %select.1 = bf16[1024,512]{1,0:T(8,128)(2,1)} custom-call(s32[32,32]{1,0:T(8,128)S(1)} %bitcast.13, bf16[512,512]{1,0:T(8,128)(2,1)} %table_in.1), custom_call_target="tpu_custom_call" | custom-call | tf_op jit(solution)/shard_map/select/pallas_call | solution.py:540
  18.5 0.0 copy-start
  18.5 2.8 %all-to-all-start.1 = ((bf16[32,32,512]{2,1,0:T(8,128)(2,1)}), bf16[32,32,512]{2,1,0:T(8,128)(2,1)S(1)}, u32[]{:S(2)}, u32[]{:S(2)}) async-start(bf16[32,32,512]{2,1,0:T(8,128)(2,1)} %bitcast.16), calls=%async_computation.1 | async-start | bytes 2097152 | tf_op jit(solution)/shard_map/all_to_all | solution.py:518
  21.3 1.7 %collective-permute-start.1 = (bf16[272,512]{1,0:T(8,128)(2,1)S(1)}, bf16[272,512]{1,0:T(8,128)(2,1)}, u32[]{:S(2)}, u32[]{:S(2)}) collective-permute-start(bf16[272,512]{1,0:T(8,128)(2,1)S(1)} %get-tuple-element.34.refs_0_.refs_6_), channel_id=1, source_target_pairs={{0,2},{1,3},{2,0},{3,1},{4,6},{5,7},{6,4},{7,5},{8,10},{9,11},{10,... | collective-permute-start | bytes 835592 | tf_op jit(solution)/shard_map/ppermute | solution.py:487
  23.0 0.0 collective-permute-start
  23.0 16.9 %collective-permute-done.1.refs_2_ = bf16[272,512]{1,0:T(8,128)(2,1)} collective-permute-done((bf16[272,512]{1,0:T(8,128)(2,1)S(1)}, bf16[272,512]{1,0:T(8,128)(2,1)}, u32[]{:S(2)}, u32[]{:S(2)}) %collective-permute-start.1) | collective-permute-done | bytes 278560 | tf_op jit(solution)/shard_map/ppermute | solution.py:487
  40.0 0.0 collective-permute-start.2
  40.0 0.0 collective-permute-done.refs_1_
  40.0 1.9 %collective-permute-done.2.refs_3_ = bf16[272,512]{1,0:T(8,128)(2,1)} collective-permute-done((bf16[272,512]{1,0:T(8,128)(2,1)}, bf16[272,512]{1,0:T(8,128)(2,1)}, u32[]{:S(2)}, u32[]{:S(2)}) %collective-permute-start.2) | collective-permute-done | bytes 278560 | tf_op jit(solution)/shard_map/ppermute | solution.py:487
  41.9 0.0 copy-start.1
  41.9 1.0 %copy-done.1 = bf16[512,512]{1,0:T(8,128)(2,1)S(1)} copy-done((bf16[512,512]{1,0:T(8,128)(2,1)S(1)}, bf16[512,512]{1,0:T(8,128)(2,1)}, u32[]{:S(2)}) %copy-start.1) | copy-done | bytes 524312
  42.9 3.8 %prep.1 = (f32[4,256,512]{2,1,0:T(8,128)}, f32[4,256,128]{2,1,0:T(8,128)}, f32[4,8,256]{2,1,0:T(8,128)}, bf16[1024,256]{1,0:T(8,128)(2,1)}, bf16[512,1024]{1,0:T(8,128)(2,1)S(1)}) custom-call(s32[4]{0:T(128)S(1)} %iota_xor_fusion.index_ref.refs_0_, s32[8,256]{1,0:T(8,128)S(1)} %get-tuple-element.32.slots_ref, s32[32,32]{1,0:T(8,128)S(1)} %bitcast.14, ...), custom_call_target="tpu_custom_call" | custom-call | tf_op jit(solution)/shard_map/prep/pallas_call | solution.py:564
  46.8 0.0 copy-done.2
  46.8 0.0 copy-start.3
  46.8 1.0 copy-done.3
  47.7 0.0 all-to-all-done.1
  47.7 0.7 embed.1.emb_ref.refs_1_
  48.5 0.2 collective-permute-start.3
  48.7 1.3 %collective-permute-start.4 = (bf16[256,512]{1,0:T(8,128)(2,1)S(1)}, bf16[256,512]{1,0:T(8,128)(2,1)S(1)}, u32[]{:S(2)}, u32[]{:S(2)}) collective-permute-start(bf16[256,512]{1,0:T(8,128)(2,1)S(1)} %embed.1.emb_ref.refs_1_), channel_id=1, source_target_pairs={{0,2},{1,3},{2,0},{3,1},{4,6},{5,7},{6,4},{7,5},{8,10},{9,11},{10,... | collective-permute-start | bytes 786440 | tf_op jit(solution)/shard_map/ppermute | solution.py:487
  49.9 0.2 collective-permute-done.3.mate_ref.refs_2_
  50.1 0.0 copy-done
  50.1 7.7 %early.1 = (bf16[2,256,2048]{2,1,0:T(8,128)(2,1)S(1)}, f32[2,256,512]{2,1,0:T(8,128)S(1)}, bf16[2,256,512]{2,1,0:T(8,128)(2,1)S(1)}, f32[256,2048]{1,0:T(8,128)S...) custom-call(s32[4]{0:T(128)S(1)} %iota_xor_fusion.index_ref.refs_0_,, ...), custom_call_target="tpu_custom_call" | custom-call | tf_op jit(solution)/shard_map/early/pallas_call | solution.py:584
  57.8 0.0 collective-permute-done.4.emb_ref.refs_3_
  57.8 0.1 collective-permute-start.5
  57.9 0.9 project_far.1.refs_5_
  58.8 0.6 collective-permute-done.5.refs_4_
  59.4 9.4 %late.1 = (bf16[256,512]{1,0:T(8,128)(2,1)}, bf16[1024,512]{1,0:T(8,128)(2,1)S(1)}) custom-call(s32[4]{0:T(128)S(1)} %iota_xor_fusion.index_ref.refs_0_, bf16[256,512]{1,0:T(8,128)(2,1)S(1)} %embed.1.emb_ref.refs_1_, bf16[256,512]{1,0:T(8,128)(2,1)S(1)} %collective-permute-done.3.mate_ref.refs_2_, ...), custom_call_target="tpu_custom_call" | custom-call | tf_op jit(solution)/shard_map/late/pallas_call | solution.py:611
  68.8 0.0 copy-start.4
  68.8 30.8 %all_to_all.22 = bf16[32,32,512]{2,1,0:T(8,128)(2,1)S(1)} all-to-all(bf16[32,32,512]{2,1,0:T(8,128)(2,1)S(1)} %bitcast.12), channel_id=1, replica_groups=mesh['table'=8,'ctx'=4] {'table','ctx'}, dimensions={0} | all-to-all | bytes 2097152 | tf_op jit(solution)/shard_map/all_to_all | solution.py:518
  99.6 0.0 copy-done.4
  99.6 1.5 %collect.1 = f32[512,512]{1,0:T(8,128)} custom-call(bf16[512,1024]{1,0:T(8,128)(2,1)S(1)} %copy-done.4, bf16[1024,512]{1,0:T(8,128)(2,1)S(1)} %bitcast.10), custom_call_target="tpu_custom_call" | custom-call | tf_op jit(solution)/shard_map/collect/pallas_call | solution.py:627
  (1 shorter events, 0.0 us)
Async XLA Ops:
  1.7 45.0 %copy-start.2 = (bf16[272,512]{1,0:T(8,128)(2,1)}, bf16[272,512]{1,0:T(8,128)(2,1)S(1)}, u32[]{:S(2)}) copy-start(bf16[272,512]{1,0:T(8,128)(2,1)S(1)} %get-tuple-element.34.refs_0_.refs_6_) | copy-start | bytes 835588
  18.5 31.5 %copy-start = (bf16[512,2048]{1,0:T(8,128)(2,1)S(1)}, bf16[512,2048]{1,0:T(8,128)(2,1)}, u32[]{:S(2)}) copy-start(bf16[512,2048]{1,0:T(8,128)(2,1)} %refs_0_.1) | copy-start | bytes 6291460
  18.5 29.2 %all-to-all-start.1 = ((bf16[32,32,512]{2,1,0:T(8,128)(2,1)}), bf16[32,32,512]{2,1,0:T(8,128)(2,1)S(1)}, u32[]{:S(2)}, u32[]{:S(2)}) async-start(bf16[32,32,512]{2,1,0:T(8,128)(2,1)} %bitcast.16), calls=%async_computation.1 | async-start | bytes 2097152 | tf_op jit(solution)/shard_map/all_to_all | solution.py:518
  21.3 18.6 %collective-permute-start.1 = (bf16[272,512]{1,0:T(8,128)(2,1)S(1)}, bf16[272,512]{1,0:T(8,128)(2,1)}, u32[]{:S(2)}, u32[]{:S(2)}) collective-permute-start(bf16[272,512]{1,0:T(8,128)(2,1)S(1)} %get-tuple-element.34.refs_0_.refs_6_), channel_id=1, source_target_pairs={{0,2},{1,3},{2,0},{3,1},{4,6},{5,7},{6,4},{7,5},{8,10},{9,11},{10,... | collective-permute-start | bytes 835592 | tf_op jit(solution)/shard_map/ppermute | solution.py:487
  23.0 16.9 %collective-permute-start = (bf16[272,512]{1,0:T(8,128)(2,1)S(1)}, bf16[272,512]{1,0:T(8,128)(2,1)}, u32[]{:S(2)}, u32[]{:S(2)}) collective-permute-start(bf16[272,512]{1,0:T(8,128)(2,1)S(1)} %get-tuple-element.34.refs_0_.refs_6_), channel_id=1, source_target_pairs={{0,1},{1,0},{2,3},{3,2},{4,5},{5,4},{6,7},{7,6},{8,9},{9,8},{10,11... | collective-permute-start | bytes 835592 | tf_op jit(solution)/shard_map/ppermute | solution.py:487
  40.0 1.9 %collective-permute-start.2 = (bf16[272,512]{1,0:T(8,128)(2,1)}, bf16[272,512]{1,0:T(8,128)(2,1)}, u32[]{:S(2)}, u32[]{:S(2)}) collective-permute-start(bf16[272,512]{1,0:T(8,128)(2,1)} %collective-permute-done.1.refs_2_), channel_id=1, source_target_pairs={{0,1},{1,0},{2,3},{3,2},{4,5},{5,4},{6,7},{7,6},{8,9},{9,8},{10,11... | collective-permute-start | bytes 835592 | tf_op jit(solution)/shard_map/ppermute | solution.py:487
  41.9 1.0 %copy-start.1 = (bf16[512,512]{1,0:T(8,128)(2,1)S(1)}, bf16[512,512]{1,0:T(8,128)(2,1)}, u32[]{:S(2)}) copy-start(bf16[512,512]{1,0:T(8,128)(2,1)} %refs_1_.1) | copy-start | bytes 1572868
  46.8 1.0 copy-start.3
  48.5 1.6 %collective-permute-start.3 = (bf16[256,512]{1,0:T(8,128)(2,1)S(1)}, bf16[256,512]{1,0:T(8,128)(2,1)S(1)}, u32[]{:S(2)}, u32[]{:S(2)}) collective-permute-start(bf16[256,512]{1,0:T(8,128)(2,1)S(1)} %embed.1.emb_ref.refs_1_), channel_id=1, source_target_pairs={{0,1},{1,0},{2,3},{3,2},{4,5},{5,4},{6,7},{7,6},{8,9},{9,8},{10,11... | collective-permute-start | bytes 786440 | tf_op jit(solution)/shard_map/ppermute | solution.py:487
  48.7 9.2 %collective-permute-start.4 = (bf16[256,512]{1,0:T(8,128)(2,1)S(1)}, bf16[256,512]{1,0:T(8,128)(2,1)S(1)}, u32[]{:S(2)}, u32[]{:S(2)}) collective-permute-start(bf16[256,512]{1,0:T(8,128)(2,1)S(1)} %embed.1.emb_ref.refs_1_), channel_id=1, source_target_pairs={{0,2},{1,3},{2,0},{3,1},{4,6},{5,7},{6,4},{7,5},{8,10},{9,11},{10,... | collective-permute-start | bytes 786440 | tf_op jit(solution)/shard_map/ppermute | solution.py:487
  57.8 1.6 %collective-permute-start.5 = (bf16[256,512]{1,0:T(8,128)(2,1)S(1)}, bf16[256,512]{1,0:T(8,128)(2,1)S(1)}, u32[]{:S(2)}, u32[]{:S(2)}) collective-permute-start(bf16[256,512]{1,0:T(8,128)(2,1)S(1)} %collective-permute-done.4.emb_ref.refs_3_), channel_id=1, source_target_pairs={{0,1},{1,0},{2,3},{3,2},{4,5},{5,4},{6,7},{7,6},{8,9},{9,8},{10,11... | collective-permute-start | bytes 786440 | tf_op jit(solution)/shard_map/ppermute | solution.py:487
  68.8 30.8 %copy-start.4 = (bf16[512,1024]{1,0:T(8,128)(2,1)S(1)}, bf16[512,1024]{1,0:T(8,128)(2,1)}, u32[]{:S(2)}) copy-start(bf16[512,1024]{1,0:T(8,128)(2,1)} %copy-done.3) | copy-start | bytes 3145732

commit v11 on v10

--- a/solution.py
+++ b/solution.py
@@ -185,15 +185,21 @@
             slope_ref[:, columns] = sigma + value - value * sigma
 
 
-def prep_kernel(count, index_ref, slots_ref, asked_ref, w_out_ref, *refs):
-    mixed_ref, segc_ref, segr_ref, spread_ref, chosen_ref = refs[count:]
-    events = spread_ref.shape[1]
+def prep_kernel(count, index_ref, w_out_in, *refs):
+    mixed_ref, segc_ref, segr_ref, w_out_ref, sems = refs[count:]
+    (copy,) = start_copies(((w_out_in, w_out_ref),), sems)
+    events = mixed_ref.shape[1]
     for t in range(count):
         place = index_ref[t]
-        mixed_ref[place] = dot_nt(refs[t][0:events, :], w_out_ref[...])
         seg = refs[t][events : events + EXTRA, 0:events].astype(F32)[0:8]
         segr_ref[place] = seg
         segc_ref[place] = jnp.broadcast_to(jnp.transpose(seg)[:, 0:1], segc_ref.shape[1:])
+    copy.wait()
+    for t in range(count):
+        mixed_ref[index_ref[t]] = dot_nt(refs[t][0:events, :], w_out_ref[...])
+
+
+def places_kernel(slots_ref, asked_ref, spread_ref, chosen_ref):
     slot = iota(spread_ref.shape, 0)
     hit = slot == slots_ref[0:1, :]
     for k in range(1, NIDS):
@@ -561,16 +567,25 @@
         jax.ShapeDtypeStruct((count, 8, events), F32),
         jax.ShapeDtypeStruct((slot_count, events), BF16),
     )
-    *prepared, chosen = pl.pallas_call(
+    pinned = [pltpu.HBM(a.shape, a.dtype) for a in prep_shapes]
+    spread, chosen = pl.pallas_call(
+        places_kernel,
+        out_shape=(pinned[3], pltpu.HBM((table.shape[0], slot_count), BF16)),
+        in_specs=[vmem, vmem],
+        out_specs=(vmem, vmem),
+        compiler_params=params(),
+        name="places",
+    )(slots, after(asked, rows))
+    prepared = pl.pallas_call(
         functools.partial(prep_kernel, count),
-        out_shape=tuple(pltpu.HBM(a.shape, a.dtype) for a in prep_shapes)
-        + (jax.ShapeDtypeStruct((table.shape[0], slot_count), BF16),),
-        in_specs=[smem] + [vmem] * (3 + count),
-        out_specs=(vmem,) * 5,
+        out_shape=tuple(pinned[:3]),
+        in_specs=[smem, hbm] + [vmem] * count,
+        out_specs=(vmem,) * 3,
+        scratch_shapes=[pltpu.VMEM(w_out.shape, BF16), pltpu.SemaphoreType.DMA((1,))],
         compiler_params=params(20),
         name="prep",
-    )(index, slots, asked, w_out, *side_blocks)
-    prepared = in_hbm(*prepared)
+    )(index, *in_hbm(w_out), *side_blocks)
+    prepared = in_hbm(*prepared, spread)
     fetched, prepared = lax.optimization_barrier((fetched, prepared))
     embedded = pl.pallas_call(
         embed_kernel,

time: 102 us -> 100 us (0.980)
  Pallas kernels: 27.7 us -> 30 us
  local copies, waits for them, and re-layouts: 2.02 us -> 0.01 us
  blocking collectives: 45 us -> 43.9 us
    pallas_call x1 -> x2, Pallas kernels: 3.84 us -> 6.15 us  [the longest x1 4.26 us: local(): pl.pallas_call(functools.partial(prep_kernel, count), out_shape=tuple(pin...]
    ppermute x6, waiting for transfers between devices: 19.6 us -> 17.5 us  [flip(): return lax.ppermute(value, axis, [(i, i ^ offset) for i in range(count)])]
    unnamed x10 -> x6, local copies, waits for them, and re-layouts: 2.02 us -> 0.01 us
    all_to_all x1, waiting for transfers between devices: 0.01 us -> 1.4 us  [exchange(): return lax.all_to_all(value, axes, split_axis=0, concat_axis=0, tiled=True)]
    all_to_all x2, blocking collectives: 45 us -> 43.9 us  [exchange(): return lax.all_to_all(value, axes, split_axis=0, concat_axis=0, tiled=True)]
  transfers between devices with their start and end apart: 7 -> 7, of which waited for: 4 -> 3; matrix products, arithmetic and copies ran while one was open for 0% -> 0% of each run, Pallas kernels for 12% -> 15%
where the time goes in v11:
time: 100 us; the launch traced here: 99.9 us
  blocking collectives  43.9 us (44%)
  Pallas kernels  30 us (30%)
  waiting for transfers between devices  18.9 us (19%)
  starting transfers between devices  6.19 us (6%)
    all_to_all x2, blocking collectives, exchange(): return lax.all_to_all(value, axes, split_axis=0, concat_axis=0, tiled=True)  43.9 us
    ppermute x6, waiting for transfers between devices, flip(): return lax.ppermute(value, axis, [(i, i ^ offset) for i in range(count)])  17.5 us
    pallas_call x1, Pallas kernels, local(): pl.pallas_call(functools.partial(late_kernel, count), out_shape=(event_sh...  9.39 us
    pallas_call x1, Pallas kernels, local(): pl.pallas_call(early_kernel, out_shape=(jax.ShapeDtypeStruct((2, events,...  7.71 us
    pallas_call x1, Pallas kernels, local(): pl.pallas_call(functools.partial(prep_kernel, count), out_shape=tuple(pin...  4.26 us
    ppermute x6, starting transfers between devices, flip(): return lax.ppermute(value, axis, [(i, i ^ offset) for i in range(count)])  3.39 us
    all_to_all x1, starting transfers between devices, exchange(): return lax.all_to_all(value, axes, split_axis=0, concat_axis=0, tiled=True)  2.8 us
    pallas_call x1, Pallas kernels, local(): pl.pallas_call(select_kernel, out_shape=pltpu.HBM((slot_count, width), BF...  2.51 us
  transfers between devices with their start and end apart: 7, of which 3 were waited for; matrix products, arithmetic and copies ran while one was open for 0% of the time, Pallas kernels for 15%

profile of v11, /device:TPU:0, one launch (start us, length us, event | category | flops | bytes accessed | tf_op | source)
XLA Modules:
  0.0 99.9 jit_solution(9206422666604935876)
XLA Ops:
  0.6 1.1 %slots.1 = (s32[8,256]{1,0:T(8,128)S(1)}, s32[32,32]{1,0:T(8,128)S(1)}, bf16[272,512]{1,0:T(8,128)(2,1)S(1)}) custom-call(s32[2,256]{1,0:T(2,128)} %bitcast.17, s32[2,256]{1,0:T(2,128)} %bitcast.18, s32[1,256]{1,0:T(1,128)} %seg_in.1, bf16[256,512]{1,0:T(8,128)(2,1)} %cot_in.1), custom_call_target="tpu_custom_call" | custom-call | tf_op jit(solution)/shard_map/slots/pallas_call | solution.py:527
  1.7 0.0 copy-start.1
  1.8 14.3 %all_to_all.21 = s32[32,1,32]{2,1,0:T(1,128)S(1)} all-to-all(s32[32,1,32]{2,1,0:T(1,128)S(1)} %bitcast.15), channel_id=1, replica_groups=mesh['table'=8,'ctx'=4] {'table','ctx'}, dimensions={0} | all-to-all | bytes 8192 | tf_op jit(solution)/shard_map/all_to_all | solution.py:524
  16.0 2.5 %select.1 = bf16[1024,512]{1,0:T(8,128)(2,1)} custom-call(s32[32,32]{1,0:T(8,128)S(1)} %bitcast.13, bf16[512,512]{1,0:T(8,128)(2,1)} %table_in.1), custom_call_target="tpu_custom_call" | custom-call | tf_op jit(solution)/shard_map/select/pallas_call | solution.py:546
  18.5 0.0 copy-start
  18.5 2.8 %all-to-all-start.1 = ((bf16[32,32,512]{2,1,0:T(8,128)(2,1)}), bf16[32,32,512]{2,1,0:T(8,128)(2,1)S(1)}, u32[]{:S(2)}, u32[]{:S(2)}) async-start(bf16[32,32,512]{2,1,0:T(8,128)(2,1)} %bitcast.16), calls=%async_computation.1 | async-start | bytes 2097152 | tf_op jit(solution)/shard_map/all_to_all | solution.py:524
  21.3 1.7 %collective-permute-start.1 = (bf16[272,512]{1,0:T(8,128)(2,1)S(1)}, bf16[272,512]{1,0:T(8,128)(2,1)}, u32[]{:S(2)}, u32[]{:S(2)}) collective-permute-start(bf16[272,512]{1,0:T(8,128)(2,1)S(1)} %get-tuple-element.35.refs_0_.refs_6_), channel_id=1, source_target_pairs={{0,2},{1,3},{2,0},{3,1},{4,6},{5,7},{6,4},{7,5},{8,10},{9,11},{10,... | collective-permute-start | bytes 835592 | tf_op jit(solution)/shard_map/ppermute | solution.py:493
  23.0 0.0 collective-permute-start
  23.0 16.9 %collective-permute-done.1.refs_2_ = bf16[272,512]{1,0:T(8,128)(2,1)} collective-permute-done((bf16[272,512]{1,0:T(8,128)(2,1)S(1)}, bf16[272,512]{1,0:T(8,128)(2,1)}, u32[]{:S(2)}, u32[]{:S(2)}) %collective-permute-start.1) | collective-permute-done | bytes 278560 | tf_op jit(solution)/shard_map/ppermute | solution.py:493
  40.0 0.0 collective-permute-start.2
  40.0 1.9 %places.1 = (bf16[1024,256]{1,0:T(8,128)(2,1)}, bf16[512,1024]{1,0:T(8,128)(2,1)}) custom-call(s32[8,256]{1,0:T(8,128)S(1)} %get-tuple-element.33.slots_ref, s32[32,32]{1,0:T(8,128)S(1)} %bitcast.14), custom_call_target="tpu_custom_call" | custom-call | tf_op jit(solution)/shard_map/places/pallas_call | solution.py:571
  41.9 0.0 collective-permute-done.refs_1_
  41.9 0.0 collective-permute-done.2.refs_3_
  41.9 4.3 %prep.1 = (f32[4,256,512]{2,1,0:T(8,128)}, f32[4,256,128]{2,1,0:T(8,128)}, f32[4,8,256]{2,1,0:T(8,128)}) custom-call(s32[4]{0:T(128)S(1)} %iota_xor_fusion.index_ref.refs_0_, bf16[512,512]{1,0:T(8,128)(2,1)} %refs_1_.1, bf16[272,512]{1,0:T(8,128)(2,1)S(1)} %get-tuple-element.35.refs_0_.refs_6_, bf16[272,512]{1,0:T(8,128)(2,1)} %collective-permute-done.refs_1_, ...), custom_call_target="tpu_custom_call" | custom-call | tf_op jit(solution)/shard_map/prep/pallas_call | solution.py:579
  46.2 0.0 copy-done.1
  46.2 1.4 %all-to-all-done.1 = bf16[32,32,512]{2,1,0:T(8,128)(2,1)S(1)} async-done(((bf16[32,32,512]{2,1,0:T(8,128)(2,1)}), bf16[32,32,512]{2,1,0:T(8,128)(2,1)S(1)}, u32[]{:S(2)}, u32[]{:S(2)}) %all-to-all-start.1) | async-done | bytes 1048608 | tf_op jit(solution)/shard_map/all_to_all | solution.py:524
  47.6 0.7 embed.1.emb_ref.refs_1_
  48.3 0.1 collective-permute-start.3
  48.4 1.5 %collective-permute-start.4 = (bf16[256,512]{1,0:T(8,128)(2,1)S(1)}, bf16[256,512]{1,0:T(8,128)(2,1)S(1)}, u32[]{:S(2)}, u32[]{:S(2)}) collective-permute-start(bf16[256,512]{1,0:T(8,128)(2,1)S(1)} %embed.1.emb_ref.refs_1_), channel_id=1, source_target_pairs={{0,2},{1,3},{2,0},{3,1},{4,6},{5,7},{6,4},{7,5},{8,10},{9,11},{10,... | collective-permute-start | bytes 786440 | tf_op jit(solution)/shard_map/ppermute | solution.py:493
  49.9 0.0 collective-permute-done.3.mate_ref.refs_2_
  49.9 0.0 copy-done
  49.9 7.7 %early.1 = (bf16[2,256,2048]{2,1,0:T(8,128)(2,1)S(1)}, f32[2,256,512]{2,1,0:T(8,128)S(1)}, bf16[2,256,512]{2,1,0:T(8,128)(2,1)S(1)}, f32[256,2048]{1,0:T(8,128)S...) custom-call(s32[4]{0:T(128)S(1)} %iota_xor_fusion.index_ref.refs_0_,, ...), custom_call_target="tpu_custom_call" | custom-call | tf_op jit(solution)/shard_map/early/pallas_call | solution.py:599
  57.6 0.0 collective-permute-done.4.emb_ref.refs_3_
  57.6 0.1 collective-permute-start.5
  57.7 0.9 project_far.1.refs_5_
  58.7 0.6 collective-permute-done.5.refs_4_
  59.2 9.4 %late.1 = (bf16[256,512]{1,0:T(8,128)(2,1)}, bf16[1024,512]{1,0:T(8,128)(2,1)S(1)}) custom-call(s32[4]{0:T(128)S(1)} %iota_xor_fusion.index_ref.refs_0_, bf16[256,512]{1,0:T(8,128)(2,1)S(1)} %embed.1.emb_ref.refs_1_, bf16[256,512]{1,0:T(8,128)(2,1)S(1)} %collective-permute-done.3.mate_ref.refs_2_, ...), custom_call_target="tpu_custom_call" | custom-call | tf_op jit(solution)/shard_map/late/pallas_call | solution.py:626
  68.6 0.0 copy-start.2
  68.7 29.6 %all_to_all.22 = bf16[32,32,512]{2,1,0:T(8,128)(2,1)S(1)} all-to-all(bf16[32,32,512]{2,1,0:T(8,128)(2,1)S(1)} %bitcast.12), channel_id=1, replica_groups=mesh['table'=8,'ctx'=4] {'table','ctx'}, dimensions={0} | all-to-all | bytes 2097152 | tf_op jit(solution)/shard_map/all_to_all | solution.py:524
  98.3 0.0 copy-done.2
  98.3 1.5 %collect.1 = f32[512,512]{1,0:T(8,128)} custom-call(bf16[512,1024]{1,0:T(8,128)(2,1)S(1)} %copy-done.2, bf16[1024,512]{1,0:T(8,128)(2,1)S(1)} %bitcast.10), custom_call_target="tpu_custom_call" | custom-call | tf_op jit(solution)/shard_map/collect/pallas_call | solution.py:642
  (1 shorter events, 0.0 us)
Async XLA Ops:
  1.7 44.4 %copy-start.1 = (bf16[272,512]{1,0:T(8,128)(2,1)}, bf16[272,512]{1,0:T(8,128)(2,1)S(1)}, u32[]{:S(2)}) copy-start(bf16[272,512]{1,0:T(8,128)(2,1)S(1)} %get-tuple-element.35.refs_0_.refs_6_) | copy-start | bytes 835588
  18.5 31.4 %copy-start = (bf16[512,2048]{1,0:T(8,128)(2,1)S(1)}, bf16[512,2048]{1,0:T(8,128)(2,1)}, u32[]{:S(2)}) copy-start(bf16[512,2048]{1,0:T(8,128)(2,1)} %refs_0_.1) | copy-start | bytes 6291460
  18.5 29.0 %all-to-all-start.1 = ((bf16[32,32,512]{2,1,0:T(8,128)(2,1)}), bf16[32,32,512]{2,1,0:T(8,128)(2,1)S(1)}, u32[]{:S(2)}, u32[]{:S(2)}) async-start(bf16[32,32,512]{2,1,0:T(8,128)(2,1)} %bitcast.16), calls=%async_computation.1 | async-start | bytes 2097152 | tf_op jit(solution)/shard_map/all_to_all | solution.py:524
  21.3 18.6 %collective-permute-start.1 = (bf16[272,512]{1,0:T(8,128)(2,1)S(1)}, bf16[272,512]{1,0:T(8,128)(2,1)}, u32[]{:S(2)}, u32[]{:S(2)}) collective-permute-start(bf16[272,512]{1,0:T(8,128)(2,1)S(1)} %get-tuple-element.35.refs_0_.refs_6_), channel_id=1, source_target_pairs={{0,2},{1,3},{2,0},{3,1},{4,6},{5,7},{6,4},{7,5},{8,10},{9,11},{10,... | collective-permute-start | bytes 835592 | tf_op jit(solution)/shard_map/ppermute | solution.py:493
  23.0 18.8 %collective-permute-start = (bf16[272,512]{1,0:T(8,128)(2,1)S(1)}, bf16[272,512]{1,0:T(8,128)(2,1)}, u32[]{:S(2)}, u32[]{:S(2)}) collective-permute-start(bf16[272,512]{1,0:T(8,128)(2,1)S(1)} %get-tuple-element.35.refs_0_.refs_6_), channel_id=1, source_target_pairs={{0,1},{1,0},{2,3},{3,2},{4,5},{5,4},{6,7},{7,6},{8,9},{9,8},{10,11... | collective-permute-start | bytes 835592 | tf_op jit(solution)/shard_map/ppermute | solution.py:493
  40.0 1.9 %collective-permute-start.2 = (bf16[272,512]{1,0:T(8,128)(2,1)}, bf16[272,512]{1,0:T(8,128)(2,1)}, u32[]{:S(2)}, u32[]{:S(2)}) collective-permute-start(bf16[272,512]{1,0:T(8,128)(2,1)} %collective-permute-done.1.refs_2_), channel_id=1, source_target_pairs={{0,1},{1,0},{2,3},{3,2},{4,5},{5,4},{6,7},{7,6},{8,9},{9,8},{10,11... | collective-permute-start | bytes 835592 | tf_op jit(solution)/shard_map/ppermute | solution.py:493
  48.3 1.6 %collective-permute-start.3 = (bf16[256,512]{1,0:T(8,128)(2,1)S(1)}, bf16[256,512]{1,0:T(8,128)(2,1)S(1)}, u32[]{:S(2)}, u32[]{:S(2)}) collective-permute-start(bf16[256,512]{1,0:T(8,128)(2,1)S(1)} %embed.1.emb_ref.refs_1_), channel_id=1, source_target_pairs={{0,1},{1,0},{2,3},{3,2},{4,5},{5,4},{6,7},{7,6},{8,9},{9,8},{10,11... | collective-permute-start | bytes 786440 | tf_op jit(solution)/shard_map/ppermute | solution.py:493
  48.4 9.3 %collective-permute-start.4 = (bf16[256,512]{1,0:T(8,128)(2,1)S(1)}, bf16[256,512]{1,0:T(8,128)(2,1)S(1)}, u32[]{:S(2)}, u32[]{:S(2)}) collective-permute-start(bf16[256,512]{1,0:T(8,128)(2,1)S(1)} %embed.1.emb_ref.refs_1_), channel_id=1, source_target_pairs={{0,2},{1,3},{2,0},{3,1},{4,6},{5,7},{6,4},{7,5},{8,10},{9,11},{10,... | collective-permute-start | bytes 786440 | tf_op jit(solution)/shard_map/ppermute | solution.py:493
  57.6 1.6 %collective-permute-start.5 = (bf16[256,512]{1,0:T(8,128)(2,1)S(1)}, bf16[256,512]{1,0:T(8,128)(2,1)S(1)}, u32[]{:S(2)}, u32[]{:S(2)}) collective-permute-start(bf16[256,512]{1,0:T(8,128)(2,1)S(1)} %collective-permute-done.4.emb_ref.refs_3_), channel_id=1, source_target_pairs={{0,1},{1,0},{2,3},{3,2},{4,5},{5,4},{6,7},{7,6},{8,9},{9,8},{10,11... | collective-permute-start | bytes 786440 | tf_op jit(solution)/shard_map/ppermute | solution.py:493
  68.6 29.6 %copy-start.2 = (bf16[512,1024]{1,0:T(8,128)(2,1)S(1)}, bf16[512,1024]{1,0:T(8,128)(2,1)}, u32[]{:S(2)}) copy-start(bf16[512,1024]{1,0:T(8,128)(2,1)} %get-tuple-element.62.chosen_ref) | copy-start | bytes 3145732

commit v12 on v11

--- a/solution.py
+++ b/solution.py
@@ -112,15 +112,16 @@
     step = owners // parts
     columns = jnp.transpose(asked_ref[...])
     lane = iota((capacity, rows), 1)
+    chosen = []
+    for part in range(parts):
+        sources = range(part * step, (part + 1) * step)
+        hits = [jnp.where(lane == columns[:, s : s + 1], 1.0, 0.0) for s in sources]
+        chosen.append(jnp.concatenate(hits, 0).astype(BF16))
+    table_copy.wait()
     copies = []
     for part in range(parts):
-        sources = range(part * step, (part + 1) * step)
-        chosen = [jnp.where(lane == columns[:, s : s + 1], 1.0, 0.0) for s in sources]
-        chosen = jnp.concatenate(chosen, 0).astype(BF16)
-        if part == 0:
-            table_copy.wait()
         place = pl.ds(part * step * capacity, step * capacity)
-        rows_ref[place, :] = dot(chosen, table_ref[...]).astype(BF16)
+        rows_ref[place, :] = dot(chosen[part], table_ref[...]).astype(BF16)
         copy = pltpu.make_async_copy(rows_ref.at[place], out_ref.at[place], sems.at[1 + part])
         copy.start()
         copies.append(copy)
@@ -142,12 +143,12 @@
 
 def collect_kernel(chosen_ref, returned_ref, out_ref, rows_ref, sems):
     parts = sems.shape[0]
-    step = rows_ref.shape[0] // parts
+    step = rows_ref.shape[1] // parts
     copies = []
     for part in range(parts):
         place = pl.ds(part * step, step)
-        rows_ref[place, :] = dot(chosen_ref[place, :], returned_ref[...])
-        copy = pltpu.make_async_copy(rows_ref.at[place], out_ref.at[place], sems.at[part])
+        rows_ref[:, place] = dot(chosen_ref[...], returned_ref[:, place])
+        copy = pltpu.make_async_copy(rows_ref.at[:, place], out_ref.at[:, place], sems.at[part])
         copy.start()
         copies.append(copy)
     for copy in copies:
@@ -179,7 +180,8 @@
         half = dot(normed, w_in_ref[:, columns])
         bend = jnp.tanh(half)
         value = half + half * bend
-        write(columns, value.astype(BF16))
+        kept = value * (0.5 * SCALE) if block == 2 else value
+        write(columns, kept.astype(BF16))
         if slope_ref is not None:
             sigma = 0.5 + 0.5 * bend
             slope_ref[:, columns] = sigma + value - value * sigma
@@ -221,7 +223,7 @@
 
 
 def bent(raw, mask):
-    half = jnp.where(mask, raw * (0.5 * SCALE), HIDDEN)
+    half = jnp.where(mask, raw, HIDDEN)
     raised = (1.0 + jnp.tanh(half)).astype(BF16)
     half = half.astype(BF16)
     one, two = BF16(1.0), BF16(2.0)
@@ -270,7 +272,7 @@
             return dot_nt(self.cut(i, 2, h), self.cut(j, 3, h))
 
         def finish(j, h, raw, mask):
-            half = jnp.where(mask, raw * (0.5 * SCALE), HIDDEN)
+            half = jnp.where(mask, raw, HIDDEN)
             weights = (half + half * jnp.tanh(half)).astype(BF16)
             att_ref[:, head(0, h, self.width)] += dot(weights, self.cut(j, 1, h))
 
@@ -471,7 +473,7 @@
     for block in range(4):
         columns = slice(block * width, (block + 1) * width)
         joined = join_ref[:, columns] * slope_ref[:, columns]
-        if block >= 2:
+        if block == 2:
             joined = joined * (0.5 * SCALE)
         part = dot_nt(joined.astype(BF16), w_in_ref[:, columns])
         grad_normed = part if block == 0 else grad_normed + part
@@ -644,7 +646,7 @@
         out_shape=pltpu.HBM(table.shape, F32),
         in_specs=[vmem, vmem],
         out_specs=hbm,
-        scratch_shapes=[pltpu.VMEM(table.shape, F32), pltpu.SemaphoreType.DMA((4,))],
+        scratch_shapes=[pltpu.VMEM(table.shape, F32), pltpu.SemaphoreType.DMA((2,))],
         compiler_params=params(),
         name="collect",
     )(chosen, returned)

time: 100 us -> 100 us (level)
  no operation moved by 1% of the time
where the time goes in v12:
time: 100 us; the launch traced here: 99.9 us
  blocking collectives  44 us (44%)
  Pallas kernels  29.9 us (30%)
  waiting for transfers between devices  18.9 us (19%)
  starting transfers between devices  6.19 us (6%)
    all_to_all x2, blocking collectives, exchange(): return lax.all_to_all(value, axes, split_axis=0, concat_axis=0, tiled=True)  44 us
    ppermute x6, waiting for transfers between devices, flip(): return lax.ppermute(value, axis, [(i, i ^ offset) for i in range(count)])  17.5 us
    pallas_call x1, Pallas kernels, local(): pl.pallas_call(functools.partial(late_kernel, count), out_shape=(event_sh...  9.17 us
    pallas_call x1, Pallas kernels, local(): pl.pallas_call(early_kernel, out_shape=(jax.ShapeDtypeStruct((2, events,...  7.62 us
    pallas_call x1, Pallas kernels, local(): pl.pallas_call(functools.partial(prep_kernel, count), out_shape=tuple(pin...  4.26 us
    ppermute x6, starting transfers between devices, flip(): return lax.ppermute(value, axis, [(i, i ^ offset) for i in range(count)])  3.39 us
    all_to_all x1, starting transfers between devices, exchange(): return lax.all_to_all(value, axes, split_axis=0, concat_axis=0, tiled=True)  2.8 us
    pallas_call x1, Pallas kernels, local(): pl.pallas_call(select_kernel, out_shape=pltpu.HBM((slot_count, width), BF...  2.5 us
  transfers between devices with their start and end apart: 7, of which 3 were waited for; matrix products, arithmetic and copies ran while one was open for 0% of the time, Pallas kernels for 15%

profile of v12, /device:TPU:0, one launch (start us, length us, event | category | flops | bytes accessed | tf_op | source)
XLA Modules:
  0.0 99.9 jit_solution(5213539930206871379)
XLA Ops:
  0.6 1.1 %slots.1 = (s32[8,256]{1,0:T(8,128)S(1)}, s32[32,32]{1,0:T(8,128)S(1)}, bf16[272,512]{1,0:T(8,128)(2,1)S(1)}) custom-call(s32[2,256]{1,0:T(2,128)} %bitcast.17, s32[2,256]{1,0:T(2,128)} %bitcast.18, s32[1,256]{1,0:T(1,128)} %seg_in.1, bf16[256,512]{1,0:T(8,128)(2,1)} %cot_in.1), custom_call_target="tpu_custom_call" | custom-call | tf_op jit(solution)/shard_map/slots/pallas_call | solution.py:529
  1.7 0.0 copy-start.1
  1.8 14.3 %all_to_all.21 = s32[32,1,32]{2,1,0:T(1,128)S(1)} all-to-all(s32[32,1,32]{2,1,0:T(1,128)S(1)} %bitcast.15), channel_id=1, replica_groups=mesh['table'=8,'ctx'=4] {'table','ctx'}, dimensions={0} | all-to-all | bytes 8192 | tf_op jit(solution)/shard_map/all_to_all | solution.py:526
  16.0 2.5 %select.1 = bf16[1024,512]{1,0:T(8,128)(2,1)} custom-call(s32[32,32]{1,0:T(8,128)S(1)} %bitcast.13, bf16[512,512]{1,0:T(8,128)(2,1)} %table_in.1), custom_call_target="tpu_custom_call" | custom-call | tf_op jit(solution)/shard_map/select/pallas_call | solution.py:548
  18.5 0.0 copy-start
  18.5 2.8 %all-to-all-start.1 = ((bf16[32,32,512]{2,1,0:T(8,128)(2,1)}), bf16[32,32,512]{2,1,0:T(8,128)(2,1)S(1)}, u32[]{:S(2)}, u32[]{:S(2)}) async-start(bf16[32,32,512]{2,1,0:T(8,128)(2,1)} %bitcast.16), calls=%async_computation.1 | async-start | bytes 2097152 | tf_op jit(solution)/shard_map/all_to_all | solution.py:526
  21.3 1.7 %collective-permute-start.1 = (bf16[272,512]{1,0:T(8,128)(2,1)S(1)}, bf16[272,512]{1,0:T(8,128)(2,1)}, u32[]{:S(2)}, u32[]{:S(2)}) collective-permute-start(bf16[272,512]{1,0:T(8,128)(2,1)S(1)} %get-tuple-element.35.refs_0_.refs_6_), channel_id=1, source_target_pairs={{0,2},{1,3},{2,0},{3,1},{4,6},{5,7},{6,4},{7,5},{8,10},{9,11},{10,... | collective-permute-start | bytes 835592 | tf_op jit(solution)/shard_map/ppermute | solution.py:495
  23.0 0.0 collective-permute-start
  23.0 16.9 %collective-permute-done.1.refs_2_ = bf16[272,512]{1,0:T(8,128)(2,1)} collective-permute-done((bf16[272,512]{1,0:T(8,128)(2,1)S(1)}, bf16[272,512]{1,0:T(8,128)(2,1)}, u32[]{:S(2)}, u32[]{:S(2)}) %collective-permute-start.1) | collective-permute-done | bytes 278560 | tf_op jit(solution)/shard_map/ppermute | solution.py:495
  40.0 0.0 collective-permute-start.2
  40.0 1.9 %places.1 = (bf16[1024,256]{1,0:T(8,128)(2,1)}, bf16[512,1024]{1,0:T(8,128)(2,1)}) custom-call(s32[8,256]{1,0:T(8,128)S(1)} %get-tuple-element.33.slots_ref, s32[32,32]{1,0:T(8,128)S(1)} %bitcast.14), custom_call_target="tpu_custom_call" | custom-call | tf_op jit(solution)/shard_map/places/pallas_call | solution.py:573
  41.9 0.0 collective-permute-done.refs_1_
  41.9 0.0 collective-permute-done.2.refs_3_
  41.9 4.3 %prep.1 = (f32[4,256,512]{2,1,0:T(8,128)}, f32[4,256,128]{2,1,0:T(8,128)}, f32[4,8,256]{2,1,0:T(8,128)}) custom-call(s32[4]{0:T(128)S(1)} %iota_xor_fusion.index_ref.refs_0_, bf16[512,512]{1,0:T(8,128)(2,1)} %refs_1_.1, bf16[272,512]{1,0:T(8,128)(2,1)S(1)} %get-tuple-element.35.refs_0_.refs_6_, bf16[272,512]{1,0:T(8,128)(2,1)} %collective-permute-done.refs_1_, ...), custom_call_target="tpu_custom_call" | custom-call | tf_op jit(solution)/shard_map/prep/pallas_call | solution.py:581
  46.1 0.0 copy-done.1
  46.2 1.4 %all-to-all-done.1 = bf16[32,32,512]{2,1,0:T(8,128)(2,1)S(1)} async-done(((bf16[32,32,512]{2,1,0:T(8,128)(2,1)}), bf16[32,32,512]{2,1,0:T(8,128)(2,1)S(1)}, u32[]{:S(2)}, u32[]{:S(2)}) %all-to-all-start.1) | async-done | bytes 1048608 | tf_op jit(solution)/shard_map/all_to_all | solution.py:526
  47.6 0.7 embed.1.emb_ref.refs_1_
  48.3 0.1 collective-permute-start.3
  48.3 1.5 %collective-permute-start.4 = (bf16[256,512]{1,0:T(8,128)(2,1)S(1)}, bf16[256,512]{1,0:T(8,128)(2,1)S(1)}, u32[]{:S(2)}, u32[]{:S(2)}) collective-permute-start(bf16[256,512]{1,0:T(8,128)(2,1)S(1)} %embed.1.emb_ref.refs_1_), channel_id=1, source_target_pairs={{0,2},{1,3},{2,0},{3,1},{4,6},{5,7},{6,4},{7,5},{8,10},{9,11},{10,... | collective-permute-start | bytes 786440 | tf_op jit(solution)/shard_map/ppermute | solution.py:495
  49.9 0.0 collective-permute-done.3.mate_ref.refs_2_
  49.9 0.0 copy-done
  49.9 7.6 %early.1 = (bf16[2,256,2048]{2,1,0:T(8,128)(2,1)S(1)}, f32[2,256,512]{2,1,0:T(8,128)S(1)}, bf16[2,256,512]{2,1,0:T(8,128)(2,1)S(1)}, f32[256,2048]{1,0:T(8,128)S...) custom-call(s32[4]{0:T(128)S(1)} %iota_xor_fusion.index_ref.refs_0_,, ...), custom_call_target="tpu_custom_call" | custom-call | tf_op jit(solution)/shard_map/early/pallas_call | solution.py:601
  57.5 0.0 collective-permute-done.4.emb_ref.refs_3_
  57.5 0.1 collective-permute-start.5
  57.6 0.9 project_far.1.refs_5_
  58.6 0.6 collective-permute-done.5.refs_4_
  59.1 9.2 %late.1 = (bf16[256,512]{1,0:T(8,128)(2,1)}, bf16[1024,512]{1,0:T(8,128)(2,1)S(1)}) custom-call(s32[4]{0:T(128)S(1)} %iota_xor_fusion.index_ref.refs_0_, bf16[256,512]{1,0:T(8,128)(2,1)S(1)} %embed.1.emb_ref.refs_1_, bf16[256,512]{1,0:T(8,128)(2,1)S(1)} %collective-permute-done.3.mate_ref.refs_2_, ...), custom_call_target="tpu_custom_call" | custom-call | tf_op jit(solution)/shard_map/late/pallas_call | solution.py:628
  68.3 0.0 copy-start.2
  68.3 29.8 %all_to_all.22 = bf16[32,32,512]{2,1,0:T(8,128)(2,1)S(1)} all-to-all(bf16[32,32,512]{2,1,0:T(8,128)(2,1)S(1)} %bitcast.12), channel_id=1, replica_groups=mesh['table'=8,'ctx'=4] {'table','ctx'}, dimensions={0} | all-to-all | bytes 2097152 | tf_op jit(solution)/shard_map/all_to_all | solution.py:526
  98.1 0.0 copy-done.2
  98.1 1.7 %collect.1 = f32[512,512]{1,0:T(8,128)} custom-call(bf16[512,1024]{1,0:T(8,128)(2,1)S(1)} %copy-done.2, bf16[1024,512]{1,0:T(8,128)(2,1)S(1)} %bitcast.10), custom_call_target="tpu_custom_call" | custom-call | tf_op jit(solution)/shard_map/collect/pallas_call | solution.py:644
  (1 shorter events, 0.0 us)
Async XLA Ops:
  1.7 44.4 %copy-start.1 = (bf16[272,512]{1,0:T(8,128)(2,1)}, bf16[272,512]{1,0:T(8,128)(2,1)S(1)}, u32[]{:S(2)}) copy-start(bf16[272,512]{1,0:T(8,128)(2,1)S(1)} %get-tuple-element.35.refs_0_.refs_6_) | copy-start | bytes 835588
  18.5 31.4 %copy-start = (bf16[512,2048]{1,0:T(8,128)(2,1)S(1)}, bf16[512,2048]{1,0:T(8,128)(2,1)}, u32[]{:S(2)}) copy-start(bf16[512,2048]{1,0:T(8,128)(2,1)} %refs_0_.1) | copy-start | bytes 6291460
  18.5 29.0 %all-to-all-start.1 = ((bf16[32,32,512]{2,1,0:T(8,128)(2,1)}), bf16[32,32,512]{2,1,0:T(8,128)(2,1)S(1)}, u32[]{:S(2)}, u32[]{:S(2)}) async-start(bf16[32,32,512]{2,1,0:T(8,128)(2,1)} %bitcast.16), calls=%async_computation.1 | async-start | bytes 2097152 | tf_op jit(solution)/shard_map/all_to_all | solution.py:526
  21.3 18.6 %collective-permute-start.1 = (bf16[272,512]{1,0:T(8,128)(2,1)S(1)}, bf16[272,512]{1,0:T(8,128)(2,1)}, u32[]{:S(2)}, u32[]{:S(2)}) collective-permute-start(bf16[272,512]{1,0:T(8,128)(2,1)S(1)} %get-tuple-element.35.refs_0_.refs_6_), channel_id=1, source_target_pairs={{0,2},{1,3},{2,0},{3,1},{4,6},{5,7},{6,4},{7,5},{8,10},{9,11},{10,... | collective-permute-start | bytes 835592 | tf_op jit(solution)/shard_map/ppermute | solution.py:495
  23.0 18.8 %collective-permute-start = (bf16[272,512]{1,0:T(8,128)(2,1)S(1)}, bf16[272,512]{1,0:T(8,128)(2,1)}, u32[]{:S(2)}, u32[]{:S(2)}) collective-permute-start(bf16[272,512]{1,0:T(8,128)(2,1)S(1)} %get-tuple-element.35.refs_0_.refs_6_), channel_id=1, source_target_pairs={{0,1},{1,0},{2,3},{3,2},{4,5},{5,4},{6,7},{7,6},{8,9},{9,8},{10,11... | collective-permute-start | bytes 835592 | tf_op jit(solution)/shard_map/ppermute | solution.py:495
  40.0 1.9 %collective-permute-start.2 = (bf16[272,512]{1,0:T(8,128)(2,1)}, bf16[272,512]{1,0:T(8,128)(2,1)}, u32[]{:S(2)}, u32[]{:S(2)}) collective-permute-start(bf16[272,512]{1,0:T(8,128)(2,1)} %collective-permute-done.1.refs_2_), channel_id=1, source_target_pairs={{0,1},{1,0},{2,3},{3,2},{4,5},{5,4},{6,7},{7,6},{8,9},{9,8},{10,11... | collective-permute-start | bytes 835592 | tf_op jit(solution)/shard_map/ppermute | solution.py:495
  48.3 1.6 %collective-permute-start.3 = (bf16[256,512]{1,0:T(8,128)(2,1)S(1)}, bf16[256,512]{1,0:T(8,128)(2,1)S(1)}, u32[]{:S(2)}, u32[]{:S(2)}) collective-permute-start(bf16[256,512]{1,0:T(8,128)(2,1)S(1)} %embed.1.emb_ref.refs_1_), channel_id=1, source_target_pairs={{0,1},{1,0},{2,3},{3,2},{4,5},{5,4},{6,7},{7,6},{8,9},{9,8},{10,11... | collective-permute-start | bytes 786440 | tf_op jit(solution)/shard_map/ppermute | solution.py:495
  48.3 9.2 %collective-permute-start.4 = (bf16[256,512]{1,0:T(8,128)(2,1)S(1)}, bf16[256,512]{1,0:T(8,128)(2,1)S(1)}, u32[]{:S(2)}, u32[]{:S(2)}) collective-permute-start(bf16[256,512]{1,0:T(8,128)(2,1)S(1)} %embed.1.emb_ref.refs_1_), channel_id=1, source_target_pairs={{0,2},{1,3},{2,0},{3,1},{4,6},{5,7},{6,4},{7,5},{8,10},{9,11},{10,... | collective-permute-start | bytes 786440 | tf_op jit(solution)/shard_map/ppermute | solution.py:495
  57.5 1.6 %collective-permute-start.5 = (bf16[256,512]{1,0:T(8,128)(2,1)S(1)}, bf16[256,512]{1,0:T(8,128)(2,1)S(1)}, u32[]{:S(2)}, u32[]{:S(2)}) collective-permute-start(bf16[256,512]{1,0:T(8,128)(2,1)S(1)} %collective-permute-done.4.emb_ref.refs_3_), channel_id=1, source_target_pairs={{0,1},{1,0},{2,3},{3,2},{4,5},{5,4},{6,7},{7,6},{8,9},{9,8},{10,11... | collective-permute-start | bytes 786440 | tf_op jit(solution)/shard_map/ppermute | solution.py:495
  68.3 29.8 %copy-start.2 = (bf16[512,1024]{1,0:T(8,128)(2,1)S(1)}, bf16[512,1024]{1,0:T(8,128)(2,1)}, u32[]{:S(2)}) copy-start(bf16[512,1024]{1,0:T(8,128)(2,1)} %get-tuple-element.62.chosen_ref) | copy-start | bytes 3145732

commit v13 on v11

--- a/solution.py
+++ b/solution.py
@@ -354,7 +354,7 @@
 
     project(emb_ref[...], w_in_in, write_to(own), slope_ref)
     project(mate_ref[...], w_in_in, write_to(mate), None)
-    for copy in copies:
+    for copy in copies[:2]:
         copy.wait()
     att_ref[...] = jnp.zeros_like(att_ref)
     join_ref[...] = jnp.zeros_like(join_ref)
@@ -368,6 +368,8 @@
         return 0
 
     lax.fori_loop(own - base, last - base + 1, forward, 0)
+    for copy in copies[2:]:
+        copy.wait()
 
     @pl.when(base == 0)
     def _():
@@ -644,7 +646,7 @@
         out_shape=pltpu.HBM(table.shape, F32),
         in_specs=[vmem, vmem],
         out_specs=hbm,
-        scratch_shapes=[pltpu.VMEM(table.shape, F32), pltpu.SemaphoreType.DMA((4,))],
+        scratch_shapes=[pltpu.VMEM(table.shape, F32), pltpu.SemaphoreType.DMA((2,))],
         compiler_params=params(),
         name="collect",
     )(chosen, returned)

time: 100 us -> 100 us (level)
  no operation moved by 1% of the time
where the time goes in v13:
time: 100 us; the launch traced here: 99.9 us
  blocking collectives  43.9 us (44%)
  Pallas kernels  30 us (30%)
  waiting for transfers between devices  18.9 us (19%)
  starting transfers between devices  6.19 us (6%)
    all_to_all x2, blocking collectives, exchange(): return lax.all_to_all(value, axes, split_axis=0, concat_axis=0, tiled=True)  43.9 us
    ppermute x6, waiting for transfers between devices, flip(): return lax.ppermute(value, axis, [(i, i ^ offset) for i in range(count)])  17.5 us
    pallas_call x1, Pallas kernels, local(): pl.pallas_call(functools.partial(late_kernel, count), out_shape=(event_sh...  9.39 us
    pallas_call x1, Pallas kernels, local(): pl.pallas_call(early_kernel, out_shape=(jax.ShapeDtypeStruct((2, events,...  7.7 us
    pallas_call x1, Pallas kernels, local(): pl.pallas_call(functools.partial(prep_kernel, count), out_shape=tuple(pin...  4.26 us
    ppermute x6, starting transfers between devices, flip(): return lax.ppermute(value, axis, [(i, i ^ offset) for i in range(count)])  3.39 us
    all_to_all x1, starting transfers between devices, exchange(): return lax.all_to_all(value, axes, split_axis=0, concat_axis=0, tiled=True)  2.8 us
    pallas_call x1, Pallas kernels, local(): pl.pallas_call(select_kernel, out_shape=pltpu.HBM((slot_count, width), BF...  2.51 us
  transfers between devices with their start and end apart: 7, of which 3 were waited for; matrix products, arithmetic and copies ran while one was open for 0% of the time, Pallas kernels for 15%

profile of v13, /device:TPU:0, one launch (start us, length us, event | category | flops | bytes accessed | tf_op | source)
XLA Modules:
  0.0 99.9 jit_solution(8145994363435287996)
XLA Ops:
  0.6 1.1 %slots.1 = (s32[8,256]{1,0:T(8,128)S(1)}, s32[32,32]{1,0:T(8,128)S(1)}, bf16[272,512]{1,0:T(8,128)(2,1)S(1)}) custom-call(s32[2,256]{1,0:T(2,128)} %bitcast.17, s32[2,256]{1,0:T(2,128)} %bitcast.18, s32[1,256]{1,0:T(1,128)} %seg_in.1, bf16[256,512]{1,0:T(8,128)(2,1)} %cot_in.1), custom_call_target="tpu_custom_call" | custom-call | tf_op jit(solution)/shard_map/slots/pallas_call | solution.py:529
  1.7 0.0 copy-start.1
  1.8 14.3 %all_to_all.21 = s32[32,1,32]{2,1,0:T(1,128)S(1)} all-to-all(s32[32,1,32]{2,1,0:T(1,128)S(1)} %bitcast.15), channel_id=1, replica_groups=mesh['table'=8,'ctx'=4] {'table','ctx'}, dimensions={0} | all-to-all | bytes 8192 | tf_op jit(solution)/shard_map/all_to_all | solution.py:526
  16.0 2.5 %select.1 = bf16[1024,512]{1,0:T(8,128)(2,1)} custom-call(s32[32,32]{1,0:T(8,128)S(1)} %bitcast.13, bf16[512,512]{1,0:T(8,128)(2,1)} %table_in.1), custom_call_target="tpu_custom_call" | custom-call | tf_op jit(solution)/shard_map/select/pallas_call | solution.py:548
  18.5 0.0 copy-start
  18.5 2.8 %all-to-all-start.1 = ((bf16[32,32,512]{2,1,0:T(8,128)(2,1)}), bf16[32,32,512]{2,1,0:T(8,128)(2,1)S(1)}, u32[]{:S(2)}, u32[]{:S(2)}) async-start(bf16[32,32,512]{2,1,0:T(8,128)(2,1)} %bitcast.16), calls=%async_computation.1 | async-start | bytes 2097152 | tf_op jit(solution)/shard_map/all_to_all | solution.py:526
  21.3 1.7 %collective-permute-start.1 = (bf16[272,512]{1,0:T(8,128)(2,1)S(1)}, bf16[272,512]{1,0:T(8,128)(2,1)}, u32[]{:S(2)}, u32[]{:S(2)}) collective-permute-start(bf16[272,512]{1,0:T(8,128)(2,1)S(1)} %get-tuple-element.35.refs_0_.refs_6_), channel_id=1, source_target_pairs={{0,2},{1,3},{2,0},{3,1},{4,6},{5,7},{6,4},{7,5},{8,10},{9,11},{10,... | collective-permute-start | bytes 835592 | tf_op jit(solution)/shard_map/ppermute | solution.py:495
  23.0 0.0 collective-permute-start
  23.0 16.9 %collective-permute-done.1.refs_2_ = bf16[272,512]{1,0:T(8,128)(2,1)} collective-permute-done((bf16[272,512]{1,0:T(8,128)(2,1)S(1)}, bf16[272,512]{1,0:T(8,128)(2,1)}, u32[]{:S(2)}, u32[]{:S(2)}) %collective-permute-start.1) | collective-permute-done | bytes 278560 | tf_op jit(solution)/shard_map/ppermute | solution.py:495
  40.0 0.0 collective-permute-start.2
  40.0 1.9 %places.1 = (bf16[1024,256]{1,0:T(8,128)(2,1)}, bf16[512,1024]{1,0:T(8,128)(2,1)}) custom-call(s32[8,256]{1,0:T(8,128)S(1)} %get-tuple-element.33.slots_ref, s32[32,32]{1,0:T(8,128)S(1)} %bitcast.14), custom_call_target="tpu_custom_call" | custom-call | tf_op jit(solution)/shard_map/places/pallas_call | solution.py:573
  41.9 0.0 collective-permute-done.refs_1_
  41.9 0.0 collective-permute-done.2.refs_3_
  41.9 4.3 %prep.1 = (f32[4,256,512]{2,1,0:T(8,128)}, f32[4,256,128]{2,1,0:T(8,128)}, f32[4,8,256]{2,1,0:T(8,128)}) custom-call(s32[4]{0:T(128)S(1)} %iota_xor_fusion.index_ref.refs_0_, bf16[512,512]{1,0:T(8,128)(2,1)} %refs_1_.1, bf16[272,512]{1,0:T(8,128)(2,1)S(1)} %get-tuple-element.35.refs_0_.refs_6_, bf16[272,512]{1,0:T(8,128)(2,1)} %collective-permute-done.refs_1_, ...), custom_call_target="tpu_custom_call" | custom-call | tf_op jit(solution)/shard_map/prep/pallas_call | solution.py:581
  46.2 0.0 copy-done.1
  46.2 1.4 %all-to-all-done.1 = bf16[32,32,512]{2,1,0:T(8,128)(2,1)S(1)} async-done(((bf16[32,32,512]{2,1,0:T(8,128)(2,1)}), bf16[32,32,512]{2,1,0:T(8,128)(2,1)S(1)}, u32[]{:S(2)}, u32[]{:S(2)}) %all-to-all-start.1) | async-done | bytes 1048608 | tf_op jit(solution)/shard_map/all_to_all | solution.py:526
  47.6 0.7 embed.1.emb_ref.refs_1_
  48.3 0.1 collective-permute-start.3
  48.4 1.5 %collective-permute-start.4 = (bf16[256,512]{1,0:T(8,128)(2,1)S(1)}, bf16[256,512]{1,0:T(8,128)(2,1)S(1)}, u32[]{:S(2)}, u32[]{:S(2)}) collective-permute-start(bf16[256,512]{1,0:T(8,128)(2,1)S(1)} %embed.1.emb_ref.refs_1_), channel_id=1, source_target_pairs={{0,2},{1,3},{2,0},{3,1},{4,6},{5,7},{6,4},{7,5},{8,10},{9,11},{10,... | collective-permute-start | bytes 786440 | tf_op jit(solution)/shard_map/ppermute | solution.py:495
  49.9 0.0 collective-permute-done.3.mate_ref.refs_2_
  49.9 0.0 copy-done
  49.9 7.7 %early.1 = (bf16[2,256,2048]{2,1,0:T(8,128)(2,1)S(1)}, f32[2,256,512]{2,1,0:T(8,128)S(1)}, bf16[2,256,512]{2,1,0:T(8,128)(2,1)S(1)}, f32[256,2048]{1,0:T(8,128)S...) custom-call(s32[4]{0:T(128)S(1)} %iota_xor_fusion.index_ref.refs_0_,, ...), custom_call_target="tpu_custom_call" | custom-call | tf_op jit(solution)/shard_map/early/pallas_call | solution.py:601
  57.6 0.0 collective-permute-done.4.emb_ref.refs_3_
  57.6 0.1 collective-permute-start.5
  57.7 0.9 project_far.1.refs_5_
  58.7 0.6 collective-permute-done.5.refs_4_
  59.2 9.4 %late.1 = (bf16[256,512]{1,0:T(8,128)(2,1)}, bf16[1024,512]{1,0:T(8,128)(2,1)S(1)}) custom-call(s32[4]{0:T(128)S(1)} %iota_xor_fusion.index_ref.refs_0_, bf16[256,512]{1,0:T(8,128)(2,1)S(1)} %embed.1.emb_ref.refs_1_, bf16[256,512]{1,0:T(8,128)(2,1)S(1)} %collective-permute-done.3.mate_ref.refs_2_, ...), custom_call_target="tpu_custom_call" | custom-call | tf_op jit(solution)/shard_map/late/pallas_call | solution.py:628
  68.6 0.0 copy-start.2
  68.7 29.6 %all_to_all.22 = bf16[32,32,512]{2,1,0:T(8,128)(2,1)S(1)} all-to-all(bf16[32,32,512]{2,1,0:T(8,128)(2,1)S(1)} %bitcast.12), channel_id=1, replica_groups=mesh['table'=8,'ctx'=4] {'table','ctx'}, dimensions={0} | all-to-all | bytes 2097152 | tf_op jit(solution)/shard_map/all_to_all | solution.py:526
  98.3 0.0 copy-done.2
  98.3 1.5 %collect.1 = f32[512,512]{1,0:T(8,128)} custom-call(bf16[512,1024]{1,0:T(8,128)(2,1)S(1)} %copy-done.2, bf16[1024,512]{1,0:T(8,128)(2,1)S(1)} %bitcast.10), custom_call_target="tpu_custom_call" | custom-call | tf_op jit(solution)/shard_map/collect/pallas_call | solution.py:644
  (1 shorter events, 0.0 us)
Async XLA Ops:
  1.7 44.4 %copy-start.1 = (bf16[272,512]{1,0:T(8,128)(2,1)}, bf16[272,512]{1,0:T(8,128)(2,1)S(1)}, u32[]{:S(2)}) copy-start(bf16[272,512]{1,0:T(8,128)(2,1)S(1)} %get-tuple-element.35.refs_0_.refs_6_) | copy-start | bytes 835588
  18.5 31.4 %copy-start = (bf16[512,2048]{1,0:T(8,128)(2,1)S(1)}, bf16[512,2048]{1,0:T(8,128)(2,1)}, u32[]{:S(2)}) copy-start(bf16[512,2048]{1,0:T(8,128)(2,1)} %refs_0_.1) | copy-start | bytes 6291460
  18.5 29.0 %all-to-all-start.1 = ((bf16[32,32,512]{2,1,0:T(8,128)(2,1)}), bf16[32,32,512]{2,1,0:T(8,128)(2,1)S(1)}, u32[]{:S(2)}, u32[]{:S(2)}) async-start(bf16[32,32,512]{2,1,0:T(8,128)(2,1)} %bitcast.16), calls=%async_computation.1 | async-start | bytes 2097152 | tf_op jit(solution)/shard_map/all_to_all | solution.py:526
  21.3 18.6 %collective-permute-start.1 = (bf16[272,512]{1,0:T(8,128)(2,1)S(1)}, bf16[272,512]{1,0:T(8,128)(2,1)}, u32[]{:S(2)}, u32[]{:S(2)}) collective-permute-start(bf16[272,512]{1,0:T(8,128)(2,1)S(1)} %get-tuple-element.35.refs_0_.refs_6_), channel_id=1, source_target_pairs={{0,2},{1,3},{2,0},{3,1},{4,6},{5,7},{6,4},{7,5},{8,10},{9,11},{10,... | collective-permute-start | bytes 835592 | tf_op jit(solution)/shard_map/ppermute | solution.py:495
  23.0 18.8 %collective-permute-start = (bf16[272,512]{1,0:T(8,128)(2,1)S(1)}, bf16[272,512]{1,0:T(8,128)(2,1)}, u32[]{:S(2)}, u32[]{:S(2)}) collective-permute-start(bf16[272,512]{1,0:T(8,128)(2,1)S(1)} %get-tuple-element.35.refs_0_.refs_6_), channel_id=1, source_target_pairs={{0,1},{1,0},{2,3},{3,2},{4,5},{5,4},{6,7},{7,6},{8,9},{9,8},{10,11... | collective-permute-start | bytes 835592 | tf_op jit(solution)/shard_map/ppermute | solution.py:495
  40.0 1.9 %collective-permute-start.2 = (bf16[272,512]{1,0:T(8,128)(2,1)}, bf16[272,512]{1,0:T(8,128)(2,1)}, u32[]{:S(2)}, u32[]{:S(2)}) collective-permute-start(bf16[272,512]{1,0:T(8,128)(2,1)} %collective-permute-done.1.refs_2_), channel_id=1, source_target_pairs={{0,1},{1,0},{2,3},{3,2},{4,5},{5,4},{6,7},{7,6},{8,9},{9,8},{10,11... | collective-permute-start | bytes 835592 | tf_op jit(solution)/shard_map/ppermute | solution.py:495
  48.3 1.6 %collective-permute-start.3 = (bf16[256,512]{1,0:T(8,128)(2,1)S(1)}, bf16[256,512]{1,0:T(8,128)(2,1)S(1)}, u32[]{:S(2)}, u32[]{:S(2)}) collective-permute-start(bf16[256,512]{1,0:T(8,128)(2,1)S(1)} %embed.1.emb_ref.refs_1_), channel_id=1, source_target_pairs={{0,1},{1,0},{2,3},{3,2},{4,5},{5,4},{6,7},{7,6},{8,9},{9,8},{10,11... | collective-permute-start | bytes 786440 | tf_op jit(solution)/shard_map/ppermute | solution.py:495
  48.4 9.3 %collective-permute-start.4 = (bf16[256,512]{1,0:T(8,128)(2,1)S(1)}, bf16[256,512]{1,0:T(8,128)(2,1)S(1)}, u32[]{:S(2)}, u32[]{:S(2)}) collective-permute-start(bf16[256,512]{1,0:T(8,128)(2,1)S(1)} %embed.1.emb_ref.refs_1_), channel_id=1, source_target_pairs={{0,2},{1,3},{2,0},{3,1},{4,6},{5,7},{6,4},{7,5},{8,10},{9,11},{10,... | collective-permute-start | bytes 786440 | tf_op jit(solution)/shard_map/ppermute | solution.py:495
  57.6 1.6 %collective-permute-start.5 = (bf16[256,512]{1,0:T(8,128)(2,1)S(1)}, bf16[256,512]{1,0:T(8,128)(2,1)S(1)}, u32[]{:S(2)}, u32[]{:S(2)}) collective-permute-start(bf16[256,512]{1,0:T(8,128)(2,1)S(1)} %collective-permute-done.4.emb_ref.refs_3_), channel_id=1, source_target_pairs={{0,1},{1,0},{2,3},{3,2},{4,5},{5,4},{6,7},{7,6},{8,9},{9,8},{10,11... | collective-permute-start | bytes 786440 | tf_op jit(solution)/shard_map/ppermute | solution.py:495
  68.6 29.6 %copy-start.2 = (bf16[512,1024]{1,0:T(8,128)(2,1)S(1)}, bf16[512,1024]{1,0:T(8,128)(2,1)}, u32[]{:S(2)}) copy-start(bf16[512,1024]{1,0:T(8,128)(2,1)} %get-tuple-element.62.chosen_ref) | copy-start | bytes 3145732

commit v14 on v13

--- a/solution.py
+++ b/solution.py
@@ -421,12 +421,15 @@
     closed = base == 0
 
     pair_rows = pl.ds(base, 2)
+    width = gatt_ref.shape[2]
+    gate_part, other_parts = pl.ds(0, width), pl.ds(width, 3 * width)
     copies = start_copies(
         (
-            (join_early_ref, join_ref),
             (proj_pair_ref, proj_ref.at[pair_rows]),
+            (proj_far_ref, proj_ref.at[index_ref[count // 2]]),
             (gatt_pair_ref, gatt_ref.at[pair_rows]),
-            (proj_far_ref, proj_ref.at[index_ref[count // 2]]),
+            (join_early_ref.at[:, gate_part], join_ref.at[:, gate_part]),
+            (join_early_ref.at[:, other_parts], join_ref.at[:, other_parts]),
         ),
         sems,
     )
@@ -441,7 +444,7 @@
         if t == count // 2:
             continue
         project(emb_refs[t][...], w_in_ref, write_to(index_ref[t]), None)
-    for copy in copies:
+    for copy in copies[:4]:
         copy.wait()
     chunks = Chunks(proj_ref, gatt_ref, segc_ref, segr_ref, join_ref)
 
@@ -465,6 +468,7 @@
         return 0
 
     lax.fori_loop(jnp.where(closed, last + 1, own), count, forward, 0)
+    copies[4].wait()
     chunks.query_side(own, jnp.where(closed, own + 1, 0), own + 1)
     chunks.key_side(own, jnp.where(closed, last + 1, own), count)
 
@@ -635,7 +639,7 @@
             pltpu.VMEM((events, width), F32),
             pltpu.VMEM((count, events, width), BF16),
             pltpu.VMEM((events, 4 * width), F32),
-            pltpu.SemaphoreType.DMA((4,)),
+            pltpu.SemaphoreType.DMA((5,)),
         ],
         compiler_params=params(28),
         name="late",

time: 100 us -> 100 us (level)
  no operation moved by 1% of the time
where the time goes in v14:
time: 100 us
  blocking collectives  43.9 us (44%)
  Pallas kernels  30.1 us (30%)
  waiting for transfers between devices  18.9 us (19%)
  starting transfers between devices  6.19 us (6%)
    all_to_all x2, blocking collectives, exchange(): return lax.all_to_all(value, axes, split_axis=0, concat_axis=0, tiled=True)  43.9 us
    ppermute x6, waiting for transfers between devices, flip(): return lax.ppermute(value, axis, [(i, i ^ offset) for i in range(count)])  17.5 us
    pallas_call x1, Pallas kernels, local(): pl.pallas_call(functools.partial(late_kernel, count), out_shape=(event_sh...  9.49 us
    pallas_call x1, Pallas kernels, local(): pl.pallas_call(early_kernel, out_shape=(jax.ShapeDtypeStruct((2, events,...  7.7 us
    pallas_call x1, Pallas kernels, local(): pl.pallas_call(functools.partial(prep_kernel, count), out_shape=tuple(pin...  4.26 us
    ppermute x6, starting transfers between devices, flip(): return lax.ppermute(value, axis, [(i, i ^ offset) for i in range(count)])  3.39 us
    all_to_all x1, starting transfers between devices, exchange(): return lax.all_to_all(value, axes, split_axis=0, concat_axis=0, tiled=True)  2.8 us
    pallas_call x1, Pallas kernels, local(): pl.pallas_call(select_kernel, out_shape=pltpu.HBM((slot_count, width), BF...  2.51 us
  transfers between devices with their start and end apart: 7, of which 3 were waited for; matrix products, arithmetic and copies ran while one was open for 0% of the time, Pallas kernels for 15%

profile of v14, /device:TPU:0, one launch (start us, length us, event | category | flops | bytes accessed | tf_op | source)
XLA Modules:
  0.0 100.0 jit_solution(14299159046492846233)
XLA Ops:
  0.6 1.1 %slots.1 = (s32[8,256]{1,0:T(8,128)S(1)}, s32[32,32]{1,0:T(8,128)S(1)}, bf16[272,512]{1,0:T(8,128)(2,1)S(1)}) custom-call(s32[2,256]{1,0:T(2,128)} %bitcast.17, s32[2,256]{1,0:T(2,128)} %bitcast.18, s32[1,256]{1,0:T(1,128)} %seg_in.1, bf16[256,512]{1,0:T(8,128)(2,1)} %cot_in.1), custom_call_target="tpu_custom_call" | custom-call | tf_op jit(solution)/shard_map/slots/pallas_call | solution.py:533
  1.7 0.0 copy-start.1
  1.8 14.3 %all_to_all.21 = s32[32,1,32]{2,1,0:T(1,128)S(1)} all-to-all(s32[32,1,32]{2,1,0:T(1,128)S(1)} %bitcast.15), channel_id=1, replica_groups=mesh['table'=8,'ctx'=4] {'table','ctx'}, dimensions={0} | all-to-all | bytes 8192 | tf_op jit(solution)/shard_map/all_to_all | solution.py:530
  16.0 2.5 %select.1 = bf16[1024,512]{1,0:T(8,128)(2,1)} custom-call(s32[32,32]{1,0:T(8,128)S(1)} %bitcast.13, bf16[512,512]{1,0:T(8,128)(2,1)} %table_in.1), custom_call_target="tpu_custom_call" | custom-call | tf_op jit(solution)/shard_map/select/pallas_call | solution.py:552
  18.5 0.0 copy-start
  18.5 2.8 %all-to-all-start.1 = ((bf16[32,32,512]{2,1,0:T(8,128)(2,1)}), bf16[32,32,512]{2,1,0:T(8,128)(2,1)S(1)}, u32[]{:S(2)}, u32[]{:S(2)}) async-start(bf16[32,32,512]{2,1,0:T(8,128)(2,1)} %bitcast.16), calls=%async_computation.1 | async-start | bytes 2097152 | tf_op jit(solution)/shard_map/all_to_all | solution.py:530
  21.3 1.7 %collective-permute-start.1 = (bf16[272,512]{1,0:T(8,128)(2,1)S(1)}, bf16[272,512]{1,0:T(8,128)(2,1)}, u32[]{:S(2)}, u32[]{:S(2)}) collective-permute-start(bf16[272,512]{1,0:T(8,128)(2,1)S(1)} %get-tuple-element.35.refs_0_.refs_6_), channel_id=1, source_target_pairs={{0,2},{1,3},{2,0},{3,1},{4,6},{5,7},{6,4},{7,5},{8,10},{9,11},{10,... | collective-permute-start | bytes 835592 | tf_op jit(solution)/shard_map/ppermute | solution.py:499
  23.0 0.0 collective-permute-start
  23.0 16.9 %collective-permute-done.1.refs_2_ = bf16[272,512]{1,0:T(8,128)(2,1)} collective-permute-done((bf16[272,512]{1,0:T(8,128)(2,1)S(1)}, bf16[272,512]{1,0:T(8,128)(2,1)}, u32[]{:S(2)}, u32[]{:S(2)}) %collective-permute-start.1) | collective-permute-done | bytes 278560 | tf_op jit(solution)/shard_map/ppermute | solution.py:499
  40.0 0.0 collective-permute-start.2
  40.0 1.9 %places.1 = (bf16[1024,256]{1,0:T(8,128)(2,1)}, bf16[512,1024]{1,0:T(8,128)(2,1)}) custom-call(s32[8,256]{1,0:T(8,128)S(1)} %get-tuple-element.33.slots_ref, s32[32,32]{1,0:T(8,128)S(1)} %bitcast.14), custom_call_target="tpu_custom_call" | custom-call | tf_op jit(solution)/shard_map/places/pallas_call | solution.py:577
  41.9 0.0 collective-permute-done.refs_1_
  41.9 0.0 collective-permute-done.2.refs_3_
  41.9 4.3 %prep.1 = (f32[4,256,512]{2,1,0:T(8,128)}, f32[4,256,128]{2,1,0:T(8,128)}, f32[4,8,256]{2,1,0:T(8,128)}) custom-call(s32[4]{0:T(128)S(1)} %iota_xor_fusion.index_ref.refs_0_, bf16[512,512]{1,0:T(8,128)(2,1)} %refs_1_.1, bf16[272,512]{1,0:T(8,128)(2,1)S(1)} %get-tuple-element.35.refs_0_.refs_6_, bf16[272,512]{1,0:T(8,128)(2,1)} %collective-permute-done.refs_1_, ...), custom_call_target="tpu_custom_call" | custom-call | tf_op jit(solution)/shard_map/prep/pallas_call | solution.py:585
  46.2 0.0 copy-done.1
  46.2 1.4 %all-to-all-done.1 = bf16[32,32,512]{2,1,0:T(8,128)(2,1)S(1)} async-done(((bf16[32,32,512]{2,1,0:T(8,128)(2,1)}), bf16[32,32,512]{2,1,0:T(8,128)(2,1)S(1)}, u32[]{:S(2)}, u32[]{:S(2)}) %all-to-all-start.1) | async-done | bytes 1048608 | tf_op jit(solution)/shard_map/all_to_all | solution.py:530
  47.6 0.7 embed.1.emb_ref.refs_1_
  48.3 0.1 collective-permute-start.3
  48.4 1.5 %collective-permute-start.4 = (bf16[256,512]{1,0:T(8,128)(2,1)S(1)}, bf16[256,512]{1,0:T(8,128)(2,1)S(1)}, u32[]{:S(2)}, u32[]{:S(2)}) collective-permute-start(bf16[256,512]{1,0:T(8,128)(2,1)S(1)} %embed.1.emb_ref.refs_1_), channel_id=1, source_target_pairs={{0,2},{1,3},{2,0},{3,1},{4,6},{5,7},{6,4},{7,5},{8,10},{9,11},{10,... | collective-permute-start | bytes 786440 | tf_op jit(solution)/shard_map/ppermute | solution.py:499
  49.9 0.0 collective-permute-done.3.mate_ref.refs_2_
  49.9 0.0 copy-done
  49.9 7.7 %early.1 = (bf16[2,256,2048]{2,1,0:T(8,128)(2,1)S(1)}, f32[2,256,512]{2,1,0:T(8,128)S(1)}, bf16[2,256,512]{2,1,0:T(8,128)(2,1)S(1)}, f32[256,2048]{1,0:T(8,128)S...) custom-call(s32[4]{0:T(128)S(1)} %iota_xor_fusion.index_ref.refs_0_,, ...), custom_call_target="tpu_custom_call" | custom-call | tf_op jit(solution)/shard_map/early/pallas_call | solution.py:605
  57.6 0.0 collective-permute-done.4.emb_ref.refs_3_
  57.6 0.1 collective-permute-start.5
  57.7 0.9 project_far.1.refs_5_
  58.7 0.6 collective-permute-done.5.refs_4_
  59.2 9.5 %late.1 = (bf16[256,512]{1,0:T(8,128)(2,1)}, bf16[1024,512]{1,0:T(8,128)(2,1)S(1)}) custom-call(s32[4]{0:T(128)S(1)} %iota_xor_fusion.index_ref.refs_0_, bf16[256,512]{1,0:T(8,128)(2,1)S(1)} %embed.1.emb_ref.refs_1_, bf16[256,512]{1,0:T(8,128)(2,1)S(1)} %collective-permute-done.3.mate_ref.refs_2_, ...), custom_call_target="tpu_custom_call" | custom-call | tf_op jit(solution)/shard_map/late/pallas_call | solution.py:632
  68.7 0.0 copy-start.2
  68.7 29.6 %all_to_all.22 = bf16[32,32,512]{2,1,0:T(8,128)(2,1)S(1)} all-to-all(bf16[32,32,512]{2,1,0:T(8,128)(2,1)S(1)} %bitcast.12), channel_id=1, replica_groups=mesh['table'=8,'ctx'=4] {'table','ctx'}, dimensions={0} | all-to-all | bytes 2097152 | tf_op jit(solution)/shard_map/all_to_all | solution.py:530
  98.4 0.0 copy-done.2
  98.4 1.5 %collect.1 = f32[512,512]{1,0:T(8,128)} custom-call(bf16[512,1024]{1,0:T(8,128)(2,1)S(1)} %copy-done.2, bf16[1024,512]{1,0:T(8,128)(2,1)S(1)} %bitcast.10), custom_call_target="tpu_custom_call" | custom-call | tf_op jit(solution)/shard_map/collect/pallas_call | solution.py:648
  (1 shorter events, 0.0 us)
Async XLA Ops:
  1.7 44.4 %copy-start.1 = (bf16[272,512]{1,0:T(8,128)(2,1)}, bf16[272,512]{1,0:T(8,128)(2,1)S(1)}, u32[]{:S(2)}) copy-start(bf16[272,512]{1,0:T(8,128)(2,1)S(1)} %get-tuple-element.35.refs_0_.refs_6_) | copy-start | bytes 835588
  18.5 31.4 %copy-start = (bf16[512,2048]{1,0:T(8,128)(2,1)S(1)}, bf16[512,2048]{1,0:T(8,128)(2,1)}, u32[]{:S(2)}) copy-start(bf16[512,2048]{1,0:T(8,128)(2,1)} %refs_0_.1) | copy-start | bytes 6291460
  18.5 29.0 %all-to-all-start.1 = ((bf16[32,32,512]{2,1,0:T(8,128)(2,1)}), bf16[32,32,512]{2,1,0:T(8,128)(2,1)S(1)}, u32[]{:S(2)}, u32[]{:S(2)}) async-start(bf16[32,32,512]{2,1,0:T(8,128)(2,1)} %bitcast.16), calls=%async_computation.1 | async-start | bytes 2097152 | tf_op jit(solution)/shard_map/all_to_all | solution.py:530
  21.3 18.6 %collective-permute-start.1 = (bf16[272,512]{1,0:T(8,128)(2,1)S(1)}, bf16[272,512]{1,0:T(8,128)(2,1)}, u32[]{:S(2)}, u32[]{:S(2)}) collective-permute-start(bf16[272,512]{1,0:T(8,128)(2,1)S(1)} %get-tuple-element.35.refs_0_.refs_6_), channel_id=1, source_target_pairs={{0,2},{1,3},{2,0},{3,1},{4,6},{5,7},{6,4},{7,5},{8,10},{9,11},{10,... | collective-permute-start | bytes 835592 | tf_op jit(solution)/shard_map/ppermute | solution.py:499
  23.0 18.8 %collective-permute-start = (bf16[272,512]{1,0:T(8,128)(2,1)S(1)}, bf16[272,512]{1,0:T(8,128)(2,1)}, u32[]{:S(2)}, u32[]{:S(2)}) collective-permute-start(bf16[272,512]{1,0:T(8,128)(2,1)S(1)} %get-tuple-element.35.refs_0_.refs_6_), channel_id=1, source_target_pairs={{0,1},{1,0},{2,3},{3,2},{4,5},{5,4},{6,7},{7,6},{8,9},{9,8},{10,11... | collective-permute-start | bytes 835592 | tf_op jit(solution)/shard_map/ppermute | solution.py:499
  40.0 1.9 %collective-permute-start.2 = (bf16[272,512]{1,0:T(8,128)(2,1)}, bf16[272,512]{1,0:T(8,128)(2,1)}, u32[]{:S(2)}, u32[]{:S(2)}) collective-permute-start(bf16[272,512]{1,0:T(8,128)(2,1)} %collective-permute-done.1.refs_2_), channel_id=1, source_target_pairs={{0,1},{1,0},{2,3},{3,2},{4,5},{5,4},{6,7},{7,6},{8,9},{9,8},{10,11... | collective-permute-start | bytes 835592 | tf_op jit(solution)/shard_map/ppermute | solution.py:499
  48.3 1.6 %collective-permute-start.3 = (bf16[256,512]{1,0:T(8,128)(2,1)S(1)}, bf16[256,512]{1,0:T(8,128)(2,1)S(1)}, u32[]{:S(2)}, u32[]{:S(2)}) collective-permute-start(bf16[256,512]{1,0:T(8,128)(2,1)S(1)} %embed.1.emb_ref.refs_1_), channel_id=1, source_target_pairs={{0,1},{1,0},{2,3},{3,2},{4,5},{5,4},{6,7},{7,6},{8,9},{9,8},{10,11... | collective-permute-start | bytes 786440 | tf_op jit(solution)/shard_map/ppermute | solution.py:499
  48.4 9.3 %collective-permute-start.4 = (bf16[256,512]{1,0:T(8,128)(2,1)S(1)}, bf16[256,512]{1,0:T(8,128)(2,1)S(1)}, u32[]{:S(2)}, u32[]{:S(2)}) collective-permute-start(bf16[256,512]{1,0:T(8,128)(2,1)S(1)} %embed.1.emb_ref.refs_1_), channel_id=1, source_target_pairs={{0,2},{1,3},{2,0},{3,1},{4,6},{5,7},{6,4},{7,5},{8,10},{9,11},{10,... | collective-permute-start | bytes 786440 | tf_op jit(solution)/shard_map/ppermute | solution.py:499
  57.6 1.6 %collective-permute-start.5 = (bf16[256,512]{1,0:T(8,128)(2,1)S(1)}, bf16[256,512]{1,0:T(8,128)(2,1)S(1)}, u32[]{:S(2)}, u32[]{:S(2)}) collective-permute-start(bf16[256,512]{1,0:T(8,128)(2,1)S(1)} %collective-permute-done.4.emb_ref.refs_3_), channel_id=1, source_target_pairs={{0,1},{1,0},{2,3},{3,2},{4,5},{5,4},{6,7},{7,6},{8,9},{9,8},{10,11... | collective-permute-start | bytes 786440 | tf_op jit(solution)/shard_map/ppermute | solution.py:499
  68.7 29.6 %copy-start.2 = (bf16[512,1024]{1,0:T(8,128)(2,1)S(1)}, bf16[512,1024]{1,0:T(8,128)(2,1)}, u32[]{:S(2)}) copy-start(bf16[512,1024]{1,0:T(8,128)(2,1)} %get-tuple-element.62.chosen_ref) | copy-start | bytes 3145732
